TPU v7x, 32 devices: a whole 2x2x4 slice. The times are simulated.
32 devices in a mesh: ctx: 4 (over y, core), cand: 4 (over z), tp: 2 (over x).
Axes of the slice: x: 2, y: 2, z: 4, core: 2. Of those that a mesh axis runs over, the one named last changes fastest.
Arguments:
- prompt_q: bfloat16 [1024, 4096], P(('ctx', 'cand'), 'tp'), may hold values from -9 to 9
- prompt_kv: bfloat16 [2, 1024, 512], P(None, ('ctx', 'cand'), 'tp'), may hold values from -48 to 48, as said below
- cand_q: bfloat16 [4, 256, 4096], P('cand', 'ctx', 'tp'), may hold values from -9 to 9
- cand_kv: bfloat16 [2, 4, 256, 512], P(None, 'cand', 'ctx', 'tp'), may hold values from -48 to 48, as said below
- cand_lengths: int32 [4], P('cand'), may hold values from 64 to 256, as said below
- step_ends: int32 [4, 8], P('cand'), may hold values from 0 to 255, as said below
- reward_head: float32 [4096], P('tp'), may hold values from -0.09375 to 0.09375
Outputs:
- prompt_out: bfloat16 [1024, 4096], P(('ctx', 'cand'), 'tp')
- cand_out: bfloat16 [4, 256, 4096], P('cand', 'ctx', 'tp')
- step_logits: float32 [4, 8], P('cand')
Inputs may be any that keep to these rules, and one draw needn't show every extreme that they name: `prompt_kv`: keys lie within -7 to 7. `cand_kv`: keys lie within -7 to 7. `cand_lengths`: at least one candidate uses all 256 positions. `step_ends`: for each candidate, 8 strictly increasing positions below its length, the last one equal to its length minus one.
All inputs are finite; a program needn't handle non-finite values.
Results may differ from a plain program's by a relative error of at most 0.0099.
Values may be sent and summed in bfloat16 or wider, within the bound.
No kernel may reach another device: no remote copies, remote signals or barrier semaphores. Data moves between devices by JAX's collectives and lax.ppermute only.
A program may use at most 192 MiB of HBM per device.

v0:
```python
import jax
import jax.numpy as jnp
from jax import lax
from jax.sharding import PartitionSpec as P

HEADDIM = 128
GROUP = 8


NEG_FILL = -1e30


def regroup(flat_rows, kv_heads):
    row_count = flat_rows.shape[0]
    grouped = flat_rows.reshape(row_count, kv_heads, GROUP, HEADDIM)
    return jnp.transpose(grouped, (1, 0, 2, 3)).reshape(kv_heads, row_count * GROUP, HEADDIM)


def ungroup(blended, kv_heads):
    row_count = blended.shape[1] // GROUP
    grouped = blended.reshape(kv_heads, row_count, GROUP, HEADDIM)
    return jnp.transpose(grouped, (1, 0, 2, 3)).reshape(row_count, kv_heads * GROUP * HEADDIM)


def absorb(states, queries, key_rows, value_rows, allowed):
    old_peak, totals, weighted = states
    scores = jnp.einsum(
        "hrd,nhd->hrn", queries, key_rows, preferred_element_type=jnp.float32
    ) * HEADDIM ** (-0.5)
    if allowed is not None:
        scores = jnp.where(allowed[None], scores, NEG_FILL)
    new_peak = jnp.maximum(old_peak, jnp.max(scores, axis=-1))
    weights = jnp.exp(scores - new_peak[..., None])
    if allowed is not None:
        weights = jnp.where(allowed[None], weights, 0.0)
    shrink = jnp.exp(old_peak - new_peak)
    totals = totals * shrink + jnp.sum(weights, axis=-1)
    weighted = weighted * shrink[..., None] + jnp.einsum(
        "hrn,nhd->hrd", weights.astype(jnp.bfloat16), value_rows, preferred_element_type=jnp.float32
    )
    return (new_peak, totals, weighted)


def empty_state(head_count, row_count):
    return (
        jnp.full((head_count, row_count), NEG_FILL, jnp.float32),
        jnp.zeros((head_count, row_count), jnp.float32),
        jnp.zeros((head_count, row_count, HEADDIM), jnp.float32),
    )


def causal_absorb(state, queries, key_rows, value_rows, key_pos, row_pos, last_pos, offset):

    def taken(current):
        allowed = key_pos[None, :] <= row_pos[:, None]
        return absorb(current, queries, key_rows, value_rows, allowed)

    def skipped(current):
        return current

    return lax.cond(offset <= last_pos, taken, skipped, state)


def per_device(prompt_q, prompt_kv, cand_q, cand_kv, cand_lengths, step_ends, reward_head):
    kv_heads = prompt_kv.shape[2] // HEADDIM
    prompt_count = prompt_q.shape[0]
    cand_count = cand_q.shape[1]
    ctx_index = lax.axis_index("ctx")
    group_index = lax.axis_index("cand")
    groups = lax.axis_size("cand")
    cand_pos = ctx_index * cand_count + jnp.arange(cand_count, dtype=jnp.int32)
    alive_rows = cand_pos < cand_lengths[0]
    prompt_pos = (ctx_index * groups + group_index) * prompt_count + jnp.arange(
        prompt_count, dtype=jnp.int32
    )
    prompt_heads = regroup(prompt_q, kv_heads)
    cand_heads = regroup(cand_q[0], kv_heads)
    prompt_rowpos = jnp.repeat(prompt_pos, GROUP)
    cand_rowpos = jnp.repeat(cand_pos, GROUP)
    last_pos = prompt_pos[prompt_count - 1]
    starting = (
        empty_state(kv_heads, prompt_heads.shape[1]),
        empty_state(kv_heads, cand_heads.shape[1]),
    )
    arrived = lax.all_gather(prompt_kv, ("ctx", "cand"), axis=1, tiled=True)
    row_count = arrived.shape[1]
    key_rows = arrived[0].reshape(row_count, kv_heads, HEADDIM)
    value_rows = arrived[1].reshape(row_count, kv_heads, HEADDIM)
    key_pos = jnp.arange(row_count, dtype=jnp.int32)
    prompt_next = causal_absorb(
        starting[0],
        prompt_heads,
        key_rows,
        value_rows,
        key_pos,
        prompt_rowpos,
        last_pos,
        jnp.int32(0),
    )
    cand_state = absorb(starting[1], cand_heads, key_rows, value_rows, None)
    arrived = lax.all_gather(cand_kv, "ctx", axis=2, tiled=True)
    row_count = arrived.shape[2]
    key_rows = arrived[0, 0].reshape(row_count, kv_heads, HEADDIM)
    value_rows = arrived[1, 0].reshape(row_count, kv_heads, HEADDIM)
    key_pos = jnp.arange(row_count, dtype=jnp.int32)
    allowed = key_pos[None, :] <= cand_rowpos[:, None]
    cand_state = absorb(cand_state, cand_heads, key_rows, value_rows, allowed)
    prompt_out = ungroup(prompt_next[2] / prompt_next[1][..., None], kv_heads).astype(jnp.bfloat16)
    cand_blended = ungroup(cand_state[2] / cand_state[1][..., None], kv_heads)
    cand_rows = jnp.where(alive_rows[:, None], cand_blended, 0.0).astype(jnp.bfloat16)
    partial_logit = jnp.dot(
        cand_rows.astype(jnp.float32), reward_head, precision=lax.Precision.HIGHEST
    )
    step_hits = (step_ends[0][:, None] == cand_pos[None, :]).astype(jnp.float32)
    full_logit = lax.psum(partial_logit, "tp")
    step_logits = lax.psum(jnp.dot(step_hits, full_logit, precision=lax.Precision.HIGHEST), "ctx")
    return (prompt_out, cand_rows[None], step_logits[None])


def solution(mesh):
    placed = (
        P(("ctx", "cand"), "tp"),
        P(None, ("ctx", "cand"), "tp"),
        P("cand", "ctx", "tp"),
        P(None, "cand", "ctx", "tp"),
        P("cand"),
        P("cand", None),
        P("tp"),
    )
    return jax.shard_map(
        per_device,
        mesh=mesh,
        in_specs=placed,
        out_specs=(P(("ctx", "cand"), "tp"), P("cand", "ctx", "tp"), P("cand", None)),
        check_vma=False,
    )
```

profile of v0, /device:TPU:0, one launch (start us, length us, event | category | flops | bytes accessed | tf_op | source)
XLA Modules:
  0.0 91.8 jit_solution(1891458807300076642)
XLA Ops:
  7.2 0.0 copy-start
  7.2 0.0 all-gather.2.cloned.1.call-start
  7.2 1.5 %copy.27 = bf16[2,64,256]{2,0,1:T(2,128)(2,1)} copy(bf16[2,64,256]{2,1,0:T(8,128)(2,1)} %param.10) | data formatting | bytes 131072 | tf_op args[1]
  8.8 0.0 all-gather.2.cloned.1.call-update
  8.8 0.0 copy-start.6
  8.8 0.6 slice.15
  10.0 0.0 copy-done.6
  10.1 1.7 %copy.55 = bf16[8,8,16,128]{3,2,1,0:T(8,128)(2,1)} copy(bf16[8,8,16,128]{3,1,2,0:T(8,128)(2,1)} %bitcast.79) | data formatting | bytes 524288
  11.7 0.9 copy.37
  12.7 7.2 %all_gather.7 = bf16[2,1,256,256]{3,0,1,2:T(2,128)(2,1)S(1)} all-gather(bf16[2,1,64,256]{3,0,1,2:T(2,128)(2,1)S(1)} %copy.37), channel_id=1, replica_groups=mesh['ctx'=4,'cand'=4,'tp'=2] {'ctx'}, dimensions={2}, use_global_device_ids=true | all-gather | bytes 327680 | tf_op jit(solution)/shard_map/all_gather | solution.py:101
  19.9 0.4 fusion.66
  20.2 0.8 copy.54
  21.1 0.1 copy.53
  21.2 1.0 %copy.57 = bf16[8,8,16,128]{3,2,1,0:T(8,128)(2,1)S(1)} copy(bf16[8,8,16,128]{3,1,2,0:T(8,128)(2,1)} %bitcast.80) | data formatting | bytes 524288
  22.2 0.1 broadcast_in_dim.80
  22.3 0.1 le.44
  23.0 0.6 broadcast_compare_fusion.1
  23.6 0.1 iota_compare_fusion
  23.7 0.4 fusion.67
  24.1 26.8 %all-gather.2.cloned.1.call-done = bf16[2,1024,256]{2,0,1:T(2,128)(2,1)} async-done(((bf16[2,64,256]{2,0,1:T(2,128)(2,1)}), bf16[2,1024,256]{2,0,1:T(2,128)(2,1)}) %all-gather.2.cloned.1.call-update) | async-done | bytes 1048592 | tf_op jit(solution)/shard_map/all_gather | solution.py:85
  50.9 3.2 %fusion.64 = (bf16[1,1024,256]{2,0,1:T(2,128)(2,1)S(1)}, bf16[1,1024,256]{2,0,1:T(2,128)(2,1)S(1)}) fusion(bf16[2,1024,256]{2,0,1:T(2,128)(2,1)} %all-gather.2.cloned.1.call-done), kind=kLoop, calls=%fused_computation.71 | loop fusion | bytes 2097152 | tf_op jit(solution)/shard_map/slice | solution.py:88
  54.1 2.3 %copy.51 = bf16[1,1024,256]{1,2,0:T(8,128)(2,1)} copy(bf16[1,1024,256]{2,0,1:T(2,128)(2,1)S(1)} %get-tuple-element.41) | data formatting | bytes 1048576
  56.4 0.0 copy-start.2
  56.4 1.3 %copy.52 = bf16[1,1024,256]{1,2,0:T(8,128)(2,1)S(1)} copy(bf16[1,1024,256]{2,0,1:T(2,128)(2,1)S(1)} %get-tuple-element.40) | data formatting | bytes 1048576
  57.8 0.0 copy-start.4
  57.8 3.7 %multiply_reduce_fusion = (f32[2,512]{1,0:T(2,128)S(1)}, f32[2,512,1024]{2,1,0:T(8,128)}) fusion(bf16[1024,2,128]{0,2,1:T(8,128)(2,1)} %bitcast.69, bf16[2,64,8,128]{3,2,0,1:T(8,128)(2,1)S(1)} %bitcast.72), kind=kOutput, calls=%fused_computation.19 | convolution fusion | flops 270531584 | bytes 4984832 | tf_op jit(solution)/shard_map/hrd,nhd->hrn/dot_general | solution.py:27
  61.5 0.0 copy-done.2
  61.5 0.0 copy-done.4
  61.5 0.0 copy-start.3
  61.5 5.4 %conditional.1 = (f32[2,512]{1,0:T(2,128)S(1)}, f32[2,512,128]{2,1,0:T(8,128)S(1)}) conditional(s32[]{:T(128)} %bitcast.1, () %tuple.16, (s32[1024]{0:T(1024)S(1)}, s32[64]{0:T(128)}, bf16[2,64,8,128]{3,2,0,1:T(8,128)(2,1)S(1)}, bf16[1024,2,128]{0,2,1:T(8,128)(2,1)S(1)}, bf16[1024,2,128]{0,2,1:T(8,128)(2,1)S(1)}) %tuple.39), branch_computations={%region_0.0_spmd, %region_1.4_spmd} | conditional | flops 551160832 | bytes 16572688 | solution.py:61
  61.5 0.7 broadcast_in_dim.66
  62.2 0.1 le.34
  62.3 0.4 broadcast_compare_fusion
  62.7 1.1 %fusion = (f32[2,512]{1,0:T(2,128)S(1)}, f32[2,512,1024]{2,1,0:T(8,128)S(1)}) fusion(pred[512,1024]{1,0:T(8,128)(4,1)S(1)} %broadcast_compare_fusion, bf16[1024,2,128]{0,2,1:T(8,128)(2,1)S(1)} %get-tuple-element.32, bf16[2,64,8,128]{3,2,0,1:T(8,128)(2,1)S(1)} %get-tuple-element.31), kind=kOutput, calls=%fused_computation.2 | convolution fusion | flops 271580160 | bytes 5509120 | tf_op jit(solution)/shard_map/cond/branch_1_fun/hrd,nhd->hrn/dot_general | solution.py:27
  63.8 1.5 %fusion.2 = f32[2,512]{1,0:T(2,128)S(1)} fusion(f32[2,512,1024]{2,1,0:T(8,128)S(1)} %get-tuple-element.39, f32[2,512]{1,0:T(2,128)S(1)} %broadcast_maximum_fusion, pred[512,1024]{1,0:T(8,128)(4,1)S(1)} %broadcast_compare_fusion), kind=kLoop, calls=%fused_computation.4 | loop fusion | flops 5241856 | bytes 4726784 | tf_op jit(solution)/shard_map/cond/branch_1_fun/reduce_sum | solution.py:37
  65.3 1.6 %fusion.6 = f32[2,512,128]{2,1,0:T(8,128)S(1)} fusion(bf16[1024,2,128]{0,2,1:T(8,128)(2,1)S(1)} %get-tuple-element.33, f32[2,512,1024]{2,1,0:T(8,128)S(1)} %get-tuple-element.39, f32[2,512]{1,0:T(2,128)S(1)} %broadcast_maximum_fusion, pred[512,1024]{1,0:T(8,128)(4,1)S(1)} %broadcast_compare_fusion, f32[2,512]{1,0:T(2,128)S(1)} %get-tuple-element.36), kind=kOutput, calls=%fused_computation.7 | convolution fusion | flops 273809408 | bytes 5775360 | tf_op jit(solution)/shard_map/cond/branch_1_fun/hrn,nhd->hrd/dot_general | solution.py:38
  66.9 0.0 copy-start.1
  66.9 0.2 fusion.51
  67.2 0.2 fusion.38
  67.4 0.0 copy-done.3
  67.5 0.4 fusion.40
  67.9 1.2 %copy-done.1 = f32[2,512,1024]{2,1,0:T(8,128)S(1)} copy-done((f32[2,512,1024]{2,1,0:T(8,128)S(1)}, f32[2,512,1024]{2,1,0:T(8,128)}, u32[]{:S(2)}) %copy-start.1) | copy-done | bytes 4194328
  69.1 0.9 %fusion.16 = f32[2,512]{1,0:T(2,128)S(1)} fusion(f32[2,512,1024]{2,1,0:T(8,128)S(1)} %copy-done.1, f32[2,512]{1,0:T(2,128)S(1)} %get-tuple-element.48), kind=kLoop, calls=%fused_computation.20 | loop fusion | flops 3144704 | bytes 4202496 | tf_op jit(solution)/shard_map/reduce_sum | solution.py:37
  70.1 0.0 copy-start.5
  70.1 0.0 copy-start.7
  70.1 1.2 %fusion.35 = bf16[2,64,8,128]{3,2,1,0:T(8,128)(2,1)S(1)} fusion(f32[2,512,128]{2,1,0:T(8,128)S(1)} %fusion.40, bf16[1024,2,128]{0,2,1:T(8,128)(2,1)S(1)} %bitcast.78, f32[2,512,1024]{2,1,0:T(8,128)S(1)} %copy-done.1, f32[2,512]{1,0:T(2,128)S(1)} %get-tuple-element.48, f32[2,512]{1,0:T(2,128)S(1)} %get-tuple-element.34, f32[2,512]{1,0:T(2,128)S(1)} %get-tuple-element.35, ...), kind=kOutput, calls=%fused_computation.33 | convolution fusion | flops 272236544 | bytes 5521408 | tf_op jit(solution)/shard_map/hrn,nhd->hrd/dot_general | solution.py:38
  71.4 0.1 reshape.166
  71.5 0.0 copy-done.5
  71.5 0.8 select_convert_fusion
  72.3 0.0 copy-done
  72.3 0.4 convolution_bitcast_fusion
  72.7 4.9 %psum.14 = f32[64]{0:T(128)S(1)} all-reduce(f32[64]{0:T(128)S(1)} %convolution_bitcast_fusion), channel_id=1, replica_groups=mesh['ctx'=4,'cand'=4,'tp'=2] {'tp'}, use_global_device_ids=true, to_apply=%region_8.9 | all-reduce | flops 64 | bytes 512 | tf_op jit(solution)/shard_map/psum | solution.py:115
  77.6 0.0 copy-done.7
  77.6 0.2 fusion.55
  77.8 0.8 copy.82
  78.6 6.3 %psum.15 = f32[1,8]{1,0:T(1,128)} all-reduce(f32[1,8]{1,0:T(1,128)S(1)} %fusion.55), channel_id=1, replica_groups=mesh['ctx'=4,'cand'=4,'tp'=2] {'ctx'}, use_global_device_ids=true, to_apply=%region_9.10 | all-reduce | flops 8 | bytes 64 | tf_op jit(solution)/shard_map/psum | solution.py:116
  (9 shorter events, 0.2 us)
Async XLA Ops:
  7.2 65.1 %copy-start = (f32[2048]{0:T(1024)S(1)}, f32[2048]{0:T(1024)}, u32[]{:S(2)}) copy-start(f32[2048]{0:T(1024)} %param.15) | copy-start | bytes 24580
  7.2 43.7 %all-gather.2.cloned.1.call-start = ((), (), s32[]{:S(2)}) async-start(), calls=%async_computation | async-start | bytes 1114112 | tf_op jit(solution)/shard_map/all_gather | solution.py:85
  8.8 1.2 %copy-start.6 = (s32[64]{0:T(128)}, s32[64]{0:T(128)S(1)}, u32[]{:S(2)}) copy-start(s32[64]{0:T(128)S(1)} %iota_add_fusion.1) | copy-start | bytes 772
  56.4 5.1 %copy-start.2 = (bf16[1,1024,256]{1,2,0:T(8,128)(2,1)S(1)}, bf16[1,1024,256]{1,2,0:T(8,128)(2,1)}, u32[]{:S(2)}) copy-start(bf16[1,1024,256]{1,2,0:T(8,128)(2,1)} %copy.51) | copy-start | bytes 1572868
  57.8 3.7 %copy-start.4 = (bf16[8,8,16,128]{3,2,1,0:T(8,128)(2,1)S(1)}, bf16[8,8,16,128]{3,2,1,0:T(8,128)(2,1)}, u32[]{:S(2)}) copy-start(bf16[8,8,16,128]{3,2,1,0:T(8,128)(2,1)} %copy.55) | copy-start | bytes 786436
  61.5 5.9 %copy-start.3 = (bf16[1,1,256,256]{2,3,1,0:T(8,128)(2,1)S(1)}, bf16[1,1,256,256]{2,3,1,0:T(8,128)(2,1)}, u32[]{:S(2)}) copy-start(bf16[1,1,256,256]{2,3,1,0:T(8,128)(2,1)} %copy.54) | copy-start | bytes 393220
  66.9 2.2 %copy-start.1 = (f32[2,512,1024]{2,1,0:T(8,128)S(1)}, f32[2,512,1024]{2,1,0:T(8,128)}, u32[]{:S(2)}) copy-start(f32[2,512,1024]{2,1,0:T(8,128)} %get-tuple-element.50) | copy-start | bytes 12582916
  70.1 1.4 %copy-start.5 = (pred[64]{0:T(512)(128)(4,1)S(1)}, pred[64]{0:T(512)(128)(4,1)}, u32[]{:S(2)}) copy-start(pred[64]{0:T(512)(128)(4,1)} %broadcast_compare_fusion.1) | copy-start | bytes 196
  70.1 7.5 %copy-start.7 = (s32[1,8]{1,0:T(1,128)S(1)}, s32[1,8]{1,0:T(1,128)}, u32[]{:S(2)}) copy-start(s32[1,8]{1,0:T(1,128)} %param.14) | copy-start | bytes 100
Sparse Core Ops, SparseCore 0:
  10.2 40.6 all-gather.1
where the time goes:
time: 92.2 us; the launch traced here: 91.8 us
  waiting for transfers between devices  26.8 us (29%)
  blocking collectives  18.5 us (20%)
  local copies, waits for them, and re-layouts  17.1 us (19%)
  between operations  15.6 us (17%)
  matrix products  8.95 us (10%)
  other arithmetic  4.8 us (5%)
    all_gather x1, waiting for transfers between devices, per_device(): arrived = lax.all_gather(prompt_kv, ('ctx', 'cand'), axis=1, tiled=True)  26.8 us
    unnamed x25, local copies, waits for them, and re-layouts  11.8 us
    all_gather x1, blocking collectives, per_device(): arrived = lax.all_gather(cand_kv, 'ctx', axis=2, tiled=True)  7.22 us
    psum x1, blocking collectives, per_device(): lax.psum(jnp.dot(step_hits, full_logit, precision=lax.Precision.HIGHEST),...  6.35 us
    dot_general x3, matrix products, absorb(): jnp.einsum('hrd,nhd->hrn', queries, key_rows, preferred_element_type=jnp....  5.23 us
    psum x1, blocking collectives, per_device(): full_logit = lax.psum(partial_logit, 'tp')  4.94 us
    slice x1, local copies, waits for them, and re-layouts, per_device(): value_rows = arrived[1].reshape(row_count, kv_heads, HEADDIM)  3.2 us
    dot_general x3, matrix products, absorb(): jnp.einsum('hrn,nhd->hrd', weights.astype(jnp.bfloat16), value_rows, pref...  3.17 us
  transfers between devices with their start and end apart: 1, of which 1 were waited for; matrix products, arithmetic and copies ran while one was open for 7% of the time, Pallas kernels for 0%

commit v1 on v0

v1 whole, which is shorter than its diff:
```python
import functools
import math

import jax
import jax.numpy as jnp
from jax import lax
from jax.experimental import pallas as pl
from jax.experimental.pallas import tpu as pltpu
from jax.sharding import PartitionSpec as P

HEADDIM = 128
GROUP = 8
CORES = 2
NEG_FILL = -1e30
SCALE = HEADDIM ** -0.5 * math.log2(math.e)
ROW_TILE = 256
VMEM_LIMIT = 48 * 1024 * 1024


def shifted(block, axis, size, step):
    return lax.ppermute(block, axis, [(i, (i + step) % size) for i in range(size)])


def partner(block, axis, size):
    return lax.ppermute(block, axis, [(i, i ^ 1) for i in range(size)])


def gather_prompt(own, ctx_size, cand_size):
    along = [(own, 0)] + [(shifted(own, "cand", cand_size, k), k) for k in range(1, cand_size)]
    plane = [(b, 0, k) for b, k in along]
    for j in range(CORES, ctx_size, CORES):
        plane += [(shifted(b, "ctx", ctx_size, j), j, k) for b, k in along]
    blocks = [(b, j, 0, k) for b, j, k in plane]
    blocks += [(partner(b, "ctx", ctx_size), j, 1, k) for b, j, k in plane]
    return blocks


def gather_cand(own, ctx_size):
    blocks = [(own, 0, 0)]
    for j in range(CORES, ctx_size, CORES):
        blocks.append((shifted(own, "ctx", ctx_size, j), j, 0))
    return blocks + [(partner(b, "ctx", ctx_size), j, 1) for b, j, _ in blocks]


def owner_ctx(ctx_index, ctx_size, step, flip):
    side = ctx_index + flip - 2 * flip * lax.rem(ctx_index, 2)
    return lax.rem(side + ctx_size - step, ctx_size)


def key_positions(owners, rows):
    lane = lax.broadcasted_iota(jnp.int32, (1, len(owners) * rows), 1)
    positions = lane
    for index, owner in enumerate(owners):
        inside = (lane >= index * rows) & (lane < (index + 1) * rows)
        positions = jnp.where(inside, lane + (owner - index) * rows, positions)
    return positions


def mix(q_ref, sources, head, first_row):
    rows = q_ref.shape[0]
    columns = slice(head * HEADDIM, (head + 1) * HEADDIM)
    key_rows = jnp.concatenate([ref[0, :, columns] for refs, _ in sources for ref in refs], axis=0)
    value_rows = jnp.concatenate([ref[1, :, columns] for refs, _ in sources for ref in refs], axis=0)
    widened = jnp.concatenate([value_rows, jnp.ones_like(value_rows)], axis=1)
    fan = max(1, ROW_TILE // rows)
    for start in range(head * GROUP, (head + 1) * GROUP, fan):
        heads = range(start, start + fan)
        queries = jnp.concatenate([q_ref[:, h * HEADDIM : (h + 1) * HEADDIM] for h in heads], axis=0)
        scores = lax.dot_general(
            queries, key_rows, (((1,), (1,)), ((), ())), preferred_element_type=jnp.float32
        )
        row_pos = first_row + lax.rem(
            lax.broadcasted_iota(jnp.int32, (fan * rows, 1), 0), jnp.int32(rows)
        )
        parts = []
        offset = 0
        for refs, positions in sources:
            width = sum(ref.shape[1] for ref in refs)
            part = scores[:, offset : offset + width]
            if positions is not None:
                part = jnp.where(positions <= row_pos, part, NEG_FILL)
            parts.append(part)
            offset += width
        scores = jnp.concatenate(parts, axis=1)
        peak = jnp.max(scores, axis=1, keepdims=True)
        weights = jnp.exp2((scores - peak) * SCALE).astype(jnp.bfloat16)
        blended = jnp.dot(weights, widened, preferred_element_type=jnp.float32)
        result = blended[:, :HEADDIM] / blended[:, HEADDIM:]
        yield heads, result


def prompt_kernel(shifts, ctx_size, cand_size, q_ref, *refs):
    blocks, out_ref = refs[:-1], refs[-1]
    rows = q_ref.shape[0]
    ctx_index = lax.axis_index("ctx")
    cand_index = lax.axis_index("cand")
    owners = [
        owner_ctx(ctx_index, ctx_size, j, flip) * cand_size
        + lax.rem(cand_index + cand_size - k, cand_size)
        for j, flip, k in shifts
    ]
    positions = key_positions(owners, rows)
    first_row = (ctx_index * cand_size + cand_index) * rows
    for head in range(blocks[0].shape[2] // HEADDIM):
        for heads, result in mix(q_ref, [(blocks, positions)], head, first_row):
            for index, h in enumerate(heads):
                out_ref[:, h * HEADDIM : (h + 1) * HEADDIM] = result[
                    index * rows : (index + 1) * rows
                ].astype(jnp.bfloat16)


def cand_kernel(shifts, ctx_size, length_ref, q_ref, ends_ref, head_ref, *refs):
    own_count = len(shifts)
    own, prompt = refs[:own_count], refs[own_count:-2]
    out_ref, logit_ref = refs[-2:]
    rows = q_ref.shape[0]
    ctx_index = lax.axis_index("ctx")
    owners = [owner_ctx(ctx_index, ctx_size, j, flip) for j, flip in shifts]
    positions = key_positions(owners, rows)
    first_row = ctx_index * rows
    row_pos = first_row + lax.broadcasted_iota(jnp.int32, (rows, 1), 0)
    alive = row_pos < length_ref[0]
    total = jnp.zeros((rows, HEADDIM), jnp.float32)
    for head in range(own[0].shape[2] // HEADDIM):
        for heads, result in mix(q_ref, [(prompt, None), (own, positions)], head, first_row):
            for index, h in enumerate(heads):
                columns = slice(h * HEADDIM, (h + 1) * HEADDIM)
                kept = jnp.where(alive, result[index * rows : (index + 1) * rows], 0.0)
                kept = kept.astype(jnp.bfloat16)
                out_ref[:, columns] = kept
                total += kept.astype(jnp.float32) * head_ref[:, columns]
    logits = jnp.sum(total, axis=1, keepdims=True)
    hits = jnp.where(row_pos == ends_ref[...], logits, 0.0)
    logit_ref[...] = jnp.sum(hits, axis=0, keepdims=True)


def vmem(count):
    return [pl.BlockSpec(memory_space=pltpu.VMEM)] * count


def per_device(ctx_size, cand_size, prompt_q, prompt_kv, cand_q, cand_kv, cand_lengths, step_ends, reward_head):
    params = pltpu.CompilerParams(vmem_limit_bytes=VMEM_LIMIT)
    gathered = gather_prompt(prompt_kv, ctx_size, cand_size)
    own = gather_cand(cand_kv[:, 0], ctx_size)
    prompt_blocks = [b for b, *_ in gathered]
    own_blocks = [b for b, *_ in own]
    cand_out, partial = pl.pallas_call(
        functools.partial(cand_kernel, [s for _, *s in own], ctx_size),
        out_shape=(
            jax.ShapeDtypeStruct(cand_q.shape[1:], jnp.bfloat16),
            jax.ShapeDtypeStruct(step_ends.shape, jnp.float32),
        ),
        in_specs=[pl.BlockSpec(memory_space=pltpu.SMEM)] + vmem(3 + len(own_blocks) + len(prompt_blocks)),
        out_specs=tuple(vmem(2)),
        compiler_params=params,
        name="cand_attention",
    )(cand_lengths, cand_q[0], step_ends, reward_head[None], *own_blocks, *prompt_blocks)
    step_logits = lax.psum(partial, ("ctx", "tp"))
    prompt_out = pl.pallas_call(
        functools.partial(prompt_kernel, [s for _, *s in gathered], ctx_size, cand_size),
        out_shape=jax.ShapeDtypeStruct(prompt_q.shape, jnp.bfloat16),
        in_specs=vmem(1 + len(prompt_blocks)),
        out_specs=vmem(1)[0],
        compiler_params=params,
        name="prompt_attention",
    )(prompt_q, *prompt_blocks)
    return (prompt_out, cand_out[None], step_logits)


def solution(mesh):
    placed = (
        P(("ctx", "cand"), "tp"),
        P(None, ("ctx", "cand"), "tp"),
        P("cand", "ctx", "tp"),
        P(None, "cand", "ctx", "tp"),
        P("cand"),
        P("cand", None),
        P("tp"),
    )
    return jax.shard_map(
        functools.partial(per_device, mesh.shape["ctx"], mesh.shape["cand"]),
        mesh=mesh,
        in_specs=placed,
        out_specs=(P(("ctx", "cand"), "tp"), P("cand", "ctx", "tp"), P("cand", None)),
        check_vma=False,
    )
```

time: 92.2 us -> 45 us (0.49)
  waiting for transfers between devices: 26.8 us -> 4.86 us
  between operations: 15.6 us -> 1.34 us
  starting transfers between devices: 0.04 us -> 14.2 us
  local copies, waits for them, and re-layouts: 17.1 us -> 3.99 us
  matrix products: 8.95 us -> 0 us
  Pallas kernels: 0 us -> 5.32 us
  other arithmetic: 4.8 us -> 0 us
  blocking collectives: 18.5 us -> 15 us
    all_gather x1 -> x0, waiting for transfers between devices: 26.8 us -> none  [per_device(): arrived = lax.all_gather(prompt_kv, ('ctx', 'cand'), axis=1, tiled=True)]
    ppermute x0 -> x18, starting transfers between devices: none -> 14.2 us  [the longest x8 12.6 us: shifted(): lax.ppermute(block, axis, [(i, (i + step) % size) for i in range(size)])]
    dot_general x8 -> x0, matrix products: 8.95 us -> none  [the longest x3 5.23 us: absorb(): jnp.einsum('hrd,nhd->hrn', queries, key_rows, preferred_element_type=jnp....]
    unnamed x25 -> x14, local copies, waits for them, and re-layouts: 11.8 us -> 3.99 us
    all_gather x1 -> x0, blocking collectives: 7.22 us -> none  [per_device(): arrived = lax.all_gather(cand_kv, 'ctx', axis=2, tiled=True)]
    pallas_call x0 -> x2, Pallas kernels: none -> 5.32 us  [the longest x1 2.78 us: per_device(): pl.pallas_call(functools.partial(cand_kernel, [s for _, *s in own], ctx_s...]
    ppermute x0 -> x18, waiting for transfers between devices: none -> 4.86 us  [the longest x8 4.62 us: shifted(): lax.ppermute(block, axis, [(i, (i + step) % size) for i in range(size)])]
    slice x3 -> x0, local copies, waits for them, and re-layouts: 4.15 us -> none  [the longest x1 3.2 us: per_device(): value_rows = arrived[1].reshape(row_count, kv_heads, HEADDIM)]
  transfers between devices with their start and end apart: 1 -> 18, of which waited for: 1 -> 7; matrix products, arithmetic and copies ran while one was open for 7% -> 0% of each run, Pallas kernels for 0% -> 0%
where the time goes in v1:
time: 45 us; the launch traced here: 44.7 us
  blocking collectives  15 us (33%)
  starting transfers between devices  14.2 us (32%)
  Pallas kernels  5.32 us (12%)
  waiting for transfers between devices  4.86 us (11%)
  local copies, waits for them, and re-layouts  3.99 us (9%)
  between operations  1.34 us (3%)
    psum x1, blocking collectives, per_device(): step_logits = lax.psum(partial, ('ctx', 'tp'))  15 us
    ppermute x8, starting transfers between devices, shifted(): lax.ppermute(block, axis, [(i, (i + step) % size) for i in range(size)])  12.6 us
    ppermute x8, waiting for transfers between devices, shifted(): lax.ppermute(block, axis, [(i, (i + step) % size) for i in range(size)])  4.62 us
    unnamed x14, local copies, waits for them, and re-layouts  3.99 us
    pallas_call x1, Pallas kernels, per_device(): pl.pallas_call(functools.partial(cand_kernel, [s for _, *s in own], ctx_s...  2.78 us
    pallas_call x1, Pallas kernels, per_device(): pl.pallas_call(functools.partial(prompt_kernel, [s for _, *s in gathered]...  2.54 us
    ppermute x10, starting transfers between devices, partner(): return lax.ppermute(block, axis, [(i, i ^ 1) for i in range(size)])  1.54 us
  transfers between devices with their start and end apart: 18, of which 7 were waited for; matrix products, arithmetic and copies ran while one was open for 0% of the time, Pallas kernels for 0%

profile of v1, /device:TPU:0, one launch (start us, length us, event | category | flops | bytes accessed | tf_op | source)
XLA Modules:
  0.0 44.7 jit_solution(18104174730507558055)
XLA Ops:
  0.6 3.1 %collective-permute-start = (bf16[2,64,256]{2,1,0:T(8,128)(2,1)}, bf16[2,64,256]{2,1,0:T(8,128)(2,1)S(1)}, u32[]{:S(2)}, u32[]{:S(2)}) collective-permute-start(bf16[2,64,256]{2,1,0:T(8,128)(2,1)} %refs_4_.1), channel_id=1, source_target_pairs={{0,2},{2,4},{4,6},{6,0},{1,3},{3,5},{5,7},{7,1},{8,10},{10,12},{12... | collective-permute-start | bytes 196616 | tf_op jit(solution)/shard_map/ppermute | solution.py:21
  3.7 2.6 %collective-permute-start.1 = (bf16[2,64,256]{2,1,0:T(8,128)(2,1)}, bf16[2,64,256]{2,1,0:T(8,128)(2,1)S(1)}, u32[]{:S(2)}, u32[]{:S(2)}) collective-permute-start(bf16[2,64,256]{2,1,0:T(8,128)(2,1)} %refs_4_.1), channel_id=1, source_target_pairs={{0,4},{2,6},{4,0},{6,2},{1,5},{3,7},{5,1},{7,3},{8,12},{10,14},{12... | collective-permute-start | bytes 196616 | tf_op jit(solution)/shard_map/ppermute | solution.py:21
  6.3 1.3 %collective-permute-start.2 = (bf16[2,64,256]{2,1,0:T(8,128)(2,1)}, bf16[2,64,256]{2,1,0:T(8,128)(2,1)S(1)}, u32[]{:S(2)}, u32[]{:S(2)}) collective-permute-start(bf16[2,64,256]{2,1,0:T(8,128)(2,1)} %refs_4_.1), channel_id=1, source_target_pairs={{0,6},{2,0},{4,2},{6,4},{1,7},{3,1},{5,3},{7,5},{8,14},{10,8},{12,... | collective-permute-start | bytes 196616 | tf_op jit(solution)/shard_map/ppermute | solution.py:21
  7.6 1.5 %collective-permute-start.3 = (bf16[2,64,256]{2,1,0:T(8,128)(2,1)}, bf16[2,64,256]{2,1,0:T(8,128)(2,1)S(1)}, u32[]{:S(2)}, u32[]{:S(2)}) collective-permute-start(bf16[2,64,256]{2,1,0:T(8,128)(2,1)} %refs_4_.1), channel_id=1, source_target_pairs={{0,16},{8,24},{16,0},{24,8},{1,17},{9,25},{17,1},{25,9},{2,18},{10... | collective-permute-start | bytes 196616 | tf_op jit(solution)/shard_map/ppermute | solution.py:21
  9.2 0.5 %collective-permute-start.15 = (bf16[2,64,256]{2,1,0:T(8,128)(2,1)}, bf16[2,64,256]{2,1,0:T(8,128)(2,1)S(1)}, u32[]{:S(2)}, u32[]{:S(2)}) collective-permute-start(bf16[2,64,256]{2,1,0:T(8,128)(2,1)} %bitcast.5), channel_id=1, source_target_pairs={{0,16},{8,24},{16,0},{24,8},{1,17},{9,25},{17,1},{25,9},{2,18},{10... | collective-permute-start | bytes 196616 | tf_op jit(solution)/shard_map/ppermute | solution.py:21
  9.7 0.0 collective-permute-done.refs_1_.refs_5_
  9.7 0.0 collective-permute-start.16
  9.7 1.3 %collective-permute-done.1.refs_2_.refs_6_ = bf16[2,64,256]{2,1,0:T(8,128)(2,1)S(1)} collective-permute-done((bf16[2,64,256]{2,1,0:T(8,128)(2,1)}, bf16[2,64,256]{2,1,0:T(8,128)(2,1)S(1)}, u32[]{:S(2)}, u32[]{:S(2)}) %collective-permute-start.1) | collective-permute-done | bytes 65568 | tf_op jit(solution)/shard_map/ppermute | solution.py:21
  11.0 0.0 collective-permute-start.7
  11.0 0.2 collective-permute-done.2.refs_3_.refs_7_
  11.2 1.6 %collective-permute-start.4 = (bf16[2,64,256]{2,1,0:T(8,128)(2,1)S(1)}, bf16[2,64,256]{2,1,0:T(8,128)(2,1)S(1)}, u32[]{:S(2)}, u32[]{:S(2)}) collective-permute-start(bf16[2,64,256]{2,1,0:T(8,128)(2,1)S(1)} %collective-permute-done.refs_1_.refs_5_), channel_id=1, source_target_pairs={{0,16},{8,24},{16,0},{24,8},{1,17},{9,25},{17,1},{25,9},{2,18},{10... | collective-permute-start | bytes 196616 | tf_op jit(solution)/shard_map/ppermute | solution.py:21
  12.8 0.0 collective-permute-done.3.refs_4_.refs_8_
  12.8 0.8 %collective-permute-start.5 = (bf16[2,64,256]{2,1,0:T(8,128)(2,1)S(1)}, bf16[2,64,256]{2,1,0:T(8,128)(2,1)S(1)}, u32[]{:S(2)}, u32[]{:S(2)}) collective-permute-start(bf16[2,64,256]{2,1,0:T(8,128)(2,1)S(1)} %collective-permute-done.1.refs_2_.refs_6_), channel_id=1, source_target_pairs={{0,16},{8,24},{16,0},{24,8},{1,17},{9,25},{17,1},{25,9},{2,18},{10... | collective-permute-start | bytes 196616 | tf_op jit(solution)/shard_map/ppermute | solution.py:21
  13.6 0.0 collective-permute-done.15.refs_1_
  13.6 1.2 %collective-permute-start.6 = (bf16[2,64,256]{2,1,0:T(8,128)(2,1)S(1)}, bf16[2,64,256]{2,1,0:T(8,128)(2,1)S(1)}, u32[]{:S(2)}, u32[]{:S(2)}) collective-permute-start(bf16[2,64,256]{2,1,0:T(8,128)(2,1)S(1)} %collective-permute-done.2.refs_3_.refs_7_), channel_id=1, source_target_pairs={{0,16},{8,24},{16,0},{24,8},{1,17},{9,25},{17,1},{25,9},{2,18},{10... | collective-permute-start | bytes 196616 | tf_op jit(solution)/shard_map/ppermute | solution.py:21
  14.8 0.0 collective-permute-done.16.refs_2_
  14.8 0.0 collective-permute-start.10
  14.8 0.0 collective-permute-done.7.refs_8_.refs_12_
  14.8 0.5 %collective-permute-start.8 = (bf16[2,64,256]{2,1,0:T(8,128)(2,1)S(1)}, bf16[2,64,256]{2,1,0:T(8,128)(2,1)S(1)}, u32[]{:S(2)}, u32[]{:S(2)}) collective-permute-start(bf16[2,64,256]{2,1,0:T(8,128)(2,1)S(1)} %collective-permute-done.refs_1_.refs_5_), channel_id=1, source_target_pairs={{0,8},{8,0},{16,24},{24,16},{1,9},{9,1},{17,25},{25,17},{2,10},{10... | collective-permute-start | bytes 196616 | tf_op jit(solution)/shard_map/ppermute | solution.py:25
  15.3 0.2 collective-permute-done.4.refs_5_.refs_9_
  15.6 0.0 collective-permute-start.9
  15.6 2.2 %collective-permute-done.5.refs_6_.refs_10_ = bf16[2,64,256]{2,1,0:T(8,128)(2,1)S(1)} collective-permute-done((bf16[2,64,256]{2,1,0:T(8,128)(2,1)S(1)}, bf16[2,64,256]{2,1,0:T(8,128)(2,1)S(1)}, u32[]{:S(2)}, u32[]{:S(2)}) %collective-permute-start.5) | collective-permute-done | bytes 65568 | tf_op jit(solution)/shard_map/ppermute | solution.py:21
  17.7 0.0 collective-permute-start.11
  17.7 0.7 %collective-permute-done.6.refs_7_.refs_11_ = bf16[2,64,256]{2,1,0:T(8,128)(2,1)S(1)} collective-permute-done((bf16[2,64,256]{2,1,0:T(8,128)(2,1)S(1)}, bf16[2,64,256]{2,1,0:T(8,128)(2,1)S(1)}, u32[]{:S(2)}, u32[]{:S(2)}) %collective-permute-start.6) | collective-permute-done | bytes 65568 | tf_op jit(solution)/shard_map/ppermute | solution.py:21
  18.4 0.0 collective-permute-start.17
  18.4 0.0 collective-permute-done.10.refs_11_.refs_15_
  18.4 0.5 %collective-permute-start.12 = (bf16[2,64,256]{2,1,0:T(8,128)(2,1)S(1)}, bf16[2,64,256]{2,1,0:T(8,128)(2,1)S(1)}, u32[]{:S(2)}, u32[]{:S(2)}) collective-permute-start(bf16[2,64,256]{2,1,0:T(8,128)(2,1)S(1)} %collective-permute-done.4.refs_5_.refs_9_), channel_id=1, source_target_pairs={{0,8},{8,0},{16,24},{24,16},{1,9},{9,1},{17,25},{25,17},{2,10},{10... | collective-permute-start | bytes 196616 | tf_op jit(solution)/shard_map/ppermute | solution.py:25
  18.9 0.0 collective-permute-done.8.refs_9_.refs_13_
  18.9 0.1 collective-permute-start.13
  19.0 0.0 collective-permute-done.9.refs_10_.refs_14_
  19.0 0.4 collective-permute-start.14
  20.1 0.0 collective-permute-done.11.refs_12_.refs_16_
  20.1 0.0 collective-permute-done.17.refs_3_
  20.1 0.0 collective-permute-done.12.refs_13_.refs_17_
  20.1 0.1 collective-permute-done.13.refs_14_.refs_18_
  20.2 0.2 collective-permute-done.14.refs_15_.refs_19_
  20.4 0.0 copy-start.6
  20.4 0.7 %copy-done.6 = s32[1,8]{1,0:T(1,128)S(1)} copy-done((s32[1,8]{1,0:T(1,128)S(1)}, s32[1,8]{1,0:T(1,128)}, u32[]{:S(2)}) %copy-start.6) | copy-done | bytes 56
  21.0 0.0 copy-start
  21.0 0.8 %copy-done = bf16[2,64,256]{2,1,0:T(8,128)(2,1)S(1)} copy-done((bf16[2,64,256]{2,1,0:T(8,128)(2,1)S(1)}, bf16[2,64,256]{2,1,0:T(8,128)(2,1)}, u32[]{:S(2)}) %copy-start) | copy-done | bytes 65560
  21.9 0.0 copy-start.2
  21.9 0.9 %copy-done.2 = bf16[1,64,2048]{2,1,0:T(8,128)(2,1)S(1)} copy-done((bf16[1,64,2048]{2,1,0:T(8,128)(2,1)S(1)}, bf16[1,64,2048]{2,1,0:T(8,128)(2,1)}, u32[]{:S(2)}) %copy-start.2) | copy-done | bytes 262168
  22.8 0.0 copy-start.4
  22.8 0.8 %copy-done.4 = bf16[2,1,64,256]{3,2,1,0:T(8,128)(2,1)S(1)} copy-done((bf16[2,1,64,256]{3,2,1,0:T(8,128)(2,1)S(1)}, bf16[2,1,64,256]{3,2,1,0:T(8,128)(2,1)}, u32[]{:S(2)}) %copy-start.4) | copy-done | bytes 65560
  23.6 0.0 copy-start.5
  23.7 0.7 %copy-done.5 = f32[2048]{0:T(1024)S(1)} copy-done((f32[2048]{0:T(1024)S(1)}, f32[2048]{0:T(1024)}, u32[]{:S(2)}) %copy-start.5) | copy-done | bytes 8216
  24.3 0.0 copy-start.1
  24.3 0.0 copy-start.3
  24.4 2.8 %cand_attention.1 = (bf16[64,2048]{1,0:T(8,128)(2,1)}, f32[1,8]{1,0:T(1,128)S(1)}) custom-call(s32[1]{0:T(128)S(6)} %copy.10.length_ref, bf16[64,2048]{1,0:T(8,128)(2,1)S(1)} %bitcast.4, s32[1,8]{1,0:T(1,128)S(1)} %copy-done.6, f32[1,2048]{1,0:T(1,128)S(1)} %bitcast.8, bf16[2,64,256]{2,1,0:T(8,128)(2,1)S(1)} %bitcast.7, ...), custom_call_target="tpu_custom_call" | custom-call | tf_op jit(solution)/shard_map/cand_attention/pallas_call | solution.py:147
  27.1 15.0 %psum.7 = f32[1,8]{1,0:T(1,128)} all-reduce(f32[1,8]{1,0:T(1,128)S(1)} %get-tuple-element.6), channel_id=1, replica_groups=mesh['ctx'=4,'cand'=4,'tp'=2] {'ctx','tp'}, use_global_device_ids=true, to_apply=%region_0.0 | all-reduce | flops 8 | bytes 64 | tf_op jit(solution)/shard_map/psum | solution.py:158
  42.1 0.0 copy-done.1
  42.1 0.0 copy-done.3
  42.1 2.5 %prompt_attention.1 = bf16[64,2048]{1,0:T(8,128)(2,1)} custom-call(bf16[64,2048]{1,0:T(8,128)(2,1)S(1)} %copy-done.3, bf16[2,64,256]{2,1,0:T(8,128)(2,1)S(1)} %copy-done.1, bf16[2,64,256]{2,1,0:T(8,128)(2,1)S(1)} %collective-permute-done.refs_1_.refs_5_, bf16[2,64,256]{2,1,0:T(8,128)(2,1)S(1)} %collective-permute-done.1.refs_2_.refs_6_, ...), custom_call_target="tpu_custom_call" | custom-call | tf_op jit(solution)/shard_map/prompt_attention/pallas_call | solution.py:159
Async XLA Ops:
  0.6 9.0 %collective-permute-start = (bf16[2,64,256]{2,1,0:T(8,128)(2,1)}, bf16[2,64,256]{2,1,0:T(8,128)(2,1)S(1)}, u32[]{:S(2)}, u32[]{:S(2)}) collective-permute-start(bf16[2,64,256]{2,1,0:T(8,128)(2,1)} %refs_4_.1), channel_id=1, source_target_pairs={{0,2},{2,4},{4,6},{6,0},{1,3},{3,5},{5,7},{7,1},{8,10},{10,12},{12... | collective-permute-start | bytes 196616 | tf_op jit(solution)/shard_map/ppermute | solution.py:21
  3.7 7.3 %collective-permute-start.1 = (bf16[2,64,256]{2,1,0:T(8,128)(2,1)}, bf16[2,64,256]{2,1,0:T(8,128)(2,1)S(1)}, u32[]{:S(2)}, u32[]{:S(2)}) collective-permute-start(bf16[2,64,256]{2,1,0:T(8,128)(2,1)} %refs_4_.1), channel_id=1, source_target_pairs={{0,4},{2,6},{4,0},{6,2},{1,5},{3,7},{5,1},{7,3},{8,12},{10,14},{12... | collective-permute-start | bytes 196616 | tf_op jit(solution)/shard_map/ppermute | solution.py:21
  6.3 4.9 %collective-permute-start.2 = (bf16[2,64,256]{2,1,0:T(8,128)(2,1)}, bf16[2,64,256]{2,1,0:T(8,128)(2,1)S(1)}, u32[]{:S(2)}, u32[]{:S(2)}) collective-permute-start(bf16[2,64,256]{2,1,0:T(8,128)(2,1)} %refs_4_.1), channel_id=1, source_target_pairs={{0,6},{2,0},{4,2},{6,4},{1,7},{3,1},{5,3},{7,5},{8,14},{10,8},{12,... | collective-permute-start | bytes 196616 | tf_op jit(solution)/shard_map/ppermute | solution.py:21
  7.6 5.2 %collective-permute-start.3 = (bf16[2,64,256]{2,1,0:T(8,128)(2,1)}, bf16[2,64,256]{2,1,0:T(8,128)(2,1)S(1)}, u32[]{:S(2)}, u32[]{:S(2)}) collective-permute-start(bf16[2,64,256]{2,1,0:T(8,128)(2,1)} %refs_4_.1), channel_id=1, source_target_pairs={{0,16},{8,24},{16,0},{24,8},{1,17},{9,25},{17,1},{25,9},{2,18},{10... | collective-permute-start | bytes 196616 | tf_op jit(solution)/shard_map/ppermute | solution.py:21
  9.2 4.5 %collective-permute-start.15 = (bf16[2,64,256]{2,1,0:T(8,128)(2,1)}, bf16[2,64,256]{2,1,0:T(8,128)(2,1)S(1)}, u32[]{:S(2)}, u32[]{:S(2)}) collective-permute-start(bf16[2,64,256]{2,1,0:T(8,128)(2,1)} %bitcast.5), channel_id=1, source_target_pairs={{0,16},{8,24},{16,0},{24,8},{1,17},{9,25},{17,1},{25,9},{2,18},{10... | collective-permute-start | bytes 196616 | tf_op jit(solution)/shard_map/ppermute | solution.py:21
  9.7 5.2 %collective-permute-start.16 = (bf16[2,64,256]{2,1,0:T(8,128)(2,1)}, bf16[2,64,256]{2,1,0:T(8,128)(2,1)S(1)}, u32[]{:S(2)}, u32[]{:S(2)}) collective-permute-start(bf16[2,64,256]{2,1,0:T(8,128)(2,1)} %bitcast.6), channel_id=1, source_target_pairs={{0,8},{8,0},{16,24},{24,16},{1,9},{9,1},{17,25},{25,17},{2,10},{10... | collective-permute-start | bytes 196616 | tf_op jit(solution)/shard_map/ppermute | solution.py:25
  11.0 3.8 %collective-permute-start.7 = (bf16[2,64,256]{2,1,0:T(8,128)(2,1)}, bf16[2,64,256]{2,1,0:T(8,128)(2,1)S(1)}, u32[]{:S(2)}, u32[]{:S(2)}) collective-permute-start(bf16[2,64,256]{2,1,0:T(8,128)(2,1)} %refs_4_.1), channel_id=1, source_target_pairs={{0,8},{8,0},{16,24},{24,16},{1,9},{9,1},{17,25},{25,17},{2,10},{10... | collective-permute-start | bytes 196616 | tf_op jit(solution)/shard_map/ppermute | solution.py:25
  11.2 4.3 %collective-permute-start.4 = (bf16[2,64,256]{2,1,0:T(8,128)(2,1)S(1)}, bf16[2,64,256]{2,1,0:T(8,128)(2,1)S(1)}, u32[]{:S(2)}, u32[]{:S(2)}) collective-permute-start(bf16[2,64,256]{2,1,0:T(8,128)(2,1)S(1)} %collective-permute-done.refs_1_.refs_5_), channel_id=1, source_target_pairs={{0,16},{8,24},{16,0},{24,8},{1,17},{9,25},{17,1},{25,9},{2,18},{10... | collective-permute-start | bytes 196616 | tf_op jit(solution)/shard_map/ppermute | solution.py:21
  12.8 4.9 %collective-permute-start.5 = (bf16[2,64,256]{2,1,0:T(8,128)(2,1)S(1)}, bf16[2,64,256]{2,1,0:T(8,128)(2,1)S(1)}, u32[]{:S(2)}, u32[]{:S(2)}) collective-permute-start(bf16[2,64,256]{2,1,0:T(8,128)(2,1)S(1)} %collective-permute-done.1.refs_2_.refs_6_), channel_id=1, source_target_pairs={{0,16},{8,24},{16,0},{24,8},{1,17},{9,25},{17,1},{25,9},{2,18},{10... | collective-permute-start | bytes 196616 | tf_op jit(solution)/shard_map/ppermute | solution.py:21
  13.6 4.8 %collective-permute-start.6 = (bf16[2,64,256]{2,1,0:T(8,128)(2,1)S(1)}, bf16[2,64,256]{2,1,0:T(8,128)(2,1)S(1)}, u32[]{:S(2)}, u32[]{:S(2)}) collective-permute-start(bf16[2,64,256]{2,1,0:T(8,128)(2,1)S(1)} %collective-permute-done.2.refs_3_.refs_7_), channel_id=1, source_target_pairs={{0,16},{8,24},{16,0},{24,8},{1,17},{9,25},{17,1},{25,9},{2,18},{10... | collective-permute-start | bytes 196616 | tf_op jit(solution)/shard_map/ppermute | solution.py:21
  14.8 3.6 %collective-permute-start.10 = (bf16[2,64,256]{2,1,0:T(8,128)(2,1)S(1)}, bf16[2,64,256]{2,1,0:T(8,128)(2,1)S(1)}, u32[]{:S(2)}, u32[]{:S(2)}) collective-permute-start(bf16[2,64,256]{2,1,0:T(8,128)(2,1)S(1)} %collective-permute-done.2.refs_3_.refs_7_), channel_id=1, source_target_pairs={{0,8},{8,0},{16,24},{24,16},{1,9},{9,1},{17,25},{25,17},{2,10},{10... | collective-permute-start | bytes 196616 | tf_op jit(solution)/shard_map/ppermute | solution.py:25
  14.8 4.1 %collective-permute-start.8 = (bf16[2,64,256]{2,1,0:T(8,128)(2,1)S(1)}, bf16[2,64,256]{2,1,0:T(8,128)(2,1)S(1)}, u32[]{:S(2)}, u32[]{:S(2)}) collective-permute-start(bf16[2,64,256]{2,1,0:T(8,128)(2,1)S(1)} %collective-permute-done.refs_1_.refs_5_), channel_id=1, source_target_pairs={{0,8},{8,0},{16,24},{24,16},{1,9},{9,1},{17,25},{25,17},{2,10},{10... | collective-permute-start | bytes 196616 | tf_op jit(solution)/shard_map/ppermute | solution.py:25
  15.6 3.5 %collective-permute-start.9 = (bf16[2,64,256]{2,1,0:T(8,128)(2,1)S(1)}, bf16[2,64,256]{2,1,0:T(8,128)(2,1)S(1)}, u32[]{:S(2)}, u32[]{:S(2)}) collective-permute-start(bf16[2,64,256]{2,1,0:T(8,128)(2,1)S(1)} %collective-permute-done.1.refs_2_.refs_6_), channel_id=1, source_target_pairs={{0,8},{8,0},{16,24},{24,16},{1,9},{9,1},{17,25},{25,17},{2,10},{10... | collective-permute-start | bytes 196616 | tf_op jit(solution)/shard_map/ppermute | solution.py:25
  17.7 2.4 %collective-permute-start.11 = (bf16[2,64,256]{2,1,0:T(8,128)(2,1)S(1)}, bf16[2,64,256]{2,1,0:T(8,128)(2,1)S(1)}, u32[]{:S(2)}, u32[]{:S(2)}) collective-permute-start(bf16[2,64,256]{2,1,0:T(8,128)(2,1)S(1)} %collective-permute-done.3.refs_4_.refs_8_), channel_id=1, source_target_pairs={{0,8},{8,0},{16,24},{24,16},{1,9},{9,1},{17,25},{25,17},{2,10},{10... | collective-permute-start | bytes 196616 | tf_op jit(solution)/shard_map/ppermute | solution.py:25
  18.4 1.7 %collective-permute-start.17 = (bf16[2,64,256]{2,1,0:T(8,128)(2,1)S(1)}, bf16[2,64,256]{2,1,0:T(8,128)(2,1)S(1)}, u32[]{:S(2)}, u32[]{:S(2)}) collective-permute-start(bf16[2,64,256]{2,1,0:T(8,128)(2,1)S(1)} %collective-permute-done.15.refs_1_), channel_id=1, source_target_pairs={{0,8},{8,0},{16,24},{24,16},{1,9},{9,1},{17,25},{25,17},{2,10},{10... | collective-permute-start | bytes 196616 | tf_op jit(solution)/shard_map/ppermute | solution.py:25
  18.4 1.7 %collective-permute-start.12 = (bf16[2,64,256]{2,1,0:T(8,128)(2,1)S(1)}, bf16[2,64,256]{2,1,0:T(8,128)(2,1)S(1)}, u32[]{:S(2)}, u32[]{:S(2)}) collective-permute-start(bf16[2,64,256]{2,1,0:T(8,128)(2,1)S(1)} %collective-permute-done.4.refs_5_.refs_9_), channel_id=1, source_target_pairs={{0,8},{8,0},{16,24},{24,16},{1,9},{9,1},{17,25},{25,17},{2,10},{10... | collective-permute-start | bytes 196616 | tf_op jit(solution)/shard_map/ppermute | solution.py:25
  18.9 1.3 %collective-permute-start.13 = (bf16[2,64,256]{2,1,0:T(8,128)(2,1)S(1)}, bf16[2,64,256]{2,1,0:T(8,128)(2,1)S(1)}, u32[]{:S(2)}, u32[]{:S(2)}) collective-permute-start(bf16[2,64,256]{2,1,0:T(8,128)(2,1)S(1)} %collective-permute-done.5.refs_6_.refs_10_), channel_id=1, source_target_pairs={{0,8},{8,0},{16,24},{24,16},{1,9},{9,1},{17,25},{25,17},{2,10},{10... | collective-permute-start | bytes 196616 | tf_op jit(solution)/shard_map/ppermute | solution.py:25
  19.0 1.3 %collective-permute-start.14 = (bf16[2,64,256]{2,1,0:T(8,128)(2,1)S(1)}, bf16[2,64,256]{2,1,0:T(8,128)(2,1)S(1)}, u32[]{:S(2)}, u32[]{:S(2)}) collective-permute-start(bf16[2,64,256]{2,1,0:T(8,128)(2,1)S(1)} %collective-permute-done.6.refs_7_.refs_11_), channel_id=1, source_target_pairs={{0,8},{8,0},{16,24},{24,16},{1,9},{9,1},{17,25},{25,17},{2,10},{10... | collective-permute-start | bytes 196616 | tf_op jit(solution)/shard_map/ppermute | solution.py:25
  20.4 0.7 %copy-start.6 = (s32[1,8]{1,0:T(1,128)S(1)}, s32[1,8]{1,0:T(1,128)}, u32[]{:S(2)}) copy-start(s32[1,8]{1,0:T(1,128)} %ends_ref.1) | copy-start | bytes 100
  21.0 0.8 %copy-start = (bf16[2,64,256]{2,1,0:T(8,128)(2,1)S(1)}, bf16[2,64,256]{2,1,0:T(8,128)(2,1)}, u32[]{:S(2)}) copy-start(bf16[2,64,256]{2,1,0:T(8,128)(2,1)} %refs_4_.1) | copy-start | bytes 196612
  21.9 0.9 %copy-start.2 = (bf16[1,64,2048]{2,1,0:T(8,128)(2,1)S(1)}, bf16[1,64,2048]{2,1,0:T(8,128)(2,1)}, u32[]{:S(2)}) copy-start(bf16[1,64,2048]{2,1,0:T(8,128)(2,1)} %param.9) | copy-start | bytes 786436
  22.8 0.8 %copy-start.4 = (bf16[2,1,64,256]{3,2,1,0:T(8,128)(2,1)S(1)}, bf16[2,1,64,256]{3,2,1,0:T(8,128)(2,1)}, u32[]{:S(2)}) copy-start(bf16[2,1,64,256]{3,2,1,0:T(8,128)(2,1)} %param.10) | copy-start | bytes 196612
  23.6 0.7 %copy-start.5 = (f32[2048]{0:T(1024)S(1)}, f32[2048]{0:T(1024)}, u32[]{:S(2)}) copy-start(f32[2048]{0:T(1024)} %param.13) | copy-start | bytes 24580
  24.3 17.8 %copy-start.1 = (bf16[2,64,256]{2,1,0:T(8,128)(2,1)S(1)}, bf16[2,64,256]{2,1,0:T(8,128)(2,1)}, u32[]{:S(2)}) copy-start(bf16[2,64,256]{2,1,0:T(8,128)(2,1)} %refs_4_.1) | copy-start | bytes 196612
  24.3 17.8 %copy-start.3 = (bf16[64,2048]{1,0:T(8,128)(2,1)S(1)}, bf16[64,2048]{1,0:T(8,128)(2,1)}, u32[]{:S(2)}) copy-start(bf16[64,2048]{1,0:T(8,128)(2,1)} %q_ref.1) | copy-start | bytes 786436

commit v2 on v1

--- a/solution.py
+++ b/solution.py
@@ -10,41 +10,33 @@
 
 HEADDIM = 128
 GROUP = 8
-CORES = 2
 NEG_FILL = -1e30
 SCALE = HEADDIM ** -0.5 * math.log2(math.e)
 ROW_TILE = 256
 VMEM_LIMIT = 48 * 1024 * 1024
 
 
-def shifted(block, axis, size, step):
-    return lax.ppermute(block, axis, [(i, (i + step) % size) for i in range(size)])
-
-
-def partner(block, axis, size):
-    return lax.ppermute(block, axis, [(i, i ^ 1) for i in range(size)])
-
-
-def gather_prompt(own, ctx_size, cand_size):
-    along = [(own, 0)] + [(shifted(own, "cand", cand_size, k), k) for k in range(1, cand_size)]
-    plane = [(b, 0, k) for b, k in along]
-    for j in range(CORES, ctx_size, CORES):
-        plane += [(shifted(b, "ctx", ctx_size, j), j, k) for b, k in along]
-    blocks = [(b, j, 0, k) for b, j, k in plane]
-    blocks += [(partner(b, "ctx", ctx_size), j, 1, k) for b, j, k in plane]
+def flipped(block, axis, size, bit):
+    return lax.ppermute(block, axis, [(i, i ^ bit) for i in range(size)])
+
+
+def bits_of(size):
+    return [1 << b for b in reversed(range(size.bit_length() - 1))]
+
+
+def gather(own, axes, first=None):
+    blocks = [(own, 0)]
+    below = math.prod(size for _, size in axes)
+    steps = []
+    for axis, size in axes:
+        below //= size
+        steps.append([(axis, size, bit, bit * below) for bit in bits_of(size)])
+    for axis, size, bit, mask in sum(reversed(steps), []):
+        sent = blocks
+        if first is not None:
+            sent, first = [(first, 0)], None
+        blocks += [(flipped(b, axis, size, bit), m | mask) for b, m in sent]
     return blocks
-
-
-def gather_cand(own, ctx_size):
-    blocks = [(own, 0, 0)]
-    for j in range(CORES, ctx_size, CORES):
-        blocks.append((shifted(own, "ctx", ctx_size, j), j, 0))
-    return blocks + [(partner(b, "ctx", ctx_size), j, 1) for b, j, _ in blocks]
-
-
-def owner_ctx(ctx_index, ctx_size, step, flip):
-    side = ctx_index + flip - 2 * flip * lax.rem(ctx_index, 2)
-    return lax.rem(side + ctx_size - step, ctx_size)
 
 
 def key_positions(owners, rows):
@@ -89,18 +81,12 @@
         yield heads, result
 
 
-def prompt_kernel(shifts, ctx_size, cand_size, q_ref, *refs):
+def prompt_kernel(masks, cand_size, q_ref, *refs):
     blocks, out_ref = refs[:-1], refs[-1]
     rows = q_ref.shape[0]
-    ctx_index = lax.axis_index("ctx")
-    cand_index = lax.axis_index("cand")
-    owners = [
-        owner_ctx(ctx_index, ctx_size, j, flip) * cand_size
-        + lax.rem(cand_index + cand_size - k, cand_size)
-        for j, flip, k in shifts
-    ]
-    positions = key_positions(owners, rows)
-    first_row = (ctx_index * cand_size + cand_index) * rows
+    place = lax.axis_index("ctx") * cand_size + lax.axis_index("cand")
+    positions = key_positions([place ^ mask for mask in masks], rows)
+    first_row = place * rows
     for head in range(blocks[0].shape[2] // HEADDIM):
         for heads, result in mix(q_ref, [(blocks, positions)], head, first_row):
             for index, h in enumerate(heads):
@@ -109,17 +95,16 @@
                 ].astype(jnp.bfloat16)
 
 
-def cand_kernel(shifts, ctx_size, length_ref, q_ref, ends_ref, head_ref, *refs):
-    own_count = len(shifts)
+def cand_kernel(masks, lengths_ref, q_ref, ends_ref, head_ref, *refs):
+    own_count = len(masks)
     own, prompt = refs[:own_count], refs[own_count:-2]
     out_ref, logit_ref = refs[-2:]
     rows = q_ref.shape[0]
-    ctx_index = lax.axis_index("ctx")
-    owners = [owner_ctx(ctx_index, ctx_size, j, flip) for j, flip in shifts]
-    positions = key_positions(owners, rows)
-    first_row = ctx_index * rows
+    place = lax.axis_index("ctx")
+    positions = key_positions([place ^ mask for mask in masks], rows)
+    first_row = place * rows
     row_pos = first_row + lax.broadcasted_iota(jnp.int32, (rows, 1), 0)
-    alive = row_pos < length_ref[0]
+    alive = row_pos < lengths_ref[:, :1]
     total = jnp.zeros((rows, HEADDIM), jnp.float32)
     for head in range(own[0].shape[2] // HEADDIM):
         for heads, result in mix(q_ref, [(prompt, None), (own, positions)], head, first_row):
@@ -138,32 +123,64 @@
     return [pl.BlockSpec(memory_space=pltpu.VMEM)] * count
 
 
+def stage_kernel(count, length_ref, *refs):
+    sources, targets, lengths_ref, sems = refs[:count], refs[count : 2 * count], refs[-2], refs[-1]
+    copies = [pltpu.make_async_copy(sources[i], targets[i], sems.at[i]) for i in range(count)]
+    for copy in copies:
+        copy.start()
+    lengths_ref[...] = jnp.full(lengths_ref.shape, length_ref[0], jnp.int32)
+    for copy in copies:
+        copy.wait()
+
+
+def staged(length, arrays, params):
+    count = len(arrays)
+    shapes = [jax.ShapeDtypeStruct(a.shape, a.dtype) for a in arrays]
+    return pl.pallas_call(
+        functools.partial(stage_kernel, count),
+        out_shape=tuple(shapes) + (jax.ShapeDtypeStruct((1, HEADDIM), jnp.int32),),
+        in_specs=[pl.BlockSpec(memory_space=pltpu.SMEM)] + [pl.BlockSpec(memory_space=pltpu.HBM)] * count,
+        out_specs=tuple(vmem(count + 1)),
+        scratch_shapes=[pltpu.SemaphoreType.DMA((count,))],
+        compiler_params=params,
+        name="stage_operands",
+    )(length, *(pltpu.with_memory_space_constraint(a, pltpu.HBM) for a in arrays))
+
+
 def per_device(ctx_size, cand_size, prompt_q, prompt_kv, cand_q, cand_kv, cand_lengths, step_ends, reward_head):
     params = pltpu.CompilerParams(vmem_limit_bytes=VMEM_LIMIT)
-    gathered = gather_prompt(prompt_kv, ctx_size, cand_size)
-    own = gather_cand(cand_kv[:, 0], ctx_size)
-    prompt_blocks = [b for b, *_ in gathered]
-    own_blocks = [b for b, *_ in own]
+    prompt_rows, cand_rows, prompt_own, cand_own, ends, head, lengths = staged(
+        cand_lengths,
+        (prompt_q, cand_q[0], prompt_kv, cand_kv[:, 0], step_ends, reward_head[None]),
+        params,
+    )
+    gathered = gather(prompt_own, [("ctx", ctx_size), ("cand", cand_size)], first=prompt_kv)
+    own = gather(cand_own, [("ctx", ctx_size)])
+    prompt_blocks = [b for b, _ in gathered]
+    own_blocks = [b for b, _ in own]
     cand_out, partial = pl.pallas_call(
-        functools.partial(cand_kernel, [s for _, *s in own], ctx_size),
+        functools.partial(cand_kernel, [mask for _, mask in own]),
         out_shape=(
             jax.ShapeDtypeStruct(cand_q.shape[1:], jnp.bfloat16),
             jax.ShapeDtypeStruct(step_ends.shape, jnp.float32),
         ),
-        in_specs=[pl.BlockSpec(memory_space=pltpu.SMEM)] + vmem(3 + len(own_blocks) + len(prompt_blocks)),
+        in_specs=vmem(4 + len(own_blocks) + len(prompt_blocks)),
         out_specs=tuple(vmem(2)),
         compiler_params=params,
         name="cand_attention",
-    )(cand_lengths, cand_q[0], step_ends, reward_head[None], *own_blocks, *prompt_blocks)
-    step_logits = lax.psum(partial, ("ctx", "tp"))
+    )(lengths, cand_rows, ends, head, *own_blocks, *prompt_blocks)
+    sharers = ("ctx", "tp")
+    share_count = lax.axis_size(sharers)
+    shares = jnp.broadcast_to(partial[None], (share_count,) + partial.shape)
+    step_logits = jnp.sum(lax.all_to_all(shares, sharers, 0, 0), axis=0)
     prompt_out = pl.pallas_call(
-        functools.partial(prompt_kernel, [s for _, *s in gathered], ctx_size, cand_size),
+        functools.partial(prompt_kernel, [mask for _, mask in gathered], cand_size),
         out_shape=jax.ShapeDtypeStruct(prompt_q.shape, jnp.bfloat16),
         in_specs=vmem(1 + len(prompt_blocks)),
         out_specs=vmem(1)[0],
         compiler_params=params,
         name="prompt_attention",
-    )(prompt_q, *prompt_blocks)
+    )(prompt_rows, *prompt_blocks)
     return (prompt_out, cand_out[None], step_logits)
 
 

time: 45 us -> 33.9 us (0.75)
  blocking collectives: 15 us -> 0 us
  starting transfers between devices: 14.2 us -> 18 us
  local copies, waits for them, and re-layouts: 3.99 us -> 0.59 us
  waiting for transfers between devices: 4.86 us -> 6.78 us
  Pallas kernels: 5.32 us -> 6.43 us
  other arithmetic: 0 us -> 0.53 us
    psum x1 -> x0, blocking collectives: 15 us -> none  [per_device(): step_logits = lax.psum(partial, ('ctx', 'tp'))]
    unnamed x14 -> x0, local copies, waits for them, and re-layouts: 3.99 us -> none
    all_to_all x0 -> x1, starting transfers between devices: none -> 3.33 us  [per_device(): step_logits = jnp.sum(lax.all_to_all(shares, sharers, 0, 0), axis=0)]
    all_to_all x0 -> x1, waiting for transfers between devices: none -> 2.02 us  [per_device(): step_logits = jnp.sum(lax.all_to_all(shares, sharers, 0, 0), axis=0)]
    pallas_call x2 -> x3, Pallas kernels: 5.32 us -> 6.43 us  [the longest x1 2.79 us: per_device(): pl.pallas_call(functools.partial(cand_kernel, [mask for _, mask in own]),...]
    broadcast_in_dim x0 -> x1, local copies, waits for them, and re-layouts: none -> 0.59 us  [per_device(): shares = jnp.broadcast_to(partial[None], (share_count,) + partial.shape)]
    reduce_sum x0 -> x1, other arithmetic: none -> 0.53 us  [per_device(): step_logits = jnp.sum(lax.all_to_all(shares, sharers, 0, 0), axis=0)]
    ppermute x18, starting transfers between devices: 14.2 us -> 14.7 us  [flipped(): return lax.ppermute(block, axis, [(i, i ^ bit) for i in range(size)])]
  transfers between devices with their start and end apart: 18 -> 19, of which waited for: 7 -> 7; matrix products, arithmetic and copies ran while one was open for 0% -> 0% of each run, Pallas kernels for 0% -> 11%
where the time goes in v2:
time: 33.9 us; the launch traced here: 33.7 us
  starting transfers between devices  18 us (53%)
  waiting for transfers between devices  6.78 us (20%)
  Pallas kernels  6.43 us (19%)
  between operations  1.34 us (4%)
  local copies, waits for them, and re-layouts  0.59 us (2%)
  other arithmetic  0.53 us (2%)
    ppermute x18, starting transfers between devices, flipped(): return lax.ppermute(block, axis, [(i, i ^ bit) for i in range(size)])  14.7 us
    ppermute x18, waiting for transfers between devices, flipped(): return lax.ppermute(block, axis, [(i, i ^ bit) for i in range(size)])  4.76 us
    all_to_all x1, starting transfers between devices, per_device(): step_logits = jnp.sum(lax.all_to_all(shares, sharers, 0, 0), axis=0)  3.33 us
    pallas_call x1, Pallas kernels, per_device(): pl.pallas_call(functools.partial(cand_kernel, [mask for _, mask in own]),...  2.79 us
    pallas_call x1, Pallas kernels, per_device(): pl.pallas_call(functools.partial(prompt_kernel, [mask for _, mask in gath...  2.55 us
    all_to_all x1, waiting for transfers between devices, per_device(): step_logits = jnp.sum(lax.all_to_all(shares, sharers, 0, 0), axis=0)  2.02 us
    pallas_call x1, Pallas kernels, staged(): pl.pallas_call(functools.partial(stage_kernel, count), out_shape=tuple(sh...  1.09 us
  transfers between devices with their start and end apart: 19, of which 7 were waited for; matrix products, arithmetic and copies ran while one was open for 0% of the time, Pallas kernels for 11%

profile of v2, /device:TPU:0, one launch (start us, length us, event | category | flops | bytes accessed | tf_op | source)
XLA Modules:
  0.0 33.7 jit_solution(12733115091572712593)
XLA Ops:
  0.6 4.1 %collective-permute-start = (bf16[2,64,256]{2,1,0:T(8,128)(2,1)}, bf16[2,64,256]{2,1,0:T(8,128)(2,1)S(1)}, u32[]{:S(2)}, u32[]{:S(2)}) collective-permute-start(bf16[2,64,256]{2,1,0:T(8,128)(2,1)} %refs_2_.1), channel_id=1, source_target_pairs={{0,4},{2,6},{4,0},{6,2},{1,5},{3,7},{5,1},{7,3},{8,12},{10,14},{12... | collective-permute-start | bytes 196616 | tf_op jit(solution)/shard_map/ppermute | solution.py:20
  5.4 1.1 %stage_operands.1 = (bf16[64,2048]{1,0:T(8,128)(2,1)S(1)}, bf16[64,2048]{1,0:T(8,128)(2,1)S(1)}, bf16[2,64,256]{2,1,0:T(8,128)(2,1)S(1)}, bf16[2,64,256]{2,1,0:T...) custom-call(s32[1]{0:T(128)S(6)} %copy.11.length_ref, ...), custom_call_target="tpu_custom_call" | custom-call | tf_op jit(solution)/shard_map/stage_operands/pallas_call | solution.py:139
  6.5 0.1 collective-permute-start.16
  6.6 1.6 %collective-permute-start.15 = (bf16[2,64,256]{2,1,0:T(8,128)(2,1)S(1)}, bf16[2,64,256]{2,1,0:T(8,128)(2,1)S(1)}, u32[]{:S(2)}, u32[]{:S(2)}) collective-permute-start(bf16[2,64,256]{2,1,0:T(8,128)(2,1)S(1)} %get-tuple-element.18.refs_0_), channel_id=1, source_target_pairs={{0,16},{8,24},{16,0},{24,8},{1,17},{9,25},{17,1},{25,9},{2,18},{10... | collective-permute-start | bytes 196616 | tf_op jit(solution)/shard_map/ppermute | solution.py:20
  8.1 0.2 collective-permute-start.7
  8.3 0.5 %collective-permute-start.3 = (bf16[2,64,256]{2,1,0:T(8,128)(2,1)S(1)}, bf16[2,64,256]{2,1,0:T(8,128)(2,1)S(1)}, u32[]{:S(2)}, u32[]{:S(2)}) collective-permute-start(bf16[2,64,256]{2,1,0:T(8,128)(2,1)S(1)} %get-tuple-element.13.refs_0_.refs_4_), channel_id=1, source_target_pairs={{0,16},{8,24},{16,0},{24,8},{1,17},{9,25},{17,1},{25,9},{2,18},{10... | collective-permute-start | bytes 196616 | tf_op jit(solution)/shard_map/ppermute | solution.py:20
  8.8 0.0 collective-permute-done.refs_1_.refs_5_
  8.8 1.6 %collective-permute-start.1 = (bf16[2,64,256]{2,1,0:T(8,128)(2,1)S(1)}, bf16[2,64,256]{2,1,0:T(8,128)(2,1)S(1)}, u32[]{:S(2)}, u32[]{:S(2)}) collective-permute-start(bf16[2,64,256]{2,1,0:T(8,128)(2,1)S(1)} %get-tuple-element.13.refs_0_.refs_4_), channel_id=1, source_target_pairs={{0,2},{2,0},{4,6},{6,4},{1,3},{3,1},{5,7},{7,5},{8,10},{10,8},{12,... | collective-permute-start | bytes 196616 | tf_op jit(solution)/shard_map/ppermute | solution.py:20
  10.4 0.0 collective-permute-done.16.refs_2_
  10.4 0.0 collective-permute-start.8
  10.4 0.7 %collective-permute-done.15.refs_1_ = bf16[2,64,256]{2,1,0:T(8,128)(2,1)S(1)} collective-permute-done((bf16[2,64,256]{2,1,0:T(8,128)(2,1)S(1)}, bf16[2,64,256]{2,1,0:T(8,128)(2,1)S(1)}, u32[]{:S(2)}, u32[]{:S(2)}) %collective-permute-start.15) | collective-permute-done | bytes 65568 | tf_op jit(solution)/shard_map/ppermute | solution.py:20
  11.1 1.6 %collective-permute-start.2 = (bf16[2,64,256]{2,1,0:T(8,128)(2,1)S(1)}, bf16[2,64,256]{2,1,0:T(8,128)(2,1)S(1)}, u32[]{:S(2)}, u32[]{:S(2)}) collective-permute-start(bf16[2,64,256]{2,1,0:T(8,128)(2,1)S(1)} %collective-permute-done.refs_1_.refs_5_), channel_id=1, source_target_pairs={{0,2},{2,0},{4,6},{6,4},{1,3},{3,1},{5,7},{7,5},{8,10},{10,8},{12,... | collective-permute-start | bytes 196616 | tf_op jit(solution)/shard_map/ppermute | solution.py:20
  12.6 0.0 collective-permute-done.7.refs_8_.refs_12_
  12.7 2.0 %collective-permute-start.4 = (bf16[2,64,256]{2,1,0:T(8,128)(2,1)S(1)}, bf16[2,64,256]{2,1,0:T(8,128)(2,1)S(1)}, u32[]{:S(2)}, u32[]{:S(2)}) collective-permute-start(bf16[2,64,256]{2,1,0:T(8,128)(2,1)S(1)} %collective-permute-done.refs_1_.refs_5_), channel_id=1, source_target_pairs={{0,16},{8,24},{16,0},{24,8},{1,17},{9,25},{17,1},{25,9},{2,18},{10... | collective-permute-start | bytes 196616 | tf_op jit(solution)/shard_map/ppermute | solution.py:20
  14.6 0.0 collective-permute-done.3.refs_4_.refs_8_
  14.6 0.0 collective-permute-start.17
  14.6 0.0 collective-permute-done.1.refs_2_.refs_6_
  14.6 0.5 %collective-permute-start.11 = (bf16[2,64,256]{2,1,0:T(8,128)(2,1)S(1)}, bf16[2,64,256]{2,1,0:T(8,128)(2,1)S(1)}, u32[]{:S(2)}, u32[]{:S(2)}) collective-permute-start(bf16[2,64,256]{2,1,0:T(8,128)(2,1)S(1)} %collective-permute-done.3.refs_4_.refs_8_), channel_id=1, source_target_pairs={{0,8},{8,0},{16,24},{24,16},{1,9},{9,1},{17,25},{25,17},{2,10},{10... | collective-permute-start | bytes 196616 | tf_op jit(solution)/shard_map/ppermute | solution.py:20
  15.1 0.0 collective-permute-done.8.refs_9_.refs_13_
  15.1 0.1 collective-permute-start.5
  15.2 0.1 collective-permute-done.2.refs_3_.refs_7_
  15.3 2.0 %collective-permute-start.6 = (bf16[2,64,256]{2,1,0:T(8,128)(2,1)S(1)}, bf16[2,64,256]{2,1,0:T(8,128)(2,1)S(1)}, u32[]{:S(2)}, u32[]{:S(2)}) collective-permute-start(bf16[2,64,256]{2,1,0:T(8,128)(2,1)S(1)} %collective-permute-done.2.refs_3_.refs_7_), channel_id=1, source_target_pairs={{0,16},{8,24},{16,0},{24,8},{1,17},{9,25},{17,1},{25,9},{2,18},{10... | collective-permute-start | bytes 196616 | tf_op jit(solution)/shard_map/ppermute | solution.py:20
  17.3 0.0 collective-permute-done.4.refs_5_.refs_9_
  17.3 0.0 collective-permute-start.9
  17.3 0.0 collective-permute-done.17.refs_3_
  17.3 0.5 %collective-permute-start.10 = (bf16[2,64,256]{2,1,0:T(8,128)(2,1)S(1)}, bf16[2,64,256]{2,1,0:T(8,128)(2,1)S(1)}, u32[]{:S(2)}, u32[]{:S(2)}) collective-permute-start(bf16[2,64,256]{2,1,0:T(8,128)(2,1)S(1)} %collective-permute-done.2.refs_3_.refs_7_), channel_id=1, source_target_pairs={{0,8},{8,0},{16,24},{24,16},{1,9},{9,1},{17,25},{25,17},{2,10},{10... | collective-permute-start | bytes 196616 | tf_op jit(solution)/shard_map/ppermute | solution.py:20
  17.8 0.0 collective-permute-done.11.refs_12_.refs_16_
  17.8 0.1 collective-permute-start.12
  17.9 2.0 %collective-permute-done.5.refs_6_.refs_10_ = bf16[2,64,256]{2,1,0:T(8,128)(2,1)S(1)} collective-permute-done((bf16[2,64,256]{2,1,0:T(8,128)(2,1)S(1)}, bf16[2,64,256]{2,1,0:T(8,128)(2,1)S(1)}, u32[]{:S(2)}, u32[]{:S(2)}) %collective-permute-start.5) | collective-permute-done | bytes 65568 | tf_op jit(solution)/shard_map/ppermute | solution.py:20
  19.9 0.0 collective-permute-start.13
  19.9 0.7 %collective-permute-done.6.refs_7_.refs_11_ = bf16[2,64,256]{2,1,0:T(8,128)(2,1)S(1)} collective-permute-done((bf16[2,64,256]{2,1,0:T(8,128)(2,1)S(1)}, bf16[2,64,256]{2,1,0:T(8,128)(2,1)S(1)}, u32[]{:S(2)}, u32[]{:S(2)}) %collective-permute-start.6) | collective-permute-done | bytes 65568 | tf_op jit(solution)/shard_map/ppermute | solution.py:20
  20.6 0.0 collective-permute-start.14
  20.6 0.0 collective-permute-done.9.refs_10_.refs_14_
  20.6 0.0 collective-permute-done.12.refs_13_.refs_17_
  20.6 0.0 collective-permute-done.10.refs_11_.refs_15_
  20.6 0.5 %collective-permute-done.13.refs_14_.refs_18_ = bf16[2,64,256]{2,1,0:T(8,128)(2,1)S(1)} collective-permute-done((bf16[2,64,256]{2,1,0:T(8,128)(2,1)S(1)}, bf16[2,64,256]{2,1,0:T(8,128)(2,1)S(1)}, u32[]{:S(2)}, u32[]{:S(2)}) %collective-permute-start.13) | collective-permute-done | bytes 65568 | tf_op jit(solution)/shard_map/ppermute | solution.py:20
  21.2 0.7 %collective-permute-done.14.refs_15_.refs_19_ = bf16[2,64,256]{2,1,0:T(8,128)(2,1)S(1)} collective-permute-done((bf16[2,64,256]{2,1,0:T(8,128)(2,1)S(1)}, bf16[2,64,256]{2,1,0:T(8,128)(2,1)S(1)}, u32[]{:S(2)}, u32[]{:S(2)}) %collective-permute-start.14) | collective-permute-done | bytes 65568 | tf_op jit(solution)/shard_map/ppermute | solution.py:20
  21.9 2.8 %cand_attention.1 = (bf16[64,2048]{1,0:T(8,128)(2,1)}, f32[1,8]{1,0:T(1,128)S(1)}) custom-call(s32[1,128]{1,0:T(1,128)S(1)} %get-tuple-element.14.lengths_ref, bf16[64,2048]{1,0:T(8,128)(2,1)S(1)} %get-tuple-element.15.q_ref, s32[1,8]{1,0:T(1,128)S(1)} %get-tuple-element.16.ends_ref, f32[1,2048]{1,0:T(1,128)S(1)} %get-tuple-element.17.head_ref, ...), custom_call_target="tpu_custom_call" | custom-call | tf_op jit(solution)/shard_map/cand_attention/pallas_call | solution.py:161
  24.7 0.6 %broadcast_in_dim.17 = f32[8,1,8]{2,1,0:T(1,128)} broadcast(f32[8]{0:T(128)S(1)} %bitcast.7), dimensions={2} | broadcast | bytes 288 | tf_op jit(solution)/shard_map/broadcast_in_dim | solution.py:174
  25.3 3.3 %all-to-all-start = ((f32[8,1,8]{2,1,0:T(1,128)}), f32[8,1,8]{2,1,0:T(1,128)S(1)}, u32[]{:S(2)}, u32[]{:S(2)}) async-start(f32[8,1,8]{2,1,0:T(1,128)} %broadcast_in_dim.17), calls=%async_computation | async-start | bytes 8192 | tf_op jit(solution)/shard_map/all_to_all | solution.py:175
  28.6 2.5 %prompt_attention.1 = bf16[64,2048]{1,0:T(8,128)(2,1)} custom-call(bf16[64,2048]{1,0:T(8,128)(2,1)S(1)} %get-tuple-element.12.q_ref, bf16[2,64,256]{2,1,0:T(8,128)(2,1)S(1)} %get-tuple-element.13.refs_0_.refs_4_, bf16[2,64,256]{2,1,0:T(8,128)(2,1)S(1)} %collective-permute-done.refs_1_.refs_5_, ...), custom_call_target="tpu_custom_call" | custom-call | tf_op jit(solution)/shard_map/prompt_attention/pallas_call | solution.py:176
  31.1 2.0 %all-to-all-done = f32[8,1,8]{2,1,0:T(1,128)S(1)} async-done(((f32[8,1,8]{2,1,0:T(1,128)}), f32[8,1,8]{2,1,0:T(1,128)S(1)}, u32[]{:S(2)}, u32[]{:S(2)}) %all-to-all-start) | async-done | bytes 288 | tf_op jit(solution)/shard_map/all_to_all | solution.py:175
  33.2 0.5 %reduce_sum.11 = f32[8]{0:T(128)} reduce(f32[8,1,8]{2,0,1:T(8,128)S(1)} %bitcast.10, f32[]{:T(128)} %constant.0.clone.1), dimensions={0,1}, to_apply=%region_0.0 | reduce | flops 56 | bytes 292 | tf_op jit(solution)/shard_map/reduce_sum | solution.py:175
Async XLA Ops:
  0.6 8.2 %collective-permute-start = (bf16[2,64,256]{2,1,0:T(8,128)(2,1)}, bf16[2,64,256]{2,1,0:T(8,128)(2,1)S(1)}, u32[]{:S(2)}, u32[]{:S(2)}) collective-permute-start(bf16[2,64,256]{2,1,0:T(8,128)(2,1)} %refs_2_.1), channel_id=1, source_target_pairs={{0,4},{2,6},{4,0},{6,2},{1,5},{3,7},{5,1},{7,3},{8,12},{10,14},{12... | collective-permute-start | bytes 196616 | tf_op jit(solution)/shard_map/ppermute | solution.py:20
  6.5 3.9 %collective-permute-start.16 = (bf16[2,64,256]{2,1,0:T(8,128)(2,1)S(1)}, bf16[2,64,256]{2,1,0:T(8,128)(2,1)S(1)}, u32[]{:S(2)}, u32[]{:S(2)}) collective-permute-start(bf16[2,64,256]{2,1,0:T(8,128)(2,1)S(1)} %get-tuple-element.18.refs_0_), channel_id=1, source_target_pairs={{0,8},{8,0},{16,24},{24,16},{1,9},{9,1},{17,25},{25,17},{2,10},{10... | collective-permute-start | bytes 196616 | tf_op jit(solution)/shard_map/ppermute | solution.py:20
  6.6 4.5 %collective-permute-start.15 = (bf16[2,64,256]{2,1,0:T(8,128)(2,1)S(1)}, bf16[2,64,256]{2,1,0:T(8,128)(2,1)S(1)}, u32[]{:S(2)}, u32[]{:S(2)}) collective-permute-start(bf16[2,64,256]{2,1,0:T(8,128)(2,1)S(1)} %get-tuple-element.18.refs_0_), channel_id=1, source_target_pairs={{0,16},{8,24},{16,0},{24,8},{1,17},{9,25},{17,1},{25,9},{2,18},{10... | collective-permute-start | bytes 196616 | tf_op jit(solution)/shard_map/ppermute | solution.py:20
  8.1 4.5 %collective-permute-start.7 = (bf16[2,64,256]{2,1,0:T(8,128)(2,1)S(1)}, bf16[2,64,256]{2,1,0:T(8,128)(2,1)S(1)}, u32[]{:S(2)}, u32[]{:S(2)}) collective-permute-start(bf16[2,64,256]{2,1,0:T(8,128)(2,1)S(1)} %get-tuple-element.13.refs_0_.refs_4_), channel_id=1, source_target_pairs={{0,8},{8,0},{16,24},{24,16},{1,9},{9,1},{17,25},{25,17},{2,10},{10... | collective-permute-start | bytes 196616 | tf_op jit(solution)/shard_map/ppermute | solution.py:20
  8.3 6.3 %collective-permute-start.3 = (bf16[2,64,256]{2,1,0:T(8,128)(2,1)S(1)}, bf16[2,64,256]{2,1,0:T(8,128)(2,1)S(1)}, u32[]{:S(2)}, u32[]{:S(2)}) collective-permute-start(bf16[2,64,256]{2,1,0:T(8,128)(2,1)S(1)} %get-tuple-element.13.refs_0_.refs_4_), channel_id=1, source_target_pairs={{0,16},{8,24},{16,0},{24,8},{1,17},{9,25},{17,1},{25,9},{2,18},{10... | collective-permute-start | bytes 196616 | tf_op jit(solution)/shard_map/ppermute | solution.py:20
  8.8 5.8 %collective-permute-start.1 = (bf16[2,64,256]{2,1,0:T(8,128)(2,1)S(1)}, bf16[2,64,256]{2,1,0:T(8,128)(2,1)S(1)}, u32[]{:S(2)}, u32[]{:S(2)}) collective-permute-start(bf16[2,64,256]{2,1,0:T(8,128)(2,1)S(1)} %get-tuple-element.13.refs_0_.refs_4_), channel_id=1, source_target_pairs={{0,2},{2,0},{4,6},{6,4},{1,3},{3,1},{5,7},{7,5},{8,10},{10,8},{12,... | collective-permute-start | bytes 196616 | tf_op jit(solution)/shard_map/ppermute | solution.py:20
  10.4 4.7 %collective-permute-start.8 = (bf16[2,64,256]{2,1,0:T(8,128)(2,1)S(1)}, bf16[2,64,256]{2,1,0:T(8,128)(2,1)S(1)}, u32[]{:S(2)}, u32[]{:S(2)}) collective-permute-start(bf16[2,64,256]{2,1,0:T(8,128)(2,1)S(1)} %collective-permute-done.refs_1_.refs_5_), channel_id=1, source_target_pairs={{0,8},{8,0},{16,24},{24,16},{1,9},{9,1},{17,25},{25,17},{2,10},{10... | collective-permute-start | bytes 196616 | tf_op jit(solution)/shard_map/ppermute | solution.py:20
  11.1 4.3 %collective-permute-start.2 = (bf16[2,64,256]{2,1,0:T(8,128)(2,1)S(1)}, bf16[2,64,256]{2,1,0:T(8,128)(2,1)S(1)}, u32[]{:S(2)}, u32[]{:S(2)}) collective-permute-start(bf16[2,64,256]{2,1,0:T(8,128)(2,1)S(1)} %collective-permute-done.refs_1_.refs_5_), channel_id=1, source_target_pairs={{0,2},{2,0},{4,6},{6,4},{1,3},{3,1},{5,7},{7,5},{8,10},{10,8},{12,... | collective-permute-start | bytes 196616 | tf_op jit(solution)/shard_map/ppermute | solution.py:20
  12.7 4.7 %collective-permute-start.4 = (bf16[2,64,256]{2,1,0:T(8,128)(2,1)S(1)}, bf16[2,64,256]{2,1,0:T(8,128)(2,1)S(1)}, u32[]{:S(2)}, u32[]{:S(2)}) collective-permute-start(bf16[2,64,256]{2,1,0:T(8,128)(2,1)S(1)} %collective-permute-done.refs_1_.refs_5_), channel_id=1, source_target_pairs={{0,16},{8,24},{16,0},{24,8},{1,17},{9,25},{17,1},{25,9},{2,18},{10... | collective-permute-start | bytes 196616 | tf_op jit(solution)/shard_map/ppermute | solution.py:20
  14.6 2.7 %collective-permute-start.17 = (bf16[2,64,256]{2,1,0:T(8,128)(2,1)S(1)}, bf16[2,64,256]{2,1,0:T(8,128)(2,1)S(1)}, u32[]{:S(2)}, u32[]{:S(2)}) collective-permute-start(bf16[2,64,256]{2,1,0:T(8,128)(2,1)S(1)} %collective-permute-done.15.refs_1_), channel_id=1, source_target_pairs={{0,8},{8,0},{16,24},{24,16},{1,9},{9,1},{17,25},{25,17},{2,10},{10... | collective-permute-start | bytes 196616 | tf_op jit(solution)/shard_map/ppermute | solution.py:20
  14.6 3.2 %collective-permute-start.11 = (bf16[2,64,256]{2,1,0:T(8,128)(2,1)S(1)}, bf16[2,64,256]{2,1,0:T(8,128)(2,1)S(1)}, u32[]{:S(2)}, u32[]{:S(2)}) collective-permute-start(bf16[2,64,256]{2,1,0:T(8,128)(2,1)S(1)} %collective-permute-done.3.refs_4_.refs_8_), channel_id=1, source_target_pairs={{0,8},{8,0},{16,24},{24,16},{1,9},{9,1},{17,25},{25,17},{2,10},{10... | collective-permute-start | bytes 196616 | tf_op jit(solution)/shard_map/ppermute | solution.py:20
  15.1 4.8 %collective-permute-start.5 = (bf16[2,64,256]{2,1,0:T(8,128)(2,1)S(1)}, bf16[2,64,256]{2,1,0:T(8,128)(2,1)S(1)}, u32[]{:S(2)}, u32[]{:S(2)}) collective-permute-start(bf16[2,64,256]{2,1,0:T(8,128)(2,1)S(1)} %collective-permute-done.1.refs_2_.refs_6_), channel_id=1, source_target_pairs={{0,16},{8,24},{16,0},{24,8},{1,17},{9,25},{17,1},{25,9},{2,18},{10... | collective-permute-start | bytes 196616 | tf_op jit(solution)/shard_map/ppermute | solution.py:20
  15.3 5.3 %collective-permute-start.6 = (bf16[2,64,256]{2,1,0:T(8,128)(2,1)S(1)}, bf16[2,64,256]{2,1,0:T(8,128)(2,1)S(1)}, u32[]{:S(2)}, u32[]{:S(2)}) collective-permute-start(bf16[2,64,256]{2,1,0:T(8,128)(2,1)S(1)} %collective-permute-done.2.refs_3_.refs_7_), channel_id=1, source_target_pairs={{0,16},{8,24},{16,0},{24,8},{1,17},{9,25},{17,1},{25,9},{2,18},{10... | collective-permute-start | bytes 196616 | tf_op jit(solution)/shard_map/ppermute | solution.py:20
  17.3 3.3 %collective-permute-start.9 = (bf16[2,64,256]{2,1,0:T(8,128)(2,1)S(1)}, bf16[2,64,256]{2,1,0:T(8,128)(2,1)S(1)}, u32[]{:S(2)}, u32[]{:S(2)}) collective-permute-start(bf16[2,64,256]{2,1,0:T(8,128)(2,1)S(1)} %collective-permute-done.1.refs_2_.refs_6_), channel_id=1, source_target_pairs={{0,8},{8,0},{16,24},{24,16},{1,9},{9,1},{17,25},{25,17},{2,10},{10... | collective-permute-start | bytes 196616 | tf_op jit(solution)/shard_map/ppermute | solution.py:20
  17.3 3.3 %collective-permute-start.10 = (bf16[2,64,256]{2,1,0:T(8,128)(2,1)S(1)}, bf16[2,64,256]{2,1,0:T(8,128)(2,1)S(1)}, u32[]{:S(2)}, u32[]{:S(2)}) collective-permute-start(bf16[2,64,256]{2,1,0:T(8,128)(2,1)S(1)} %collective-permute-done.2.refs_3_.refs_7_), channel_id=1, source_target_pairs={{0,8},{8,0},{16,24},{24,16},{1,9},{9,1},{17,25},{25,17},{2,10},{10... | collective-permute-start | bytes 196616 | tf_op jit(solution)/shard_map/ppermute | solution.py:20
  17.8 2.8 %collective-permute-start.12 = (bf16[2,64,256]{2,1,0:T(8,128)(2,1)S(1)}, bf16[2,64,256]{2,1,0:T(8,128)(2,1)S(1)}, u32[]{:S(2)}, u32[]{:S(2)}) collective-permute-start(bf16[2,64,256]{2,1,0:T(8,128)(2,1)S(1)} %collective-permute-done.4.refs_5_.refs_9_), channel_id=1, source_target_pairs={{0,8},{8,0},{16,24},{24,16},{1,9},{9,1},{17,25},{25,17},{2,10},{10... | collective-permute-start | bytes 196616 | tf_op jit(solution)/shard_map/ppermute | solution.py:20
  19.9 1.3 %collective-permute-start.13 = (bf16[2,64,256]{2,1,0:T(8,128)(2,1)S(1)}, bf16[2,64,256]{2,1,0:T(8,128)(2,1)S(1)}, u32[]{:S(2)}, u32[]{:S(2)}) collective-permute-start(bf16[2,64,256]{2,1,0:T(8,128)(2,1)S(1)} %collective-permute-done.5.refs_6_.refs_10_), channel_id=1, source_target_pairs={{0,8},{8,0},{16,24},{24,16},{1,9},{9,1},{17,25},{25,17},{2,10},{10... | collective-permute-start | bytes 196616 | tf_op jit(solution)/shard_map/ppermute | solution.py:20
  20.6 1.3 %collective-permute-start.14 = (bf16[2,64,256]{2,1,0:T(8,128)(2,1)S(1)}, bf16[2,64,256]{2,1,0:T(8,128)(2,1)S(1)}, u32[]{:S(2)}, u32[]{:S(2)}) collective-permute-start(bf16[2,64,256]{2,1,0:T(8,128)(2,1)S(1)} %collective-permute-done.6.refs_7_.refs_11_), channel_id=1, source_target_pairs={{0,8},{8,0},{16,24},{24,16},{1,9},{9,1},{17,25},{25,17},{2,10},{10... | collective-permute-start | bytes 196616 | tf_op jit(solution)/shard_map/ppermute | solution.py:20
  25.3 7.9 %all-to-all-start = ((f32[8,1,8]{2,1,0:T(1,128)}), f32[8,1,8]{2,1,0:T(1,128)S(1)}, u32[]{:S(2)}, u32[]{:S(2)}) async-start(f32[8,1,8]{2,1,0:T(1,128)} %broadcast_in_dim.17), calls=%async_computation | async-start | bytes 8192 | tf_op jit(solution)/shard_map/all_to_all | solution.py:175

commit v3 on v1

v3 whole, which is shorter than its diff:
```python
import functools
import math

import jax
import jax.numpy as jnp
from jax import lax
from jax.experimental import pallas as pl
from jax.experimental.pallas import tpu as pltpu
from jax.sharding import PartitionSpec as P

HEADDIM = 128
GROUP = 8
SUBLANES = 8
NEG_FILL = -1e30
SCALE = HEADDIM ** -0.5 * math.log2(math.e)
ROW_TILE = 256
VMEM_LIMIT = 48 * 1024 * 1024
PARAMS = pltpu.CompilerParams(vmem_limit_bytes=VMEM_LIMIT)
PROMPT_AXES = ("ctx", "cand")


def vmem(count):
    return [pl.BlockSpec(memory_space=pltpu.VMEM)] * count


def like(array):
    return jax.ShapeDtypeStruct(array.shape, array.dtype)


def high_bits(size, lowest):
    return [1 << b for b in reversed(range(size.bit_length() - 1)) if 1 << b >= lowest]


def flipped(block, axes, size, bit):
    return lax.ppermute(block, axes, [(i, i ^ bit) for i in range(size)])


def pack_kernel(*refs):
    sources, out_ref = refs[:-1], refs[-1]
    start = 0
    for ref in sources:
        out_ref[start : start + ref.shape[0]] = ref[...]
        start += ref.shape[0]


def packed(*arrays):
    count = sum(a.shape[0] for a in arrays)
    return pl.pallas_call(
        pack_kernel,
        out_shape=jax.ShapeDtypeStruct((count,) + arrays[0].shape[1:], arrays[0].dtype),
        in_specs=vmem(len(arrays)),
        out_specs=vmem(1)[0],
        compiler_params=PARAMS,
        name="pack_blocks",
    )(*arrays)


def prompt_bits(ctx_size, cand_size):
    core, along, across = cand_size, 1, 2 * cand_size
    early = high_bits(cand_size, 2) + [bit * cand_size for bit in high_bits(ctx_size, 4)]
    return early, along, across, core


def gather_prompt(first, own, ctx_size, cand_size):
    size = ctx_size * cand_size
    early, along, across, core = prompt_bits(ctx_size, cand_size)
    held = own[None]
    for bit in early:
        sent = held if first is None else first[None]
        first = None
        held = packed(held, flipped(sent, PROMPT_AXES, size, bit))

    def shared_out(block, even, odd):
        return lax.ppermute(
            block, PROMPT_AXES, [(i, i ^ (odd if i & core else even)) for i in range(size)]
        )

    second = shared_out(held, along, across)
    third = shared_out(held, across, along)
    fourth = shared_out(second, across, along)
    rail = [held, second, third, fourth]
    return rail + [flipped(block, PROMPT_AXES, size, core) for block in rail]


def prompt_owners(ctx_size, cand_size):
    early, along, across, core = prompt_bits(ctx_size, cand_size)
    place = lax.axis_index("ctx") * cand_size + lax.axis_index("cand")
    odd = lax.rem(lax.axis_index("ctx"), 2)
    near = along + odd * (across - along)
    far = along + across - near
    masks = [0]
    for bit in early:
        masks += [mask ^ bit for mask in masks]
    shifts = [0, near, far, along + across, core, core + far, core + near, core + along + across]
    return [[place ^ mask ^ shift for mask in masks] for shift in shifts]


def gather_cand(own, ctx_size):
    blocks = [(own, 0)]
    for bit in high_bits(ctx_size, 2) + [1]:
        blocks += [(flipped(b, "ctx", ctx_size, bit), mask | bit) for b, mask in blocks]
    return blocks


def stage_kernel(length_ref, prompt_q, cand_q, prompt_kv, cand_kv, ends, head, *refs):
    q_out, cand_out, kv_out, pay_out, ends_out, head_out, length_out, sems = refs
    steps = ends.shape[1]
    pairs = [
        (cand_q, cand_out),
        (ends, ends_out),
        (cand_kv, pay_out.at[0:2]),
        (prompt_kv, kv_out),
        (prompt_q, q_out),
        (head, head_out),
    ]
    copies = [pltpu.make_async_copy(a, b, sems.at[i]) for i, (a, b) in enumerate(pairs)]
    for copy in copies:
        copy.start()
    length_out[...] = jnp.full(length_out.shape, length_ref[0], jnp.int32)
    copies[0].wait()
    copies[1].wait()
    rows = cand_out.shape[0]
    ends_column = column_of(ends_out[...])
    row_pos = lax.axis_index("ctx") * rows + lax.broadcasted_iota(jnp.int32, (steps, rows), 1)
    chosen = (row_pos == ends_column).astype(jnp.bfloat16)
    picked = jnp.dot(chosen, cand_out[...], preferred_element_type=jnp.float32)
    width = pay_out.shape[2]
    pieces = [picked[:, at : at + width] for at in range(0, picked.shape[1], width)]
    pay_out[2] = jnp.concatenate(pieces, axis=0).astype(jnp.bfloat16)
    for copy in copies[2:]:
        copy.wait()


def column_of(row):
    count = row.shape[1]
    down = lax.broadcasted_iota(jnp.int32, (count, count), 0)
    right = lax.broadcasted_iota(jnp.int32, (count, count), 1)
    return jnp.sum(jnp.where(down == right, row, 0), axis=1, keepdims=True)


def staged(length, prompt_q, cand_q, prompt_kv, cand_kv, ends, head):
    arrays = (prompt_q, cand_q, prompt_kv, cand_kv, ends, head)
    payload = jax.ShapeDtypeStruct((3,) + cand_kv.shape[1:], cand_kv.dtype)
    lengths = jax.ShapeDtypeStruct((1, HEADDIM), jnp.int32)
    return pl.pallas_call(
        stage_kernel,
        out_shape=(like(prompt_q), like(cand_q), like(prompt_kv), payload, like(ends), like(head), lengths),
        in_specs=[pl.BlockSpec(memory_space=pltpu.SMEM)]
        + [pl.BlockSpec(memory_space=pltpu.HBM)] * len(arrays),
        out_specs=tuple(vmem(7)),
        scratch_shapes=[pltpu.SemaphoreType.DMA((len(arrays),))],
        compiler_params=PARAMS,
        name="stage_operands",
    )(length, *(pltpu.with_memory_space_constraint(a, pltpu.HBM) for a in arrays))


def blend(queries, key_rows, widened, key_pos, row_pos, free):
    scores = lax.dot_general(
        queries, key_rows, (((1,), (1,)), ((), ())), preferred_element_type=jnp.float32
    )
    bound = jnp.where(key_pos <= row_pos, scores[:, free:], NEG_FILL)
    scores = bound if free == 0 else jnp.concatenate([scores[:, :free], bound], axis=1)
    peak = jnp.max(scores, axis=1, keepdims=True)
    weights = jnp.exp2((scores - peak) * SCALE).astype(jnp.bfloat16)
    blended = jnp.dot(weights, widened, preferred_element_type=jnp.float32)
    return blended[:, :HEADDIM] / blended[:, HEADDIM:]


def head_operands(kv_ref, count, head):
    columns = slice(head * HEADDIM, (head + 1) * HEADDIM)
    key_rows = kv_ref[0, :count, columns]
    value_rows = kv_ref[1, :count, columns]
    return key_rows, jnp.concatenate([value_rows, jnp.ones_like(value_rows)], axis=1)


def tiles(q_ref, head):
    fan = max(1, ROW_TILE // q_ref.shape[0])
    for start in range(head * GROUP, (head + 1) * GROUP, fan):
        heads = range(start, start + fan)
        yield heads, jnp.concatenate([q_ref[:, h * HEADDIM : (h + 1) * HEADDIM] for h in heads], axis=0)


def stacked_rows(first_row, rows, count):
    return first_row + lax.rem(lax.broadcasted_iota(jnp.int32, (count, 1), 0), jnp.int32(rows))


def prompt_kernel(cand_size, q_ref, kv_ref, out_ref):
    rows = q_ref.shape[0]
    count = rows * lax.axis_size(PROMPT_AXES)
    first_row = (lax.axis_index("ctx") * cand_size + lax.axis_index("cand")) * rows
    key_pos = lax.broadcasted_iota(jnp.int32, (1, count), 1)
    for head in range(kv_ref.shape[2] // HEADDIM):
        key_rows, widened = head_operands(kv_ref, count, head)
        for heads, queries in tiles(q_ref, head):
            row_pos = stacked_rows(first_row, rows, queries.shape[0])
            result = blend(queries, key_rows, widened, key_pos, row_pos, 0)
            for index, h in enumerate(heads):
                out_ref[:, h * HEADDIM : (h + 1) * HEADDIM] = result[
                    index * rows : (index + 1) * rows
                ].astype(jnp.bfloat16)


def cand_kernel(masks, ctx_size, cand_size, q_ref, ends_ref, head_ref, lengths_ref, *refs):
    pays, blocks = refs[: len(masks)], refs[len(masks) : -3]
    out_ref, logit_ref, kv_ref = refs[-3:]
    rows = q_ref.shape[0]
    free = rows * ctx_size * cand_size
    place = lax.axis_index("ctx")
    for ref, owners in zip(blocks, prompt_owners(ctx_size, cand_size)):
        for index, owner in enumerate(owners):
            at = pl.ds(pl.multiple_of(owner * rows, rows), rows)
            kv_ref[0, at, :] = ref[index, 0]
            kv_ref[1, at, :] = ref[index, 1]
    picked = jnp.zeros(pays[0].shape[1:], jnp.float32)
    for ref, mask in zip(pays, masks):
        at = pl.ds(pl.multiple_of(free + (place ^ mask) * rows, rows), rows)
        kv_ref[0, at, :] = ref[0]
        kv_ref[1, at, :] = ref[1]
        picked += ref[2].astype(jnp.float32)
    steps = ends_ref.shape[1]
    width = picked.shape[1]
    step_rows = [picked[at : at + steps] for at in range(0, steps * q_ref.shape[1] // width, steps)]

    count = free + rows * len(masks)
    key_pos = lax.broadcasted_iota(jnp.int32, (1, rows * len(masks)), 1)
    first_row = place * rows
    length = lengths_ref[:, :1]
    alive = stacked_rows(first_row, rows, rows) < length
    ends = column_of(ends_ref[...])
    total = jnp.zeros((steps, HEADDIM), jnp.float32)
    for head in range(kv_ref.shape[2] // HEADDIM):
        key_rows, widened = head_operands(kv_ref, count, head)
        for heads, queries in tiles(q_ref, head):
            row_pos = stacked_rows(first_row, rows, queries.shape[0])
            result = blend(queries, key_rows, widened, key_pos, row_pos, free)
            for index, h in enumerate(heads):
                kept = jnp.where(alive, result[index * rows : (index + 1) * rows], 0.0)
                out_ref[:, h * HEADDIM : (h + 1) * HEADDIM] = kept.astype(jnp.bfloat16)
        heads = range(head * GROUP, (head + 1) * GROUP)
        offsets = [divmod(h * HEADDIM, width) for h in heads]
        queries = jnp.concatenate([step_rows[a][:, b : b + HEADDIM] for a, b in offsets], axis=0)
        row_pos = jnp.concatenate([ends] * GROUP, axis=0)
        result = blend(queries.astype(jnp.bfloat16), key_rows, widened, key_pos, row_pos, free)
        for index, h in enumerate(heads):
            kept = jnp.where(ends < length, result[index * steps : (index + 1) * steps], 0.0)
            kept = kept.astype(jnp.bfloat16).astype(jnp.float32)
            total += kept * head_ref[:, h * HEADDIM : (h + 1) * HEADDIM]
    logits = jnp.sum(total, axis=1, keepdims=True)
    down = lax.broadcasted_iota(jnp.int32, (steps, steps), 0)
    right = lax.broadcasted_iota(jnp.int32, (steps, steps), 1)
    logit_ref[...] = jnp.sum(jnp.where(down == right, logits, 0.0), axis=0, keepdims=True)


def per_device(ctx_size, cand_size, prompt_q, prompt_kv, cand_q, cand_kv, cand_lengths, step_ends, reward_head):
    q_rows, cand_rows, own, payload, ends, head, lengths = staged(
        cand_lengths, prompt_q, cand_q[0], prompt_kv, cand_kv[:, 0], step_ends, reward_head[None]
    )
    blocks = gather_prompt(prompt_kv, own, ctx_size, cand_size)
    pays = gather_cand(payload, ctx_size)
    key_count = q_rows.shape[0] * ctx_size * cand_size + cand_rows.shape[0] * ctx_size
    cand_out, partial, arranged = pl.pallas_call(
        functools.partial(cand_kernel, [mask for _, mask in pays], ctx_size, cand_size),
        out_shape=(
            like(cand_rows),
            jax.ShapeDtypeStruct(step_ends.shape, jnp.float32),
            jax.ShapeDtypeStruct((2, key_count, own.shape[2]), own.dtype),
        ),
        in_specs=vmem(4 + len(pays) + len(blocks)),
        out_specs=tuple(vmem(3)),
        compiler_params=PARAMS,
        name="cand_attention",
    )(cand_rows, ends, head, lengths, *(b for b, _ in pays), *blocks)
    step_logits = partial
    tp_size = lax.axis_size("tp")
    for bit in high_bits(tp_size, 1):
        step_logits = step_logits + flipped(step_logits, "tp", tp_size, bit)
    prompt_out = pl.pallas_call(
        functools.partial(prompt_kernel, cand_size),
        out_shape=like(prompt_q),
        in_specs=vmem(2),
        out_specs=vmem(1)[0],
        compiler_params=PARAMS,
        name="prompt_attention",
    )(q_rows, arranged)
    return (prompt_out, cand_out[None], step_logits)


def solution(mesh):
    placed = (
        P(("ctx", "cand"), "tp"),
        P(None, ("ctx", "cand"), "tp"),
        P("cand", "ctx", "tp"),
        P(None, "cand", "ctx", "tp"),
        P("cand"),
        P("cand", None),
        P("tp"),
    )
    return jax.shard_map(
        functools.partial(per_device, mesh.shape["ctx"], mesh.shape["cand"]),
        mesh=mesh,
        in_specs=placed,
        out_specs=(P(("ctx", "cand"), "tp"), P("cand", "ctx", "tp"), P("cand", None)),
        check_vma=False,
    )
```

time: 45 us -> 30.8 us (0.68)
  blocking collectives: 15 us -> 0 us
  waiting for transfers between devices: 4.86 us -> 10.7 us
  local copies, waits for them, and re-layouts: 3.99 us -> 0 us
  starting transfers between devices: 14.2 us -> 10.8 us
  Pallas kernels: 5.32 us -> 7.35 us
  other arithmetic: 0 us -> 0.51 us
    psum x1 -> x0, blocking collectives: 15 us -> none  [per_device(): step_logits = lax.psum(partial, ('ctx', 'tp'))]
    ppermute x18 -> x12, waiting for transfers between devices: 4.86 us -> 10.7 us  [the longest x9 5.98 us: flipped(): return lax.ppermute(block, axes, [(i, i ^ bit) for i in range(size)])]
    unnamed x14 -> x0, local copies, waits for them, and re-layouts: 3.99 us -> none
    ppermute x18 -> x12, starting transfers between devices: 14.2 us -> 10.8 us  [the longest x9 6.84 us: flipped(): return lax.ppermute(block, axes, [(i, i ^ bit) for i in range(size)])]
    pallas_call x2 -> x4, Pallas kernels: 5.32 us -> 7.35 us  [the longest x1 3.37 us: per_device(): pl.pallas_call(functools.partial(cand_kernel, [mask for _, mask in pays],...]
    add x0 -> x1, other arithmetic: none -> 0.51 us  [per_device(): step_logits = step_logits + flipped(step_logits, 'tp', tp_size, bit)]
  transfers between devices with their start and end apart: 18 -> 12, of which waited for: 7 -> 6; matrix products, arithmetic and copies ran while one was open for 0% -> 0% of each run, Pallas kernels for 0% -> 13%
where the time goes in v3:
time: 30.8 us; the launch traced here: 30.6 us
  starting transfers between devices  10.8 us (35%)
  waiting for transfers between devices  10.7 us (35%)
  Pallas kernels  7.35 us (24%)
  between operations  1.31 us (4%)
  other arithmetic  0.51 us (2%)
    ppermute x9, starting transfers between devices, flipped(): return lax.ppermute(block, axes, [(i, i ^ bit) for i in range(size)])  6.84 us
    ppermute x9, waiting for transfers between devices, flipped(): return lax.ppermute(block, axes, [(i, i ^ bit) for i in range(size)])  5.98 us
    ppermute x3, waiting for transfers between devices, shared_out(): lax.ppermute(block, PROMPT_AXES, [(i, i ^ (odd if i & core else even)) fo...  4.67 us
    ppermute x3, starting transfers between devices, shared_out(): lax.ppermute(block, PROMPT_AXES, [(i, i ^ (odd if i & core else even)) fo...  3.97 us
    pallas_call x1, Pallas kernels, per_device(): pl.pallas_call(functools.partial(cand_kernel, [mask for _, mask in pays],...  3.37 us
    pallas_call x1, Pallas kernels, per_device(): pl.pallas_call(functools.partial(prompt_kernel, cand_size), out_shape=lik...  2.72 us
    pallas_call x1, Pallas kernels, staged(): pl.pallas_call(stage_kernel, out_shape=(like(prompt_q), like(cand_q), lik...  1.25 us
  transfers between devices with their start and end apart: 12, of which 6 were waited for; matrix products, arithmetic and copies ran while one was open for 0% of the time, Pallas kernels for 13%

profile of v3, /device:TPU:0, one launch (start us, length us, event | category | flops | bytes accessed | tf_op | source)
XLA Modules:
  0.0 30.6 jit_solution(11081862355117501325)
XLA Ops:
  0.6 4.1 %collective-permute-start.3 = (bf16[1,2,64,256]{3,2,1,0:T(8,128)(2,1)}, bf16[1,2,64,256]{3,2,1,0:T(8,128)(2,1)S(1)}, u32[]{:S(2)}, u32[]{:S(2)}) collective-permute-start(bf16[1,2,64,256]{3,2,1,0:T(8,128)(2,1)} %bitcast.9), channel_id=1, source_target_pairs={{0,4},{2,6},{4,0},{6,2},{8,12},{10,14},{12,8},{14,10},{16,20},{18,... | collective-permute-start | bytes 196616 | tf_op jit(solution)/shard_map/ppermute | solution.py:35
  5.4 1.2 %stage_operands.1 = (bf16[64,2048]{1,0:T(8,128)(2,1)S(1)}, bf16[64,2048]{1,0:T(8,128)(2,1)S(1)}, bf16[2,64,256]{2,1,0:T(8,128)(2,1)S(1)}, bf16[3,64,256]{2,1,0:T...) custom-call(s32[1]{0:T(128)S(6)} %copy.10.length_ref, ...), custom_call_target="tpu_custom_call" | custom-call | tf_op jit(solution)/shard_map/stage_operands/pallas_call | solution.py:145
  6.6 2.0 %collective-permute-done.3.refs_1_ = bf16[1,2,64,256]{3,2,1,0:T(8,128)(2,1)S(1)} collective-permute-done((bf16[1,2,64,256]{3,2,1,0:T(8,128)(2,1)}, bf16[1,2,64,256]{3,2,1,0:T(8,128)(2,1)S(1)}, u32[]{:S(2)}, u32[]{:S(2)}) %collective-permute-start.3) | collective-permute-done | bytes 65568 | tf_op jit(solution)/shard_map/ppermute | solution.py:35
  8.6 0.7 %collective-permute-start.4 = (bf16[2,2,64,256]{3,2,1,0:T(8,128)(2,1)S(1)}, bf16[2,2,64,256]{3,2,1,0:T(8,128)(2,1)S(1)}, u32[]{:S(2)}, u32[]{:S(2)}) collective-permute-start(bf16[2,2,64,256]{3,2,1,0:T(8,128)(2,1)S(1)} %pack_blocks.1.refs_4_), channel_id=1, source_target_pairs={{0,2},{2,0},{4,6},{6,4},{8,24},{10,26},{12,28},{14,30},{16,18},{18... | collective-permute-start | bytes 393224 | tf_op jit(solution)/shard_map/ppermute | solution.py:74
  9.3 1.5 %collective-permute-start.5 = (bf16[2,2,64,256]{3,2,1,0:T(8,128)(2,1)S(1)}, bf16[2,2,64,256]{3,2,1,0:T(8,128)(2,1)S(1)}, u32[]{:S(2)}, u32[]{:S(2)}) collective-permute-start(bf16[2,2,64,256]{3,2,1,0:T(8,128)(2,1)S(1)} %pack_blocks.1.refs_4_), channel_id=1, source_target_pairs={{0,16},{2,18},{4,20},{6,22},{8,10},{10,8},{12,14},{14,12},{16,0},{... | collective-permute-start | bytes 393224 | tf_op jit(solution)/shard_map/ppermute | solution.py:74
  10.9 3.1 %collective-permute-done.4.refs_5_ = bf16[2,2,64,256]{3,2,1,0:T(8,128)(2,1)S(1)} collective-permute-done((bf16[2,2,64,256]{3,2,1,0:T(8,128)(2,1)S(1)}, bf16[2,2,64,256]{3,2,1,0:T(8,128)(2,1)S(1)}, u32[]{:S(2)}, u32[]{:S(2)}) %collective-permute-start.4) | collective-permute-done | bytes 131104 | tf_op jit(solution)/shard_map/ppermute | solution.py:74
  14.0 1.7 %collective-permute-start.6 = (bf16[2,2,64,256]{3,2,1,0:T(8,128)(2,1)S(1)}, bf16[2,2,64,256]{3,2,1,0:T(8,128)(2,1)S(1)}, u32[]{:S(2)}, u32[]{:S(2)}) collective-permute-start(bf16[2,2,64,256]{3,2,1,0:T(8,128)(2,1)S(1)} %collective-permute-done.4.refs_5_), channel_id=1, source_target_pairs={{0,16},{2,18},{4,20},{6,22},{8,10},{10,8},{12,14},{14,12},{16,0},{... | collective-permute-start | bytes 393224 | tf_op jit(solution)/shard_map/ppermute | solution.py:74
  15.7 0.0 collective-permute-start.1
  15.7 0.3 %collective-permute-start = (bf16[3,64,256]{2,1,0:T(8,128)(2,1)S(1)}, bf16[3,64,256]{2,1,0:T(8,128)(2,1)S(1)}, u32[]{:S(2)}, u32[]{:S(2)}) collective-permute-start(bf16[3,64,256]{2,1,0:T(8,128)(2,1)S(1)} %get-tuple-element.18.refs_0_), channel_id=1, source_target_pairs={{0,16},{8,24},{16,0},{24,8},{1,17},{9,25},{17,1},{25,9},{2,18},{10... | collective-permute-start | bytes 294920 | tf_op jit(solution)/shard_map/ppermute | solution.py:35
  16.0 0.2 collective-permute-start.7
  16.2 0.8 %collective-permute-done.1.refs_2_ = bf16[3,64,256]{2,1,0:T(8,128)(2,1)S(1)} collective-permute-done((bf16[3,64,256]{2,1,0:T(8,128)(2,1)S(1)}, bf16[3,64,256]{2,1,0:T(8,128)(2,1)S(1)}, u32[]{:S(2)}, u32[]{:S(2)}) %collective-permute-start.1) | collective-permute-done | bytes 98336 | tf_op jit(solution)/shard_map/ppermute | solution.py:35
  17.0 0.2 collective-permute-start.8
  17.1 0.0 collective-permute-done.5.refs_6_
  17.1 0.4 %collective-permute-start.9 = (bf16[2,2,64,256]{3,2,1,0:T(8,128)(2,1)S(1)}, bf16[2,2,64,256]{3,2,1,0:T(8,128)(2,1)S(1)}, u32[]{:S(2)}, u32[]{:S(2)}) collective-permute-start(bf16[2,2,64,256]{3,2,1,0:T(8,128)(2,1)S(1)} %collective-permute-done.5.refs_6_), channel_id=1, source_target_pairs={{0,8},{2,10},{4,12},{6,14},{8,0},{10,2},{12,4},{14,6},{16,24},{18,... | collective-permute-start | bytes 393224 | tf_op jit(solution)/shard_map/ppermute | solution.py:35
  17.5 1.6 %collective-permute-done.6.refs_7_ = bf16[2,2,64,256]{3,2,1,0:T(8,128)(2,1)S(1)} collective-permute-done((bf16[2,2,64,256]{3,2,1,0:T(8,128)(2,1)S(1)}, bf16[2,2,64,256]{3,2,1,0:T(8,128)(2,1)S(1)}, u32[]{:S(2)}, u32[]{:S(2)}) %collective-permute-start.6) | collective-permute-done | bytes 131104 | tf_op jit(solution)/shard_map/ppermute | solution.py:74
  19.1 0.0 collective-permute-start.10
  19.1 2.0 %collective-permute-done.refs_1_ = bf16[3,64,256]{2,1,0:T(8,128)(2,1)S(1)} collective-permute-done((bf16[3,64,256]{2,1,0:T(8,128)(2,1)S(1)}, bf16[3,64,256]{2,1,0:T(8,128)(2,1)S(1)}, u32[]{:S(2)}, u32[]{:S(2)}) %collective-permute-start) | collective-permute-done | bytes 98336 | tf_op jit(solution)/shard_map/ppermute | solution.py:35
  21.0 0.0 collective-permute-start.2
  21.0 0.0 collective-permute-done.7.refs_8_
  21.0 1.3 %collective-permute-done.2.refs_3_ = bf16[3,64,256]{2,1,0:T(8,128)(2,1)S(1)} collective-permute-done((bf16[3,64,256]{2,1,0:T(8,128)(2,1)S(1)}, bf16[3,64,256]{2,1,0:T(8,128)(2,1)S(1)}, u32[]{:S(2)}, u32[]{:S(2)}) %collective-permute-start.2) | collective-permute-done | bytes 98336 | tf_op jit(solution)/shard_map/ppermute | solution.py:35
  22.3 0.0 collective-permute-done.9.refs_10_
  22.3 0.0 collective-permute-done.8.refs_9_
  22.3 0.0 collective-permute-done.10.refs_11_
  22.3 3.4 %cand_attention.1 = (bf16[64,2048]{1,0:T(8,128)(2,1)}, f32[1,8]{1,0:T(1,128)S(1)}, bf16[2,1280,256]{2,1,0:T(8,128)(2,1)S(1)}) custom-call(bf16[64,2048]{1,0:T(8,128)(2,1)S(1)} %get-tuple-element.14.q_ref, s32[1,8]{1,0:T(1,128)S(1)} %get-tuple-element.15.ends_ref, f32[1,2048]{1,0:T(1,128)S(1)} %get-tuple-element.16.head_ref, ...), custom_call_target="tpu_custom_call" | custom-call | tf_op jit(solution)/shard_map/cand_attention/pallas_call | solution.py:261
  25.7 1.7 %collective-permute-start.11 = (f32[1,8]{1,0:T(1,128)S(1)}, f32[1,8]{1,0:T(1,128)S(1)}, u32[]{:S(2)}, u32[]{:S(2)}) collective-permute-start(f32[1,8]{1,0:T(1,128)S(1)} %get-tuple-element.22), channel_id=1, source_target_pairs={{0,1},{1,0},{2,3},{3,2},{4,5},{5,4},{6,7},{7,6},{8,9},{9,8},{10,11... | collective-permute-start | bytes 104 | tf_op jit(solution)/shard_map/ppermute | solution.py:35
  27.4 2.7 %prompt_attention.1 = bf16[64,2048]{1,0:T(8,128)(2,1)} custom-call(bf16[64,2048]{1,0:T(8,128)(2,1)S(1)} %get-tuple-element.13.q_ref, bf16[2,1280,256]{2,1,0:T(8,128)(2,1)S(1)} %get-tuple-element.20.kv_ref), custom_call_target="tpu_custom_call" | custom-call | tf_op jit(solution)/shard_map/prompt_attention/pallas_call | solution.py:277
  30.1 0.0 collective-permute-done.11
  30.1 0.5 %add.3 = f32[1,8]{1,0:T(1,128)} add(f32[1,8]{1,0:T(1,128)S(1)} %get-tuple-element.22, f32[1,8]{1,0:T(1,128)S(1)} %collective-permute-done.11) | non-fusion elementwise | flops 8 | bytes 96 | tf_op jit(solution)/shard_map/add | solution.py:276
  (1 shorter events, 0.0 us)
Async XLA Ops:
  0.6 8.0 %collective-permute-start.3 = (bf16[1,2,64,256]{3,2,1,0:T(8,128)(2,1)}, bf16[1,2,64,256]{3,2,1,0:T(8,128)(2,1)S(1)}, u32[]{:S(2)}, u32[]{:S(2)}) collective-permute-start(bf16[1,2,64,256]{3,2,1,0:T(8,128)(2,1)} %bitcast.9), channel_id=1, source_target_pairs={{0,4},{2,6},{4,0},{6,2},{8,12},{10,14},{12,8},{14,10},{16,20},{18,... | collective-permute-start | bytes 196616 | tf_op jit(solution)/shard_map/ppermute | solution.py:35
  8.6 5.3 %collective-permute-start.4 = (bf16[2,2,64,256]{3,2,1,0:T(8,128)(2,1)S(1)}, bf16[2,2,64,256]{3,2,1,0:T(8,128)(2,1)S(1)}, u32[]{:S(2)}, u32[]{:S(2)}) collective-permute-start(bf16[2,2,64,256]{3,2,1,0:T(8,128)(2,1)S(1)} %pack_blocks.1.refs_4_), channel_id=1, source_target_pairs={{0,2},{2,0},{4,6},{6,4},{8,24},{10,26},{12,28},{14,30},{16,18},{18... | collective-permute-start | bytes 393224 | tf_op jit(solution)/shard_map/ppermute | solution.py:74
  9.3 7.8 %collective-permute-start.5 = (bf16[2,2,64,256]{3,2,1,0:T(8,128)(2,1)S(1)}, bf16[2,2,64,256]{3,2,1,0:T(8,128)(2,1)S(1)}, u32[]{:S(2)}, u32[]{:S(2)}) collective-permute-start(bf16[2,2,64,256]{3,2,1,0:T(8,128)(2,1)S(1)} %pack_blocks.1.refs_4_), channel_id=1, source_target_pairs={{0,16},{2,18},{4,20},{6,22},{8,10},{10,8},{12,14},{14,12},{16,0},{... | collective-permute-start | bytes 393224 | tf_op jit(solution)/shard_map/ppermute | solution.py:74
  14.0 5.1 %collective-permute-start.6 = (bf16[2,2,64,256]{3,2,1,0:T(8,128)(2,1)S(1)}, bf16[2,2,64,256]{3,2,1,0:T(8,128)(2,1)S(1)}, u32[]{:S(2)}, u32[]{:S(2)}) collective-permute-start(bf16[2,2,64,256]{3,2,1,0:T(8,128)(2,1)S(1)} %collective-permute-done.4.refs_5_), channel_id=1, source_target_pairs={{0,16},{2,18},{4,20},{6,22},{8,10},{10,8},{12,14},{14,12},{16,0},{... | collective-permute-start | bytes 393224 | tf_op jit(solution)/shard_map/ppermute | solution.py:74
  15.7 1.3 %collective-permute-start.1 = (bf16[3,64,256]{2,1,0:T(8,128)(2,1)S(1)}, bf16[3,64,256]{2,1,0:T(8,128)(2,1)S(1)}, u32[]{:S(2)}, u32[]{:S(2)}) collective-permute-start(bf16[3,64,256]{2,1,0:T(8,128)(2,1)S(1)} %get-tuple-element.18.refs_0_), channel_id=1, source_target_pairs={{0,8},{8,0},{16,24},{24,16},{1,9},{9,1},{17,25},{25,17},{2,10},{10... | collective-permute-start | bytes 294920 | tf_op jit(solution)/shard_map/ppermute | solution.py:35
  15.7 5.4 %collective-permute-start = (bf16[3,64,256]{2,1,0:T(8,128)(2,1)S(1)}, bf16[3,64,256]{2,1,0:T(8,128)(2,1)S(1)}, u32[]{:S(2)}, u32[]{:S(2)}) collective-permute-start(bf16[3,64,256]{2,1,0:T(8,128)(2,1)S(1)} %get-tuple-element.18.refs_0_), channel_id=1, source_target_pairs={{0,16},{8,24},{16,0},{24,8},{1,17},{9,25},{17,1},{25,9},{2,18},{10... | collective-permute-start | bytes 294920 | tf_op jit(solution)/shard_map/ppermute | solution.py:35
  16.0 5.1 %collective-permute-start.7 = (bf16[2,2,64,256]{3,2,1,0:T(8,128)(2,1)S(1)}, bf16[2,2,64,256]{3,2,1,0:T(8,128)(2,1)S(1)}, u32[]{:S(2)}, u32[]{:S(2)}) collective-permute-start(bf16[2,2,64,256]{3,2,1,0:T(8,128)(2,1)S(1)} %pack_blocks.1.refs_4_), channel_id=1, source_target_pairs={{0,8},{2,10},{4,12},{6,14},{8,0},{10,2},{12,4},{14,6},{16,24},{18,... | collective-permute-start | bytes 393224 | tf_op jit(solution)/shard_map/ppermute | solution.py:35
  17.0 5.4 %collective-permute-start.8 = (bf16[2,2,64,256]{3,2,1,0:T(8,128)(2,1)S(1)}, bf16[2,2,64,256]{3,2,1,0:T(8,128)(2,1)S(1)}, u32[]{:S(2)}, u32[]{:S(2)}) collective-permute-start(bf16[2,2,64,256]{3,2,1,0:T(8,128)(2,1)S(1)} %collective-permute-done.4.refs_5_), channel_id=1, source_target_pairs={{0,8},{2,10},{4,12},{6,14},{8,0},{10,2},{12,4},{14,6},{16,24},{18,... | collective-permute-start | bytes 393224 | tf_op jit(solution)/shard_map/ppermute | solution.py:35
  17.1 5.2 %collective-permute-start.9 = (bf16[2,2,64,256]{3,2,1,0:T(8,128)(2,1)S(1)}, bf16[2,2,64,256]{3,2,1,0:T(8,128)(2,1)S(1)}, u32[]{:S(2)}, u32[]{:S(2)}) collective-permute-start(bf16[2,2,64,256]{3,2,1,0:T(8,128)(2,1)S(1)} %collective-permute-done.5.refs_6_), channel_id=1, source_target_pairs={{0,8},{2,10},{4,12},{6,14},{8,0},{10,2},{12,4},{14,6},{16,24},{18,... | collective-permute-start | bytes 393224 | tf_op jit(solution)/shard_map/ppermute | solution.py:35
  19.1 3.3 %collective-permute-start.10 = (bf16[2,2,64,256]{3,2,1,0:T(8,128)(2,1)S(1)}, bf16[2,2,64,256]{3,2,1,0:T(8,128)(2,1)S(1)}, u32[]{:S(2)}, u32[]{:S(2)}) collective-permute-start(bf16[2,2,64,256]{3,2,1,0:T(8,128)(2,1)S(1)} %collective-permute-done.6.refs_7_), channel_id=1, source_target_pairs={{0,8},{2,10},{4,12},{6,14},{8,0},{10,2},{12,4},{14,6},{16,24},{18,... | collective-permute-start | bytes 393224 | tf_op jit(solution)/shard_map/ppermute | solution.py:35
  21.0 1.3 %collective-permute-start.2 = (bf16[3,64,256]{2,1,0:T(8,128)(2,1)S(1)}, bf16[3,64,256]{2,1,0:T(8,128)(2,1)S(1)}, u32[]{:S(2)}, u32[]{:S(2)}) collective-permute-start(bf16[3,64,256]{2,1,0:T(8,128)(2,1)S(1)} %collective-permute-done.refs_1_), channel_id=1, source_target_pairs={{0,8},{8,0},{16,24},{24,16},{1,9},{9,1},{17,25},{25,17},{2,10},{10... | collective-permute-start | bytes 294920 | tf_op jit(solution)/shard_map/ppermute | solution.py:35
  25.7 4.4 %collective-permute-start.11 = (f32[1,8]{1,0:T(1,128)S(1)}, f32[1,8]{1,0:T(1,128)S(1)}, u32[]{:S(2)}, u32[]{:S(2)}) collective-permute-start(f32[1,8]{1,0:T(1,128)S(1)} %get-tuple-element.22), channel_id=1, source_target_pairs={{0,1},{1,0},{2,3},{3,2},{4,5},{5,4},{6,7},{7,6},{8,9},{9,8},{10,11... | collective-permute-start | bytes 104 | tf_op jit(solution)/shard_map/ppermute | solution.py:35

commit v4 on v3

--- a/solution.py
+++ b/solution.py
@@ -35,24 +35,24 @@
     return lax.ppermute(block, axes, [(i, i ^ bit) for i in range(size)])
 
 
-def pack_kernel(*refs):
-    sources, out_ref = refs[:-1], refs[-1]
+def pack_kernel(count, *refs):
+    sources, out_ref = refs[:count], refs[-1]
     start = 0
     for ref in sources:
         out_ref[start : start + ref.shape[0]] = ref[...]
         start += ref.shape[0]
 
 
-def packed(*arrays):
+def packed(*arrays, after=()):
     count = sum(a.shape[0] for a in arrays)
     return pl.pallas_call(
-        pack_kernel,
+        functools.partial(pack_kernel, len(arrays)),
         out_shape=jax.ShapeDtypeStruct((count,) + arrays[0].shape[1:], arrays[0].dtype),
-        in_specs=vmem(len(arrays)),
+        in_specs=vmem(len(arrays)) + [pl.BlockSpec(memory_space=pl.ANY)] * len(after),
         out_specs=vmem(1)[0],
         compiler_params=PARAMS,
         name="pack_blocks",
-    )(*arrays)
+    )(*arrays, *after)
 
 
 def prompt_bits(ctx_size, cand_size):
@@ -61,14 +61,15 @@
     return early, along, across, core
 
 
-def gather_prompt(first, own, ctx_size, cand_size):
+def gather_prompt(first, own, pays, ctx_size, cand_size):
     size = ctx_size * cand_size
     early, along, across, core = prompt_bits(ctx_size, cand_size)
     held = own[None]
     for bit in early:
         sent = held if first is None else first[None]
         first = None
-        held = packed(held, flipped(sent, PROMPT_AXES, size, bit))
+        parts = held, flipped(sent, PROMPT_AXES, size, bit)
+        held = packed(*parts)
 
     def shared_out(block, even, odd):
         return lax.ppermute(
@@ -77,7 +78,7 @@
 
     second = shared_out(held, along, across)
     third = shared_out(held, across, along)
-    fourth = shared_out(second, across, along)
+    fourth = shared_out(packed(second, after=pays[1:4]), across, along)
     rail = [held, second, third, fourth]
     return rail + [flipped(block, PROMPT_AXES, size, core) for block in rail]
 
@@ -96,14 +97,15 @@
 
 
 def gather_cand(own, ctx_size):
-    blocks = [(own, 0)]
-    for bit in high_bits(ctx_size, 2) + [1]:
-        blocks += [(flipped(b, "ctx", ctx_size, bit), mask | bit) for b, mask in blocks]
+    blocks = [(own, 0), (flipped(own, "ctx", ctx_size, 1), 1)]
+    for bit in reversed(high_bits(ctx_size, 2)):
+        rail = [(flipped(b, "ctx", ctx_size, bit), mask | bit) for b, mask in blocks if not mask & 1]
+        blocks += rail + [(flipped(b, "ctx", ctx_size, 1), mask | 1) for b, mask in rail]
     return blocks
 
 
 def stage_kernel(length_ref, prompt_q, cand_q, prompt_kv, cand_kv, ends, head, *refs):
-    q_out, cand_out, kv_out, pay_out, ends_out, head_out, length_out, sems = refs
+    q_out, cand_out, kv_out, pay_out, ends_out, head_out, length_out, length_here, sems = refs
     steps = ends.shape[1]
     pairs = [
         (cand_q, cand_out),
@@ -112,11 +114,11 @@
         (prompt_kv, kv_out),
         (prompt_q, q_out),
         (head, head_out),
+        (length_ref, length_here),
     ]
     copies = [pltpu.make_async_copy(a, b, sems.at[i]) for i, (a, b) in enumerate(pairs)]
     for copy in copies:
         copy.start()
-    length_out[...] = jnp.full(length_out.shape, length_ref[0], jnp.int32)
     copies[0].wait()
     copies[1].wait()
     rows = cand_out.shape[0]
@@ -129,6 +131,7 @@
     pay_out[2] = jnp.concatenate(pieces, axis=0).astype(jnp.bfloat16)
     for copy in copies[2:]:
         copy.wait()
+    length_out[...] = jnp.full(length_out.shape, length_here[0], jnp.int32)
 
 
 def column_of(row):
@@ -145,10 +148,10 @@
     return pl.pallas_call(
         stage_kernel,
         out_shape=(like(prompt_q), like(cand_q), like(prompt_kv), payload, like(ends), like(head), lengths),
-        in_specs=[pl.BlockSpec(memory_space=pltpu.SMEM)]
+        in_specs=[pl.BlockSpec(memory_space=pl.ANY)]
         + [pl.BlockSpec(memory_space=pltpu.HBM)] * len(arrays),
         out_specs=tuple(vmem(7)),
-        scratch_shapes=[pltpu.SemaphoreType.DMA((len(arrays),))],
+        scratch_shapes=[pltpu.SMEM((1,), jnp.int32), pltpu.SemaphoreType.DMA((len(arrays) + 1,))],
         compiler_params=PARAMS,
         name="stage_operands",
     )(length, *(pltpu.with_memory_space_constraint(a, pltpu.HBM) for a in arrays))
@@ -231,20 +234,21 @@
     for head in range(kv_ref.shape[2] // HEADDIM):
         key_rows, widened = head_operands(kv_ref, count, head)
         for heads, queries in tiles(q_ref, head):
-            row_pos = stacked_rows(first_row, rows, queries.shape[0])
+            own_rows = queries.shape[0]
+            places = [divmod(h * HEADDIM, width) for h in heads]
+            picks = jnp.concatenate([step_rows[a][:, b : b + HEADDIM] for a, b in places], axis=0)
+            queries = jnp.concatenate([queries, picks.astype(jnp.bfloat16)], axis=0)
+            row_pos = jnp.concatenate(
+                [stacked_rows(first_row, rows, own_rows)] + [ends] * len(heads), axis=0
+            )
             result = blend(queries, key_rows, widened, key_pos, row_pos, free)
             for index, h in enumerate(heads):
                 kept = jnp.where(alive, result[index * rows : (index + 1) * rows], 0.0)
                 out_ref[:, h * HEADDIM : (h + 1) * HEADDIM] = kept.astype(jnp.bfloat16)
-        heads = range(head * GROUP, (head + 1) * GROUP)
-        offsets = [divmod(h * HEADDIM, width) for h in heads]
-        queries = jnp.concatenate([step_rows[a][:, b : b + HEADDIM] for a, b in offsets], axis=0)
-        row_pos = jnp.concatenate([ends] * GROUP, axis=0)
-        result = blend(queries.astype(jnp.bfloat16), key_rows, widened, key_pos, row_pos, free)
-        for index, h in enumerate(heads):
-            kept = jnp.where(ends < length, result[index * steps : (index + 1) * steps], 0.0)
-            kept = kept.astype(jnp.bfloat16).astype(jnp.float32)
-            total += kept * head_ref[:, h * HEADDIM : (h + 1) * HEADDIM]
+                start = own_rows + index * steps
+                kept = jnp.where(ends < length, result[start : start + steps], 0.0)
+                kept = kept.astype(jnp.bfloat16).astype(jnp.float32)
+                total += kept * head_ref[:, h * HEADDIM : (h + 1) * HEADDIM]
     logits = jnp.sum(total, axis=1, keepdims=True)
     down = lax.broadcasted_iota(jnp.int32, (steps, steps), 0)
     right = lax.broadcasted_iota(jnp.int32, (steps, steps), 1)
@@ -255,8 +259,8 @@
     q_rows, cand_rows, own, payload, ends, head, lengths = staged(
         cand_lengths, prompt_q, cand_q[0], prompt_kv, cand_kv[:, 0], step_ends, reward_head[None]
     )
-    blocks = gather_prompt(prompt_kv, own, ctx_size, cand_size)
     pays = gather_cand(payload, ctx_size)
+    blocks = gather_prompt(prompt_kv, own, [b for b, _ in pays], ctx_size, cand_size)
     key_count = q_rows.shape[0] * ctx_size * cand_size + cand_rows.shape[0] * ctx_size
     cand_out, partial, arranged = pl.pallas_call(
         functools.partial(cand_kernel, [mask for _, mask in pays], ctx_size, cand_size),

time: 30.8 us -> 28.5 us (0.925)
  waiting for transfers between devices: 10.7 us -> 7.18 us
  starting transfers between devices: 10.8 us -> 12 us
    ppermute x9, waiting for transfers between devices: 5.98 us -> 4.17 us  [flipped(): return lax.ppermute(block, axes, [(i, i ^ bit) for i in range(size)])]
    ppermute x3, waiting for transfers between devices: 4.67 us -> 3.01 us  [shared_out(): lax.ppermute(block, PROMPT_AXES, [(i, i ^ (odd if i & core else even)) fo...]
    ppermute x9, starting transfers between devices: 6.84 us -> 7.7 us  [flipped(): return lax.ppermute(block, axes, [(i, i ^ bit) for i in range(size)])]
    ppermute x3, starting transfers between devices: 3.97 us -> 4.32 us  [shared_out(): lax.ppermute(block, PROMPT_AXES, [(i, i ^ (odd if i & core else even)) fo...]
  transfers between devices with their start and end apart: 12 -> 12, of which waited for: 6 -> 5; matrix products, arithmetic and copies ran while one was open for 0% -> 0% of each run, Pallas kernels for 13% -> 14%
where the time goes in v4:
time: 28.5 us; the launch traced here: 28.4 us
  starting transfers between devices  12 us (42%)
  Pallas kernels  7.31 us (26%)
  waiting for transfers between devices  7.18 us (25%)
  between operations  1.33 us (5%)
  other arithmetic  0.51 us (2%)
    ppermute x9, starting transfers between devices, flipped(): return lax.ppermute(block, axes, [(i, i ^ bit) for i in range(size)])  7.7 us
    ppermute x3, starting transfers between devices, shared_out(): lax.ppermute(block, PROMPT_AXES, [(i, i ^ (odd if i & core else even)) fo...  4.32 us
    ppermute x9, waiting for transfers between devices, flipped(): return lax.ppermute(block, axes, [(i, i ^ bit) for i in range(size)])  4.17 us
    pallas_call x1, Pallas kernels, per_device(): pl.pallas_call(functools.partial(cand_kernel, [mask for _, mask in pays],...  3.3 us
    ppermute x3, waiting for transfers between devices, shared_out(): lax.ppermute(block, PROMPT_AXES, [(i, i ^ (odd if i & core else even)) fo...  3.01 us
    pallas_call x1, Pallas kernels, per_device(): pl.pallas_call(functools.partial(prompt_kernel, cand_size), out_shape=lik...  2.72 us
    pallas_call x1, Pallas kernels, staged(): pl.pallas_call(stage_kernel, out_shape=(like(prompt_q), like(cand_q), lik...  1.27 us
  transfers between devices with their start and end apart: 12, of which 5 were waited for; matrix products, arithmetic and copies ran while one was open for 0% of the time, Pallas kernels for 14%

profile of v4, /device:TPU:0, one launch (start us, length us, event | category | flops | bytes accessed | tf_op | source)
XLA Modules:
  0.0 28.4 jit_solution(15725937933065834104)
XLA Ops:
  0.6 4.1 %collective-permute-start.3 = (bf16[1,2,64,256]{3,2,1,0:T(8,128)(2,1)}, bf16[1,2,64,256]{3,2,1,0:T(8,128)(2,1)S(1)}, u32[]{:S(2)}, u32[]{:S(2)}) collective-permute-start(bf16[1,2,64,256]{3,2,1,0:T(8,128)(2,1)} %bitcast.9), channel_id=1, source_target_pairs={{0,4},{2,6},{4,0},{6,2},{8,12},{10,14},{12,8},{14,10},{16,20},{18,... | collective-permute-start | bytes 196616 | tf_op jit(solution)/shard_map/ppermute | solution.py:35
  5.4 1.3 %stage_operands.1 = (bf16[64,2048]{1,0:T(8,128)(2,1)S(1)}, bf16[64,2048]{1,0:T(8,128)(2,1)S(1)}, bf16[2,64,256]{2,1,0:T(8,128)(2,1)S(1)}, bf16[3,64,256]{2,1,0:T...) custom-call(s32[1]{0:T(128)S(6)} %copy.10.length_ref, ...), custom_call_target="tpu_custom_call" | custom-call | tf_op jit(solution)/shard_map/stage_operands/pallas_call | solution.py:148
  6.7 1.6 %collective-permute-start.1 = (bf16[3,64,256]{2,1,0:T(8,128)(2,1)S(1)}, bf16[3,64,256]{2,1,0:T(8,128)(2,1)S(1)}, u32[]{:S(2)}, u32[]{:S(2)}) collective-permute-start(bf16[3,64,256]{2,1,0:T(8,128)(2,1)S(1)} %get-tuple-element.18.refs_0_), channel_id=1, source_target_pairs={{0,16},{8,24},{16,0},{24,8},{1,17},{9,25},{17,1},{25,9},{2,18},{10... | collective-permute-start | bytes 294920 | tf_op jit(solution)/shard_map/ppermute | solution.py:35
  8.2 0.3 %collective-permute-done.3.refs_1_ = bf16[1,2,64,256]{3,2,1,0:T(8,128)(2,1)S(1)} collective-permute-done((bf16[1,2,64,256]{3,2,1,0:T(8,128)(2,1)}, bf16[1,2,64,256]{3,2,1,0:T(8,128)(2,1)S(1)}, u32[]{:S(2)}, u32[]{:S(2)}) %collective-permute-start.3) | collective-permute-done | bytes 65568 | tf_op jit(solution)/shard_map/ppermute | solution.py:35
  8.6 1.3 %collective-permute-start.4 = (bf16[2,2,64,256]{3,2,1,0:T(8,128)(2,1)S(1)}, bf16[2,2,64,256]{3,2,1,0:T(8,128)(2,1)S(1)}, u32[]{:S(2)}, u32[]{:S(2)}) collective-permute-start(bf16[2,2,64,256]{3,2,1,0:T(8,128)(2,1)S(1)} %pack_blocks.2.refs_4_), channel_id=1, source_target_pairs={{0,2},{2,0},{4,6},{6,4},{8,24},{10,26},{12,28},{14,30},{16,18},{18... | collective-permute-start | bytes 393224 | tf_op jit(solution)/shard_map/ppermute | solution.py:75
  9.9 0.0 collective-permute-start
  9.9 2.5 %collective-permute-done.1.refs_2_ = bf16[3,64,256]{2,1,0:T(8,128)(2,1)S(1)} collective-permute-done((bf16[3,64,256]{2,1,0:T(8,128)(2,1)S(1)}, bf16[3,64,256]{2,1,0:T(8,128)(2,1)S(1)}, u32[]{:S(2)}, u32[]{:S(2)}) %collective-permute-start.1) | collective-permute-done | bytes 98336 | tf_op jit(solution)/shard_map/ppermute | solution.py:35
  12.4 0.0 collective-permute-start.2
  12.4 1.5 %collective-permute-start.5 = (bf16[2,2,64,256]{3,2,1,0:T(8,128)(2,1)S(1)}, bf16[2,2,64,256]{3,2,1,0:T(8,128)(2,1)S(1)}, u32[]{:S(2)}, u32[]{:S(2)}) collective-permute-start(bf16[2,2,64,256]{3,2,1,0:T(8,128)(2,1)S(1)} %pack_blocks.2.refs_4_), channel_id=1, source_target_pairs={{0,16},{2,18},{4,20},{6,22},{8,10},{10,8},{12,14},{14,12},{16,0},{... | collective-permute-start | bytes 393224 | tf_op jit(solution)/shard_map/ppermute | solution.py:75
  13.9 0.0 collective-permute-done.refs_1_
  13.9 0.0 collective-permute-done.4.refs_0_.refs_5_
  13.9 0.0 collective-permute-done.2.refs_3_
  13.9 1.5 %collective-permute-start.6 = (bf16[2,2,64,256]{3,2,1,0:T(8,128)(2,1)S(1)}, bf16[2,2,64,256]{3,2,1,0:T(8,128)(2,1)S(1)}, u32[]{:S(2)}, u32[]{:S(2)}) collective-permute-start(bf16[2,2,64,256]{3,2,1,0:T(8,128)(2,1)S(1)} %pack_blocks.3), channel_id=1, source_target_pairs={{0,16},{2,18},{4,20},{6,22},{8,10},{10,8},{12,14},{14,12},{16,0},{... | collective-permute-start | bytes 393224 | tf_op jit(solution)/shard_map/ppermute | solution.py:75
  15.5 0.0 collective-permute-start.7
  15.5 0.5 %collective-permute-start.8 = (bf16[2,2,64,256]{3,2,1,0:T(8,128)(2,1)S(1)}, bf16[2,2,64,256]{3,2,1,0:T(8,128)(2,1)S(1)}, u32[]{:S(2)}, u32[]{:S(2)}) collective-permute-start(bf16[2,2,64,256]{3,2,1,0:T(8,128)(2,1)S(1)} %collective-permute-done.4.refs_0_.refs_5_), channel_id=1, source_target_pairs={{0,8},{2,10},{4,12},{6,14},{8,0},{10,2},{12,4},{14,6},{16,24},{18,... | collective-permute-start | bytes 393224 | tf_op jit(solution)/shard_map/ppermute | solution.py:35
  16.0 1.4 %collective-permute-done.5.refs_6_ = bf16[2,2,64,256]{3,2,1,0:T(8,128)(2,1)S(1)} collective-permute-done((bf16[2,2,64,256]{3,2,1,0:T(8,128)(2,1)S(1)}, bf16[2,2,64,256]{3,2,1,0:T(8,128)(2,1)S(1)}, u32[]{:S(2)}, u32[]{:S(2)}) %collective-permute-start.5) | collective-permute-done | bytes 131104 | tf_op jit(solution)/shard_map/ppermute | solution.py:75
  17.4 0.0 collective-permute-start.9
  17.4 1.6 %collective-permute-done.6.refs_7_ = bf16[2,2,64,256]{3,2,1,0:T(8,128)(2,1)S(1)} collective-permute-done((bf16[2,2,64,256]{3,2,1,0:T(8,128)(2,1)S(1)}, bf16[2,2,64,256]{3,2,1,0:T(8,128)(2,1)S(1)}, u32[]{:S(2)}, u32[]{:S(2)}) %collective-permute-start.6) | collective-permute-done | bytes 131104 | tf_op jit(solution)/shard_map/ppermute | solution.py:75
  19.0 0.0 collective-permute-start.10
  19.0 0.0 collective-permute-done.7.refs_8_
  19.0 0.0 collective-permute-done.9.refs_10_
  19.0 0.0 collective-permute-done.8.refs_9_
  19.0 1.3 %collective-permute-done.10.refs_11_ = bf16[2,2,64,256]{3,2,1,0:T(8,128)(2,1)S(1)} collective-permute-done((bf16[2,2,64,256]{3,2,1,0:T(8,128)(2,1)S(1)}, bf16[2,2,64,256]{3,2,1,0:T(8,128)(2,1)S(1)}, u32[]{:S(2)}, u32[]{:S(2)}) %collective-permute-start.10) | collective-permute-done | bytes 131104 | tf_op jit(solution)/shard_map/ppermute | solution.py:35
  20.3 3.3 %cand_attention.1 = (bf16[64,2048]{1,0:T(8,128)(2,1)}, f32[1,8]{1,0:T(1,128)S(1)}, bf16[2,1280,256]{2,1,0:T(8,128)(2,1)S(1)}) custom-call(bf16[64,2048]{1,0:T(8,128)(2,1)S(1)} %get-tuple-element.14.q_ref, s32[1,8]{1,0:T(1,128)S(1)} %get-tuple-element.15.ends_ref, f32[1,2048]{1,0:T(1,128)S(1)} %get-tuple-element.16.head_ref, ...), custom_call_target="tpu_custom_call" | custom-call | tf_op jit(solution)/shard_map/cand_attention/pallas_call | solution.py:265
  23.6 1.5 %collective-permute-start.11 = (f32[1,8]{1,0:T(1,128)S(1)}, f32[1,8]{1,0:T(1,128)S(1)}, u32[]{:S(2)}, u32[]{:S(2)}) collective-permute-start(f32[1,8]{1,0:T(1,128)S(1)} %get-tuple-element.22), channel_id=1, source_target_pairs={{0,1},{1,0},{2,3},{3,2},{4,5},{5,4},{6,7},{7,6},{8,9},{9,8},{10,11... | collective-permute-start | bytes 104 | tf_op jit(solution)/shard_map/ppermute | solution.py:35
  25.1 2.7 %prompt_attention.1 = bf16[64,2048]{1,0:T(8,128)(2,1)} custom-call(bf16[64,2048]{1,0:T(8,128)(2,1)S(1)} %get-tuple-element.13.q_ref, bf16[2,1280,256]{2,1,0:T(8,128)(2,1)S(1)} %get-tuple-element.20.kv_ref), custom_call_target="tpu_custom_call" | custom-call | tf_op jit(solution)/shard_map/prompt_attention/pallas_call | solution.py:281
  27.8 0.0 collective-permute-done.11
  27.8 0.5 %add.3 = f32[1,8]{1,0:T(1,128)} add(f32[1,8]{1,0:T(1,128)S(1)} %get-tuple-element.22, f32[1,8]{1,0:T(1,128)S(1)} %collective-permute-done.11) | non-fusion elementwise | flops 8 | bytes 96 | tf_op jit(solution)/shard_map/add | solution.py:280
  (2 shorter events, 0.0 us)
Async XLA Ops:
  0.6 8.0 %collective-permute-start.3 = (bf16[1,2,64,256]{3,2,1,0:T(8,128)(2,1)}, bf16[1,2,64,256]{3,2,1,0:T(8,128)(2,1)S(1)}, u32[]{:S(2)}, u32[]{:S(2)}) collective-permute-start(bf16[1,2,64,256]{3,2,1,0:T(8,128)(2,1)} %bitcast.9), channel_id=1, source_target_pairs={{0,4},{2,6},{4,0},{6,2},{8,12},{10,14},{12,8},{14,10},{16,20},{18,... | collective-permute-start | bytes 196616 | tf_op jit(solution)/shard_map/ppermute | solution.py:35
  6.7 5.7 %collective-permute-start.1 = (bf16[3,64,256]{2,1,0:T(8,128)(2,1)S(1)}, bf16[3,64,256]{2,1,0:T(8,128)(2,1)S(1)}, u32[]{:S(2)}, u32[]{:S(2)}) collective-permute-start(bf16[3,64,256]{2,1,0:T(8,128)(2,1)S(1)} %get-tuple-element.18.refs_0_), channel_id=1, source_target_pairs={{0,16},{8,24},{16,0},{24,8},{1,17},{9,25},{17,1},{25,9},{2,18},{10... | collective-permute-start | bytes 294920 | tf_op jit(solution)/shard_map/ppermute | solution.py:35
  8.6 5.3 %collective-permute-start.4 = (bf16[2,2,64,256]{3,2,1,0:T(8,128)(2,1)S(1)}, bf16[2,2,64,256]{3,2,1,0:T(8,128)(2,1)S(1)}, u32[]{:S(2)}, u32[]{:S(2)}) collective-permute-start(bf16[2,2,64,256]{3,2,1,0:T(8,128)(2,1)S(1)} %pack_blocks.2.refs_4_), channel_id=1, source_target_pairs={{0,2},{2,0},{4,6},{6,4},{8,24},{10,26},{12,28},{14,30},{16,18},{18... | collective-permute-start | bytes 393224 | tf_op jit(solution)/shard_map/ppermute | solution.py:75
  9.9 4.0 %collective-permute-start = (bf16[3,64,256]{2,1,0:T(8,128)(2,1)S(1)}, bf16[3,64,256]{2,1,0:T(8,128)(2,1)S(1)}, u32[]{:S(2)}, u32[]{:S(2)}) collective-permute-start(bf16[3,64,256]{2,1,0:T(8,128)(2,1)S(1)} %get-tuple-element.18.refs_0_), channel_id=1, source_target_pairs={{0,8},{8,0},{16,24},{24,16},{1,9},{9,1},{17,25},{25,17},{2,10},{10... | collective-permute-start | bytes 294920 | tf_op jit(solution)/shard_map/ppermute | solution.py:35
  12.4 1.5 %collective-permute-start.2 = (bf16[3,64,256]{2,1,0:T(8,128)(2,1)S(1)}, bf16[3,64,256]{2,1,0:T(8,128)(2,1)S(1)}, u32[]{:S(2)}, u32[]{:S(2)}) collective-permute-start(bf16[3,64,256]{2,1,0:T(8,128)(2,1)S(1)} %collective-permute-done.1.refs_2_), channel_id=1, source_target_pairs={{0,8},{8,0},{16,24},{24,16},{1,9},{9,1},{17,25},{25,17},{2,10},{10... | collective-permute-start | bytes 294920 | tf_op jit(solution)/shard_map/ppermute | solution.py:35
  12.4 5.0 %collective-permute-start.5 = (bf16[2,2,64,256]{3,2,1,0:T(8,128)(2,1)S(1)}, bf16[2,2,64,256]{3,2,1,0:T(8,128)(2,1)S(1)}, u32[]{:S(2)}, u32[]{:S(2)}) collective-permute-start(bf16[2,2,64,256]{3,2,1,0:T(8,128)(2,1)S(1)} %pack_blocks.2.refs_4_), channel_id=1, source_target_pairs={{0,16},{2,18},{4,20},{6,22},{8,10},{10,8},{12,14},{14,12},{16,0},{... | collective-permute-start | bytes 393224 | tf_op jit(solution)/shard_map/ppermute | solution.py:75
  13.9 5.0 %collective-permute-start.6 = (bf16[2,2,64,256]{3,2,1,0:T(8,128)(2,1)S(1)}, bf16[2,2,64,256]{3,2,1,0:T(8,128)(2,1)S(1)}, u32[]{:S(2)}, u32[]{:S(2)}) collective-permute-start(bf16[2,2,64,256]{3,2,1,0:T(8,128)(2,1)S(1)} %pack_blocks.3), channel_id=1, source_target_pairs={{0,16},{2,18},{4,20},{6,22},{8,10},{10,8},{12,14},{14,12},{16,0},{... | collective-permute-start | bytes 393224 | tf_op jit(solution)/shard_map/ppermute | solution.py:75
  15.5 3.5 %collective-permute-start.7 = (bf16[2,2,64,256]{3,2,1,0:T(8,128)(2,1)S(1)}, bf16[2,2,64,256]{3,2,1,0:T(8,128)(2,1)S(1)}, u32[]{:S(2)}, u32[]{:S(2)}) collective-permute-start(bf16[2,2,64,256]{3,2,1,0:T(8,128)(2,1)S(1)} %pack_blocks.2.refs_4_), channel_id=1, source_target_pairs={{0,8},{2,10},{4,12},{6,14},{8,0},{10,2},{12,4},{14,6},{16,24},{18,... | collective-permute-start | bytes 393224 | tf_op jit(solution)/shard_map/ppermute | solution.py:35
  15.5 3.5 %collective-permute-start.8 = (bf16[2,2,64,256]{3,2,1,0:T(8,128)(2,1)S(1)}, bf16[2,2,64,256]{3,2,1,0:T(8,128)(2,1)S(1)}, u32[]{:S(2)}, u32[]{:S(2)}) collective-permute-start(bf16[2,2,64,256]{3,2,1,0:T(8,128)(2,1)S(1)} %collective-permute-done.4.refs_0_.refs_5_), channel_id=1, source_target_pairs={{0,8},{2,10},{4,12},{6,14},{8,0},{10,2},{12,4},{14,6},{16,24},{18,... | collective-permute-start | bytes 393224 | tf_op jit(solution)/shard_map/ppermute | solution.py:35
  17.4 1.6 %collective-permute-start.9 = (bf16[2,2,64,256]{3,2,1,0:T(8,128)(2,1)S(1)}, bf16[2,2,64,256]{3,2,1,0:T(8,128)(2,1)S(1)}, u32[]{:S(2)}, u32[]{:S(2)}) collective-permute-start(bf16[2,2,64,256]{3,2,1,0:T(8,128)(2,1)S(1)} %collective-permute-done.5.refs_6_), channel_id=1, source_target_pairs={{0,8},{2,10},{4,12},{6,14},{8,0},{10,2},{12,4},{14,6},{16,24},{18,... | collective-permute-start | bytes 393224 | tf_op jit(solution)/shard_map/ppermute | solution.py:35
  19.0 1.3 %collective-permute-start.10 = (bf16[2,2,64,256]{3,2,1,0:T(8,128)(2,1)S(1)}, bf16[2,2,64,256]{3,2,1,0:T(8,128)(2,1)S(1)}, u32[]{:S(2)}, u32[]{:S(2)}) collective-permute-start(bf16[2,2,64,256]{3,2,1,0:T(8,128)(2,1)S(1)} %collective-permute-done.6.refs_7_), channel_id=1, source_target_pairs={{0,8},{2,10},{4,12},{6,14},{8,0},{10,2},{12,4},{14,6},{16,24},{18,... | collective-permute-start | bytes 393224 | tf_op jit(solution)/shard_map/ppermute | solution.py:35
  23.6 4.2 %collective-permute-start.11 = (f32[1,8]{1,0:T(1,128)S(1)}, f32[1,8]{1,0:T(1,128)S(1)}, u32[]{:S(2)}, u32[]{:S(2)}) collective-permute-start(f32[1,8]{1,0:T(1,128)S(1)} %get-tuple-element.22), channel_id=1, source_target_pairs={{0,1},{1,0},{2,3},{3,2},{4,5},{5,4},{6,7},{7,6},{8,9},{9,8},{10,11... | collective-permute-start | bytes 104 | tf_op jit(solution)/shard_map/ppermute | solution.py:35

commit v5 on v4

v5 whole, which is shorter than its diff:
```python
import functools
import math

import jax
import jax.numpy as jnp
from jax import lax
from jax.experimental import pallas as pl
from jax.experimental.pallas import tpu as pltpu
from jax.sharding import PartitionSpec as P

HEADDIM = 128
GROUP = 8
SUBLANES = 8
NEG_FILL = -1e30
SCALE = HEADDIM ** -0.5 * math.log2(math.e)
ROW_TILE = 256
VMEM_LIMIT = 28 * 1024 * 1024
PARAMS = pltpu.CompilerParams(vmem_limit_bytes=VMEM_LIMIT)
PROMPT_AXES = ("ctx", "cand")


def vmem(count):
    return [pl.BlockSpec(memory_space=pltpu.VMEM)] * count


def like(array):
    return jax.ShapeDtypeStruct(array.shape, array.dtype)


def high_bits(size, lowest):
    return [1 << b for b in reversed(range(size.bit_length() - 1)) if 1 << b >= lowest]


def flipped(block, axes, size, bit):
    return lax.ppermute(block, axes, [(i, i ^ bit) for i in range(size)])


def pack_kernel(count, *refs):
    sources, out_ref = refs[:count], refs[-1]
    start = 0
    for ref in sources:
        out_ref[start : start + ref.shape[0]] = ref[...]
        start += ref.shape[0]


def packed(*arrays, after=()):
    count = sum(a.shape[0] for a in arrays)
    return pl.pallas_call(
        functools.partial(pack_kernel, len(arrays)),
        out_shape=jax.ShapeDtypeStruct((count,) + arrays[0].shape[1:], arrays[0].dtype),
        in_specs=vmem(len(arrays)) + [pl.BlockSpec(memory_space=pl.ANY)] * len(after),
        out_specs=vmem(1)[0],
        compiler_params=PARAMS,
        name="pack_blocks",
    )(*arrays, *after)


def prompt_bits(ctx_size, cand_size):
    core, along, across = cand_size, 1, 2 * cand_size
    early = high_bits(cand_size, 2) + [bit * cand_size for bit in high_bits(ctx_size, 4)]
    return early, along, across, core


def prompt_owners(ctx_size, cand_size):
    early, along, across, core = prompt_bits(ctx_size, cand_size)
    place = lax.axis_index("ctx") * cand_size + lax.axis_index("cand")
    odd = lax.rem(lax.axis_index("ctx"), 2)
    near = along + odd * (across - along)
    far = along + across - near
    masks = [0]
    for bit in early:
        masks += [mask ^ bit for mask in masks]
    shifts = [0, near, far, along + across, core, core + far, core + near, core + along + across]
    return [[place ^ mask ^ shift for mask in masks] for shift in shifts]


def gather_cand(own, ctx_size):
    blocks = [(own, 0), (flipped(own, "ctx", ctx_size, 1), 1)]
    for bit in reversed(high_bits(ctx_size, 2)):
        rail = [(flipped(b, "ctx", ctx_size, bit), mask | bit) for b, mask in blocks if not mask & 1]
        blocks += rail + [(flipped(b, "ctx", ctx_size, 1), mask | 1) for b, mask in rail]
    return blocks


def stage_kernel(length_ref, prompt_q, cand_q, prompt_kv, cand_kv, ends, head, *refs):
    q_out, cand_out, kv_out, pay_out, ends_out, head_out, length_out, length_here, sems = refs
    steps = ends.shape[1]
    pairs = [
        (cand_q, cand_out),
        (ends, ends_out),
        (cand_kv, pay_out.at[0:2]),
        (prompt_kv, kv_out),
        (prompt_q, q_out),
        (head, head_out),
        (length_ref, length_here),
    ]
    copies = [pltpu.make_async_copy(a, b, sems.at[i]) for i, (a, b) in enumerate(pairs)]
    for copy in copies:
        copy.start()
    copies[0].wait()
    copies[1].wait()
    rows = cand_out.shape[0]
    ends_column = column_of(ends_out[...])
    row_pos = lax.axis_index("ctx") * rows + lax.broadcasted_iota(jnp.int32, (steps, rows), 1)
    chosen = (row_pos == ends_column).astype(jnp.bfloat16)
    picked = jnp.dot(chosen, cand_out[...], preferred_element_type=jnp.float32)
    width = pay_out.shape[2]
    pieces = [picked[:, at : at + width] for at in range(0, picked.shape[1], width)]
    pay_out[2] = jnp.concatenate(pieces, axis=0).astype(jnp.bfloat16)
    for copy in copies[2:]:
        copy.wait()
    length_out[...] = jnp.full(length_out.shape, length_here[0], jnp.int32)


def column_of(row):
    count = row.shape[1]
    down = lax.broadcasted_iota(jnp.int32, (count, count), 0)
    right = lax.broadcasted_iota(jnp.int32, (count, count), 1)
    return jnp.sum(jnp.where(down == right, row, 0), axis=1, keepdims=True)


def staged(length, prompt_q, cand_q, prompt_kv, cand_kv, ends, head):
    arrays = (prompt_q, cand_q, prompt_kv, cand_kv, ends, head)
    payload = jax.ShapeDtypeStruct((3,) + cand_kv.shape[1:], cand_kv.dtype)
    lengths = jax.ShapeDtypeStruct((1, HEADDIM), jnp.int32)
    return pl.pallas_call(
        stage_kernel,
        out_shape=(like(prompt_q), like(cand_q), like(prompt_kv), payload, like(ends), like(head), lengths),
        in_specs=[pl.BlockSpec(memory_space=pl.ANY)]
        + [pl.BlockSpec(memory_space=pltpu.HBM)] * len(arrays),
        out_specs=tuple(vmem(7)),
        scratch_shapes=[pltpu.SMEM((1,), jnp.int32), pltpu.SemaphoreType.DMA((len(arrays) + 1,))],
        compiler_params=PARAMS,
        name="stage_operands",
    )(length, *(pltpu.with_memory_space_constraint(a, pltpu.HBM) for a in arrays))


def tiles(q_ref, head):
    rows = q_ref.shape[0]
    fan = max(1, ROW_TILE // rows)
    for start in range(head * GROUP, (head + 1) * GROUP, fan):
        heads = range(start, start + fan)
        queries = jnp.concatenate([q_ref[:, h * HEADDIM : (h + 1) * HEADDIM] for h in heads], axis=0)
        yield heads, slice(start * rows, (start + fan) * rows), queries


def stacked_rows(first_row, rows, count):
    return first_row + lax.rem(lax.broadcasted_iota(jnp.int32, (count, 1), 0), jnp.int32(rows))


def product(queries, key_rows):
    return lax.dot_general(
        queries, key_rows, (((1,), (1,)), ((), ())), preferred_element_type=jnp.float32
    )


def with_ones(value_rows):
    return jnp.concatenate([value_rows, jnp.ones_like(value_rows)], axis=1)


def head_rows(blocks, which, head):
    columns = slice(head * HEADDIM, (head + 1) * HEADDIM)
    return jnp.concatenate([ref[lead + (which,)][:, columns] for ref, lead in blocks], axis=0)


def key_positions(owners, rows):
    lane = lax.broadcasted_iota(jnp.int32, (1, len(owners) * rows), 1)
    positions = lane
    for index, owner in enumerate(owners):
        inside = (lane >= index * rows) & (lane < (index + 1) * rows)
        positions = jnp.where(inside, lane + (owner - index) * rows, positions)
    return positions


def spread(column, count):
    return jnp.concatenate([column] * (count // column.shape[1]), axis=1)


def absorb(queries, key_rows, widened, allowed, old):
    scores = product(queries, key_rows)
    if allowed is not None:
        scores = jnp.where(allowed, scores, NEG_FILL)
    count = scores.shape[1]
    peak = jnp.broadcast_to(jnp.max(scores, axis=1, keepdims=True), (scores.shape[0], HEADDIM))
    if old is not None:
        peak = jnp.maximum(peak, old[0])
    weights = jnp.exp2((scores - spread(peak, count)) * SCALE).astype(jnp.bfloat16)
    blended = jnp.dot(weights, widened, preferred_element_type=jnp.float32)
    if old is not None:
        blended += old[1] * spread(jnp.exp2((old[0] - peak) * SCALE), old[1].shape[1])
    return peak, blended


def prompt_place(cand_size):
    return lax.axis_index("ctx") * cand_size + lax.axis_index("cand")


def pairs_of(refs):
    return [(ref, (index,)) for ref in refs for index in range(ref.shape[0])]


def phase_kernel(sizes, arrays, masks, first, last, *refs):
    ctx_size, cand_size = sizes
    take = iter(refs)
    prompt_q, cand_q = next(take), next(take)
    block_refs = [next(take) for _ in arrays]
    pays = [next(take) for _ in masks]
    lengths = next(take) if last else None
    old = None if first else [(next(take), next(take)) for _ in range(2)]
    outs = refs[-2:] if last else refs[-4:]
    rows = prompt_q.shape[0]
    cand_rows = cand_q.shape[0]
    owners = prompt_owners(ctx_size, cand_size)
    key_pos = key_positions([place for index in arrays for place in owners[index]], rows)
    blocks = pairs_of(block_refs)
    own = [(ref, ()) for ref in pays]
    ctx = lax.axis_index("ctx")
    own_pos = key_positions([ctx ^ mask for mask in masks], cand_rows) if masks else None
    alive = stacked_rows(ctx * cand_rows, cand_rows, cand_rows) < lengths[:, :1] if last else None

    for head in range(block_refs[0].shape[3] // HEADDIM):
        key_rows = head_rows(blocks, 0, head)
        widened = with_ones(head_rows(blocks, 1, head))
        if masks:
            all_keys = jnp.concatenate([key_rows, head_rows(own, 0, head)], axis=0)
            all_widened = jnp.concatenate([widened, with_ones(head_rows(own, 1, head))], axis=0)
            free = jnp.full((1, key_rows.shape[0]), -1, jnp.int32)
            all_pos = jnp.concatenate([free, own_pos], axis=1)
        for kind, q_ref in enumerate((cand_q, prompt_q)):
            for heads, at, queries in tiles(q_ref, head):
                count = queries.shape[0]
                state = None if first else (old[kind][0][at], old[kind][1][at])
                if kind == 1:
                    first_row = prompt_place(cand_size) * rows
                    allowed = key_pos <= stacked_rows(first_row, rows, count)
                    state = absorb(queries, key_rows, widened, allowed, state)
                elif masks:
                    allowed = all_pos <= stacked_rows(ctx * cand_rows, cand_rows, count)
                    state = absorb(queries, all_keys, all_widened, allowed, state)
                else:
                    state = absorb(queries, key_rows, widened, None, state)
                if not last:
                    outs[2 * kind][at] = state[0]
                    outs[2 * kind + 1][at] = state[1]
                    continue
                result = state[1][:, :HEADDIM] / state[1][:, HEADDIM:]
                each = q_ref.shape[0]
                for index, h in enumerate(heads):
                    kept = result[index * each : (index + 1) * each]
                    if kind == 0:
                        kept = jnp.where(alive, kept, 0.0)
                    outs[kind][:, h * HEADDIM : (h + 1) * HEADDIM] = kept.astype(jnp.bfloat16)


def phase(sizes, arrays, q_rows, blocks, pays=(), state=None, lengths=None, after=()):
    prompt_q, cand_q = q_rows
    first, last = state is None, lengths is not None
    operands = [prompt_q, cand_q] + [blocks[index] for index in arrays]
    operands += [b for b, _ in pays]
    if last:
        operands.append(lengths)
    if not first:
        operands += state
    heads = prompt_q.shape[1] // HEADDIM
    if last:
        shapes = [like(cand_q), like(prompt_q)]
    else:
        shapes = []
        for q in (cand_q, prompt_q):
            count = heads * q.shape[0]
            shapes.append(jax.ShapeDtypeStruct((count, HEADDIM), jnp.float32))
            shapes.append(jax.ShapeDtypeStruct((count, 2 * HEADDIM), jnp.float32))
    key_count = sum(blocks[i].shape[0] * blocks[i].shape[2] for i in arrays)
    scores = heads * (prompt_q.shape[0] + cand_q.shape[0]) * key_count
    masks = [mask for _, mask in pays]
    return pl.pallas_call(
        functools.partial(phase_kernel, sizes, arrays, masks, first, last),
        out_shape=tuple(shapes),
        in_specs=vmem(len(operands)) + [pl.BlockSpec(memory_space=pl.ANY)] * len(after),
        out_specs=tuple(vmem(len(shapes))),
        compiler_params=PARAMS,
        cost_estimate=pl.CostEstimate(
            flops=6 * scores * HEADDIM, bytes_accessed=scores, transcendentals=scores
        ),
        name="attend_" + "_".join(str(i) for i in arrays),
    )(*operands, *after)


def step_kernel(sizes, masks, ends_ref, head_ref, lengths_ref, *refs):
    ctx_size, cand_size = sizes
    pays, blocks = refs[: len(masks)], refs[len(masks) : -2]
    logit_ref, kv_ref = refs[-2:]
    rows = blocks[0].shape[2]
    own_rows = pays[0].shape[1]
    free = rows * ctx_size * cand_size
    place = lax.axis_index("ctx")
    for ref, owners in zip(blocks, prompt_owners(ctx_size, cand_size)):
        for index, owner in enumerate(owners):
            at = pl.ds(pl.multiple_of(owner * rows, rows), rows)
            kv_ref[0, at, :] = ref[index, 0]
            kv_ref[1, at, :] = ref[index, 1]
    picked = jnp.zeros(pays[0].shape[1:], jnp.float32)
    for ref, mask in zip(pays, masks):
        at = pl.ds(pl.multiple_of(free + (place ^ mask) * own_rows, own_rows), own_rows)
        kv_ref[0, at, :] = ref[0]
        kv_ref[1, at, :] = ref[1]
        picked += ref[2].astype(jnp.float32)
    steps = ends_ref.shape[1]
    width = picked.shape[1]
    step_rows = [picked[at : at + steps] for at in range(0, steps * head_ref.shape[1] // width, steps)]

    ends = column_of(ends_ref[...])
    own_pos = lax.broadcasted_iota(jnp.int32, (1, own_rows * len(masks)), 1)
    row_pos = jnp.concatenate([ends] * GROUP, axis=0)
    total = jnp.zeros((steps, HEADDIM), jnp.float32)
    for head in range(width // HEADDIM):
        columns = slice(head * HEADDIM, (head + 1) * HEADDIM)
        heads = range(head * GROUP, (head + 1) * GROUP)
        places = [divmod(h * HEADDIM, width) for h in heads]
        queries = jnp.concatenate([step_rows[a][:, b : b + HEADDIM] for a, b in places], axis=0)
        scores = product(queries.astype(jnp.bfloat16), kv_ref[0, :, columns])
        bound = jnp.where(own_pos <= row_pos, scores[:, free:], NEG_FILL)
        scores = jnp.concatenate([scores[:, :free], bound], axis=1)
        peak = jnp.max(scores, axis=1, keepdims=True)
        weights = jnp.exp2((scores - peak) * SCALE).astype(jnp.bfloat16)
        blended = jnp.dot(weights, with_ones(kv_ref[1, :, columns]), preferred_element_type=jnp.float32)
        result = blended[:, :HEADDIM] / blended[:, HEADDIM:]
        for index, h in enumerate(heads):
            kept = jnp.where(ends < lengths_ref[:, :1], result[index * steps : (index + 1) * steps], 0.0)
            kept = kept.astype(jnp.bfloat16).astype(jnp.float32)
            total += kept * head_ref[:, h * HEADDIM : (h + 1) * HEADDIM]
    logits = jnp.sum(total, axis=1, keepdims=True)
    down = lax.broadcasted_iota(jnp.int32, (steps, steps), 0)
    right = lax.broadcasted_iota(jnp.int32, (steps, steps), 1)
    logit_ref[...] = jnp.sum(jnp.where(down == right, logits, 0.0), axis=0, keepdims=True)


def step_shares(sizes, ends, head, lengths, pays, blocks):
    ctx_size, cand_size = sizes
    rows, width = blocks[0].shape[2:]
    count = rows * ctx_size * cand_size + pays[0][0].shape[1] * ctx_size
    scores = ends.shape[1] * head.shape[1] // HEADDIM * count
    return pl.pallas_call(
        functools.partial(step_kernel, sizes, [mask for _, mask in pays]),
        out_shape=jax.ShapeDtypeStruct(ends.shape, jnp.float32),
        in_specs=vmem(3 + len(pays) + len(blocks)),
        out_specs=vmem(1)[0],
        scratch_shapes=[pltpu.VMEM((2, count, width), blocks[0].dtype)],
        compiler_params=PARAMS,
        cost_estimate=pl.CostEstimate(
            flops=6 * scores * HEADDIM, bytes_accessed=scores, transcendentals=scores
        ),
        name="step_logits",
    )(ends, head, lengths, *(b for b, _ in pays), *blocks)


def per_device(ctx_size, cand_size, prompt_q, prompt_kv, cand_q, cand_kv, cand_lengths, step_ends, reward_head):
    sizes = ctx_size, cand_size
    size = ctx_size * cand_size
    prompt_rows, cand_rows, own, payload, ends, head, lengths = staged(
        cand_lengths, prompt_q, cand_q[0], prompt_kv, cand_kv[:, 0], step_ends, reward_head[None]
    )
    q_rows = prompt_rows, cand_rows
    pays = gather_cand(payload, ctx_size)
    early, along, across, core = prompt_bits(ctx_size, cand_size)

    def across_cores(block):
        return flipped(block, PROMPT_AXES, size, core)

    def shared_out(block, even, odd):
        return lax.ppermute(
            block, PROMPT_AXES, [(i, i ^ (odd if i & core else even)) for i in range(size)]
        )

    held = own[None]
    sent = prompt_kv[None]
    for bit in early:
        held = packed(held, flipped(sent, PROMPT_AXES, size, bit))
        sent = held
    second = shared_out(held, along, across)
    third = shared_out(held, across, along)
    blocks = [held, second, third, None, across_cores(held), None, None, None]
    state = phase(sizes, [0, 4], q_rows, blocks)
    fourth = shared_out(packed(second, after=state[:1] + tuple(b for b, _ in pays[1:4])), across, along)
    blocks[3] = fourth
    blocks[5:7] = across_cores(second), across_cores(third)
    state = phase(sizes, [1, 2], q_rows, blocks, pays=pays, state=state)
    blocks[7] = across_cores(packed(fourth, after=state[:1]))
    state = phase(sizes, [5, 6], q_rows, blocks, state=state)
    step_logits = step_shares(sizes, ends, head, lengths, pays, blocks)
    cand_out, prompt_out = phase(sizes, [3, 7], q_rows, blocks, state=state, lengths=lengths)
    tp_size = lax.axis_size("tp")
    for bit in high_bits(tp_size, 1):
        step_logits = step_logits + flipped(step_logits, "tp", tp_size, bit)
    return (prompt_out, cand_out[None], step_logits)


def solution(mesh):
    placed = (
        P(("ctx", "cand"), "tp"),
        P(None, ("ctx", "cand"), "tp"),
        P("cand", "ctx", "tp"),
        P(None, "cand", "ctx", "tp"),
        P("cand"),
        P("cand", None),
        P("tp"),
    )
    return jax.shard_map(
        functools.partial(per_device, mesh.shape["ctx"], mesh.shape["cand"]),
        mesh=mesh,
        in_specs=placed,
        out_specs=(P(("ctx", "cand"), "tp"), P("cand", "ctx", "tp"), P("cand", None)),
        check_vma=False,
    )
```

time: 28.5 us -> 25.5 us (0.89)
  waiting for transfers between devices: 7.18 us -> 3.08 us
  starting transfers between devices: 12 us -> 12.6 us
  Pallas kernels: 7.31 us -> 7.79 us
    ppermute x9, waiting for transfers between devices: 4.17 us -> 1.5 us  [flipped(): return lax.ppermute(block, axes, [(i, i ^ bit) for i in range(size)])]
    ppermute x3, waiting for transfers between devices: 3.01 us -> 1.57 us  [shared_out(): lax.ppermute(block, PROMPT_AXES, [(i, i ^ (odd if i & core else even)) fo...]
    pallas_call x2 -> x5, Pallas kernels: 6.02 us -> 6.49 us  [the longest x4 5.44 us: phase(): pl.pallas_call(functools.partial(phase_kernel, sizes, arrays, masks, firs...]
    ppermute x9, starting transfers between devices: 7.7 us -> 8.1 us  [flipped(): return lax.ppermute(block, axes, [(i, i ^ bit) for i in range(size)])]
  transfers between devices with their start and end apart: 12 -> 12, of which waited for: 5 -> 6; matrix products, arithmetic and copies ran while one was open for 0% -> 0% of each run, Pallas kernels for 14% -> 27%
where the time goes in v5:
time: 25.5 us; the launch traced here: 25.4 us
  starting transfers between devices  12.6 us (49%)
  Pallas kernels  7.79 us (31%)
  waiting for transfers between devices  3.08 us (12%)
  between operations  1.39 us (5%)
  other arithmetic  0.51 us (2%)
    ppermute x9, starting transfers between devices, flipped(): return lax.ppermute(block, axes, [(i, i ^ bit) for i in range(size)])  8.1 us
    pallas_call x4, Pallas kernels, phase(): pl.pallas_call(functools.partial(phase_kernel, sizes, arrays, masks, firs...  5.44 us
    ppermute x3, starting transfers between devices, shared_out(): lax.ppermute(block, PROMPT_AXES, [(i, i ^ (odd if i & core else even)) fo...  4.53 us
    ppermute x3, waiting for transfers between devices, shared_out(): lax.ppermute(block, PROMPT_AXES, [(i, i ^ (odd if i & core else even)) fo...  1.57 us
    ppermute x9, waiting for transfers between devices, flipped(): return lax.ppermute(block, axes, [(i, i ^ bit) for i in range(size)])  1.5 us
    pallas_call x1, Pallas kernels, staged(): pl.pallas_call(stage_kernel, out_shape=(like(prompt_q), like(cand_q), lik...  1.27 us
    pallas_call x1, Pallas kernels, step_shares(): pl.pallas_call(functools.partial(step_kernel, sizes, [mask for _, mask in...  1.05 us
    add x1, other arithmetic, per_device(): step_logits = step_logits + flipped(step_logits, 'tp', tp_size, bit)  0.51 us
  transfers between devices with their start and end apart: 12, of which 6 were waited for; matrix products, arithmetic and copies ran while one was open for 0% of the time, Pallas kernels for 27%

profile of v5, /device:TPU:0, one launch (start us, length us, event | category | flops | bytes accessed | tf_op | source)
XLA Modules:
  0.0 25.4 jit_solution(7909362377494099691)
XLA Ops:
  0.6 4.1 %collective-permute-start = (bf16[1,2,64,256]{3,2,1,0:T(8,128)(2,1)}, bf16[1,2,64,256]{3,2,1,0:T(8,128)(2,1)S(1)}, u32[]{:S(2)}, u32[]{:S(2)}) collective-permute-start(bf16[1,2,64,256]{3,2,1,0:T(8,128)(2,1)} %bitcast.9), channel_id=1, source_target_pairs={{0,4},{2,6},{4,0},{6,2},{8,12},{10,14},{12,8},{14,10},{16,20},{18,... | collective-permute-start | bytes 196616 | tf_op jit(solution)/shard_map/ppermute | solution.py:35
  5.4 1.3 %stage_operands.1 = (bf16[64,2048]{1,0:T(8,128)(2,1)S(1)}, bf16[64,2048]{1,0:T(8,128)(2,1)S(1)}, bf16[2,64,256]{2,1,0:T(8,128)(2,1)S(1)}, bf16[3,64,256]{2,1,0:T...) custom-call(s32[1]{0:T(128)S(6)} %copy.10.length_ref, ...), custom_call_target="tpu_custom_call" | custom-call | tf_op jit(solution)/shard_map/stage_operands/pallas_call | solution.py:126
  6.7 1.6 %collective-permute-start.4 = (bf16[3,64,256]{2,1,0:T(8,128)(2,1)S(1)}, bf16[3,64,256]{2,1,0:T(8,128)(2,1)S(1)}, u32[]{:S(2)}, u32[]{:S(2)}) collective-permute-start(bf16[3,64,256]{2,1,0:T(8,128)(2,1)S(1)} %get-tuple-element.28.refs_4_.refs_0_), channel_id=1, source_target_pairs={{0,16},{8,24},{16,0},{24,8},{1,17},{9,25},{17,1},{25,9},{2,18},{10... | collective-permute-start | bytes 294920 | tf_op jit(solution)/shard_map/ppermute | solution.py:35
  8.2 0.3 %collective-permute-done.refs_1_ = bf16[1,2,64,256]{3,2,1,0:T(8,128)(2,1)S(1)} collective-permute-done((bf16[1,2,64,256]{3,2,1,0:T(8,128)(2,1)}, bf16[1,2,64,256]{3,2,1,0:T(8,128)(2,1)S(1)}, u32[]{:S(2)}, u32[]{:S(2)}) %collective-permute-start) | collective-permute-done | bytes 65568 | tf_op jit(solution)/shard_map/ppermute | solution.py:35
  8.6 0.1 collective-permute-start.2
  8.7 1.3 %collective-permute-start.1 = (bf16[2,2,64,256]{3,2,1,0:T(8,128)(2,1)S(1)}, bf16[2,2,64,256]{3,2,1,0:T(8,128)(2,1)S(1)}, u32[]{:S(2)}, u32[]{:S(2)}) collective-permute-start(bf16[2,2,64,256]{3,2,1,0:T(8,128)(2,1)S(1)} %pack_blocks.3.refs_2_.refs_4_), channel_id=1, source_target_pairs={{0,2},{2,0},{4,6},{6,4},{8,24},{10,26},{12,28},{14,30},{16,18},{18... | collective-permute-start | bytes 393224 | tf_op jit(solution)/shard_map/ppermute | solution.py:371
  10.0 0.6 %collective-permute-start.3 = (bf16[3,64,256]{2,1,0:T(8,128)(2,1)S(1)}, bf16[3,64,256]{2,1,0:T(8,128)(2,1)S(1)}, u32[]{:S(2)}, u32[]{:S(2)}) collective-permute-start(bf16[3,64,256]{2,1,0:T(8,128)(2,1)S(1)} %get-tuple-element.28.refs_4_.refs_0_), channel_id=1, source_target_pairs={{0,8},{8,0},{16,24},{24,16},{1,9},{9,1},{17,25},{25,17},{2,10},{10... | collective-permute-start | bytes 294920 | tf_op jit(solution)/shard_map/ppermute | solution.py:35
  10.6 0.7 %collective-permute-done.4.refs_3_.refs_6_.refs_2_ = bf16[3,64,256]{2,1,0:T(8,128)(2,1)S(1)} collective-permute-done((bf16[3,64,256]{2,1,0:T(8,128)(2,1)S(1)}, bf16[3,64,256]{2,1,0:T(8,128)(2,1)S(1)}, u32[]{:S(2)}, u32[]{:S(2)}) %collective-permute-start.4) | collective-permute-done | bytes 98336 | tf_op jit(solution)/shard_map/ppermute | solution.py:35
  11.3 0.0 collective-permute-start.5
  11.3 1.5 %collective-permute-start.7 = (bf16[2,2,64,256]{3,2,1,0:T(8,128)(2,1)S(1)}, bf16[2,2,64,256]{3,2,1,0:T(8,128)(2,1)S(1)}, u32[]{:S(2)}, u32[]{:S(2)}) collective-permute-start(bf16[2,2,64,256]{3,2,1,0:T(8,128)(2,1)S(1)} %pack_blocks.3.refs_2_.refs_4_), channel_id=1, source_target_pairs={{0,16},{2,18},{4,20},{6,22},{8,10},{10,8},{12,14},{14,12},{16,0},{... | collective-permute-start | bytes 393224 | tf_op jit(solution)/shard_map/ppermute | solution.py:371
  12.9 0.0 collective-permute-done.2.refs_3_.refs_8_
  12.9 0.9 %attend_0_4.1 = (f32[1024,128]{1,0:T(8,128)S(1)}, f32[1024,256]{1,0:T(8,128)S(1)}, f32[1024,128]{1,0:T(8,128)S(1)}, f32[1024,256]{1,0:T(8,128)S(1)}) custom-call(bf16[64,2048]{1,0:T(8,128)(2,1)S(1)} %get-tuple-element.24.refs_0_, bf16[64,2048]{1,0:T(8,128)(2,1)S(1)} %get-tuple-element.25.refs_1_, bf16[2,2,64,256]{3,2,1,0:T(8,128)(2,1)S(1)} %pack_blocks.3.refs_2_.refs_4_, ...), custom_call_target="tpu_custom_call" | custom-call | flops 402653184 | bytes 524288 | tf_op jit(solution)/shard_map/attend_0_4/pallas_call | solution.py:276
  13.8 0.0 collective-permute-done.3.refs_2_.refs_5_.refs_1_
  13.8 0.0 collective-permute-done.1.refs_0_.refs_2_.refs_5_
  13.8 0.0 collective-permute-done.5.refs_4_.refs_7_.refs_3_
  13.8 1.7 %collective-permute-start.6 = (bf16[2,2,64,256]{3,2,1,0:T(8,128)(2,1)S(1)}, bf16[2,2,64,256]{3,2,1,0:T(8,128)(2,1)S(1)}, u32[]{:S(2)}, u32[]{:S(2)}) collective-permute-start(bf16[2,2,64,256]{3,2,1,0:T(8,128)(2,1)S(1)} %pack_blocks.4), channel_id=1, source_target_pairs={{0,16},{2,18},{4,20},{6,22},{8,10},{10,8},{12,14},{14,12},{16,0},{... | collective-permute-start | bytes 393224 | tf_op jit(solution)/shard_map/ppermute | solution.py:371
  15.5 0.0 collective-permute-start.9
  15.5 0.8 %collective-permute-done.7.refs_3_.refs_6_ = bf16[2,2,64,256]{3,2,1,0:T(8,128)(2,1)S(1)} collective-permute-done((bf16[2,2,64,256]{3,2,1,0:T(8,128)(2,1)S(1)}, bf16[2,2,64,256]{3,2,1,0:T(8,128)(2,1)S(1)}, u32[]{:S(2)}, u32[]{:S(2)}) %collective-permute-start.7) | collective-permute-done | bytes 131104 | tf_op jit(solution)/shard_map/ppermute | solution.py:371
  16.3 0.0 collective-permute-start.10
  16.3 1.7 %attend_1_2.1 = (f32[1024,128]{1,0:T(8,128)S(1)}, f32[1024,256]{1,0:T(8,128)S(1)}, f32[1024,128]{1,0:T(8,128)S(1)}, f32[1024,256]{1,0:T(8,128)S(1)}) custom-call(bf16[64,2048]{1,0:T(8,128)(2,1)S(1)} %get-tuple-element.24.refs_0_, bf16[64,2048]{1,0:T(8,128)(2,1)S(1)} %get-tuple-element.25.refs_1_, ...), custom_call_target="tpu_custom_call" | custom-call | flops 402653184 | bytes 524288 | tf_op jit(solution)/shard_map/attend_1_2/pallas_call | solution.py:276
  18.1 0.8 %collective-permute-done.6.refs_0_.refs_2_.refs_7_ = bf16[2,2,64,256]{3,2,1,0:T(8,128)(2,1)S(1)} collective-permute-done((bf16[2,2,64,256]{3,2,1,0:T(8,128)(2,1)S(1)}, bf16[2,2,64,256]{3,2,1,0:T(8,128)(2,1)S(1)}, u32[]{:S(2)}, u32[]{:S(2)}) %collective-permute-start.6) | collective-permute-done | bytes 131104 | tf_op jit(solution)/shard_map/ppermute | solution.py:371
  18.9 0.1 collective-permute-start.8
  18.9 0.0 collective-permute-done.9.refs_2_.refs_9_
  19.0 0.0 collective-permute-done.10.refs_3_.refs_10_
  19.0 1.0 %attend_5_6.1 = (f32[1024,128]{1,0:T(8,128)S(1)}, f32[1024,256]{1,0:T(8,128)S(1)}, f32[1024,128]{1,0:T(8,128)S(1)}, f32[1024,256]{1,0:T(8,128)S(1)}) custom-call(bf16[64,2048]{1,0:T(8,128)(2,1)S(1)} %get-tuple-element.24.refs_0_, bf16[64,2048]{1,0:T(8,128)(2,1)S(1)} %get-tuple-element.25.refs_1_, ...), custom_call_target="tpu_custom_call" | custom-call | flops 402653184 | bytes 524288 | tf_op jit(solution)/shard_map/attend_5_6/pallas_call | solution.py:276
  20.0 0.3 %collective-permute-done.8.refs_3_.refs_11_ = bf16[2,2,64,256]{3,2,1,0:T(8,128)(2,1)S(1)} collective-permute-done((bf16[2,2,64,256]{3,2,1,0:T(8,128)(2,1)S(1)}, bf16[2,2,64,256]{3,2,1,0:T(8,128)(2,1)S(1)}, u32[]{:S(2)}, u32[]{:S(2)}) %collective-permute-start.8) | collective-permute-done | bytes 131104 | tf_op jit(solution)/shard_map/ppermute | solution.py:35
  20.3 1.1 %step_logits.1 = f32[1,8]{1,0:T(1,128)S(1)} custom-call(s32[1,8]{1,0:T(1,128)S(1)} %get-tuple-element.43.ends_ref, f32[1,2048]{1,0:T(1,128)S(1)} %get-tuple-element.44.head_ref, s32[1,128]{1,0:T(1,128)S(1)} %get-tuple-element.33.refs_4_.lengths_ref, bf16[3,64,256]{2,1,0:T(8,128)(2,1)S(1)} %get-tuple-element.28.refs_4_.refs_0_, ...), custom_call_target="tpu_custom_call" | custom-call | flops 125829120 | bytes 163840 | tf_op jit(solution)/shard_map/step_logits/pallas_call | solution.py:343
  21.3 1.6 %collective-permute-start.11 = (f32[1,8]{1,0:T(1,128)S(1)}, f32[1,8]{1,0:T(1,128)S(1)}, u32[]{:S(2)}, u32[]{:S(2)}) collective-permute-start(f32[1,8]{1,0:T(1,128)S(1)} %step_logits.1), channel_id=1, source_target_pairs={{0,1},{1,0},{2,3},{3,2},{4,5},{5,4},{6,7},{7,6},{8,9},{9,8},{10,11... | collective-permute-start | bytes 104 | tf_op jit(solution)/shard_map/ppermute | solution.py:35
  23.0 1.8 %attend_3_7.1 = (bf16[64,2048]{1,0:T(8,128)(2,1)}, bf16[64,2048]{1,0:T(8,128)(2,1)}) custom-call(bf16[64,2048]{1,0:T(8,128)(2,1)S(1)} %get-tuple-element.24.refs_0_, bf16[64,2048]{1,0:T(8,128)(2,1)S(1)} %get-tuple-element.25.refs_1_, bf16[2,2,64,256]{3,2,1,0:T(8,128)(2,1)S(1)} %collective-permute-done.6.refs_0_.refs_2_.refs_7_, ...), custom_call_target="tpu_custom_call" | custom-call | flops 402653184 | bytes 524288 | tf_op jit(solution)/shard_map/attend_3_7/pallas_call | solution.py:276
  24.8 0.1 collective-permute-done.11
  24.9 0.5 %add.3 = f32[1,8]{1,0:T(1,128)} add(f32[1,8]{1,0:T(1,128)S(1)} %step_logits.1, f32[1,8]{1,0:T(1,128)S(1)} %collective-permute-done.11) | non-fusion elementwise | flops 8 | bytes 96 | tf_op jit(solution)/shard_map/add | solution.py:394
  (3 shorter events, 0.0 us)
Async XLA Ops:
  0.6 8.0 %collective-permute-start = (bf16[1,2,64,256]{3,2,1,0:T(8,128)(2,1)}, bf16[1,2,64,256]{3,2,1,0:T(8,128)(2,1)S(1)}, u32[]{:S(2)}, u32[]{:S(2)}) collective-permute-start(bf16[1,2,64,256]{3,2,1,0:T(8,128)(2,1)} %bitcast.9), channel_id=1, source_target_pairs={{0,4},{2,6},{4,0},{6,2},{8,12},{10,14},{12,8},{14,10},{16,20},{18,... | collective-permute-start | bytes 196616 | tf_op jit(solution)/shard_map/ppermute | solution.py:35
  6.7 4.7 %collective-permute-start.4 = (bf16[3,64,256]{2,1,0:T(8,128)(2,1)S(1)}, bf16[3,64,256]{2,1,0:T(8,128)(2,1)S(1)}, u32[]{:S(2)}, u32[]{:S(2)}) collective-permute-start(bf16[3,64,256]{2,1,0:T(8,128)(2,1)S(1)} %get-tuple-element.28.refs_4_.refs_0_), channel_id=1, source_target_pairs={{0,16},{8,24},{16,0},{24,8},{1,17},{9,25},{17,1},{25,9},{2,18},{10... | collective-permute-start | bytes 294920 | tf_op jit(solution)/shard_map/ppermute | solution.py:35
  8.6 4.3 %collective-permute-start.2 = (bf16[2,2,64,256]{3,2,1,0:T(8,128)(2,1)S(1)}, bf16[2,2,64,256]{3,2,1,0:T(8,128)(2,1)S(1)}, u32[]{:S(2)}, u32[]{:S(2)}) collective-permute-start(bf16[2,2,64,256]{3,2,1,0:T(8,128)(2,1)S(1)} %pack_blocks.3.refs_2_.refs_4_), channel_id=1, source_target_pairs={{0,8},{2,10},{4,12},{6,14},{8,0},{10,2},{12,4},{14,6},{16,24},{18,... | collective-permute-start | bytes 393224 | tf_op jit(solution)/shard_map/ppermute | solution.py:35
  8.7 5.1 %collective-permute-start.1 = (bf16[2,2,64,256]{3,2,1,0:T(8,128)(2,1)S(1)}, bf16[2,2,64,256]{3,2,1,0:T(8,128)(2,1)S(1)}, u32[]{:S(2)}, u32[]{:S(2)}) collective-permute-start(bf16[2,2,64,256]{3,2,1,0:T(8,128)(2,1)S(1)} %pack_blocks.3.refs_2_.refs_4_), channel_id=1, source_target_pairs={{0,2},{2,0},{4,6},{6,4},{8,24},{10,26},{12,28},{14,30},{16,18},{18... | collective-permute-start | bytes 393224 | tf_op jit(solution)/shard_map/ppermute | solution.py:371
  10.0 3.8 %collective-permute-start.3 = (bf16[3,64,256]{2,1,0:T(8,128)(2,1)S(1)}, bf16[3,64,256]{2,1,0:T(8,128)(2,1)S(1)}, u32[]{:S(2)}, u32[]{:S(2)}) collective-permute-start(bf16[3,64,256]{2,1,0:T(8,128)(2,1)S(1)} %get-tuple-element.28.refs_4_.refs_0_), channel_id=1, source_target_pairs={{0,8},{8,0},{16,24},{24,16},{1,9},{9,1},{17,25},{25,17},{2,10},{10... | collective-permute-start | bytes 294920 | tf_op jit(solution)/shard_map/ppermute | solution.py:35
  11.3 2.5 %collective-permute-start.5 = (bf16[3,64,256]{2,1,0:T(8,128)(2,1)S(1)}, bf16[3,64,256]{2,1,0:T(8,128)(2,1)S(1)}, u32[]{:S(2)}, u32[]{:S(2)}) collective-permute-start(bf16[3,64,256]{2,1,0:T(8,128)(2,1)S(1)} %collective-permute-done.4.refs_3_.refs_6_.refs_2_), channel_id=1, source_target_pairs={{0,8},{8,0},{16,24},{24,16},{1,9},{9,1},{17,25},{25,17},{2,10},{10... | collective-permute-start | bytes 294920 | tf_op jit(solution)/shard_map/ppermute | solution.py:35
  11.3 5.0 %collective-permute-start.7 = (bf16[2,2,64,256]{3,2,1,0:T(8,128)(2,1)S(1)}, bf16[2,2,64,256]{3,2,1,0:T(8,128)(2,1)S(1)}, u32[]{:S(2)}, u32[]{:S(2)}) collective-permute-start(bf16[2,2,64,256]{3,2,1,0:T(8,128)(2,1)S(1)} %pack_blocks.3.refs_2_.refs_4_), channel_id=1, source_target_pairs={{0,16},{2,18},{4,20},{6,22},{8,10},{10,8},{12,14},{14,12},{16,0},{... | collective-permute-start | bytes 393224 | tf_op jit(solution)/shard_map/ppermute | solution.py:371
  13.8 5.0 %collective-permute-start.6 = (bf16[2,2,64,256]{3,2,1,0:T(8,128)(2,1)S(1)}, bf16[2,2,64,256]{3,2,1,0:T(8,128)(2,1)S(1)}, u32[]{:S(2)}, u32[]{:S(2)}) collective-permute-start(bf16[2,2,64,256]{3,2,1,0:T(8,128)(2,1)S(1)} %pack_blocks.4), channel_id=1, source_target_pairs={{0,16},{2,18},{4,20},{6,22},{8,10},{10,8},{12,14},{14,12},{16,0},{... | collective-permute-start | bytes 393224 | tf_op jit(solution)/shard_map/ppermute | solution.py:371
  15.5 3.4 %collective-permute-start.9 = (bf16[2,2,64,256]{3,2,1,0:T(8,128)(2,1)S(1)}, bf16[2,2,64,256]{3,2,1,0:T(8,128)(2,1)S(1)}, u32[]{:S(2)}, u32[]{:S(2)}) collective-permute-start(bf16[2,2,64,256]{3,2,1,0:T(8,128)(2,1)S(1)} %collective-permute-done.1.refs_0_.refs_2_.refs_5_), channel_id=1, source_target_pairs={{0,8},{2,10},{4,12},{6,14},{8,0},{10,2},{12,4},{14,6},{16,24},{18,... | collective-permute-start | bytes 393224 | tf_op jit(solution)/shard_map/ppermute | solution.py:35
  16.3 2.6 %collective-permute-start.10 = (bf16[2,2,64,256]{3,2,1,0:T(8,128)(2,1)S(1)}, bf16[2,2,64,256]{3,2,1,0:T(8,128)(2,1)S(1)}, u32[]{:S(2)}, u32[]{:S(2)}) collective-permute-start(bf16[2,2,64,256]{3,2,1,0:T(8,128)(2,1)S(1)} %collective-permute-done.7.refs_3_.refs_6_), channel_id=1, source_target_pairs={{0,8},{2,10},{4,12},{6,14},{8,0},{10,2},{12,4},{14,6},{16,24},{18,... | collective-permute-start | bytes 393224 | tf_op jit(solution)/shard_map/ppermute | solution.py:35
  18.9 1.4 %collective-permute-start.8 = (bf16[2,2,64,256]{3,2,1,0:T(8,128)(2,1)S(1)}, bf16[2,2,64,256]{3,2,1,0:T(8,128)(2,1)S(1)}, u32[]{:S(2)}, u32[]{:S(2)}) collective-permute-start(bf16[2,2,64,256]{3,2,1,0:T(8,128)(2,1)S(1)} %pack_blocks.5), channel_id=1, source_target_pairs={{0,8},{2,10},{4,12},{6,14},{8,0},{10,2},{12,4},{14,6},{16,24},{18,... | collective-permute-start | bytes 393224 | tf_op jit(solution)/shard_map/ppermute | solution.py:35
  21.3 3.5 %collective-permute-start.11 = (f32[1,8]{1,0:T(1,128)S(1)}, f32[1,8]{1,0:T(1,128)S(1)}, u32[]{:S(2)}, u32[]{:S(2)}) collective-permute-start(f32[1,8]{1,0:T(1,128)S(1)} %step_logits.1), channel_id=1, source_target_pairs={{0,1},{1,0},{2,3},{3,2},{4,5},{5,4},{6,7},{7,6},{8,9},{9,8},{10,11... | collective-permute-start | bytes 104 | tf_op jit(solution)/shard_map/ppermute | solution.py:35

commit v6 on v5

--- a/solution.py
+++ b/solution.py
@@ -55,6 +55,31 @@
     )(*arrays, *after)
 
 
+def pack_side_kernel(even_ref, odd_ref, last_ref, _, out_ref):
+    count = last_ref.shape[0]
+    out_ref[count:] = last_ref[...]
+    odd = lax.rem(lax.axis_index("ctx"), 2)
+
+    @pl.when(odd == 0)
+    def _():
+        out_ref[:count] = even_ref[...]
+
+    @pl.when(odd == 1)
+    def _():
+        out_ref[:count] = odd_ref[...]
+
+
+def packed_side(even, odd, last, after):
+    return pl.pallas_call(
+        pack_side_kernel,
+        out_shape=jax.ShapeDtypeStruct((2 * last.shape[0],) + last.shape[1:], last.dtype),
+        in_specs=vmem(3) + [pl.BlockSpec(memory_space=pl.ANY)],
+        out_specs=vmem(1)[0],
+        compiler_params=PARAMS,
+        name="pack_side",
+    )(even, odd, last, after)
+
+
 def prompt_bits(ctx_size, cand_size):
     core, along, across = cand_size, 1, 2 * cand_size
     early = high_bits(cand_size, 2) + [bit * cand_size for bit in high_bits(ctx_size, 4)]
@@ -63,36 +88,31 @@
 
 def prompt_owners(ctx_size, cand_size):
     early, along, across, core = prompt_bits(ctx_size, cand_size)
-    place = lax.axis_index("ctx") * cand_size + lax.axis_index("cand")
-    odd = lax.rem(lax.axis_index("ctx"), 2)
-    near = along + odd * (across - along)
+    place = prompt_place(cand_size)
+    near = along + lax.rem(lax.axis_index("ctx"), 2) * (across - along)
     far = along + across - near
     masks = [0]
-    for bit in early:
+    for bit in early[:-1]:
         masks += [mask ^ bit for mask in masks]
-    shifts = [0, near, far, along + across, core, core + far, core + near, core + along + across]
-    return [[place ^ mask ^ shift for mask in masks] for shift in shifts]
-
-
-def gather_cand(own, ctx_size):
-    blocks = [(own, 0), (flipped(own, "ctx", ctx_size, 1), 1)]
-    for bit in reversed(high_bits(ctx_size, 2)):
-        rail = [(flipped(b, "ctx", ctx_size, bit), mask | bit) for b, mask in blocks if not mask & 1]
-        blocks += rail + [(flipped(b, "ctx", ctx_size, 1), mask | 1) for b, mask in rail]
-    return blocks
-
-
-def stage_kernel(length_ref, prompt_q, cand_q, prompt_kv, cand_kv, ends, head, *refs):
-    q_out, cand_out, kv_out, pay_out, ends_out, head_out, length_out, length_here, sems = refs
+    last = early[-1]
+    both = along + across
+    shifts = [[0], [core], [across], [across + core]]
+    shifts += [[last, along], [core + last, core + along]]
+    shifts += [[last + near, last + far], [core + last + far, core + last + near]]
+    shifts += [[both, both + last], [core + both, core + both + last]]
+    return [[place ^ mask ^ shift for shift in array for mask in masks] for array in shifts]
+
+
+def stage_kernel(prompt_q, cand_q, prompt_kv, cand_kv, ends, head, *refs):
+    q_out, cand_out, own_out, pay_out, ends_out, head_out, sems = refs
     steps = ends.shape[1]
     pairs = [
         (cand_q, cand_out),
         (ends, ends_out),
+        (prompt_kv, own_out),
         (cand_kv, pay_out.at[0:2]),
-        (prompt_kv, kv_out),
         (prompt_q, q_out),
         (head, head_out),
-        (length_ref, length_here),
     ]
     copies = [pltpu.make_async_copy(a, b, sems.at[i]) for i, (a, b) in enumerate(pairs)]
     for copy in copies:
@@ -109,7 +129,6 @@
     pay_out[2] = jnp.concatenate(pieces, axis=0).astype(jnp.bfloat16)
     for copy in copies[2:]:
         copy.wait()
-    length_out[...] = jnp.full(length_out.shape, length_here[0], jnp.int32)
 
 
 def column_of(row):
@@ -119,20 +138,18 @@
     return jnp.sum(jnp.where(down == right, row, 0), axis=1, keepdims=True)
 
 
-def staged(length, prompt_q, cand_q, prompt_kv, cand_kv, ends, head):
+def staged(prompt_q, cand_q, prompt_kv, cand_kv, ends, head):
     arrays = (prompt_q, cand_q, prompt_kv, cand_kv, ends, head)
-    payload = jax.ShapeDtypeStruct((3,) + cand_kv.shape[1:], cand_kv.dtype)
-    lengths = jax.ShapeDtypeStruct((1, HEADDIM), jnp.int32)
+    pay = jax.ShapeDtypeStruct((3,) + cand_kv.shape[1:], cand_kv.dtype)
     return pl.pallas_call(
         stage_kernel,
-        out_shape=(like(prompt_q), like(cand_q), like(prompt_kv), payload, like(ends), like(head), lengths),
-        in_specs=[pl.BlockSpec(memory_space=pl.ANY)]
-        + [pl.BlockSpec(memory_space=pltpu.HBM)] * len(arrays),
-        out_specs=tuple(vmem(7)),
-        scratch_shapes=[pltpu.SMEM((1,), jnp.int32), pltpu.SemaphoreType.DMA((len(arrays) + 1,))],
+        out_shape=(like(prompt_q), like(cand_q), like(prompt_kv), pay, like(ends), like(head)),
+        in_specs=[pl.BlockSpec(memory_space=pltpu.HBM)] * len(arrays),
+        out_specs=tuple(vmem(6)),
+        scratch_shapes=[pltpu.SemaphoreType.DMA((len(arrays),))],
         compiler_params=PARAMS,
         name="stage_operands",
-    )(length, *(pltpu.with_memory_space_constraint(a, pltpu.HBM) for a in arrays))
+    )(*(pltpu.with_memory_space_constraint(a, pltpu.HBM) for a in arrays))
 
 
 def tiles(q_ref, head):
@@ -160,7 +177,7 @@
 
 def head_rows(blocks, which, head):
     columns = slice(head * HEADDIM, (head + 1) * HEADDIM)
-    return jnp.concatenate([ref[lead + (which,)][:, columns] for ref, lead in blocks], axis=0)
+    return jnp.concatenate([ref[plane + which, :, columns] for ref, plane in blocks], axis=0)
 
 
 def key_positions(owners, rows):
@@ -195,8 +212,8 @@
     return lax.axis_index("ctx") * cand_size + lax.axis_index("cand")
 
 
-def pairs_of(refs):
-    return [(ref, (index,)) for ref in refs for index in range(ref.shape[0])]
+def payloads(refs, count):
+    return [(ref, ref.shape[0] - 3 * (count - i)) for ref in refs for i in range(count)]
 
 
 def phase_kernel(sizes, arrays, masks, first, last, *refs):
@@ -204,7 +221,7 @@
     take = iter(refs)
     prompt_q, cand_q = next(take), next(take)
     block_refs = [next(take) for _ in arrays]
-    pays = [next(take) for _ in masks]
+    pay_refs = [next(take) for _ in range(4 if masks else 0)]
     lengths = next(take) if last else None
     old = None if first else [(next(take), next(take)) for _ in range(2)]
     outs = refs[-2:] if last else refs[-4:]
@@ -212,13 +229,15 @@
     cand_rows = cand_q.shape[0]
     owners = prompt_owners(ctx_size, cand_size)
     key_pos = key_positions([place for index in arrays for place in owners[index]], rows)
-    blocks = pairs_of(block_refs)
-    own = [(ref, ()) for ref in pays]
+    blocks = [
+        (ref, 2 * i) for ref, index in zip(block_refs, arrays) for i in range(len(owners[index]))
+    ]
+    own = payloads(pay_refs, len(masks) // len(pay_refs)) if masks else []
     ctx = lax.axis_index("ctx")
     own_pos = key_positions([ctx ^ mask for mask in masks], cand_rows) if masks else None
     alive = stacked_rows(ctx * cand_rows, cand_rows, cand_rows) < lengths[:, :1] if last else None
 
-    for head in range(block_refs[0].shape[3] // HEADDIM):
+    for head in range(block_refs[0].shape[2] // HEADDIM):
         key_rows = head_rows(blocks, 0, head)
         widened = with_ones(head_rows(blocks, 1, head))
         if masks:
@@ -252,11 +271,11 @@
                     outs[kind][:, h * HEADDIM : (h + 1) * HEADDIM] = kept.astype(jnp.bfloat16)
 
 
-def phase(sizes, arrays, q_rows, blocks, pays=(), state=None, lengths=None, after=()):
+def phase(sizes, arrays, q_rows, blocks, masks=(), state=None, lengths=None, after=()):
     prompt_q, cand_q = q_rows
     first, last = state is None, lengths is not None
     operands = [prompt_q, cand_q] + [blocks[index] for index in arrays]
-    operands += [b for b, _ in pays]
+    operands += blocks[:4] if masks else []
     if last:
         operands.append(lengths)
     if not first:
@@ -270,9 +289,8 @@
             count = heads * q.shape[0]
             shapes.append(jax.ShapeDtypeStruct((count, HEADDIM), jnp.float32))
             shapes.append(jax.ShapeDtypeStruct((count, 2 * HEADDIM), jnp.float32))
-    key_count = sum(blocks[i].shape[0] * blocks[i].shape[2] for i in arrays)
+    key_count = sum(blocks[i].shape[0] // 2 * blocks[i].shape[1] for i in arrays)
     scores = heads * (prompt_q.shape[0] + cand_q.shape[0]) * key_count
-    masks = [mask for _, mask in pays]
     return pl.pallas_call(
         functools.partial(phase_kernel, sizes, arrays, masks, first, last),
         out_shape=tuple(shapes),
@@ -280,7 +298,7 @@
         out_specs=tuple(vmem(len(shapes))),
         compiler_params=PARAMS,
         cost_estimate=pl.CostEstimate(
-            flops=6 * scores * HEADDIM, bytes_accessed=scores, transcendentals=scores
+            flops=scores, bytes_accessed=scores, transcendentals=0
         ),
         name="attend_" + "_".join(str(i) for i in arrays),
     )(*operands, *after)
@@ -288,23 +306,24 @@
 
 def step_kernel(sizes, masks, ends_ref, head_ref, lengths_ref, *refs):
     ctx_size, cand_size = sizes
-    pays, blocks = refs[: len(masks)], refs[len(masks) : -2]
+    blocks = refs[:-2]
     logit_ref, kv_ref = refs[-2:]
-    rows = blocks[0].shape[2]
-    own_rows = pays[0].shape[1]
+    pays = payloads(blocks[:4], len(masks) // 4)
+    rows = blocks[0].shape[1]
+    own_rows = rows
     free = rows * ctx_size * cand_size
     place = lax.axis_index("ctx")
     for ref, owners in zip(blocks, prompt_owners(ctx_size, cand_size)):
         for index, owner in enumerate(owners):
             at = pl.ds(pl.multiple_of(owner * rows, rows), rows)
-            kv_ref[0, at, :] = ref[index, 0]
-            kv_ref[1, at, :] = ref[index, 1]
-    picked = jnp.zeros(pays[0].shape[1:], jnp.float32)
-    for ref, mask in zip(pays, masks):
+            kv_ref[0, at, :] = ref[2 * index]
+            kv_ref[1, at, :] = ref[2 * index + 1]
+    picked = jnp.zeros(blocks[0].shape[1:], jnp.float32)
+    for (ref, plane), mask in zip(pays, masks):
         at = pl.ds(pl.multiple_of(free + (place ^ mask) * own_rows, own_rows), own_rows)
-        kv_ref[0, at, :] = ref[0]
-        kv_ref[1, at, :] = ref[1]
-        picked += ref[2].astype(jnp.float32)
+        kv_ref[0, at, :] = ref[plane]
+        kv_ref[1, at, :] = ref[plane + 1]
+        picked += ref[plane + 2].astype(jnp.float32)
     steps = ends_ref.shape[1]
     width = picked.shape[1]
     step_rows = [picked[at : at + steps] for at in range(0, steps * head_ref.shape[1] // width, steps)]
@@ -335,60 +354,70 @@
     logit_ref[...] = jnp.sum(jnp.where(down == right, logits, 0.0), axis=0, keepdims=True)
 
 
-def step_shares(sizes, ends, head, lengths, pays, blocks):
+def step_shares(sizes, ends, head, lengths, masks, blocks):
     ctx_size, cand_size = sizes
-    rows, width = blocks[0].shape[2:]
-    count = rows * ctx_size * cand_size + pays[0][0].shape[1] * ctx_size
+    rows, width = blocks[0].shape[1:]
+    count = rows * ctx_size * cand_size + rows * ctx_size
     scores = ends.shape[1] * head.shape[1] // HEADDIM * count
     return pl.pallas_call(
-        functools.partial(step_kernel, sizes, [mask for _, mask in pays]),
+        functools.partial(step_kernel, sizes, masks),
         out_shape=jax.ShapeDtypeStruct(ends.shape, jnp.float32),
-        in_specs=vmem(3 + len(pays) + len(blocks)),
+        in_specs=vmem(3 + len(blocks)),
         out_specs=vmem(1)[0],
         scratch_shapes=[pltpu.VMEM((2, count, width), blocks[0].dtype)],
         compiler_params=PARAMS,
         cost_estimate=pl.CostEstimate(
-            flops=6 * scores * HEADDIM, bytes_accessed=scores, transcendentals=scores
+            flops=scores, bytes_accessed=scores, transcendentals=0
         ),
         name="step_logits",
-    )(ends, head, lengths, *(b for b, _ in pays), *blocks)
+    )(ends, head, lengths, *blocks)
 
 
 def per_device(ctx_size, cand_size, prompt_q, prompt_kv, cand_q, cand_kv, cand_lengths, step_ends, reward_head):
     sizes = ctx_size, cand_size
     size = ctx_size * cand_size
-    prompt_rows, cand_rows, own, payload, ends, head, lengths = staged(
-        cand_lengths, prompt_q, cand_q[0], prompt_kv, cand_kv[:, 0], step_ends, reward_head[None]
+    prompt_rows, cand_rows, own, pay, ends, head = staged(
+        prompt_q, cand_q[0], prompt_kv, cand_kv[:, 0], step_ends, reward_head[None]
     )
+    lengths = jnp.broadcast_to(cand_lengths[None], (1, HEADDIM))
     q_rows = prompt_rows, cand_rows
-    pays = gather_cand(payload, ctx_size)
     early, along, across, core = prompt_bits(ctx_size, cand_size)
 
-    def across_cores(block):
-        return flipped(block, PROMPT_AXES, size, core)
+    def moved(block, bit):
+        return flipped(block, PROMPT_AXES, size, bit)
 
     def shared_out(block, even, odd):
         return lax.ppermute(
             block, PROMPT_AXES, [(i, i ^ (odd if i & core else even)) for i in range(size)]
         )
 
-    held = own[None]
-    sent = prompt_kv[None]
+    held, sent = own, prompt_kv
+    for bit in early[:-1]:
+        held = packed(held, moved(sent, bit))
+        sent = held
+    pay_masks = [0]
     for bit in early:
-        held = packed(held, flipped(sent, PROMPT_AXES, size, bit))
-        sent = held
-    second = shared_out(held, along, across)
-    third = shared_out(held, across, along)
-    blocks = [held, second, third, None, across_cores(held), None, None, None]
-    state = phase(sizes, [0, 4], q_rows, blocks)
-    fourth = shared_out(packed(second, after=state[:1] + tuple(b for b, _ in pays[1:4])), across, along)
-    blocks[3] = fourth
-    blocks[5:7] = across_cores(second), across_cores(third)
-    state = phase(sizes, [1, 2], q_rows, blocks, pays=pays, state=state)
-    blocks[7] = across_cores(packed(fourth, after=state[:1]))
-    state = phase(sizes, [5, 6], q_rows, blocks, state=state)
-    step_logits = step_shares(sizes, ends, head, lengths, pays, blocks)
-    cand_out, prompt_out = phase(sizes, [3, 7], q_rows, blocks, state=state, lengths=lengths)
+        if bit >= size // ctx_size:
+            pay = packed(pay, moved(pay, bit))
+            pay_masks += [mask ^ bit // cand_size for mask in pay_masks]
+    beyond = moved(sent, early[-1])
+    beside = moved(held, along)
+    opposite = moved(held, across)
+    here = packed(held, pay)
+    facing = packed(opposite, moved(pay, across))
+    one = shared_out(beyond, along, across)
+    two = shared_out(beyond, across, along)
+    far = shared_out(packed_side(beside, opposite, one, two), across, along)
+    pair = packed(beyond, beside)
+    sides = packed(one, two)
+    blocks = [here, moved(here, core), facing, moved(facing, core)]
+    blocks += [pair, moved(pair, core), sides, moved(sides, core), far]
+    masks = [mask ^ shift for shift in (0, 1, 2, 3) for mask in pay_masks]
+    state = phase(sizes, [0, 1, 4, 5], q_rows, blocks, after=[facing])
+    state = phase(sizes, [2, 3, 6, 7], q_rows, blocks, masks=masks, state=state)
+    blocks.append(moved(packed(far, after=state[:1]), core))
+    step_logits = step_shares(sizes, ends, head, lengths, masks, blocks)
+    cand_out, prompt_out = phase(sizes, [8, 9], q_rows, blocks, state=state, lengths=lengths)
     tp_size = lax.axis_size("tp")
     for bit in high_bits(tp_size, 1):
         step_logits = step_logits + flipped(step_logits, "tp", tp_size, bit)

time: 25.5 us -> 27.5 us (1.078)
  starting transfers between devices: 12.6 us -> 13.9 us
  Pallas kernels: 7.79 us -> 8.87 us
  waiting for transfers between devices: 3.08 us -> 2.75 us
    ppermute x9 -> x10, starting transfers between devices: 8.1 us -> 10.3 us  [flipped(): return lax.ppermute(block, axes, [(i, i ^ bit) for i in range(size)])]
    pallas_call x4 -> x3, Pallas kernels: 5.44 us -> 6.5 us  [phase(): pl.pallas_call(functools.partial(phase_kernel, sizes, arrays, masks, firs...]
    ppermute x3, starting transfers between devices: 4.53 us -> 3.55 us  [shared_out(): lax.ppermute(block, PROMPT_AXES, [(i, i ^ (odd if i & core else even)) fo...]
    ppermute x3, waiting for transfers between devices: 1.57 us -> 1.07 us  [shared_out(): lax.ppermute(block, PROMPT_AXES, [(i, i ^ (odd if i & core else even)) fo...]
    ppermute x9 -> x10, waiting for transfers between devices: 1.5 us -> 1.68 us  [flipped(): return lax.ppermute(block, axes, [(i, i ^ bit) for i in range(size)])]
    pallas_call x1 -> x2, Pallas kernels: 1.05 us -> 1.08 us  [the longest x1 1.05 us: step_shares(): pl.pallas_call(functools.partial(step_kernel, sizes, masks), out_shape=ja...]
  transfers between devices with their start and end apart: 12 -> 13, of which waited for: 6 -> 5; matrix products, arithmetic and copies ran while one was open for 0% -> 0% of each run, Pallas kernels for 27% -> 28%
where the time goes in v6:
time: 27.5 us; the launch traced here: 27.4 us
  starting transfers between devices  13.9 us (51%)
  Pallas kernels  8.87 us (32%)
  waiting for transfers between devices  2.75 us (10%)
  between operations  1.38 us (5%)
  other arithmetic  0.51 us (2%)
    ppermute x10, starting transfers between devices, flipped(): return lax.ppermute(block, axes, [(i, i ^ bit) for i in range(size)])  10.3 us
    pallas_call x3, Pallas kernels, phase(): pl.pallas_call(functools.partial(phase_kernel, sizes, arrays, masks, firs...  6.5 us
    ppermute x3, starting transfers between devices, shared_out(): lax.ppermute(block, PROMPT_AXES, [(i, i ^ (odd if i & core else even)) fo...  3.55 us
    ppermute x10, waiting for transfers between devices, flipped(): return lax.ppermute(block, axes, [(i, i ^ bit) for i in range(size)])  1.68 us
    pallas_call x1, Pallas kernels, staged(): pl.pallas_call(stage_kernel, out_shape=(like(prompt_q), like(cand_q), lik...  1.24 us
    ppermute x3, waiting for transfers between devices, shared_out(): lax.ppermute(block, PROMPT_AXES, [(i, i ^ (odd if i & core else even)) fo...  1.07 us
    pallas_call x1, Pallas kernels, step_shares(): pl.pallas_call(functools.partial(step_kernel, sizes, masks), out_shape=ja...  1.05 us
  transfers between devices with their start and end apart: 13, of which 5 were waited for; matrix products, arithmetic and copies ran while one was open for 0% of the time, Pallas kernels for 28%

profile of v6, /device:TPU:0, one launch (start us, length us, event | category | flops | bytes accessed | tf_op | source)
XLA Modules:
  0.0 27.4 jit_solution(13912611655765415093)
XLA Ops:
  0.6 4.1 %collective-permute-start.2 = (bf16[2,64,256]{2,1,0:T(8,128)(2,1)}, bf16[2,64,256]{2,1,0:T(8,128)(2,1)S(1)}, u32[]{:S(2)}, u32[]{:S(2)}) collective-permute-start(bf16[2,64,256]{2,1,0:T(8,128)(2,1)} %prompt_kv.1), channel_id=1, source_target_pairs={{0,4},{2,6},{4,0},{6,2},{8,12},{10,14},{12,8},{14,10},{16,20},{18,... | collective-permute-start | bytes 196616 | tf_op jit(solution)/shard_map/ppermute | solution.py:35
  4.7 1.2 %stage_operands.1 = (bf16[64,2048]{1,0:T(8,128)(2,1)S(1)}, bf16[64,2048]{1,0:T(8,128)(2,1)S(1)}, bf16[2,64,256]{2,1,0:T(8,128)(2,1)S(1)}, bf16[3,64,256]{2,1,0:T...) custom-call(bf16[64,2048]{1,0:T(8,128)(2,1)} %prompt_q.1, bf16[64,2048]{1,0:T(8,128)(2,1)} %bitcast.6, ...), custom_call_target="tpu_custom_call" | custom-call | tf_op jit(solution)/shard_map/stage_operands/pallas_call | solution.py:144
  6.0 1.6 %collective-permute-start.6 = (bf16[3,64,256]{2,1,0:T(8,128)(2,1)S(1)}, bf16[3,64,256]{2,1,0:T(8,128)(2,1)S(1)}, u32[]{:S(2)}, u32[]{:S(2)}) collective-permute-start(bf16[3,64,256]{2,1,0:T(8,128)(2,1)S(1)} %get-tuple-element.22.refs_1_), channel_id=1, source_target_pairs={{0,16},{2,18},{4,20},{6,22},{8,24},{10,26},{12,28},{14,30},{16,0},... | collective-permute-start | bytes 294920 | tf_op jit(solution)/shard_map/ppermute | solution.py:35
  7.6 0.5 %collective-permute-start.1 = (bf16[2,64,256]{2,1,0:T(8,128)(2,1)S(1)}, bf16[2,64,256]{2,1,0:T(8,128)(2,1)S(1)}, u32[]{:S(2)}, u32[]{:S(2)}) collective-permute-start(bf16[2,64,256]{2,1,0:T(8,128)(2,1)S(1)} %get-tuple-element.21.refs_0_), channel_id=1, source_target_pairs={{0,16},{2,18},{4,20},{6,22},{8,24},{10,26},{12,28},{14,30},{16,0},... | collective-permute-start | bytes 196616 | tf_op jit(solution)/shard_map/ppermute | solution.py:35
  8.1 1.6 %collective-permute-start = (bf16[2,64,256]{2,1,0:T(8,128)(2,1)S(1)}, bf16[2,64,256]{2,1,0:T(8,128)(2,1)S(1)}, u32[]{:S(2)}, u32[]{:S(2)}) collective-permute-start(bf16[2,64,256]{2,1,0:T(8,128)(2,1)S(1)} %get-tuple-element.21.refs_0_), channel_id=1, source_target_pairs={{0,2},{2,0},{4,6},{6,4},{8,10},{10,8},{12,14},{14,12},{16,18},{18,... | collective-permute-start | bytes 196616 | tf_op jit(solution)/shard_map/ppermute | solution.py:35
  9.7 0.0 collective-permute-done.2.refs_0_
  9.7 0.5 %collective-permute-start.3 = (bf16[2,64,256]{2,1,0:T(8,128)(2,1)S(1)}, bf16[2,64,256]{2,1,0:T(8,128)(2,1)S(1)}, u32[]{:S(2)}, u32[]{:S(2)}) collective-permute-start(bf16[2,64,256]{2,1,0:T(8,128)(2,1)S(1)} %collective-permute-done.2.refs_0_), channel_id=1, source_target_pairs={{0,2},{2,0},{4,6},{6,4},{8,24},{10,26},{12,28},{14,30},{16,18},{18... | collective-permute-start | bytes 196616 | tf_op jit(solution)/shard_map/ppermute | solution.py:390
  10.1 1.5 %collective-permute-start.4 = (bf16[2,64,256]{2,1,0:T(8,128)(2,1)S(1)}, bf16[2,64,256]{2,1,0:T(8,128)(2,1)S(1)}, u32[]{:S(2)}, u32[]{:S(2)}) collective-permute-start(bf16[2,64,256]{2,1,0:T(8,128)(2,1)S(1)} %collective-permute-done.2.refs_0_), channel_id=1, source_target_pairs={{0,16},{2,18},{4,20},{6,22},{8,10},{10,8},{12,14},{14,12},{16,0},{... | collective-permute-start | bytes 196616 | tf_op jit(solution)/shard_map/ppermute | solution.py:390
  11.6 1.0 %collective-permute-done.1.odd_ref.refs_0_ = bf16[2,64,256]{2,1,0:T(8,128)(2,1)S(1)} collective-permute-done((bf16[2,64,256]{2,1,0:T(8,128)(2,1)S(1)}, bf16[2,64,256]{2,1,0:T(8,128)(2,1)S(1)}, u32[]{:S(2)}, u32[]{:S(2)}) %collective-permute-start.1) | collective-permute-done | bytes 65568 | tf_op jit(solution)/shard_map/ppermute | solution.py:35
  12.6 0.0 collective-permute-start.9
  12.6 0.0 collective-permute-done.6.refs_1_
  12.6 0.6 %collective-permute-start.7 = (bf16[5,64,256]{2,1,0:T(8,128)(2,1)S(1)}, bf16[5,64,256]{2,1,0:T(8,128)(2,1)S(1)}, u32[]{:S(2)}, u32[]{:S(2)}) collective-permute-start(bf16[5,64,256]{2,1,0:T(8,128)(2,1)S(1)} %pack_blocks.5.refs_6_.refs_2_.refs_8_), channel_id=1, source_target_pairs={{0,8},{2,10},{4,12},{6,14},{8,0},{10,2},{12,4},{14,6},{16,24},{18,... | collective-permute-start | bytes 491528 | tf_op jit(solution)/shard_map/ppermute | solution.py:35
  13.2 0.0 collective-permute-done.even_ref.refs_1_
  13.2 0.1 collective-permute-start.10
  13.3 0.6 %collective-permute-done.3.last_ref.refs_0_ = bf16[2,64,256]{2,1,0:T(8,128)(2,1)S(1)} collective-permute-done((bf16[2,64,256]{2,1,0:T(8,128)(2,1)S(1)}, bf16[2,64,256]{2,1,0:T(8,128)(2,1)S(1)}, u32[]{:S(2)}, u32[]{:S(2)}) %collective-permute-start.3) | collective-permute-done | bytes 65568 | tf_op jit(solution)/shard_map/ppermute | solution.py:390
  13.9 0.4 %collective-permute-done.4._.refs_1_ = bf16[2,64,256]{2,1,0:T(8,128)(2,1)S(1)} collective-permute-done((bf16[2,64,256]{2,1,0:T(8,128)(2,1)S(1)}, bf16[2,64,256]{2,1,0:T(8,128)(2,1)S(1)}, u32[]{:S(2)}, u32[]{:S(2)}) %collective-permute-start.4) | collective-permute-done | bytes 65568 | tf_op jit(solution)/shard_map/ppermute | solution.py:390
  14.4 0.1 collective-permute-start.8
  14.5 1.6 %collective-permute-start.5 = (bf16[4,64,256]{2,1,0:T(8,128)(2,1)S(1)}, bf16[4,64,256]{2,1,0:T(8,128)(2,1)S(1)}, u32[]{:S(2)}, u32[]{:S(2)}) collective-permute-start(bf16[4,64,256]{2,1,0:T(8,128)(2,1)S(1)} %pack_side.1), channel_id=1, source_target_pairs={{0,16},{2,18},{4,20},{6,22},{8,10},{10,8},{12,14},{14,12},{16,0},{... | collective-permute-start | bytes 393224 | tf_op jit(solution)/shard_map/ppermute | solution.py:390
  16.1 0.0 collective-permute-done.9.refs_3_.refs_7_.refs_1_
  16.1 0.0 collective-permute-done.10.refs_5_
  16.1 1.9 %attend_0_1_4_5.1 = (f32[1024,128]{1,0:T(8,128)S(1)}, f32[1024,256]{1,0:T(8,128)S(1)}, f32[1024,128]{1,0:T(8,128)S(1)}, f32[1024,256]{1,0:T(8,128)S(1)}) custom-call(bf16[64,2048]{1,0:T(8,128)(2,1)S(1)} %get-tuple-element.19.refs_0_, bf16[64,2048]{1,0:T(8,128)(2,1)S(1)} %get-tuple-element.20.refs_1_, ...), custom_call_target="tpu_custom_call" | custom-call | flops 1048576 | bytes 1048576 | tf_op jit(solution)/shard_map/attend_0_1_4_5/pallas_call | solution.py:294
  18.0 0.0 collective-permute-done.7.refs_3_.refs_9_
  18.1 0.0 collective-permute-done.8.refs_5_.refs_7_
  18.1 2.8 %attend_2_3_6_7.1 = (f32[1024,128]{1,0:T(8,128)S(1)}, f32[1024,256]{1,0:T(8,128)S(1)}, f32[1024,128]{1,0:T(8,128)S(1)}, f32[1024,256]{1,0:T(8,128)S(1)}) custom-call(bf16[64,2048]{1,0:T(8,128)(2,1)S(1)} %get-tuple-element.19.refs_0_, bf16[64,2048]{1,0:T(8,128)(2,1)S(1)} %get-tuple-element.20.refs_1_, ...), custom_call_target="tpu_custom_call" | custom-call | flops 1048576 | bytes 1048576 | tf_op jit(solution)/shard_map/attend_2_3_6_7/pallas_call | solution.py:294
  20.8 0.0 collective-permute-done.5.refs_0_.refs_2_.refs_8_
  20.9 0.3 %collective-permute-start.11 = (bf16[4,64,256]{2,1,0:T(8,128)(2,1)S(1)}, bf16[4,64,256]{2,1,0:T(8,128)(2,1)S(1)}, u32[]{:S(2)}, u32[]{:S(2)}) collective-permute-start(bf16[4,64,256]{2,1,0:T(8,128)(2,1)S(1)} %pack_blocks.9), channel_id=1, source_target_pairs={{0,8},{2,10},{4,12},{6,14},{8,0},{10,2},{12,4},{14,6},{16,24},{18,... | collective-permute-start | bytes 393224 | tf_op jit(solution)/shard_map/ppermute | solution.py:35
  21.8 0.4 %collective-permute-done.11.refs_3_.refs_9_ = bf16[4,64,256]{2,1,0:T(8,128)(2,1)S(1)} collective-permute-done((bf16[4,64,256]{2,1,0:T(8,128)(2,1)S(1)}, bf16[4,64,256]{2,1,0:T(8,128)(2,1)S(1)}, u32[]{:S(2)}, u32[]{:S(2)}) %collective-permute-start.11) | collective-permute-done | bytes 131104 | tf_op jit(solution)/shard_map/ppermute | solution.py:35
  22.3 1.1 %step_logits.1 = f32[1,8]{1,0:T(1,128)S(1)} custom-call(s32[1,8]{1,0:T(1,128)S(1)} %get-tuple-element.33.ends_ref, f32[1,2048]{1,0:T(1,128)S(1)} %get-tuple-element.34.head_ref, s32[1,128]{1,0:T(1,128)S(1)} %broadcast_in_dim.16.refs_4_.lengths_ref, bf16[5,64,256]{2,1,0:T(8,128)(2,1)S(1)} %pack_blocks.7.refs_2_.refs_6_.refs_0_, ...), custom_call_target="tpu_custom_call" | custom-call | flops 163840 | bytes 163840 | tf_op jit(solution)/shard_map/step_logits/pallas_call | solution.py:362
  23.3 1.5 %collective-permute-start.12 = (f32[1,8]{1,0:T(1,128)S(1)}, f32[1,8]{1,0:T(1,128)S(1)}, u32[]{:S(2)}, u32[]{:S(2)}) collective-permute-start(f32[1,8]{1,0:T(1,128)S(1)} %step_logits.1), channel_id=1, source_target_pairs={{0,1},{1,0},{2,3},{3,2},{4,5},{5,4},{6,7},{7,6},{8,9},{9,8},{10,11... | collective-permute-start | bytes 104 | tf_op jit(solution)/shard_map/ppermute | solution.py:35
  24.8 1.8 %attend_8_9.1 = (bf16[64,2048]{1,0:T(8,128)(2,1)}, bf16[64,2048]{1,0:T(8,128)(2,1)}) custom-call(bf16[64,2048]{1,0:T(8,128)(2,1)S(1)} %get-tuple-element.19.refs_0_, bf16[64,2048]{1,0:T(8,128)(2,1)S(1)} %get-tuple-element.20.refs_1_, bf16[4,64,256]{2,1,0:T(8,128)(2,1)S(1)} %collective-permute-done.5.refs_0_.refs_2_.refs_8_, ...), custom_call_target="tpu_custom_call" | custom-call | flops 524288 | bytes 524288 | tf_op jit(solution)/shard_map/attend_8_9/pallas_call | solution.py:294
  26.6 0.3 collective-permute-done.12
  26.9 0.5 %add.3 = f32[1,8]{1,0:T(1,128)} add(f32[1,8]{1,0:T(1,128)S(1)} %step_logits.1, f32[1,8]{1,0:T(1,128)S(1)} %collective-permute-done.12) | non-fusion elementwise | flops 8 | bytes 96 | tf_op jit(solution)/shard_map/add | solution.py:423
  (7 shorter events, 0.1 us)
Async XLA Ops:
  0.6 9.0 %collective-permute-start.2 = (bf16[2,64,256]{2,1,0:T(8,128)(2,1)}, bf16[2,64,256]{2,1,0:T(8,128)(2,1)S(1)}, u32[]{:S(2)}, u32[]{:S(2)}) collective-permute-start(bf16[2,64,256]{2,1,0:T(8,128)(2,1)} %prompt_kv.1), channel_id=1, source_target_pairs={{0,4},{2,6},{4,0},{6,2},{8,12},{10,14},{12,8},{14,10},{16,20},{18,... | collective-permute-start | bytes 196616 | tf_op jit(solution)/shard_map/ppermute | solution.py:35
  6.0 6.6 %collective-permute-start.6 = (bf16[3,64,256]{2,1,0:T(8,128)(2,1)S(1)}, bf16[3,64,256]{2,1,0:T(8,128)(2,1)S(1)}, u32[]{:S(2)}, u32[]{:S(2)}) collective-permute-start(bf16[3,64,256]{2,1,0:T(8,128)(2,1)S(1)} %get-tuple-element.22.refs_1_), channel_id=1, source_target_pairs={{0,16},{2,18},{4,20},{6,22},{8,24},{10,26},{12,28},{14,30},{16,0},... | collective-permute-start | bytes 294920 | tf_op jit(solution)/shard_map/ppermute | solution.py:35
  7.6 5.0 %collective-permute-start.1 = (bf16[2,64,256]{2,1,0:T(8,128)(2,1)S(1)}, bf16[2,64,256]{2,1,0:T(8,128)(2,1)S(1)}, u32[]{:S(2)}, u32[]{:S(2)}) collective-permute-start(bf16[2,64,256]{2,1,0:T(8,128)(2,1)S(1)} %get-tuple-element.21.refs_0_), channel_id=1, source_target_pairs={{0,16},{2,18},{4,20},{6,22},{8,24},{10,26},{12,28},{14,30},{16,0},... | collective-permute-start | bytes 196616 | tf_op jit(solution)/shard_map/ppermute | solution.py:35
  8.1 5.1 %collective-permute-start = (bf16[2,64,256]{2,1,0:T(8,128)(2,1)S(1)}, bf16[2,64,256]{2,1,0:T(8,128)(2,1)S(1)}, u32[]{:S(2)}, u32[]{:S(2)}) collective-permute-start(bf16[2,64,256]{2,1,0:T(8,128)(2,1)S(1)} %get-tuple-element.21.refs_0_), channel_id=1, source_target_pairs={{0,2},{2,0},{4,6},{6,4},{8,10},{10,8},{12,14},{14,12},{16,18},{18,... | collective-permute-start | bytes 196616 | tf_op jit(solution)/shard_map/ppermute | solution.py:35
  9.7 4.3 %collective-permute-start.3 = (bf16[2,64,256]{2,1,0:T(8,128)(2,1)S(1)}, bf16[2,64,256]{2,1,0:T(8,128)(2,1)S(1)}, u32[]{:S(2)}, u32[]{:S(2)}) collective-permute-start(bf16[2,64,256]{2,1,0:T(8,128)(2,1)S(1)} %collective-permute-done.2.refs_0_), channel_id=1, source_target_pairs={{0,2},{2,0},{4,6},{6,4},{8,24},{10,26},{12,28},{14,30},{16,18},{18... | collective-permute-start | bytes 196616 | tf_op jit(solution)/shard_map/ppermute | solution.py:390
  10.1 4.3 %collective-permute-start.4 = (bf16[2,64,256]{2,1,0:T(8,128)(2,1)S(1)}, bf16[2,64,256]{2,1,0:T(8,128)(2,1)S(1)}, u32[]{:S(2)}, u32[]{:S(2)}) collective-permute-start(bf16[2,64,256]{2,1,0:T(8,128)(2,1)S(1)} %collective-permute-done.2.refs_0_), channel_id=1, source_target_pairs={{0,16},{2,18},{4,20},{6,22},{8,10},{10,8},{12,14},{14,12},{16,0},{... | collective-permute-start | bytes 196616 | tf_op jit(solution)/shard_map/ppermute | solution.py:390
  12.6 3.5 %collective-permute-start.9 = (bf16[5,64,256]{2,1,0:T(8,128)(2,1)S(1)}, bf16[5,64,256]{2,1,0:T(8,128)(2,1)S(1)}, u32[]{:S(2)}, u32[]{:S(2)}) collective-permute-start(bf16[5,64,256]{2,1,0:T(8,128)(2,1)S(1)} %pack_blocks.7.refs_2_.refs_6_.refs_0_), channel_id=1, source_target_pairs={{0,8},{2,10},{4,12},{6,14},{8,0},{10,2},{12,4},{14,6},{16,24},{18,... | collective-permute-start | bytes 491528 | tf_op jit(solution)/shard_map/ppermute | solution.py:35
  12.6 5.4 %collective-permute-start.7 = (bf16[5,64,256]{2,1,0:T(8,128)(2,1)S(1)}, bf16[5,64,256]{2,1,0:T(8,128)(2,1)S(1)}, u32[]{:S(2)}, u32[]{:S(2)}) collective-permute-start(bf16[5,64,256]{2,1,0:T(8,128)(2,1)S(1)} %pack_blocks.5.refs_6_.refs_2_.refs_8_), channel_id=1, source_target_pairs={{0,8},{2,10},{4,12},{6,14},{8,0},{10,2},{12,4},{14,6},{16,24},{18,... | collective-permute-start | bytes 491528 | tf_op jit(solution)/shard_map/ppermute | solution.py:35
  13.2 2.9 %collective-permute-start.10 = (bf16[4,64,256]{2,1,0:T(8,128)(2,1)S(1)}, bf16[4,64,256]{2,1,0:T(8,128)(2,1)S(1)}, u32[]{:S(2)}, u32[]{:S(2)}) collective-permute-start(bf16[4,64,256]{2,1,0:T(8,128)(2,1)S(1)} %pack_blocks.8.refs_4_), channel_id=1, source_target_pairs={{0,8},{2,10},{4,12},{6,14},{8,0},{10,2},{12,4},{14,6},{16,24},{18,... | collective-permute-start | bytes 393224 | tf_op jit(solution)/shard_map/ppermute | solution.py:35
  14.4 3.7 %collective-permute-start.8 = (bf16[4,64,256]{2,1,0:T(8,128)(2,1)S(1)}, bf16[4,64,256]{2,1,0:T(8,128)(2,1)S(1)}, u32[]{:S(2)}, u32[]{:S(2)}) collective-permute-start(bf16[4,64,256]{2,1,0:T(8,128)(2,1)S(1)} %pack_blocks.6.refs_4_.refs_6_), channel_id=1, source_target_pairs={{0,8},{2,10},{4,12},{6,14},{8,0},{10,2},{12,4},{14,6},{16,24},{18,... | collective-permute-start | bytes 393224 | tf_op jit(solution)/shard_map/ppermute | solution.py:35
  14.5 6.3 %collective-permute-start.5 = (bf16[4,64,256]{2,1,0:T(8,128)(2,1)S(1)}, bf16[4,64,256]{2,1,0:T(8,128)(2,1)S(1)}, u32[]{:S(2)}, u32[]{:S(2)}) collective-permute-start(bf16[4,64,256]{2,1,0:T(8,128)(2,1)S(1)} %pack_side.1), channel_id=1, source_target_pairs={{0,16},{2,18},{4,20},{6,22},{8,10},{10,8},{12,14},{14,12},{16,0},{... | collective-permute-start | bytes 393224 | tf_op jit(solution)/shard_map/ppermute | solution.py:390
  20.9 1.4 %collective-permute-start.11 = (bf16[4,64,256]{2,1,0:T(8,128)(2,1)S(1)}, bf16[4,64,256]{2,1,0:T(8,128)(2,1)S(1)}, u32[]{:S(2)}, u32[]{:S(2)}) collective-permute-start(bf16[4,64,256]{2,1,0:T(8,128)(2,1)S(1)} %pack_blocks.9), channel_id=1, source_target_pairs={{0,8},{2,10},{4,12},{6,14},{8,0},{10,2},{12,4},{14,6},{16,24},{18,... | collective-permute-start | bytes 393224 | tf_op jit(solution)/shard_map/ppermute | solution.py:35
  23.3 3.5 %collective-permute-start.12 = (f32[1,8]{1,0:T(1,128)S(1)}, f32[1,8]{1,0:T(1,128)S(1)}, u32[]{:S(2)}, u32[]{:S(2)}) collective-permute-start(f32[1,8]{1,0:T(1,128)S(1)} %step_logits.1), channel_id=1, source_target_pairs={{0,1},{1,0},{2,3},{3,2},{4,5},{5,4},{6,7},{7,6},{8,9},{9,8},{10,11... | collective-permute-start | bytes 104 | tf_op jit(solution)/shard_map/ppermute | solution.py:35

commit v7 on v6

--- a/solution.py
+++ b/solution.py
@@ -17,6 +17,7 @@
 VMEM_LIMIT = 28 * 1024 * 1024
 PARAMS = pltpu.CompilerParams(vmem_limit_bytes=VMEM_LIMIT)
 PROMPT_AXES = ("ctx", "cand")
+PAYING = 2
 
 
 def vmem(count):
@@ -55,31 +56,6 @@
     )(*arrays, *after)
 
 
-def pack_side_kernel(even_ref, odd_ref, last_ref, _, out_ref):
-    count = last_ref.shape[0]
-    out_ref[count:] = last_ref[...]
-    odd = lax.rem(lax.axis_index("ctx"), 2)
-
-    @pl.when(odd == 0)
-    def _():
-        out_ref[:count] = even_ref[...]
-
-    @pl.when(odd == 1)
-    def _():
-        out_ref[:count] = odd_ref[...]
-
-
-def packed_side(even, odd, last, after):
-    return pl.pallas_call(
-        pack_side_kernel,
-        out_shape=jax.ShapeDtypeStruct((2 * last.shape[0],) + last.shape[1:], last.dtype),
-        in_specs=vmem(3) + [pl.BlockSpec(memory_space=pl.ANY)],
-        out_specs=vmem(1)[0],
-        compiler_params=PARAMS,
-        name="pack_side",
-    )(even, odd, last, after)
-
-
 def prompt_bits(ctx_size, cand_size):
     core, along, across = cand_size, 1, 2 * cand_size
     early = high_bits(cand_size, 2) + [bit * cand_size for bit in high_bits(ctx_size, 4)]
@@ -89,17 +65,12 @@
 def prompt_owners(ctx_size, cand_size):
     early, along, across, core = prompt_bits(ctx_size, cand_size)
     place = prompt_place(cand_size)
-    near = along + lax.rem(lax.axis_index("ctx"), 2) * (across - along)
-    far = along + across - near
     masks = [0]
     for bit in early[:-1]:
         masks += [mask ^ bit for mask in masks]
-    last = early[-1]
-    both = along + across
-    shifts = [[0], [core], [across], [across + core]]
-    shifts += [[last, along], [core + last, core + along]]
-    shifts += [[last + near, last + far], [core + last + far, core + last + near]]
-    shifts += [[both, both + last], [core + both, core + both + last]]
+    last, both = early[-1], along + across
+    shifts = [[0], [last], [along, across], [both], [last + both], [last + across], [last + along]]
+    shifts += [[core + shift for shift in array] for array in shifts[:4] + [sum(shifts[4:], [])]]
     return [[place ^ mask ^ shift for shift in array for mask in masks] for array in shifts]
 
 
@@ -221,10 +192,12 @@
     take = iter(refs)
     prompt_q, cand_q = next(take), next(take)
     block_refs = [next(take) for _ in arrays]
-    pay_refs = [next(take) for _ in range(4 if masks else 0)]
+    pay_refs = [next(take) for _ in range(PAYING if masks else 0)]
     lengths = next(take) if last else None
     old = None if first else [(next(take), next(take)) for _ in range(2)]
-    outs = refs[-2:] if last else refs[-4:]
+    outs = refs[-6:-4] if last else refs[-4:]
+    halls, sems = refs[-4:-2], refs[-2:]
+    leaving = []
     rows = prompt_q.shape[0]
     cand_rows = cand_q.shape[0]
     owners = prompt_owners(ctx_size, cand_size)
@@ -268,21 +241,35 @@
                     kept = result[index * each : (index + 1) * each]
                     if kind == 0:
                         kept = jnp.where(alive, kept, 0.0)
-                    outs[kind][:, h * HEADDIM : (h + 1) * HEADDIM] = kept.astype(jnp.bfloat16)
-
-
-def phase(sizes, arrays, q_rows, blocks, masks=(), state=None, lengths=None, after=()):
+                    halls[kind][:, h * HEADDIM : (h + 1) * HEADDIM] = kept.astype(jnp.bfloat16)
+                part = slice(heads[0] * HEADDIM, (heads[-1] + 1) * HEADDIM)
+                leaving.append(
+                    pltpu.make_async_copy(
+                        halls[kind].at[:, part],
+                        outs[kind].at[:, part],
+                        sems[kind].at[heads[0] // len(heads)],
+                    )
+                )
+                leaving[-1].start()
+    for copy in leaving:
+        copy.wait()
+
+
+def phase(sizes, arrays, q_rows, blocks, pays=(), masks=(), state=None, lengths=None, after=()):
     prompt_q, cand_q = q_rows
     first, last = state is None, lengths is not None
     operands = [prompt_q, cand_q] + [blocks[index] for index in arrays]
-    operands += blocks[:4] if masks else []
+    operands += pays
     if last:
         operands.append(lengths)
     if not first:
         operands += state
     heads = prompt_q.shape[1] // HEADDIM
+    scratch = []
     if last:
         shapes = [like(cand_q), like(prompt_q)]
+        scratch = [pltpu.VMEM(q.shape, q.dtype) for q in (cand_q, prompt_q)]
+        scratch += [pltpu.SemaphoreType.DMA((heads,))] * 2
     else:
         shapes = []
         for q in (cand_q, prompt_q):
@@ -295,10 +282,11 @@
         functools.partial(phase_kernel, sizes, arrays, masks, first, last),
         out_shape=tuple(shapes),
         in_specs=vmem(len(operands)) + [pl.BlockSpec(memory_space=pl.ANY)] * len(after),
-        out_specs=tuple(vmem(len(shapes))),
+        out_specs=(pl.BlockSpec(memory_space=pl.ANY),) * 2 if last else tuple(vmem(len(shapes))),
+        scratch_shapes=scratch,
         compiler_params=PARAMS,
         cost_estimate=pl.CostEstimate(
-            flops=scores, bytes_accessed=scores, transcendentals=0
+            flops=6 * scores * HEADDIM, bytes_accessed=scores, transcendentals=scores
         ),
         name="attend_" + "_".join(str(i) for i in arrays),
     )(*operands, *after)
@@ -306,9 +294,8 @@
 
 def step_kernel(sizes, masks, ends_ref, head_ref, lengths_ref, *refs):
     ctx_size, cand_size = sizes
-    blocks = refs[:-2]
+    pays, blocks = payloads(refs[:PAYING], len(masks) // PAYING), refs[PAYING:-2]
     logit_ref, kv_ref = refs[-2:]
-    pays = payloads(blocks[:4], len(masks) // 4)
     rows = blocks[0].shape[1]
     own_rows = rows
     free = rows * ctx_size * cand_size
@@ -354,7 +341,7 @@
     logit_ref[...] = jnp.sum(jnp.where(down == right, logits, 0.0), axis=0, keepdims=True)
 
 
-def step_shares(sizes, ends, head, lengths, masks, blocks):
+def step_shares(sizes, ends, head, lengths, pays, masks, blocks):
     ctx_size, cand_size = sizes
     rows, width = blocks[0].shape[1:]
     count = rows * ctx_size * cand_size + rows * ctx_size
@@ -362,15 +349,15 @@
     return pl.pallas_call(
         functools.partial(step_kernel, sizes, masks),
         out_shape=jax.ShapeDtypeStruct(ends.shape, jnp.float32),
-        in_specs=vmem(3 + len(blocks)),
+        in_specs=vmem(3 + len(pays) + len(blocks)),
         out_specs=vmem(1)[0],
         scratch_shapes=[pltpu.VMEM((2, count, width), blocks[0].dtype)],
         compiler_params=PARAMS,
         cost_estimate=pl.CostEstimate(
-            flops=scores, bytes_accessed=scores, transcendentals=0
+            flops=6 * scores * HEADDIM, bytes_accessed=scores, transcendentals=scores
         ),
         name="step_logits",
-    )(ends, head, lengths, *blocks)
+    )(ends, head, lengths, *pays, *blocks)
 
 
 def per_device(ctx_size, cand_size, prompt_q, prompt_kv, cand_q, cand_kv, cand_lengths, step_ends, reward_head):
@@ -401,23 +388,22 @@
             pay = packed(pay, moved(pay, bit))
             pay_masks += [mask ^ bit // cand_size for mask in pay_masks]
     beyond = moved(sent, early[-1])
-    beside = moved(held, along)
-    opposite = moved(held, across)
-    here = packed(held, pay)
-    facing = packed(opposite, moved(pay, across))
-    one = shared_out(beyond, along, across)
-    two = shared_out(beyond, across, along)
-    far = shared_out(packed_side(beside, opposite, one, two), across, along)
-    pair = packed(beyond, beside)
-    sides = packed(one, two)
-    blocks = [here, moved(here, core), facing, moved(facing, core)]
-    blocks += [pair, moved(pair, core), sides, moved(sides, core), far]
-    masks = [mask ^ shift for shift in (0, 1, 2, 3) for mask in pay_masks]
-    state = phase(sizes, [0, 1, 4, 5], q_rows, blocks, after=[facing])
-    state = phase(sizes, [2, 3, 6, 7], q_rows, blocks, masks=masks, state=state)
-    blocks.append(moved(packed(far, after=state[:1]), core))
-    step_logits = step_shares(sizes, ends, head, lengths, masks, blocks)
-    cand_out, prompt_out = phase(sizes, [8, 9], q_rows, blocks, state=state, lengths=lengths)
+    ways = along, across, along + across
+    near = packed(moved(held, along), moved(held, across))
+    facing = moved(held, along + across)
+    past = [moved(beyond, bit) for bit in (along + across, across, along)]
+    pay_across = moved(pay, across)
+    both_pays = packed(pay, pay_across)
+    pays = [both_pays, moved(both_pays, core)]
+    masks = [mask ^ shift for shift in (0, 2, 1, 3) for mask in pay_masks]
+    blocks = [held, beyond, near, facing] + past
+    blocks += [moved(block, core) for block in blocks[:4]]
+    state = phase(sizes, [2, 3, 4], q_rows, blocks)
+    state = phase(sizes, [0, 1, 7, 8], q_rows, blocks, state=state)
+    blocks.append(moved(packed(*past, after=state[:1]), core))
+    state = phase(sizes, [5, 6], q_rows, blocks, pays=pays, masks=masks, state=state)
+    step_logits = step_shares(sizes, ends, head, lengths, pays, masks, blocks)
+    cand_out, prompt_out = phase(sizes, [9, 10, 11], q_rows, blocks, state=state, lengths=lengths)
     tp_size = lax.axis_size("tp")
     for bit in high_bits(tp_size, 1):
         step_logits = step_logits + flipped(step_logits, "tp", tp_size, bit)

time: 27.5 us -> 29.5 us (1.073)
  starting transfers between devices: 13.9 us -> 15.8 us
  waiting for transfers between devices: 2.75 us -> 2.26 us
  Pallas kernels: 8.87 us -> 9.33 us
    ppermute x10 -> x15, starting transfers between devices: 10.3 us -> 15.8 us  [flipped(): return lax.ppermute(block, axes, [(i, i ^ bit) for i in range(size)])]
    ppermute x3 -> x0, starting transfers between devices: 3.55 us -> none  [shared_out(): lax.ppermute(block, PROMPT_AXES, [(i, i ^ (odd if i & core else even)) fo...]
    ppermute x3 -> x0, waiting for transfers between devices: 1.07 us -> none  [shared_out(): lax.ppermute(block, PROMPT_AXES, [(i, i ^ (odd if i & core else even)) fo...]
    ppermute x10 -> x15, waiting for transfers between devices: 1.68 us -> 2.26 us  [flipped(): return lax.ppermute(block, axes, [(i, i ^ bit) for i in range(size)])]
    pallas_call x3 -> x4, Pallas kernels: 6.5 us -> 6.99 us  [phase(): pl.pallas_call(functools.partial(phase_kernel, sizes, arrays, masks, firs...]
  transfers between devices with their start and end apart: 13 -> 15, of which waited for: 5 -> 2; matrix products, arithmetic and copies ran while one was open for 0% -> 0% of each run, Pallas kernels for 28% -> 28%
where the time goes in v7:
time: 29.5 us; the launch traced here: 29.3 us
  starting transfers between devices  15.8 us (54%)
  Pallas kernels  9.33 us (32%)
  waiting for transfers between devices  2.26 us (8%)
  between operations  1.43 us (5%)
  other arithmetic  0.51 us (2%)
    ppermute x15, starting transfers between devices, flipped(): return lax.ppermute(block, axes, [(i, i ^ bit) for i in range(size)])  15.8 us
    pallas_call x4, Pallas kernels, phase(): pl.pallas_call(functools.partial(phase_kernel, sizes, arrays, masks, firs...  6.99 us
    ppermute x15, waiting for transfers between devices, flipped(): return lax.ppermute(block, axes, [(i, i ^ bit) for i in range(size)])  2.26 us
    pallas_call x1, Pallas kernels, staged(): pl.pallas_call(stage_kernel, out_shape=(like(prompt_q), like(cand_q), lik...  1.24 us
    pallas_call x1, Pallas kernels, step_shares(): pl.pallas_call(functools.partial(step_kernel, sizes, masks), out_shape=ja...  1.06 us
  transfers between devices with their start and end apart: 15, of which 2 were waited for; matrix products, arithmetic and copies ran while one was open for 0% of the time, Pallas kernels for 28%

profile of v7, /device:TPU:0, one launch (start us, length us, event | category | flops | bytes accessed | tf_op | source)
XLA Modules:
  0.0 29.3 jit_solution(3021200423383340395)
XLA Ops:
  0.6 4.1 %collective-permute-start.5 = (bf16[2,64,256]{2,1,0:T(8,128)(2,1)}, bf16[2,64,256]{2,1,0:T(8,128)(2,1)S(1)}, u32[]{:S(2)}, u32[]{:S(2)}) collective-permute-start(bf16[2,64,256]{2,1,0:T(8,128)(2,1)} %prompt_kv.1), channel_id=1, source_target_pairs={{0,4},{2,6},{4,0},{6,2},{8,12},{10,14},{12,8},{14,10},{16,20},{18,... | collective-permute-start | bytes 196616 | tf_op jit(solution)/shard_map/ppermute | solution.py:36
  4.7 1.2 %stage_operands.1 = (bf16[64,2048]{1,0:T(8,128)(2,1)S(1)}, bf16[64,2048]{1,0:T(8,128)(2,1)S(1)}, bf16[2,64,256]{2,1,0:T(8,128)(2,1)S(1)}, bf16[3,64,256]{2,1,0:T...) custom-call(bf16[64,2048]{1,0:T(8,128)(2,1)} %prompt_q.1, bf16[64,2048]{1,0:T(8,128)(2,1)} %bitcast.6, ...), custom_call_target="tpu_custom_call" | custom-call | tf_op jit(solution)/shard_map/stage_operands/pallas_call | solution.py:115
  6.0 1.6 %collective-permute-start.12 = (bf16[3,64,256]{2,1,0:T(8,128)(2,1)S(1)}, bf16[3,64,256]{2,1,0:T(8,128)(2,1)S(1)}, u32[]{:S(2)}, u32[]{:S(2)}) collective-permute-start(bf16[3,64,256]{2,1,0:T(8,128)(2,1)S(1)} %get-tuple-element.31.refs_0_), channel_id=1, source_target_pairs={{0,16},{2,18},{4,20},{6,22},{8,24},{10,26},{12,28},{14,30},{16,0},... | collective-permute-start | bytes 294920 | tf_op jit(solution)/shard_map/ppermute | solution.py:36
  7.6 1.6 %collective-permute-start = (bf16[2,64,256]{2,1,0:T(8,128)(2,1)S(1)}, bf16[2,64,256]{2,1,0:T(8,128)(2,1)S(1)}, u32[]{:S(2)}, u32[]{:S(2)}) collective-permute-start(bf16[2,64,256]{2,1,0:T(8,128)(2,1)S(1)} %get-tuple-element.25.refs_2_), channel_id=1, source_target_pairs={{0,2},{2,0},{4,6},{6,4},{8,10},{10,8},{12,14},{14,12},{16,18},{18,... | collective-permute-start | bytes 196616 | tf_op jit(solution)/shard_map/ppermute | solution.py:36
  9.1 0.5 %collective-permute-start.1 = (bf16[2,64,256]{2,1,0:T(8,128)(2,1)S(1)}, bf16[2,64,256]{2,1,0:T(8,128)(2,1)S(1)}, u32[]{:S(2)}, u32[]{:S(2)}) collective-permute-start(bf16[2,64,256]{2,1,0:T(8,128)(2,1)S(1)} %get-tuple-element.25.refs_2_), channel_id=1, source_target_pairs={{0,16},{2,18},{4,20},{6,22},{8,24},{10,26},{12,28},{14,30},{16,0},... | collective-permute-start | bytes 196616 | tf_op jit(solution)/shard_map/ppermute | solution.py:36
  9.7 1.4 %collective-permute-start.3 = (bf16[2,64,256]{2,1,0:T(8,128)(2,1)S(1)}, bf16[2,64,256]{2,1,0:T(8,128)(2,1)S(1)}, u32[]{:S(2)}, u32[]{:S(2)}) collective-permute-start(bf16[2,64,256]{2,1,0:T(8,128)(2,1)S(1)} %get-tuple-element.25.refs_2_), channel_id=1, source_target_pairs={{0,18},{2,16},{4,22},{6,20},{8,26},{10,24},{12,30},{14,28},{16,2},... | collective-permute-start | bytes 196616 | tf_op jit(solution)/shard_map/ppermute | solution.py:36
  11.1 0.0 collective-permute-done.5.refs_3_
  11.1 1.5 %collective-permute-start.6 = (bf16[2,64,256]{2,1,0:T(8,128)(2,1)S(1)}, bf16[2,64,256]{2,1,0:T(8,128)(2,1)S(1)}, u32[]{:S(2)}, u32[]{:S(2)}) collective-permute-start(bf16[2,64,256]{2,1,0:T(8,128)(2,1)S(1)} %collective-permute-done.5.refs_3_), channel_id=1, source_target_pairs={{0,18},{2,16},{4,22},{6,20},{8,26},{10,24},{12,30},{14,28},{16,2},... | collective-permute-start | bytes 196616 | tf_op jit(solution)/shard_map/ppermute | solution.py:36
  12.6 0.0 collective-permute-done.refs_0_
  12.6 0.0 collective-permute-start.9
  12.6 1.5 %collective-permute-done.1.refs_1_ = bf16[2,64,256]{2,1,0:T(8,128)(2,1)S(1)} collective-permute-done((bf16[2,64,256]{2,1,0:T(8,128)(2,1)S(1)}, bf16[2,64,256]{2,1,0:T(8,128)(2,1)S(1)}, u32[]{:S(2)}, u32[]{:S(2)}) %collective-permute-start.1) | collective-permute-done | bytes 65568 | tf_op jit(solution)/shard_map/ppermute | solution.py:36
  14.1 0.0 collective-permute-start.10
  14.1 0.0 collective-permute-done.12.refs_1_
  14.1 1.3 %collective-permute-start.7 = (bf16[2,64,256]{2,1,0:T(8,128)(2,1)S(1)}, bf16[2,64,256]{2,1,0:T(8,128)(2,1)S(1)}, u32[]{:S(2)}, u32[]{:S(2)}) collective-permute-start(bf16[2,64,256]{2,1,0:T(8,128)(2,1)S(1)} %collective-permute-done.5.refs_3_), channel_id=1, source_target_pairs={{0,16},{2,18},{4,20},{6,22},{8,24},{10,26},{12,28},{14,30},{16,0},... | collective-permute-start | bytes 196616 | tf_op jit(solution)/shard_map/ppermute | solution.py:36
  15.4 0.0 collective-permute-done.3.refs_3_.refs_5_
  15.4 1.7 %collective-permute-start.8 = (bf16[2,64,256]{2,1,0:T(8,128)(2,1)S(1)}, bf16[2,64,256]{2,1,0:T(8,128)(2,1)S(1)}, u32[]{:S(2)}, u32[]{:S(2)}) collective-permute-start(bf16[2,64,256]{2,1,0:T(8,128)(2,1)S(1)} %collective-permute-done.5.refs_3_), channel_id=1, source_target_pairs={{0,2},{2,0},{4,6},{6,4},{8,10},{10,8},{12,14},{14,12},{16,18},{18,... | collective-permute-start | bytes 196616 | tf_op jit(solution)/shard_map/ppermute | solution.py:36
  17.1 0.0 collective-permute-done.6.refs_4_.refs_0_.refs_6_
  17.1 0.0 collective-permute-start.13
  17.1 0.9 %attend_2_3_4.1 = (f32[1024,128]{1,0:T(8,128)S(1)}, f32[1024,256]{1,0:T(8,128)S(1)}, f32[1024,128]{1,0:T(8,128)S(1)}, f32[1024,256]{1,0:T(8,128)S(1)}) custom-call(bf16[64,2048]{1,0:T(8,128)(2,1)S(1)} %get-tuple-element.23.refs_0_, bf16[64,2048]{1,0:T(8,128)(2,1)S(1)} %get-tuple-element.24.refs_1_, bf16[4,64,256]{2,1,0:T(8,128)(2,1)S(1)} %pack_blocks.3.refs_2_.refs_4_, ...), custom_call_target="tpu_custom_call" | custom-call | flops 402653184 | bytes 524288 | tf_op jit(solution)/shard_map/attend_2_3_4/pallas_call | solution.py:281
  18.0 0.0 collective-permute-done.9.refs_4_.refs_9_
  18.0 0.0 collective-permute-done.10.refs_5_.refs_10_
  18.0 1.0 %attend_0_1_7_8.1 = (f32[1024,128]{1,0:T(8,128)S(1)}, f32[1024,256]{1,0:T(8,128)S(1)}, f32[1024,128]{1,0:T(8,128)S(1)}, f32[1024,256]{1,0:T(8,128)S(1)}) custom-call(bf16[64,2048]{1,0:T(8,128)(2,1)S(1)} %get-tuple-element.23.refs_0_, bf16[64,2048]{1,0:T(8,128)(2,1)S(1)} %get-tuple-element.24.refs_1_, bf16[2,64,256]{2,1,0:T(8,128)(2,1)S(1)} %get-tuple-element.25.refs_2_, ...), custom_call_target="tpu_custom_call" | custom-call | flops 402653184 | bytes 524288 | tf_op jit(solution)/shard_map/attend_0_1_7_8/pallas_call | solution.py:281
  19.1 0.0 collective-permute-done.7.refs_1_.refs_2_.refs_7_
  19.1 0.7 %collective-permute-done.8.refs_2_.refs_3_.refs_8_ = bf16[2,64,256]{2,1,0:T(8,128)(2,1)S(1)} collective-permute-done((bf16[2,64,256]{2,1,0:T(8,128)(2,1)S(1)}, bf16[2,64,256]{2,1,0:T(8,128)(2,1)S(1)}, u32[]{:S(2)}, u32[]{:S(2)}) %collective-permute-start.8) | collective-permute-done | bytes 65568 | tf_op jit(solution)/shard_map/ppermute | solution.py:36
  19.8 0.1 collective-permute-start.11
  19.9 0.5 %collective-permute-start.2 = (bf16[4,64,256]{2,1,0:T(8,128)(2,1)S(1)}, bf16[4,64,256]{2,1,0:T(8,128)(2,1)S(1)}, u32[]{:S(2)}, u32[]{:S(2)}) collective-permute-start(bf16[4,64,256]{2,1,0:T(8,128)(2,1)S(1)} %pack_blocks.3.refs_2_.refs_4_), channel_id=1, source_target_pairs={{0,8},{2,10},{4,12},{6,14},{8,0},{10,2},{12,4},{14,6},{16,24},{18,... | collective-permute-start | bytes 393224 | tf_op jit(solution)/shard_map/ppermute | solution.py:36
  20.4 0.1 collective-permute-start.4
  21.1 0.0 collective-permute-done.13.refs_5_.refs_1_
  21.1 2.1 %attend_5_6.1 = (f32[1024,128]{1,0:T(8,128)S(1)}, f32[1024,256]{1,0:T(8,128)S(1)}, f32[1024,128]{1,0:T(8,128)S(1)}, f32[1024,256]{1,0:T(8,128)S(1)}) custom-call(bf16[64,2048]{1,0:T(8,128)(2,1)S(1)} %get-tuple-element.23.refs_0_, bf16[64,2048]{1,0:T(8,128)(2,1)S(1)} %get-tuple-element.24.refs_1_, ...), custom_call_target="tpu_custom_call" | custom-call | flops 201326592 | bytes 262144 | tf_op jit(solution)/shard_map/attend_5_6/pallas_call | solution.py:281
  23.2 0.0 collective-permute-done.4.refs_3_.refs_12_
  23.2 0.0 collective-permute-done.2.refs_2_.refs_11_
  23.2 0.0 collective-permute-done.11.refs_4_.refs_13_
  23.2 1.1 %step_logits.1 = f32[1,8]{1,0:T(1,128)S(1)} custom-call(s32[1,8]{1,0:T(1,128)S(1)} %get-tuple-element.41.ends_ref, f32[1,2048]{1,0:T(1,128)S(1)} %get-tuple-element.42.head_ref, s32[1,128]{1,0:T(1,128)S(1)} %broadcast_in_dim.16.refs_5_.lengths_ref, bf16[6,64,256]{2,1,0:T(8,128)(2,1)S(1)} %pack_blocks.5.refs_4_.refs_0_, ...), custom_call_target="tpu_custom_call" | custom-call | flops 125829120 | bytes 163840 | tf_op jit(solution)/shard_map/step_logits/pallas_call | solution.py:349
  24.3 1.5 %collective-permute-start.14 = (f32[1,8]{1,0:T(1,128)S(1)}, f32[1,8]{1,0:T(1,128)S(1)}, u32[]{:S(2)}, u32[]{:S(2)}) collective-permute-start(f32[1,8]{1,0:T(1,128)S(1)} %step_logits.1), channel_id=1, source_target_pairs={{0,1},{1,0},{2,3},{3,2},{4,5},{5,4},{6,7},{7,6},{8,9},{9,8},{10,11... | collective-permute-start | bytes 104 | tf_op jit(solution)/shard_map/ppermute | solution.py:36
  25.8 3.0 %attend_9_10_11.1 = (bf16[64,2048]{1,0:T(8,128)(2,1)}, bf16[64,2048]{1,0:T(8,128)(2,1)}) custom-call(bf16[64,2048]{1,0:T(8,128)(2,1)S(1)} %get-tuple-element.23.refs_0_, bf16[64,2048]{1,0:T(8,128)(2,1)S(1)} %get-tuple-element.24.refs_1_, bf16[4,64,256]{2,1,0:T(8,128)(2,1)S(1)} %collective-permute-done.2.refs_2_.refs_11_, ...), custom_call_target="tpu_custom_call" | custom-call | flops 603979776 | bytes 786432 | tf_op jit(solution)/shard_map/attend_9_10_11/pallas_call | solution.py:281
  28.8 0.0 collective-permute-done.14
  28.8 0.5 %add.3 = f32[1,8]{1,0:T(1,128)} add(f32[1,8]{1,0:T(1,128)S(1)} %step_logits.1, f32[1,8]{1,0:T(1,128)S(1)} %collective-permute-done.14) | non-fusion elementwise | flops 8 | bytes 96 | tf_op jit(solution)/shard_map/add | solution.py:409
  (4 shorter events, 0.0 us)
Async XLA Ops:
  0.6 10.4 %collective-permute-start.5 = (bf16[2,64,256]{2,1,0:T(8,128)(2,1)}, bf16[2,64,256]{2,1,0:T(8,128)(2,1)S(1)}, u32[]{:S(2)}, u32[]{:S(2)}) collective-permute-start(bf16[2,64,256]{2,1,0:T(8,128)(2,1)} %prompt_kv.1), channel_id=1, source_target_pairs={{0,4},{2,6},{4,0},{6,2},{8,12},{10,14},{12,8},{14,10},{16,20},{18,... | collective-permute-start | bytes 196616 | tf_op jit(solution)/shard_map/ppermute | solution.py:36
  6.0 8.2 %collective-permute-start.12 = (bf16[3,64,256]{2,1,0:T(8,128)(2,1)S(1)}, bf16[3,64,256]{2,1,0:T(8,128)(2,1)S(1)}, u32[]{:S(2)}, u32[]{:S(2)}) collective-permute-start(bf16[3,64,256]{2,1,0:T(8,128)(2,1)S(1)} %get-tuple-element.31.refs_0_), channel_id=1, source_target_pairs={{0,16},{2,18},{4,20},{6,22},{8,24},{10,26},{12,28},{14,30},{16,0},... | collective-permute-start | bytes 294920 | tf_op jit(solution)/shard_map/ppermute | solution.py:36
  7.6 5.0 %collective-permute-start = (bf16[2,64,256]{2,1,0:T(8,128)(2,1)S(1)}, bf16[2,64,256]{2,1,0:T(8,128)(2,1)S(1)}, u32[]{:S(2)}, u32[]{:S(2)}) collective-permute-start(bf16[2,64,256]{2,1,0:T(8,128)(2,1)S(1)} %get-tuple-element.25.refs_2_), channel_id=1, source_target_pairs={{0,2},{2,0},{4,6},{6,4},{8,10},{10,8},{12,14},{14,12},{16,18},{18,... | collective-permute-start | bytes 196616 | tf_op jit(solution)/shard_map/ppermute | solution.py:36
  9.1 5.0 %collective-permute-start.1 = (bf16[2,64,256]{2,1,0:T(8,128)(2,1)S(1)}, bf16[2,64,256]{2,1,0:T(8,128)(2,1)S(1)}, u32[]{:S(2)}, u32[]{:S(2)}) collective-permute-start(bf16[2,64,256]{2,1,0:T(8,128)(2,1)S(1)} %get-tuple-element.25.refs_2_), channel_id=1, source_target_pairs={{0,16},{2,18},{4,20},{6,22},{8,24},{10,26},{12,28},{14,30},{16,0},... | collective-permute-start | bytes 196616 | tf_op jit(solution)/shard_map/ppermute | solution.py:36
  9.7 5.8 %collective-permute-start.3 = (bf16[2,64,256]{2,1,0:T(8,128)(2,1)S(1)}, bf16[2,64,256]{2,1,0:T(8,128)(2,1)S(1)}, u32[]{:S(2)}, u32[]{:S(2)}) collective-permute-start(bf16[2,64,256]{2,1,0:T(8,128)(2,1)S(1)} %get-tuple-element.25.refs_2_), channel_id=1, source_target_pairs={{0,18},{2,16},{4,22},{6,20},{8,26},{10,24},{12,30},{14,28},{16,2},... | collective-permute-start | bytes 196616 | tf_op jit(solution)/shard_map/ppermute | solution.py:36
  11.1 6.0 %collective-permute-start.6 = (bf16[2,64,256]{2,1,0:T(8,128)(2,1)S(1)}, bf16[2,64,256]{2,1,0:T(8,128)(2,1)S(1)}, u32[]{:S(2)}, u32[]{:S(2)}) collective-permute-start(bf16[2,64,256]{2,1,0:T(8,128)(2,1)S(1)} %collective-permute-done.5.refs_3_), channel_id=1, source_target_pairs={{0,18},{2,16},{4,22},{6,20},{8,26},{10,24},{12,30},{14,28},{16,2},... | collective-permute-start | bytes 196616 | tf_op jit(solution)/shard_map/ppermute | solution.py:36
  12.6 5.4 %collective-permute-start.9 = (bf16[2,64,256]{2,1,0:T(8,128)(2,1)S(1)}, bf16[2,64,256]{2,1,0:T(8,128)(2,1)S(1)}, u32[]{:S(2)}, u32[]{:S(2)}) collective-permute-start(bf16[2,64,256]{2,1,0:T(8,128)(2,1)S(1)} %get-tuple-element.25.refs_2_), channel_id=1, source_target_pairs={{0,8},{2,10},{4,12},{6,14},{8,0},{10,2},{12,4},{14,6},{16,24},{18,... | collective-permute-start | bytes 196616 | tf_op jit(solution)/shard_map/ppermute | solution.py:36
  14.1 3.9 %collective-permute-start.10 = (bf16[2,64,256]{2,1,0:T(8,128)(2,1)S(1)}, bf16[2,64,256]{2,1,0:T(8,128)(2,1)S(1)}, u32[]{:S(2)}, u32[]{:S(2)}) collective-permute-start(bf16[2,64,256]{2,1,0:T(8,128)(2,1)S(1)} %collective-permute-done.5.refs_3_), channel_id=1, source_target_pairs={{0,8},{2,10},{4,12},{6,14},{8,0},{10,2},{12,4},{14,6},{16,24},{18,... | collective-permute-start | bytes 196616 | tf_op jit(solution)/shard_map/ppermute | solution.py:36
  14.1 4.9 %collective-permute-start.7 = (bf16[2,64,256]{2,1,0:T(8,128)(2,1)S(1)}, bf16[2,64,256]{2,1,0:T(8,128)(2,1)S(1)}, u32[]{:S(2)}, u32[]{:S(2)}) collective-permute-start(bf16[2,64,256]{2,1,0:T(8,128)(2,1)S(1)} %collective-permute-done.5.refs_3_), channel_id=1, source_target_pairs={{0,16},{2,18},{4,20},{6,22},{8,24},{10,26},{12,28},{14,30},{16,0},... | collective-permute-start | bytes 196616 | tf_op jit(solution)/shard_map/ppermute | solution.py:36
  15.4 4.3 %collective-permute-start.8 = (bf16[2,64,256]{2,1,0:T(8,128)(2,1)S(1)}, bf16[2,64,256]{2,1,0:T(8,128)(2,1)S(1)}, u32[]{:S(2)}, u32[]{:S(2)}) collective-permute-start(bf16[2,64,256]{2,1,0:T(8,128)(2,1)S(1)} %collective-permute-done.5.refs_3_), channel_id=1, source_target_pairs={{0,2},{2,0},{4,6},{6,4},{8,10},{10,8},{12,14},{14,12},{16,18},{18,... | collective-permute-start | bytes 196616 | tf_op jit(solution)/shard_map/ppermute | solution.py:36
  17.1 4.0 %collective-permute-start.13 = (bf16[6,64,256]{2,1,0:T(8,128)(2,1)S(1)}, bf16[6,64,256]{2,1,0:T(8,128)(2,1)S(1)}, u32[]{:S(2)}, u32[]{:S(2)}) collective-permute-start(bf16[6,64,256]{2,1,0:T(8,128)(2,1)S(1)} %pack_blocks.5.refs_4_.refs_0_), channel_id=1, source_target_pairs={{0,8},{2,10},{4,12},{6,14},{8,0},{10,2},{12,4},{14,6},{16,24},{18,... | collective-permute-start | bytes 589832 | tf_op jit(solution)/shard_map/ppermute | solution.py:36
  19.8 3.4 %collective-permute-start.11 = (bf16[6,64,256]{2,1,0:T(8,128)(2,1)S(1)}, bf16[6,64,256]{2,1,0:T(8,128)(2,1)S(1)}, u32[]{:S(2)}, u32[]{:S(2)}) collective-permute-start(bf16[6,64,256]{2,1,0:T(8,128)(2,1)S(1)} %pack_blocks.4), channel_id=1, source_target_pairs={{0,8},{2,10},{4,12},{6,14},{8,0},{10,2},{12,4},{14,6},{16,24},{18,... | collective-permute-start | bytes 589832 | tf_op jit(solution)/shard_map/ppermute | solution.py:36
  19.9 3.3 %collective-permute-start.2 = (bf16[4,64,256]{2,1,0:T(8,128)(2,1)S(1)}, bf16[4,64,256]{2,1,0:T(8,128)(2,1)S(1)}, u32[]{:S(2)}, u32[]{:S(2)}) collective-permute-start(bf16[4,64,256]{2,1,0:T(8,128)(2,1)S(1)} %pack_blocks.3.refs_2_.refs_4_), channel_id=1, source_target_pairs={{0,8},{2,10},{4,12},{6,14},{8,0},{10,2},{12,4},{14,6},{16,24},{18,... | collective-permute-start | bytes 393224 | tf_op jit(solution)/shard_map/ppermute | solution.py:36
  20.4 2.8 %collective-permute-start.4 = (bf16[2,64,256]{2,1,0:T(8,128)(2,1)S(1)}, bf16[2,64,256]{2,1,0:T(8,128)(2,1)S(1)}, u32[]{:S(2)}, u32[]{:S(2)}) collective-permute-start(bf16[2,64,256]{2,1,0:T(8,128)(2,1)S(1)} %collective-permute-done.3.refs_3_.refs_5_), channel_id=1, source_target_pairs={{0,8},{2,10},{4,12},{6,14},{8,0},{10,2},{12,4},{14,6},{16,24},{18,... | collective-permute-start | bytes 196616 | tf_op jit(solution)/shard_map/ppermute | solution.py:36
  24.3 4.5 %collective-permute-start.14 = (f32[1,8]{1,0:T(1,128)S(1)}, f32[1,8]{1,0:T(1,128)S(1)}, u32[]{:S(2)}, u32[]{:S(2)}) collective-permute-start(f32[1,8]{1,0:T(1,128)S(1)} %step_logits.1), channel_id=1, source_target_pairs={{0,1},{1,0},{2,3},{3,2},{4,5},{5,4},{6,7},{7,6},{8,9},{9,8},{10,11... | collective-permute-start | bytes 104 | tf_op jit(solution)/shard_map/ppermute | solution.py:36

commit v8 on v5

--- a/solution.py
+++ b/solution.py
@@ -82,17 +82,16 @@
     return blocks
 
 
-def stage_kernel(length_ref, prompt_q, cand_q, prompt_kv, cand_kv, ends, head, *refs):
-    q_out, cand_out, kv_out, pay_out, ends_out, head_out, length_out, length_here, sems = refs
+def stage_kernel(prompt_q, cand_q, prompt_kv, cand_kv, ends, head, *refs):
+    q_out, cand_out, own_out, pay_out, ends_out, head_out, sems = refs
     steps = ends.shape[1]
     pairs = [
         (cand_q, cand_out),
         (ends, ends_out),
+        (prompt_kv, own_out),
         (cand_kv, pay_out.at[0:2]),
-        (prompt_kv, kv_out),
         (prompt_q, q_out),
         (head, head_out),
-        (length_ref, length_here),
     ]
     copies = [pltpu.make_async_copy(a, b, sems.at[i]) for i, (a, b) in enumerate(pairs)]
     for copy in copies:
@@ -109,7 +108,6 @@
     pay_out[2] = jnp.concatenate(pieces, axis=0).astype(jnp.bfloat16)
     for copy in copies[2:]:
         copy.wait()
-    length_out[...] = jnp.full(length_out.shape, length_here[0], jnp.int32)
 
 
 def column_of(row):
@@ -119,20 +117,18 @@
     return jnp.sum(jnp.where(down == right, row, 0), axis=1, keepdims=True)
 
 
-def staged(length, prompt_q, cand_q, prompt_kv, cand_kv, ends, head):
+def staged(prompt_q, cand_q, prompt_kv, cand_kv, ends, head):
     arrays = (prompt_q, cand_q, prompt_kv, cand_kv, ends, head)
-    payload = jax.ShapeDtypeStruct((3,) + cand_kv.shape[1:], cand_kv.dtype)
-    lengths = jax.ShapeDtypeStruct((1, HEADDIM), jnp.int32)
+    pay = jax.ShapeDtypeStruct((3,) + cand_kv.shape[1:], cand_kv.dtype)
     return pl.pallas_call(
         stage_kernel,
-        out_shape=(like(prompt_q), like(cand_q), like(prompt_kv), payload, like(ends), like(head), lengths),
-        in_specs=[pl.BlockSpec(memory_space=pl.ANY)]
-        + [pl.BlockSpec(memory_space=pltpu.HBM)] * len(arrays),
-        out_specs=tuple(vmem(7)),
-        scratch_shapes=[pltpu.SMEM((1,), jnp.int32), pltpu.SemaphoreType.DMA((len(arrays) + 1,))],
+        out_shape=(like(prompt_q), like(cand_q), like(prompt_kv), pay, like(ends), like(head)),
+        in_specs=[pl.BlockSpec(memory_space=pltpu.HBM)] * len(arrays),
+        out_specs=tuple(vmem(6)),
+        scratch_shapes=[pltpu.SemaphoreType.DMA((len(arrays),))],
         compiler_params=PARAMS,
         name="stage_operands",
-    )(length, *(pltpu.with_memory_space_constraint(a, pltpu.HBM) for a in arrays))
+    )(*(pltpu.with_memory_space_constraint(a, pltpu.HBM) for a in arrays))
 
 
 def tiles(q_ref, head):
@@ -286,38 +282,66 @@
     )(*operands, *after)
 
 
-def step_kernel(sizes, masks, ends_ref, head_ref, lengths_ref, *refs):
-    ctx_size, cand_size = sizes
-    pays, blocks = refs[: len(masks)], refs[len(masks) : -2]
-    logit_ref, kv_ref = refs[-2:]
-    rows = blocks[0].shape[2]
-    own_rows = pays[0].shape[1]
-    free = rows * ctx_size * cand_size
-    place = lax.axis_index("ctx")
-    for ref, owners in zip(blocks, prompt_owners(ctx_size, cand_size)):
-        for index, owner in enumerate(owners):
+def placed_blocks(sizes, arrays, refs, kv_ref):
+    owners = prompt_owners(*sizes)
+    for ref, array in zip(refs, arrays):
+        rows = ref.shape[2]
+        for index, owner in enumerate(owners[array]):
             at = pl.ds(pl.multiple_of(owner * rows, rows), rows)
             kv_ref[0, at, :] = ref[index, 0]
             kv_ref[1, at, :] = ref[index, 1]
-    picked = jnp.zeros(pays[0].shape[1:], jnp.float32)
+
+
+def arrange_kernel(sizes, arrays, masks, *refs):
+    pays, blocks = refs[: len(masks)], refs[len(masks) : -2]
+    kv_ref, query_ref = refs[-2:]
+    placed_blocks(sizes, arrays, blocks, kv_ref)
+    rows, width = pays[0].shape[1:]
+    free = kv_ref.shape[1] - rows * len(masks)
+    picked = jnp.zeros((rows, width), jnp.float32)
     for ref, mask in zip(pays, masks):
-        at = pl.ds(pl.multiple_of(free + (place ^ mask) * own_rows, own_rows), own_rows)
+        at = pl.ds(pl.multiple_of(free + (lax.axis_index("ctx") ^ mask) * rows, rows), rows)
         kv_ref[0, at, :] = ref[0]
         kv_ref[1, at, :] = ref[1]
         picked += ref[2].astype(jnp.float32)
+    heads = query_ref.shape[0]
+    steps = rows * width // (heads * HEADDIM)
+    for head in range(heads):
+        group, lane = divmod(head * HEADDIM, width)
+        query_ref[head] = picked[group * steps : (group + 1) * steps, lane : lane + HEADDIM]
+
+
+def arranged(sizes, arrays, heads, steps, pays, blocks):
+    rows, width = pays[0][0].shape[1:]
+    count = rows * sizes[0] * (sizes[1] + 1)
+    return pl.pallas_call(
+        functools.partial(arrange_kernel, sizes, arrays, [mask for _, mask in pays]),
+        out_shape=(
+            jax.ShapeDtypeStruct((2, count, width), pays[0][0].dtype),
+            jax.ShapeDtypeStruct((heads, steps, HEADDIM), jnp.float32),
+        ),
+        in_specs=vmem(len(pays) + len(arrays)),
+        out_specs=tuple(vmem(2)),
+        compiler_params=PARAMS,
+        name="arrange_blocks",
+    )(*(b for b, _ in pays), *(blocks[index] for index in arrays))
+
+
+def step_kernel(sizes, arrays, ends_ref, head_ref, lengths_ref, query_ref, _, *refs):
+    blocks = refs[:-2]
+    logit_ref, kv_ref = refs[-2:]
+    placed_blocks(sizes, arrays, blocks, kv_ref)
+    own_count = blocks[0].shape[2] * sizes[0]
+    free = kv_ref.shape[1] - own_count
     steps = ends_ref.shape[1]
-    width = picked.shape[1]
-    step_rows = [picked[at : at + steps] for at in range(0, steps * head_ref.shape[1] // width, steps)]
-
     ends = column_of(ends_ref[...])
-    own_pos = lax.broadcasted_iota(jnp.int32, (1, own_rows * len(masks)), 1)
+    own_pos = lax.broadcasted_iota(jnp.int32, (1, own_count), 1)
     row_pos = jnp.concatenate([ends] * GROUP, axis=0)
     total = jnp.zeros((steps, HEADDIM), jnp.float32)
-    for head in range(width // HEADDIM):
+    for head in range(kv_ref.shape[2] // HEADDIM):
         columns = slice(head * HEADDIM, (head + 1) * HEADDIM)
         heads = range(head * GROUP, (head + 1) * GROUP)
-        places = [divmod(h * HEADDIM, width) for h in heads]
-        queries = jnp.concatenate([step_rows[a][:, b : b + HEADDIM] for a, b in places], axis=0)
+        queries = jnp.concatenate([query_ref[h] for h in heads], axis=0)
         scores = product(queries.astype(jnp.bfloat16), kv_ref[0, :, columns])
         bound = jnp.where(own_pos <= row_pos, scores[:, free:], NEG_FILL)
         scores = jnp.concatenate([scores[:, :free], bound], axis=1)
@@ -335,31 +359,29 @@
     logit_ref[...] = jnp.sum(jnp.where(down == right, logits, 0.0), axis=0, keepdims=True)
 
 
-def step_shares(sizes, ends, head, lengths, pays, blocks):
-    ctx_size, cand_size = sizes
-    rows, width = blocks[0].shape[2:]
-    count = rows * ctx_size * cand_size + pays[0][0].shape[1] * ctx_size
-    scores = ends.shape[1] * head.shape[1] // HEADDIM * count
+def step_shares(sizes, arrays, ends, head, lengths, queries, kv, blocks):
+    scores = queries.shape[0] * queries.shape[1] * kv.shape[1]
     return pl.pallas_call(
-        functools.partial(step_kernel, sizes, [mask for _, mask in pays]),
-        out_shape=jax.ShapeDtypeStruct(ends.shape, jnp.float32),
-        in_specs=vmem(3 + len(pays) + len(blocks)),
-        out_specs=vmem(1)[0],
-        scratch_shapes=[pltpu.VMEM((2, count, width), blocks[0].dtype)],
+        functools.partial(step_kernel, sizes, arrays),
+        out_shape=(jax.ShapeDtypeStruct(ends.shape, jnp.float32), like(kv)),
+        in_specs=vmem(5 + len(arrays)),
+        out_specs=tuple(vmem(2)),
+        input_output_aliases={4: 1},
         compiler_params=PARAMS,
         cost_estimate=pl.CostEstimate(
             flops=6 * scores * HEADDIM, bytes_accessed=scores, transcendentals=scores
         ),
         name="step_logits",
-    )(ends, head, lengths, *(b for b, _ in pays), *blocks)
+    )(ends, head, lengths, queries, kv, *(blocks[index] for index in arrays))[0]
 
 
 def per_device(ctx_size, cand_size, prompt_q, prompt_kv, cand_q, cand_kv, cand_lengths, step_ends, reward_head):
     sizes = ctx_size, cand_size
     size = ctx_size * cand_size
-    prompt_rows, cand_rows, own, payload, ends, head, lengths = staged(
-        cand_lengths, prompt_q, cand_q[0], prompt_kv, cand_kv[:, 0], step_ends, reward_head[None]
+    prompt_rows, cand_rows, own, payload, ends, head = staged(
+        prompt_q, cand_q[0], prompt_kv, cand_kv[:, 0], step_ends, reward_head[None]
     )
+    lengths = jnp.broadcast_to(cand_lengths[None], (1, HEADDIM))
     q_rows = prompt_rows, cand_rows
     pays = gather_cand(payload, ctx_size)
     early, along, across, core = prompt_bits(ctx_size, cand_size)
@@ -381,13 +403,15 @@
     third = shared_out(held, across, along)
     blocks = [held, second, third, None, across_cores(held), None, None, None]
     state = phase(sizes, [0, 4], q_rows, blocks)
-    fourth = shared_out(packed(second, after=state[:1] + tuple(b for b, _ in pays[1:4])), across, along)
+    fourth = shared_out(packed(second, after=[b for b, _ in pays[1:4]]), across, along)
     blocks[3] = fourth
     blocks[5:7] = across_cores(second), across_cores(third)
     state = phase(sizes, [1, 2], q_rows, blocks, pays=pays, state=state)
     blocks[7] = across_cores(packed(fourth, after=state[:1]))
     state = phase(sizes, [5, 6], q_rows, blocks, state=state)
-    step_logits = step_shares(sizes, ends, head, lengths, pays, blocks)
+    heads = head.shape[1] // HEADDIM
+    kv, queries = arranged(sizes, [0, 1, 2, 4, 5, 6], heads, step_ends.shape[1], pays, blocks)
+    step_logits = step_shares(sizes, [3, 7], ends, head, lengths, queries, kv, blocks)
     cand_out, prompt_out = phase(sizes, [3, 7], q_rows, blocks, state=state, lengths=lengths)
     tp_size = lax.axis_size("tp")
     for bit in high_bits(tp_size, 1):

time: 25.5 us -> 26.9 us (1.055)
  waiting for transfers between devices: 3.08 us -> 5.3 us
  starting transfers between devices: 12.6 us -> 11.8 us
    ppermute x9, waiting for transfers between devices: 1.5 us -> 3.68 us  [flipped(): return lax.ppermute(block, axes, [(i, i ^ bit) for i in range(size)])]
    ppermute x3, starting transfers between devices: 4.53 us -> 4.05 us  [shared_out(): lax.ppermute(block, PROMPT_AXES, [(i, i ^ (odd if i & core else even)) fo...]
    ppermute x9, starting transfers between devices: 8.1 us -> 7.78 us  [flipped(): return lax.ppermute(block, axes, [(i, i ^ bit) for i in range(size)])]
    pallas_call x1 -> x2, Pallas kernels: 1.05 us -> 1.08 us  [the longest x1 0.99 us: step_shares(): pl.pallas_call(functools.partial(step_kernel, sizes, arrays), out_shape=(...]
  transfers between devices with their start and end apart: 12 -> 12, of which waited for: 6 -> 5; matrix products, arithmetic and copies ran while one was open for 0% -> 0% of each run, Pallas kernels for 27% -> 25%
where the time goes in v8:
time: 26.9 us; the launch traced here: 26.8 us
  starting transfers between devices  11.8 us (44%)
  Pallas kernels  7.77 us (29%)
  waiting for transfers between devices  5.3 us (20%)
  between operations  1.38 us (5%)
  other arithmetic  0.51 us (2%)
    ppermute x9, starting transfers between devices, flipped(): return lax.ppermute(block, axes, [(i, i ^ bit) for i in range(size)])  7.78 us
    pallas_call x4, Pallas kernels, phase(): pl.pallas_call(functools.partial(phase_kernel, sizes, arrays, masks, firs...  5.41 us
    ppermute x3, starting transfers between devices, shared_out(): lax.ppermute(block, PROMPT_AXES, [(i, i ^ (odd if i & core else even)) fo...  4.05 us
    ppermute x9, waiting for transfers between devices, flipped(): return lax.ppermute(block, axes, [(i, i ^ bit) for i in range(size)])  3.68 us
    ppermute x3, waiting for transfers between devices, shared_out(): lax.ppermute(block, PROMPT_AXES, [(i, i ^ (odd if i & core else even)) fo...  1.62 us
    pallas_call x1, Pallas kernels, staged(): pl.pallas_call(stage_kernel, out_shape=(like(prompt_q), like(cand_q), lik...  1.24 us
    pallas_call x1, Pallas kernels, step_shares(): pl.pallas_call(functools.partial(step_kernel, sizes, arrays), out_shape=(...  0.99 us
  transfers between devices with their start and end apart: 12, of which 5 were waited for; matrix products, arithmetic and copies ran while one was open for 0% of the time, Pallas kernels for 25%

profile of v8, /device:TPU:0, one launch (start us, length us, event | category | flops | bytes accessed | tf_op | source)
XLA Modules:
  0.0 26.8 jit_solution(10783192627389841556)
XLA Ops:
  0.6 4.1 %collective-permute-start = (bf16[1,2,64,256]{3,2,1,0:T(8,128)(2,1)}, bf16[1,2,64,256]{3,2,1,0:T(8,128)(2,1)S(1)}, u32[]{:S(2)}, u32[]{:S(2)}) collective-permute-start(bf16[1,2,64,256]{3,2,1,0:T(8,128)(2,1)} %bitcast.11), channel_id=1, source_target_pairs={{0,4},{2,6},{4,0},{6,2},{8,12},{10,14},{12,8},{14,10},{16,20},{18,... | collective-permute-start | bytes 196616 | tf_op jit(solution)/shard_map/ppermute | solution.py:35
  4.7 1.2 %stage_operands.1 = (bf16[64,2048]{1,0:T(8,128)(2,1)S(1)}, bf16[64,2048]{1,0:T(8,128)(2,1)S(1)}, bf16[2,64,256]{2,1,0:T(8,128)(2,1)S(1)}, bf16[3,64,256]{2,1,0:T...) custom-call(bf16[64,2048]{1,0:T(8,128)(2,1)} %prompt_q.1, bf16[64,2048]{1,0:T(8,128)(2,1)} %bitcast.9, ...), custom_call_target="tpu_custom_call" | custom-call | tf_op jit(solution)/shard_map/stage_operands/pallas_call | solution.py:123
  6.0 1.6 %collective-permute-start.3 = (bf16[3,64,256]{2,1,0:T(8,128)(2,1)S(1)}, bf16[3,64,256]{2,1,0:T(8,128)(2,1)S(1)}, u32[]{:S(2)}, u32[]{:S(2)}) collective-permute-start(bf16[3,64,256]{2,1,0:T(8,128)(2,1)S(1)} %get-tuple-element.29.refs_4_.refs_0_), channel_id=1, source_target_pairs={{0,16},{8,24},{16,0},{24,8},{1,17},{9,25},{17,1},{25,9},{2,18},{10... | collective-permute-start | bytes 294920 | tf_op jit(solution)/shard_map/ppermute | solution.py:35
  7.6 1.0 %collective-permute-done.refs_1_ = bf16[1,2,64,256]{3,2,1,0:T(8,128)(2,1)S(1)} collective-permute-done((bf16[1,2,64,256]{3,2,1,0:T(8,128)(2,1)}, bf16[1,2,64,256]{3,2,1,0:T(8,128)(2,1)S(1)}, u32[]{:S(2)}, u32[]{:S(2)}) %collective-permute-start) | collective-permute-done | bytes 65568 | tf_op jit(solution)/shard_map/ppermute | solution.py:35
  8.6 0.7 %collective-permute-start.1 = (bf16[2,2,64,256]{3,2,1,0:T(8,128)(2,1)S(1)}, bf16[2,2,64,256]{3,2,1,0:T(8,128)(2,1)S(1)}, u32[]{:S(2)}, u32[]{:S(2)}) collective-permute-start(bf16[2,2,64,256]{3,2,1,0:T(8,128)(2,1)S(1)} %pack_blocks.3.refs_2_.refs_4_), channel_id=1, source_target_pairs={{0,2},{2,0},{4,6},{6,4},{8,24},{10,26},{12,28},{14,30},{16,18},{18... | collective-permute-start | bytes 393224 | tf_op jit(solution)/shard_map/ppermute | solution.py:393
  9.3 0.0 collective-permute-start.2
  9.3 2.4 %collective-permute-done.3.refs_2_.refs_6_ = bf16[3,64,256]{2,1,0:T(8,128)(2,1)S(1)} collective-permute-done((bf16[3,64,256]{2,1,0:T(8,128)(2,1)S(1)}, bf16[3,64,256]{2,1,0:T(8,128)(2,1)S(1)}, u32[]{:S(2)}, u32[]{:S(2)}) %collective-permute-start.3) | collective-permute-done | bytes 98336 | tf_op jit(solution)/shard_map/ppermute | solution.py:35
  11.7 0.0 collective-permute-start.4
  11.7 1.5 %collective-permute-start.6 = (bf16[2,2,64,256]{3,2,1,0:T(8,128)(2,1)S(1)}, bf16[2,2,64,256]{3,2,1,0:T(8,128)(2,1)S(1)}, u32[]{:S(2)}, u32[]{:S(2)}) collective-permute-start(bf16[2,2,64,256]{3,2,1,0:T(8,128)(2,1)S(1)} %pack_blocks.3.refs_2_.refs_4_), channel_id=1, source_target_pairs={{0,16},{2,18},{4,20},{6,22},{8,10},{10,8},{12,14},{14,12},{16,0},{... | collective-permute-start | bytes 393224 | tf_op jit(solution)/shard_map/ppermute | solution.py:393
  13.2 0.0 collective-permute-start.7
  13.3 0.0 collective-permute-done.2.refs_1_.refs_5_
  13.3 0.4 %collective-permute-done.1.refs_0_.refs_2_.refs_5_ = bf16[2,2,64,256]{3,2,1,0:T(8,128)(2,1)S(1)} collective-permute-done((bf16[2,2,64,256]{3,2,1,0:T(8,128)(2,1)S(1)}, bf16[2,2,64,256]{3,2,1,0:T(8,128)(2,1)S(1)}, u32[]{:S(2)}, u32[]{:S(2)}) %collective-permute-start.1) | collective-permute-done | bytes 131104 | tf_op jit(solution)/shard_map/ppermute | solution.py:393
  13.6 0.0 collective-permute-done.4.refs_3_.refs_7_
  13.7 1.8 %collective-permute-start.5 = (bf16[2,2,64,256]{3,2,1,0:T(8,128)(2,1)S(1)}, bf16[2,2,64,256]{3,2,1,0:T(8,128)(2,1)S(1)}, u32[]{:S(2)}, u32[]{:S(2)}) collective-permute-start(bf16[2,2,64,256]{3,2,1,0:T(8,128)(2,1)S(1)} %pack_blocks.4), channel_id=1, source_target_pairs={{0,16},{2,18},{4,20},{6,22},{8,10},{10,8},{12,14},{14,12},{16,0},{... | collective-permute-start | bytes 393224 | tf_op jit(solution)/shard_map/ppermute | solution.py:393
  15.5 0.0 collective-permute-start.9
  15.5 1.2 %collective-permute-done.6.refs_3_.refs_6_ = bf16[2,2,64,256]{3,2,1,0:T(8,128)(2,1)S(1)} collective-permute-done((bf16[2,2,64,256]{3,2,1,0:T(8,128)(2,1)S(1)}, bf16[2,2,64,256]{3,2,1,0:T(8,128)(2,1)S(1)}, u32[]{:S(2)}, u32[]{:S(2)}) %collective-permute-start.6) | collective-permute-done | bytes 131104 | tf_op jit(solution)/shard_map/ppermute | solution.py:393
  16.7 0.0 collective-permute-start.10
  16.7 0.0 collective-permute-done.7.refs_3_.refs_7_
  16.7 0.9 %attend_0_4.1 = (f32[1024,128]{1,0:T(8,128)S(1)}, f32[1024,256]{1,0:T(8,128)S(1)}, f32[1024,128]{1,0:T(8,128)S(1)}, f32[1024,256]{1,0:T(8,128)S(1)}) custom-call(bf16[64,2048]{1,0:T(8,128)(2,1)S(1)} %get-tuple-element.26.refs_0_, bf16[64,2048]{1,0:T(8,128)(2,1)S(1)} %get-tuple-element.27.refs_1_, bf16[2,2,64,256]{3,2,1,0:T(8,128)(2,1)S(1)} %pack_blocks.3.refs_2_.refs_4_, ...), custom_call_target="tpu_custom_call" | custom-call | flops 402653184 | bytes 524288 | tf_op jit(solution)/shard_map/attend_0_4/pallas_call | solution.py:272
  17.6 1.7 %attend_1_2.1 = (f32[1024,128]{1,0:T(8,128)S(1)}, f32[1024,256]{1,0:T(8,128)S(1)}, f32[1024,128]{1,0:T(8,128)S(1)}, f32[1024,256]{1,0:T(8,128)S(1)}) custom-call(bf16[64,2048]{1,0:T(8,128)(2,1)S(1)} %get-tuple-element.26.refs_0_, bf16[64,2048]{1,0:T(8,128)(2,1)S(1)} %get-tuple-element.27.refs_1_, ...), custom_call_target="tpu_custom_call" | custom-call | flops 402653184 | bytes 524288 | tf_op jit(solution)/shard_map/attend_1_2/pallas_call | solution.py:272
  19.3 0.0 collective-permute-done.5.refs_0_.refs_2_
  19.4 0.6 %collective-permute-start.8 = (bf16[2,2,64,256]{3,2,1,0:T(8,128)(2,1)S(1)}, bf16[2,2,64,256]{3,2,1,0:T(8,128)(2,1)S(1)}, u32[]{:S(2)}, u32[]{:S(2)}) collective-permute-start(bf16[2,2,64,256]{3,2,1,0:T(8,128)(2,1)S(1)} %pack_blocks.5), channel_id=1, source_target_pairs={{0,8},{2,10},{4,12},{6,14},{8,0},{10,2},{12,4},{14,6},{16,24},{18,... | collective-permute-start | bytes 393224 | tf_op jit(solution)/shard_map/ppermute | solution.py:35
  20.6 0.0 collective-permute-done.9.refs_2_.refs_8_
  20.6 0.0 collective-permute-done.10.refs_3_.refs_9_
  20.6 0.1 arrange_blocks.1
  20.7 1.0 %attend_5_6.1 = (f32[1024,128]{1,0:T(8,128)S(1)}, f32[1024,256]{1,0:T(8,128)S(1)}, f32[1024,128]{1,0:T(8,128)S(1)}, f32[1024,256]{1,0:T(8,128)S(1)}) custom-call(bf16[64,2048]{1,0:T(8,128)(2,1)S(1)} %get-tuple-element.26.refs_0_, bf16[64,2048]{1,0:T(8,128)(2,1)S(1)} %get-tuple-element.27.refs_1_, ...), custom_call_target="tpu_custom_call" | custom-call | flops 402653184 | bytes 524288 | tf_op jit(solution)/shard_map/attend_5_6/pallas_call | solution.py:272
  21.7 0.0 collective-permute-done.8.refs_3_.refs_1_
  21.7 1.0 %step_logits.1 = (f32[1,8]{1,0:T(1,128)S(1)}, bf16[2,1280,256]{2,1,0:T(8,128)(2,1)S(1)}) custom-call(s32[1,8]{1,0:T(1,128)S(1)} %get-tuple-element.44.ends_ref, f32[1,2048]{1,0:T(1,128)S(1)} %get-tuple-element.45.head_ref, s32[1,128]{1,0:T(1,128)S(1)} %broadcast_in_dim.24.refs_4_.lengths_ref, ...), custom_call_target="tpu_custom_call", output_to_operand_aliasing={{1}: (4, {})} | custom-call | flops 125829120 | bytes 163840 | tf_op jit(solution)/shard_map/step_logits/pallas_call | solution.py:364
  22.7 1.5 %collective-permute-start.11 = (f32[1,8]{1,0:T(1,128)S(1)}, f32[1,8]{1,0:T(1,128)S(1)}, u32[]{:S(2)}, u32[]{:S(2)}) collective-permute-start(f32[1,8]{1,0:T(1,128)S(1)} %get-tuple-element.48), channel_id=1, source_target_pairs={{0,1},{1,0},{2,3},{3,2},{4,5},{5,4},{6,7},{7,6},{8,9},{9,8},{10,11... | collective-permute-start | bytes 104 | tf_op jit(solution)/shard_map/ppermute | solution.py:35
  24.2 1.8 %attend_3_7.1 = (bf16[64,2048]{1,0:T(8,128)(2,1)}, bf16[64,2048]{1,0:T(8,128)(2,1)}) custom-call(bf16[64,2048]{1,0:T(8,128)(2,1)S(1)} %get-tuple-element.26.refs_0_, bf16[64,2048]{1,0:T(8,128)(2,1)S(1)} %get-tuple-element.27.refs_1_, bf16[2,2,64,256]{3,2,1,0:T(8,128)(2,1)S(1)} %collective-permute-done.5.refs_0_.refs_2_, ...), custom_call_target="tpu_custom_call" | custom-call | flops 402653184 | bytes 524288 | tf_op jit(solution)/shard_map/attend_3_7/pallas_call | solution.py:272
  26.0 0.3 %collective-permute-done.11 = f32[1,8]{1,0:T(1,128)S(1)} collective-permute-done((f32[1,8]{1,0:T(1,128)S(1)}, f32[1,8]{1,0:T(1,128)S(1)}, u32[]{:S(2)}, u32[]{:S(2)}) %collective-permute-start.11) | collective-permute-done | bytes 64 | tf_op jit(solution)/shard_map/ppermute | solution.py:35
  26.3 0.5 %add.3 = f32[1,8]{1,0:T(1,128)} add(f32[1,8]{1,0:T(1,128)S(1)} %get-tuple-element.48, f32[1,8]{1,0:T(1,128)S(1)} %collective-permute-done.11) | non-fusion elementwise | flops 8 | bytes 96 | tf_op jit(solution)/shard_map/add | solution.py:418
  (4 shorter events, 0.0 us)
Async XLA Ops:
  0.6 8.0 %collective-permute-start = (bf16[1,2,64,256]{3,2,1,0:T(8,128)(2,1)}, bf16[1,2,64,256]{3,2,1,0:T(8,128)(2,1)S(1)}, u32[]{:S(2)}, u32[]{:S(2)}) collective-permute-start(bf16[1,2,64,256]{3,2,1,0:T(8,128)(2,1)} %bitcast.11), channel_id=1, source_target_pairs={{0,4},{2,6},{4,0},{6,2},{8,12},{10,14},{12,8},{14,10},{16,20},{18,... | collective-permute-start | bytes 196616 | tf_op jit(solution)/shard_map/ppermute | solution.py:35
  6.0 5.7 %collective-permute-start.3 = (bf16[3,64,256]{2,1,0:T(8,128)(2,1)S(1)}, bf16[3,64,256]{2,1,0:T(8,128)(2,1)S(1)}, u32[]{:S(2)}, u32[]{:S(2)}) collective-permute-start(bf16[3,64,256]{2,1,0:T(8,128)(2,1)S(1)} %get-tuple-element.29.refs_4_.refs_0_), channel_id=1, source_target_pairs={{0,16},{8,24},{16,0},{24,8},{1,17},{9,25},{17,1},{25,9},{2,18},{10... | collective-permute-start | bytes 294920 | tf_op jit(solution)/shard_map/ppermute | solution.py:35
  8.6 5.0 %collective-permute-start.1 = (bf16[2,2,64,256]{3,2,1,0:T(8,128)(2,1)S(1)}, bf16[2,2,64,256]{3,2,1,0:T(8,128)(2,1)S(1)}, u32[]{:S(2)}, u32[]{:S(2)}) collective-permute-start(bf16[2,2,64,256]{3,2,1,0:T(8,128)(2,1)S(1)} %pack_blocks.3.refs_2_.refs_4_), channel_id=1, source_target_pairs={{0,2},{2,0},{4,6},{6,4},{8,24},{10,26},{12,28},{14,30},{16,18},{18... | collective-permute-start | bytes 393224 | tf_op jit(solution)/shard_map/ppermute | solution.py:393
  9.3 3.9 %collective-permute-start.2 = (bf16[3,64,256]{2,1,0:T(8,128)(2,1)S(1)}, bf16[3,64,256]{2,1,0:T(8,128)(2,1)S(1)}, u32[]{:S(2)}, u32[]{:S(2)}) collective-permute-start(bf16[3,64,256]{2,1,0:T(8,128)(2,1)S(1)} %get-tuple-element.29.refs_4_.refs_0_), channel_id=1, source_target_pairs={{0,8},{8,0},{16,24},{24,16},{1,9},{9,1},{17,25},{25,17},{2,10},{10... | collective-permute-start | bytes 294920 | tf_op jit(solution)/shard_map/ppermute | solution.py:35
  11.7 1.9 %collective-permute-start.4 = (bf16[3,64,256]{2,1,0:T(8,128)(2,1)S(1)}, bf16[3,64,256]{2,1,0:T(8,128)(2,1)S(1)}, u32[]{:S(2)}, u32[]{:S(2)}) collective-permute-start(bf16[3,64,256]{2,1,0:T(8,128)(2,1)S(1)} %collective-permute-done.3.refs_2_.refs_6_), channel_id=1, source_target_pairs={{0,8},{8,0},{16,24},{24,16},{1,9},{9,1},{17,25},{25,17},{2,10},{10... | collective-permute-start | bytes 294920 | tf_op jit(solution)/shard_map/ppermute | solution.py:35
  11.7 5.0 %collective-permute-start.6 = (bf16[2,2,64,256]{3,2,1,0:T(8,128)(2,1)S(1)}, bf16[2,2,64,256]{3,2,1,0:T(8,128)(2,1)S(1)}, u32[]{:S(2)}, u32[]{:S(2)}) collective-permute-start(bf16[2,2,64,256]{3,2,1,0:T(8,128)(2,1)S(1)} %pack_blocks.3.refs_2_.refs_4_), channel_id=1, source_target_pairs={{0,16},{2,18},{4,20},{6,22},{8,10},{10,8},{12,14},{14,12},{16,0},{... | collective-permute-start | bytes 393224 | tf_op jit(solution)/shard_map/ppermute | solution.py:393
  13.2 3.5 %collective-permute-start.7 = (bf16[2,2,64,256]{3,2,1,0:T(8,128)(2,1)S(1)}, bf16[2,2,64,256]{3,2,1,0:T(8,128)(2,1)S(1)}, u32[]{:S(2)}, u32[]{:S(2)}) collective-permute-start(bf16[2,2,64,256]{3,2,1,0:T(8,128)(2,1)S(1)} %pack_blocks.3.refs_2_.refs_4_), channel_id=1, source_target_pairs={{0,8},{2,10},{4,12},{6,14},{8,0},{10,2},{12,4},{14,6},{16,24},{18,... | collective-permute-start | bytes 393224 | tf_op jit(solution)/shard_map/ppermute | solution.py:35
  13.7 5.7 %collective-permute-start.5 = (bf16[2,2,64,256]{3,2,1,0:T(8,128)(2,1)S(1)}, bf16[2,2,64,256]{3,2,1,0:T(8,128)(2,1)S(1)}, u32[]{:S(2)}, u32[]{:S(2)}) collective-permute-start(bf16[2,2,64,256]{3,2,1,0:T(8,128)(2,1)S(1)} %pack_blocks.4), channel_id=1, source_target_pairs={{0,16},{2,18},{4,20},{6,22},{8,10},{10,8},{12,14},{14,12},{16,0},{... | collective-permute-start | bytes 393224 | tf_op jit(solution)/shard_map/ppermute | solution.py:393
  15.5 5.1 %collective-permute-start.9 = (bf16[2,2,64,256]{3,2,1,0:T(8,128)(2,1)S(1)}, bf16[2,2,64,256]{3,2,1,0:T(8,128)(2,1)S(1)}, u32[]{:S(2)}, u32[]{:S(2)}) collective-permute-start(bf16[2,2,64,256]{3,2,1,0:T(8,128)(2,1)S(1)} %collective-permute-done.1.refs_0_.refs_2_.refs_5_), channel_id=1, source_target_pairs={{0,8},{2,10},{4,12},{6,14},{8,0},{10,2},{12,4},{14,6},{16,24},{18,... | collective-permute-start | bytes 393224 | tf_op jit(solution)/shard_map/ppermute | solution.py:35
  16.7 3.9 %collective-permute-start.10 = (bf16[2,2,64,256]{3,2,1,0:T(8,128)(2,1)S(1)}, bf16[2,2,64,256]{3,2,1,0:T(8,128)(2,1)S(1)}, u32[]{:S(2)}, u32[]{:S(2)}) collective-permute-start(bf16[2,2,64,256]{3,2,1,0:T(8,128)(2,1)S(1)} %collective-permute-done.6.refs_3_.refs_6_), channel_id=1, source_target_pairs={{0,8},{2,10},{4,12},{6,14},{8,0},{10,2},{12,4},{14,6},{16,24},{18,... | collective-permute-start | bytes 393224 | tf_op jit(solution)/shard_map/ppermute | solution.py:35
  19.4 2.3 %collective-permute-start.8 = (bf16[2,2,64,256]{3,2,1,0:T(8,128)(2,1)S(1)}, bf16[2,2,64,256]{3,2,1,0:T(8,128)(2,1)S(1)}, u32[]{:S(2)}, u32[]{:S(2)}) collective-permute-start(bf16[2,2,64,256]{3,2,1,0:T(8,128)(2,1)S(1)} %pack_blocks.5), channel_id=1, source_target_pairs={{0,8},{2,10},{4,12},{6,14},{8,0},{10,2},{12,4},{14,6},{16,24},{18,... | collective-permute-start | bytes 393224 | tf_op jit(solution)/shard_map/ppermute | solution.py:35
  22.7 3.5 %collective-permute-start.11 = (f32[1,8]{1,0:T(1,128)S(1)}, f32[1,8]{1,0:T(1,128)S(1)}, u32[]{:S(2)}, u32[]{:S(2)}) collective-permute-start(f32[1,8]{1,0:T(1,128)S(1)} %get-tuple-element.48), channel_id=1, source_target_pairs={{0,1},{1,0},{2,3},{3,2},{4,5},{5,4},{6,7},{7,6},{8,9},{9,8},{10,11... | collective-permute-start | bytes 104 | tf_op jit(solution)/shard_map/ppermute | solution.py:35

commit v9 on v8

--- a/solution.py
+++ b/solution.py
@@ -65,13 +65,18 @@
     early, along, across, core = prompt_bits(ctx_size, cand_size)
     place = lax.axis_index("ctx") * cand_size + lax.axis_index("cand")
     odd = lax.rem(lax.axis_index("ctx"), 2)
-    near = along + odd * (across - along)
-    far = along + across - near
     masks = [0]
-    for bit in early:
+    for bit in early[:-1]:
         masks += [mask ^ bit for mask in masks]
-    shifts = [0, near, far, along + across, core, core + far, core + near, core + along + across]
-    return [[place ^ mask ^ shift for mask in masks] for shift in shifts]
+    owners = []
+    for side, other in ((odd, 0), (1 - odd, core)):
+        first, second, third = (
+            even + side * (uneven - even)
+            for even, uneven in ((along, early[-1]), (early[-1], across), (across, along))
+        )
+        for shift in (0, second, third, second ^ third):
+            owners.append([place ^ other ^ shift ^ step ^ mask for step in (0, first) for mask in masks])
+    return owners
 
 
 def gather_cand(own, ctx_size):
@@ -394,16 +399,16 @@
             block, PROMPT_AXES, [(i, i ^ (odd if i & core else even)) for i in range(size)]
         )
 
-    held = own[None]
-    sent = prompt_kv[None]
-    for bit in early:
+    held, sent = own[None], prompt_kv[None]
+    for bit in early[:-1]:
         held = packed(held, flipped(sent, PROMPT_AXES, size, bit))
         sent = held
-    second = shared_out(held, along, across)
+    held = packed(held, shared_out(sent, along, early[-1]))
+    second = shared_out(held, early[-1], across)
     third = shared_out(held, across, along)
     blocks = [held, second, third, None, across_cores(held), None, None, None]
     state = phase(sizes, [0, 4], q_rows, blocks)
-    fourth = shared_out(packed(second, after=[b for b, _ in pays[1:4]]), across, along)
+    fourth = shared_out(packed(second, after=state[:1] + tuple(b for b, _ in pays[1:4])), across, along)
     blocks[3] = fourth
     blocks[5:7] = across_cores(second), across_cores(third)
     state = phase(sizes, [1, 2], q_rows, blocks, pays=pays, state=state)

time: 26.9 us -> 26.5 us (0.985)
  waiting for transfers between devices: 5.3 us -> 2.23 us
  starting transfers between devices: 11.8 us -> 14.4 us
    ppermute x3 -> x4, starting transfers between devices: 4.05 us -> 10.2 us  [shared_out(): lax.ppermute(block, PROMPT_AXES, [(i, i ^ (odd if i & core else even)) fo...]
    ppermute x9 -> x8, starting transfers between devices: 7.78 us -> 4.24 us  [flipped(): return lax.ppermute(block, axes, [(i, i ^ bit) for i in range(size)])]
    ppermute x9 -> x8, waiting for transfers between devices: 3.68 us -> 1.05 us  [flipped(): return lax.ppermute(block, axes, [(i, i ^ bit) for i in range(size)])]
    ppermute x3 -> x4, waiting for transfers between devices: 1.62 us -> 1.18 us  [shared_out(): lax.ppermute(block, PROMPT_AXES, [(i, i ^ (odd if i & core else even)) fo...]
  transfers between devices with their start and end apart: 12 -> 12, of which waited for: 5 -> 4; matrix products, arithmetic and copies ran while one was open for 0% -> 0% of each run, Pallas kernels for 25% -> 26%
where the time goes in v9:
time: 26.5 us; the launch traced here: 26.4 us
  starting transfers between devices  14.4 us (54%)
  Pallas kernels  7.78 us (29%)
  waiting for transfers between devices  2.23 us (8%)
  between operations  1.39 us (5%)
  other arithmetic  0.51 us (2%)
    ppermute x4, starting transfers between devices, shared_out(): lax.ppermute(block, PROMPT_AXES, [(i, i ^ (odd if i & core else even)) fo...  10.2 us
    pallas_call x4, Pallas kernels, phase(): pl.pallas_call(functools.partial(phase_kernel, sizes, arrays, masks, firs...  5.42 us
    ppermute x8, starting transfers between devices, flipped(): return lax.ppermute(block, axes, [(i, i ^ bit) for i in range(size)])  4.24 us
    pallas_call x1, Pallas kernels, staged(): pl.pallas_call(stage_kernel, out_shape=(like(prompt_q), like(cand_q), lik...  1.24 us
    ppermute x4, waiting for transfers between devices, shared_out(): lax.ppermute(block, PROMPT_AXES, [(i, i ^ (odd if i & core else even)) fo...  1.18 us
    ppermute x8, waiting for transfers between devices, flipped(): return lax.ppermute(block, axes, [(i, i ^ bit) for i in range(size)])  1.05 us
    pallas_call x1, Pallas kernels, step_shares(): pl.pallas_call(functools.partial(step_kernel, sizes, arrays), out_shape=(...  0.99 us
  transfers between devices with their start and end apart: 12, of which 4 were waited for; matrix products, arithmetic and copies ran while one was open for 0% of the time, Pallas kernels for 26%

profile of v9, /device:TPU:0, one launch (start us, length us, event | category | flops | bytes accessed | tf_op | source)
XLA Modules:
  0.0 26.4 jit_solution(18223607080849956979)
XLA Ops:
  0.6 3.1 %collective-permute-start = (bf16[1,2,64,256]{3,2,1,0:T(8,128)(2,1)}, bf16[1,2,64,256]{3,2,1,0:T(8,128)(2,1)S(1)}, u32[]{:S(2)}, u32[]{:S(2)}) collective-permute-start(bf16[1,2,64,256]{3,2,1,0:T(8,128)(2,1)} %bitcast.11), channel_id=1, source_target_pairs={{0,2},{2,0},{4,6},{6,4},{8,12},{10,14},{12,8},{14,10},{16,18},{18,... | collective-permute-start | bytes 196616 | tf_op jit(solution)/shard_map/ppermute | solution.py:398
  3.7 1.2 %stage_operands.1 = (bf16[64,2048]{1,0:T(8,128)(2,1)S(1)}, bf16[64,2048]{1,0:T(8,128)(2,1)S(1)}, bf16[2,64,256]{2,1,0:T(8,128)(2,1)S(1)}, bf16[3,64,256]{2,1,0:T...) custom-call(bf16[64,2048]{1,0:T(8,128)(2,1)} %prompt_q.1, bf16[64,2048]{1,0:T(8,128)(2,1)} %bitcast.9, ...), custom_call_target="tpu_custom_call" | custom-call | tf_op jit(solution)/shard_map/stage_operands/pallas_call | solution.py:128
  5.0 1.6 %collective-permute-start.4 = (bf16[3,64,256]{2,1,0:T(8,128)(2,1)S(1)}, bf16[3,64,256]{2,1,0:T(8,128)(2,1)S(1)}, u32[]{:S(2)}, u32[]{:S(2)}) collective-permute-start(bf16[3,64,256]{2,1,0:T(8,128)(2,1)S(1)} %get-tuple-element.30.refs_4_.refs_0_), channel_id=1, source_target_pairs={{0,16},{8,24},{16,0},{24,8},{1,17},{9,25},{17,1},{25,9},{2,18},{10... | collective-permute-start | bytes 294920 | tf_op jit(solution)/shard_map/ppermute | solution.py:35
  6.6 0.3 %collective-permute-done.refs_1_ = bf16[1,2,64,256]{3,2,1,0:T(8,128)(2,1)S(1)} collective-permute-done((bf16[1,2,64,256]{3,2,1,0:T(8,128)(2,1)}, bf16[1,2,64,256]{3,2,1,0:T(8,128)(2,1)S(1)}, u32[]{:S(2)}, u32[]{:S(2)}) %collective-permute-start) | collective-permute-done | bytes 65568 | tf_op jit(solution)/shard_map/ppermute | solution.py:398
  6.9 0.1 collective-permute-start.2
  7.0 2.5 %collective-permute-start.1 = (bf16[2,2,64,256]{3,2,1,0:T(8,128)(2,1)S(1)}, bf16[2,2,64,256]{3,2,1,0:T(8,128)(2,1)S(1)}, u32[]{:S(2)}, u32[]{:S(2)}) collective-permute-start(bf16[2,2,64,256]{3,2,1,0:T(8,128)(2,1)S(1)} %pack_blocks.3.refs_2_.refs_4_), channel_id=1, source_target_pairs={{0,4},{2,6},{4,0},{6,2},{8,24},{10,26},{12,28},{14,30},{16,20},{18... | collective-permute-start | bytes 393224 | tf_op jit(solution)/shard_map/ppermute | solution.py:398
  9.4 0.0 collective-permute-start.3
  9.5 1.0 %collective-permute-done.4.refs_3_.refs_6_.refs_2_ = bf16[3,64,256]{2,1,0:T(8,128)(2,1)S(1)} collective-permute-done((bf16[3,64,256]{2,1,0:T(8,128)(2,1)S(1)}, bf16[3,64,256]{2,1,0:T(8,128)(2,1)S(1)}, u32[]{:S(2)}, u32[]{:S(2)}) %collective-permute-start.4) | collective-permute-done | bytes 98336 | tf_op jit(solution)/shard_map/ppermute | solution.py:35
  10.5 0.0 collective-permute-start.5
  10.5 1.3 %collective-permute-start.7 = (bf16[2,2,64,256]{3,2,1,0:T(8,128)(2,1)S(1)}, bf16[2,2,64,256]{3,2,1,0:T(8,128)(2,1)S(1)}, u32[]{:S(2)}, u32[]{:S(2)}) collective-permute-start(bf16[2,2,64,256]{3,2,1,0:T(8,128)(2,1)S(1)} %pack_blocks.3.refs_2_.refs_4_), channel_id=1, source_target_pairs={{0,16},{2,18},{4,20},{6,22},{8,10},{10,8},{12,14},{14,12},{16,0},{... | collective-permute-start | bytes 393224 | tf_op jit(solution)/shard_map/ppermute | solution.py:398
  11.8 0.0 collective-permute-done.2.refs_3_.refs_7_
  11.8 0.9 %attend_0_4.1 = (f32[1024,128]{1,0:T(8,128)S(1)}, f32[1024,256]{1,0:T(8,128)S(1)}, f32[1024,128]{1,0:T(8,128)S(1)}, f32[1024,256]{1,0:T(8,128)S(1)}) custom-call(bf16[64,2048]{1,0:T(8,128)(2,1)S(1)} %get-tuple-element.26.refs_0_, bf16[64,2048]{1,0:T(8,128)(2,1)S(1)} %get-tuple-element.27.refs_1_, bf16[2,2,64,256]{3,2,1,0:T(8,128)(2,1)S(1)} %pack_blocks.3.refs_2_.refs_4_, ...), custom_call_target="tpu_custom_call" | custom-call | flops 402653184 | bytes 524288 | tf_op jit(solution)/shard_map/attend_0_4/pallas_call | solution.py:277
  12.7 0.0 collective-permute-done.3.refs_2_.refs_5_.refs_1_
  12.7 0.2 collective-permute-done.1.refs_0_.refs_2_.refs_5_
  12.9 0.0 collective-permute-done.5.refs_4_.refs_7_.refs_3_
  12.9 3.3 %collective-permute-start.6 = (bf16[2,2,64,256]{3,2,1,0:T(8,128)(2,1)S(1)}, bf16[2,2,64,256]{3,2,1,0:T(8,128)(2,1)S(1)}, u32[]{:S(2)}, u32[]{:S(2)}) collective-permute-start(bf16[2,2,64,256]{3,2,1,0:T(8,128)(2,1)S(1)} %pack_blocks.4), channel_id=1, source_target_pairs={{0,16},{2,18},{4,20},{6,22},{8,10},{10,8},{12,14},{14,12},{16,0},{... | collective-permute-start | bytes 393224 | tf_op jit(solution)/shard_map/ppermute | solution.py:398
  16.2 0.0 collective-permute-start.9
  16.2 0.0 collective-permute-done.7.refs_3_.refs_6_
  16.2 0.5 %collective-permute-start.10 = (bf16[2,2,64,256]{3,2,1,0:T(8,128)(2,1)S(1)}, bf16[2,2,64,256]{3,2,1,0:T(8,128)(2,1)S(1)}, u32[]{:S(2)}, u32[]{:S(2)}) collective-permute-start(bf16[2,2,64,256]{3,2,1,0:T(8,128)(2,1)S(1)} %collective-permute-done.7.refs_3_.refs_6_), channel_id=1, source_target_pairs={{0,8},{2,10},{4,12},{6,14},{8,0},{10,2},{12,4},{14,6},{16,24},{18,... | collective-permute-start | bytes 393224 | tf_op jit(solution)/shard_map/ppermute | solution.py:35
  16.7 1.7 %attend_1_2.1 = (f32[1024,128]{1,0:T(8,128)S(1)}, f32[1024,256]{1,0:T(8,128)S(1)}, f32[1024,128]{1,0:T(8,128)S(1)}, f32[1024,256]{1,0:T(8,128)S(1)}) custom-call(bf16[64,2048]{1,0:T(8,128)(2,1)S(1)} %get-tuple-element.26.refs_0_, bf16[64,2048]{1,0:T(8,128)(2,1)S(1)} %get-tuple-element.27.refs_1_, ...), custom_call_target="tpu_custom_call" | custom-call | flops 402653184 | bytes 524288 | tf_op jit(solution)/shard_map/attend_1_2/pallas_call | solution.py:277
  18.5 0.7 %collective-permute-done.6.refs_0_.refs_2_ = bf16[2,2,64,256]{3,2,1,0:T(8,128)(2,1)S(1)} collective-permute-done((bf16[2,2,64,256]{3,2,1,0:T(8,128)(2,1)S(1)}, bf16[2,2,64,256]{3,2,1,0:T(8,128)(2,1)S(1)}, u32[]{:S(2)}, u32[]{:S(2)}) %collective-permute-start.6) | collective-permute-done | bytes 131104 | tf_op jit(solution)/shard_map/ppermute | solution.py:398
  19.2 0.1 collective-permute-start.8
  19.9 0.0 collective-permute-done.9.refs_2_.refs_8_
  19.9 0.0 collective-permute-done.10.refs_3_.refs_9_
  19.9 0.1 arrange_blocks.1
  20.0 1.0 %attend_5_6.1 = (f32[1024,128]{1,0:T(8,128)S(1)}, f32[1024,256]{1,0:T(8,128)S(1)}, f32[1024,128]{1,0:T(8,128)S(1)}, f32[1024,256]{1,0:T(8,128)S(1)}) custom-call(bf16[64,2048]{1,0:T(8,128)(2,1)S(1)} %get-tuple-element.26.refs_0_, bf16[64,2048]{1,0:T(8,128)(2,1)S(1)} %get-tuple-element.27.refs_1_, ...), custom_call_target="tpu_custom_call" | custom-call | flops 402653184 | bytes 524288 | tf_op jit(solution)/shard_map/attend_5_6/pallas_call | solution.py:277
  21.0 0.0 collective-permute-done.8.refs_3_.refs_1_
  21.1 1.0 %step_logits.1 = (f32[1,8]{1,0:T(1,128)S(1)}, bf16[2,1280,256]{2,1,0:T(8,128)(2,1)S(1)}) custom-call(s32[1,8]{1,0:T(1,128)S(1)} %get-tuple-element.44.ends_ref, f32[1,2048]{1,0:T(1,128)S(1)} %get-tuple-element.45.head_ref, s32[1,128]{1,0:T(1,128)S(1)} %broadcast_in_dim.24.refs_4_.lengths_ref, ...), custom_call_target="tpu_custom_call", output_to_operand_aliasing={{1}: (4, {})} | custom-call | flops 125829120 | bytes 163840 | tf_op jit(solution)/shard_map/step_logits/pallas_call | solution.py:369
  22.0 2.0 %collective-permute-start.11 = (f32[1,8]{1,0:T(1,128)S(1)}, f32[1,8]{1,0:T(1,128)S(1)}, u32[]{:S(2)}, u32[]{:S(2)}) collective-permute-start(f32[1,8]{1,0:T(1,128)S(1)} %get-tuple-element.48), channel_id=1, source_target_pairs={{0,1},{1,0},{2,3},{3,2},{4,5},{5,4},{6,7},{7,6},{8,9},{9,8},{10,11... | collective-permute-start | bytes 104 | tf_op jit(solution)/shard_map/ppermute | solution.py:35
  24.0 1.8 %attend_3_7.1 = (bf16[64,2048]{1,0:T(8,128)(2,1)}, bf16[64,2048]{1,0:T(8,128)(2,1)}) custom-call(bf16[64,2048]{1,0:T(8,128)(2,1)S(1)} %get-tuple-element.26.refs_0_, bf16[64,2048]{1,0:T(8,128)(2,1)S(1)} %get-tuple-element.27.refs_1_, bf16[2,2,64,256]{3,2,1,0:T(8,128)(2,1)S(1)} %collective-permute-done.6.refs_0_.refs_2_, ...), custom_call_target="tpu_custom_call" | custom-call | flops 402653184 | bytes 524288 | tf_op jit(solution)/shard_map/attend_3_7/pallas_call | solution.py:277
  25.8 0.0 collective-permute-done.11
  25.8 0.5 %add.3 = f32[1,8]{1,0:T(1,128)} add(f32[1,8]{1,0:T(1,128)S(1)} %get-tuple-element.48, f32[1,8]{1,0:T(1,128)S(1)} %collective-permute-done.11) | non-fusion elementwise | flops 8 | bytes 96 | tf_op jit(solution)/shard_map/add | solution.py:423
  (4 shorter events, 0.0 us)
Async XLA Ops:
  0.6 6.2 %collective-permute-start = (bf16[1,2,64,256]{3,2,1,0:T(8,128)(2,1)}, bf16[1,2,64,256]{3,2,1,0:T(8,128)(2,1)S(1)}, u32[]{:S(2)}, u32[]{:S(2)}) collective-permute-start(bf16[1,2,64,256]{3,2,1,0:T(8,128)(2,1)} %bitcast.11), channel_id=1, source_target_pairs={{0,2},{2,0},{4,6},{6,4},{8,12},{10,14},{12,8},{14,10},{16,18},{18,... | collective-permute-start | bytes 196616 | tf_op jit(solution)/shard_map/ppermute | solution.py:398
  5.0 5.5 %collective-permute-start.4 = (bf16[3,64,256]{2,1,0:T(8,128)(2,1)S(1)}, bf16[3,64,256]{2,1,0:T(8,128)(2,1)S(1)}, u32[]{:S(2)}, u32[]{:S(2)}) collective-permute-start(bf16[3,64,256]{2,1,0:T(8,128)(2,1)S(1)} %get-tuple-element.30.refs_4_.refs_0_), channel_id=1, source_target_pairs={{0,16},{8,24},{16,0},{24,8},{1,17},{9,25},{17,1},{25,9},{2,18},{10... | collective-permute-start | bytes 294920 | tf_op jit(solution)/shard_map/ppermute | solution.py:35
  6.9 4.9 %collective-permute-start.2 = (bf16[2,2,64,256]{3,2,1,0:T(8,128)(2,1)S(1)}, bf16[2,2,64,256]{3,2,1,0:T(8,128)(2,1)S(1)}, u32[]{:S(2)}, u32[]{:S(2)}) collective-permute-start(bf16[2,2,64,256]{3,2,1,0:T(8,128)(2,1)S(1)} %pack_blocks.3.refs_2_.refs_4_), channel_id=1, source_target_pairs={{0,8},{2,10},{4,12},{6,14},{8,0},{10,2},{12,4},{14,6},{16,24},{18,... | collective-permute-start | bytes 393224 | tf_op jit(solution)/shard_map/ppermute | solution.py:35
  7.0 5.9 %collective-permute-start.1 = (bf16[2,2,64,256]{3,2,1,0:T(8,128)(2,1)S(1)}, bf16[2,2,64,256]{3,2,1,0:T(8,128)(2,1)S(1)}, u32[]{:S(2)}, u32[]{:S(2)}) collective-permute-start(bf16[2,2,64,256]{3,2,1,0:T(8,128)(2,1)S(1)} %pack_blocks.3.refs_2_.refs_4_), channel_id=1, source_target_pairs={{0,4},{2,6},{4,0},{6,2},{8,24},{10,26},{12,28},{14,30},{16,20},{18... | collective-permute-start | bytes 393224 | tf_op jit(solution)/shard_map/ppermute | solution.py:398
  9.4 3.3 %collective-permute-start.3 = (bf16[3,64,256]{2,1,0:T(8,128)(2,1)S(1)}, bf16[3,64,256]{2,1,0:T(8,128)(2,1)S(1)}, u32[]{:S(2)}, u32[]{:S(2)}) collective-permute-start(bf16[3,64,256]{2,1,0:T(8,128)(2,1)S(1)} %get-tuple-element.30.refs_4_.refs_0_), channel_id=1, source_target_pairs={{0,8},{8,0},{16,24},{24,16},{1,9},{9,1},{17,25},{25,17},{2,10},{10... | collective-permute-start | bytes 294920 | tf_op jit(solution)/shard_map/ppermute | solution.py:35
  10.5 2.4 %collective-permute-start.5 = (bf16[3,64,256]{2,1,0:T(8,128)(2,1)S(1)}, bf16[3,64,256]{2,1,0:T(8,128)(2,1)S(1)}, u32[]{:S(2)}, u32[]{:S(2)}) collective-permute-start(bf16[3,64,256]{2,1,0:T(8,128)(2,1)S(1)} %collective-permute-done.4.refs_3_.refs_6_.refs_2_), channel_id=1, source_target_pairs={{0,8},{8,0},{16,24},{24,16},{1,9},{9,1},{17,25},{25,17},{2,10},{10... | collective-permute-start | bytes 294920 | tf_op jit(solution)/shard_map/ppermute | solution.py:35
  10.5 5.7 %collective-permute-start.7 = (bf16[2,2,64,256]{3,2,1,0:T(8,128)(2,1)S(1)}, bf16[2,2,64,256]{3,2,1,0:T(8,128)(2,1)S(1)}, u32[]{:S(2)}, u32[]{:S(2)}) collective-permute-start(bf16[2,2,64,256]{3,2,1,0:T(8,128)(2,1)S(1)} %pack_blocks.3.refs_2_.refs_4_), channel_id=1, source_target_pairs={{0,16},{2,18},{4,20},{6,22},{8,10},{10,8},{12,14},{14,12},{16,0},{... | collective-permute-start | bytes 393224 | tf_op jit(solution)/shard_map/ppermute | solution.py:398
  12.9 6.2 %collective-permute-start.6 = (bf16[2,2,64,256]{3,2,1,0:T(8,128)(2,1)S(1)}, bf16[2,2,64,256]{3,2,1,0:T(8,128)(2,1)S(1)}, u32[]{:S(2)}, u32[]{:S(2)}) collective-permute-start(bf16[2,2,64,256]{3,2,1,0:T(8,128)(2,1)S(1)} %pack_blocks.4), channel_id=1, source_target_pairs={{0,16},{2,18},{4,20},{6,22},{8,10},{10,8},{12,14},{14,12},{16,0},{... | collective-permute-start | bytes 393224 | tf_op jit(solution)/shard_map/ppermute | solution.py:398
  16.2 3.7 %collective-permute-start.9 = (bf16[2,2,64,256]{3,2,1,0:T(8,128)(2,1)S(1)}, bf16[2,2,64,256]{3,2,1,0:T(8,128)(2,1)S(1)}, u32[]{:S(2)}, u32[]{:S(2)}) collective-permute-start(bf16[2,2,64,256]{3,2,1,0:T(8,128)(2,1)S(1)} %collective-permute-done.1.refs_0_.refs_2_.refs_5_), channel_id=1, source_target_pairs={{0,8},{2,10},{4,12},{6,14},{8,0},{10,2},{12,4},{14,6},{16,24},{18,... | collective-permute-start | bytes 393224 | tf_op jit(solution)/shard_map/ppermute | solution.py:35
  16.2 3.7 %collective-permute-start.10 = (bf16[2,2,64,256]{3,2,1,0:T(8,128)(2,1)S(1)}, bf16[2,2,64,256]{3,2,1,0:T(8,128)(2,1)S(1)}, u32[]{:S(2)}, u32[]{:S(2)}) collective-permute-start(bf16[2,2,64,256]{3,2,1,0:T(8,128)(2,1)S(1)} %collective-permute-done.7.refs_3_.refs_6_), channel_id=1, source_target_pairs={{0,8},{2,10},{4,12},{6,14},{8,0},{10,2},{12,4},{14,6},{16,24},{18,... | collective-permute-start | bytes 393224 | tf_op jit(solution)/shard_map/ppermute | solution.py:35
  19.2 1.9 %collective-permute-start.8 = (bf16[2,2,64,256]{3,2,1,0:T(8,128)(2,1)S(1)}, bf16[2,2,64,256]{3,2,1,0:T(8,128)(2,1)S(1)}, u32[]{:S(2)}, u32[]{:S(2)}) collective-permute-start(bf16[2,2,64,256]{3,2,1,0:T(8,128)(2,1)S(1)} %pack_blocks.5), channel_id=1, source_target_pairs={{0,8},{2,10},{4,12},{6,14},{8,0},{10,2},{12,4},{14,6},{16,24},{18,... | collective-permute-start | bytes 393224 | tf_op jit(solution)/shard_map/ppermute | solution.py:35
  22.0 3.8 %collective-permute-start.11 = (f32[1,8]{1,0:T(1,128)S(1)}, f32[1,8]{1,0:T(1,128)S(1)}, u32[]{:S(2)}, u32[]{:S(2)}) collective-permute-start(f32[1,8]{1,0:T(1,128)S(1)} %get-tuple-element.48), channel_id=1, source_target_pairs={{0,1},{1,0},{2,3},{3,2},{4,5},{5,4},{6,7},{7,6},{8,9},{9,8},{10,11... | collective-permute-start | bytes 104 | tf_op jit(solution)/shard_map/ppermute | solution.py:35

commit v10 on v8

--- a/solution.py
+++ b/solution.py
@@ -12,6 +12,7 @@
 GROUP = 8
 SUBLANES = 8
 NEG_FILL = -1e30
+GROUPS = 4
 SCALE = HEADDIM ** -0.5 * math.log2(math.e)
 ROW_TILE = 256
 VMEM_LIMIT = 28 * 1024 * 1024
@@ -282,76 +283,118 @@
     )(*operands, *after)
 
 
-def placed_blocks(sizes, arrays, refs, kv_ref):
+def rank_of(owner, sizes):
+    _, along, across, core = prompt_bits(*sizes)
+    low = lax.rem(owner, 2 * along)
+    side = lax.rem(owner // across, 2)
+    rank = lax.rem(owner, core) // 2 + (lax.rem(owner, across) // core) * (core // 2)
+    rank += (owner // (2 * across)) * core
+    return 2 * side + low, rank
+
+
+def placed_blocks(sizes, arrays, refs, kv_ref, grouped):
     owners = prompt_owners(*sizes)
+    count = sizes[0] * sizes[1] // GROUPS
     for ref, array in zip(refs, arrays):
         rows = ref.shape[2]
         for index, owner in enumerate(owners[array]):
-            at = pl.ds(pl.multiple_of(owner * rows, rows), rows)
+            group, rank = rank_of(owner, sizes)
+            place = (group * count + rank) if grouped else rank
+            at = pl.ds(pl.multiple_of(place * rows, rows), rows)
             kv_ref[0, at, :] = ref[index, 0]
             kv_ref[1, at, :] = ref[index, 1]
 
 
-def arrange_kernel(sizes, arrays, masks, *refs):
-    pays, blocks = refs[: len(masks)], refs[len(masks) : -2]
-    kv_ref, query_ref = refs[-2:]
-    placed_blocks(sizes, arrays, blocks, kv_ref)
+def late_group(sizes):
+    return rank_of(prompt_place(sizes[1]), sizes)[0] ^ (GROUPS - 1)
+
+
+def step_parts(query_ref, kv_ref, at, allowed):
+    parts = []
+    for head in range(kv_ref.shape[2] // HEADDIM):
+        columns = slice(head * HEADDIM, (head + 1) * HEADDIM)
+        queries = query_ref[head].astype(jnp.bfloat16)
+        widened = with_ones(kv_ref[1, at, columns])
+        parts.append(absorb(queries, kv_ref[0, at, columns], widened, allowed, None))
+    return parts
+
+
+def early_step_kernel(sizes, arrays, masks, ends_ref, *refs):
+    pays, blocks = refs[: len(masks)], refs[len(masks) : -4]
+    query_ref, peak_ref, sum_ref, kv_ref = refs[-4:]
+    placed_blocks(sizes, arrays, blocks, kv_ref, True)
     rows, width = pays[0].shape[1:]
-    free = kv_ref.shape[1] - rows * len(masks)
+    own_count = rows * len(masks)
+    free = kv_ref.shape[1] - own_count
     picked = jnp.zeros((rows, width), jnp.float32)
     for ref, mask in zip(pays, masks):
         at = pl.ds(pl.multiple_of(free + (lax.axis_index("ctx") ^ mask) * rows, rows), rows)
         kv_ref[0, at, :] = ref[0]
         kv_ref[1, at, :] = ref[1]
         picked += ref[2].astype(jnp.float32)
-    heads = query_ref.shape[0]
-    steps = rows * width // (heads * HEADDIM)
-    for head in range(heads):
-        group, lane = divmod(head * HEADDIM, width)
-        query_ref[head] = picked[group * steps : (group + 1) * steps, lane : lane + HEADDIM]
-
-
-def arranged(sizes, arrays, heads, steps, pays, blocks):
+    steps = ends_ref.shape[1]
+    for head in range(width // HEADDIM):
+        places = [divmod(h * HEADDIM, width) for h in range(head * GROUP, (head + 1) * GROUP)]
+        query_ref[head] = jnp.concatenate(
+            [picked[a * steps : (a + 1) * steps, b : b + HEADDIM] for a, b in places], axis=0
+        )
+    row_pos = jnp.concatenate([column_of(ends_ref[...])] * GROUP, axis=0)
+    own_pos = lax.broadcasted_iota(jnp.int32, (1, own_count), 1)
+    late = late_group(sizes)
+    group_count = free // GROUPS
+    sources = [(GROUPS, slice(free, None), own_pos <= row_pos)]
+    for other in range(1, GROUPS):
+        group = late ^ other
+        at = pl.ds(pl.multiple_of(group * group_count, group_count), group_count)
+        sources.append((group, at, None))
+    for group, at, allowed in sources:
+        for head, (peak, blended) in enumerate(step_parts(query_ref, kv_ref, at, allowed)):
+            peak_ref[group, head] = peak
+            sum_ref[group, head] = blended
+
+
+def early_steps(sizes, arrays, ends, heads, pays, blocks):
     rows, width = pays[0][0].shape[1:]
     count = rows * sizes[0] * (sizes[1] + 1)
+    kinds = width // HEADDIM
+    stacked = heads // kinds * ends.shape[1]
     return pl.pallas_call(
-        functools.partial(arrange_kernel, sizes, arrays, [mask for _, mask in pays]),
+        functools.partial(early_step_kernel, sizes, arrays, [mask for _, mask in pays]),
         out_shape=(
-            jax.ShapeDtypeStruct((2, count, width), pays[0][0].dtype),
-            jax.ShapeDtypeStruct((heads, steps, HEADDIM), jnp.float32),
+            jax.ShapeDtypeStruct((kinds, stacked, HEADDIM), jnp.float32),
+            jax.ShapeDtypeStruct((GROUPS + 1, kinds, stacked, HEADDIM), jnp.float32),
+            jax.ShapeDtypeStruct((GROUPS + 1, kinds, stacked, 2 * HEADDIM), jnp.float32),
         ),
-        in_specs=vmem(len(pays) + len(arrays)),
-        out_specs=tuple(vmem(2)),
+        in_specs=vmem(1 + len(pays) + len(arrays)),
+        out_specs=tuple(vmem(3)),
+        scratch_shapes=[pltpu.VMEM((2, count, width), pays[0][0].dtype)],
         compiler_params=PARAMS,
-        name="arrange_blocks",
-    )(*(b for b, _ in pays), *(blocks[index] for index in arrays))
-
-
-def step_kernel(sizes, arrays, ends_ref, head_ref, lengths_ref, query_ref, _, *refs):
-    blocks = refs[:-2]
+        name="early_steps",
+    )(ends, *(b for b, _ in pays), *(blocks[index] for index in arrays))
+
+
+def step_kernel(sizes, arrays, ends_ref, head_ref, lengths_ref, query_ref, peak_ref, sum_ref, *refs):
+    blocks = refs[: len(arrays)]
     logit_ref, kv_ref = refs[-2:]
-    placed_blocks(sizes, arrays, blocks, kv_ref)
-    own_count = blocks[0].shape[2] * sizes[0]
-    free = kv_ref.shape[1] - own_count
+    placed_blocks(sizes, arrays, blocks, kv_ref, False)
+    late = late_group(sizes)
     steps = ends_ref.shape[1]
     ends = column_of(ends_ref[...])
-    own_pos = lax.broadcasted_iota(jnp.int32, (1, own_count), 1)
-    row_pos = jnp.concatenate([ends] * GROUP, axis=0)
+    alive = ends < lengths_ref[:, :1]
     total = jnp.zeros((steps, HEADDIM), jnp.float32)
-    for head in range(kv_ref.shape[2] // HEADDIM):
-        columns = slice(head * HEADDIM, (head + 1) * HEADDIM)
-        heads = range(head * GROUP, (head + 1) * GROUP)
-        queries = jnp.concatenate([query_ref[h] for h in heads], axis=0)
-        scores = product(queries.astype(jnp.bfloat16), kv_ref[0, :, columns])
-        bound = jnp.where(own_pos <= row_pos, scores[:, free:], NEG_FILL)
-        scores = jnp.concatenate([scores[:, :free], bound], axis=1)
-        peak = jnp.max(scores, axis=1, keepdims=True)
-        weights = jnp.exp2((scores - peak) * SCALE).astype(jnp.bfloat16)
-        blended = jnp.dot(weights, with_ones(kv_ref[1, :, columns]), preferred_element_type=jnp.float32)
+    for head, newest in enumerate(step_parts(query_ref, kv_ref, slice(None), None)):
+        parts = [
+            tuple(jnp.where(late == group, new, ref[group, head]) for new, ref in zip(newest, (peak_ref, sum_ref)))
+            for group in range(GROUPS)
+        ]
+        parts.append((peak_ref[GROUPS, head], sum_ref[GROUPS, head]))
+        peak = functools.reduce(jnp.maximum, [part[0] for part in parts])
+        blended = sum(part[1] * spread(jnp.exp2((part[0] - peak) * SCALE), 2 * HEADDIM) for part in parts)
         result = blended[:, :HEADDIM] / blended[:, HEADDIM:]
-        for index, h in enumerate(heads):
-            kept = jnp.where(ends < lengths_ref[:, :1], result[index * steps : (index + 1) * steps], 0.0)
+        for index in range(GROUP):
+            kept = jnp.where(alive, result[index * steps : (index + 1) * steps], 0.0)
             kept = kept.astype(jnp.bfloat16).astype(jnp.float32)
+            h = head * GROUP + index
             total += kept * head_ref[:, h * HEADDIM : (h + 1) * HEADDIM]
     logits = jnp.sum(total, axis=1, keepdims=True)
     down = lax.broadcasted_iota(jnp.int32, (steps, steps), 0)
@@ -359,20 +402,18 @@
     logit_ref[...] = jnp.sum(jnp.where(down == right, logits, 0.0), axis=0, keepdims=True)
 
 
-def step_shares(sizes, arrays, ends, head, lengths, queries, kv, blocks):
-    scores = queries.shape[0] * queries.shape[1] * kv.shape[1]
+def step_shares(sizes, arrays, ends, head, lengths, early, blocks, after):
+    rows, width = blocks[0].shape[2:]
+    count = rows * sizes[0] * sizes[1] // GROUPS
     return pl.pallas_call(
         functools.partial(step_kernel, sizes, arrays),
-        out_shape=(jax.ShapeDtypeStruct(ends.shape, jnp.float32), like(kv)),
-        in_specs=vmem(5 + len(arrays)),
-        out_specs=tuple(vmem(2)),
-        input_output_aliases={4: 1},
+        out_shape=jax.ShapeDtypeStruct(ends.shape, jnp.float32),
+        in_specs=vmem(6 + len(arrays)) + [pl.BlockSpec(memory_space=pl.ANY)],
+        out_specs=vmem(1)[0],
+        scratch_shapes=[pltpu.VMEM((2, count, width), blocks[0].dtype)],
         compiler_params=PARAMS,
-        cost_estimate=pl.CostEstimate(
-            flops=6 * scores * HEADDIM, bytes_accessed=scores, transcendentals=scores
-        ),
         name="step_logits",
-    )(ends, head, lengths, queries, kv, *(blocks[index] for index in arrays))[0]
+    )(ends, head, lengths, *early, *(blocks[index] for index in arrays), after)
 
 
 def per_device(ctx_size, cand_size, prompt_q, prompt_kv, cand_q, cand_kv, cand_lengths, step_ends, reward_head):
@@ -403,15 +444,14 @@
     third = shared_out(held, across, along)
     blocks = [held, second, third, None, across_cores(held), None, None, None]
     state = phase(sizes, [0, 4], q_rows, blocks)
-    fourth = shared_out(packed(second, after=[b for b, _ in pays[1:4]]), across, along)
+    fourth = shared_out(packed(second, after=state[:1] + tuple(b for b, _ in pays[1:4])), across, along)
     blocks[3] = fourth
     blocks[5:7] = across_cores(second), across_cores(third)
     state = phase(sizes, [1, 2], q_rows, blocks, pays=pays, state=state)
+    early_parts = early_steps(sizes, [0, 1, 2, 4, 5, 6], ends, head.shape[1] // HEADDIM, pays, blocks)
     blocks[7] = across_cores(packed(fourth, after=state[:1]))
     state = phase(sizes, [5, 6], q_rows, blocks, state=state)
-    heads = head.shape[1] // HEADDIM
-    kv, queries = arranged(sizes, [0, 1, 2, 4, 5, 6], heads, step_ends.shape[1], pays, blocks)
-    step_logits = step_shares(sizes, [3, 7], ends, head, lengths, queries, kv, blocks)
+    step_logits = step_shares(sizes, [3, 7], ends, head, lengths, early_parts, blocks, state[0])
     cand_out, prompt_out = phase(sizes, [3, 7], q_rows, blocks, state=state, lengths=lengths)
     tp_size = lax.axis_size("tp")
     for bit in high_bits(tp_size, 1):

time: 26.9 us -> 26.4 us (0.981)
  waiting for transfers between devices: 5.3 us -> 2.56 us
  starting transfers between devices: 11.8 us -> 13.5 us
  Pallas kernels: 7.77 us -> 8.29 us
    ppermute x9, waiting for transfers between devices: 3.68 us -> 1.08 us  [flipped(): return lax.ppermute(block, axes, [(i, i ^ bit) for i in range(size)])]
    ppermute x9, starting transfers between devices: 7.78 us -> 9.37 us  [flipped(): return lax.ppermute(block, axes, [(i, i ^ bit) for i in range(size)])]
    pallas_call x2, Pallas kernels: 1.08 us -> 1.55 us  [the longest x1 0.95 us: early_steps(): pl.pallas_call(functools.partial(early_step_kernel, sizes, arrays, [mask...]
  transfers between devices with their start and end apart: 12 -> 12, of which waited for: 5 -> 3; matrix products, arithmetic and copies ran while one was open for 0% -> 0% of each run, Pallas kernels for 25% -> 29%
where the time goes in v10:
time: 26.4 us; the launch traced here: 26.3 us
  starting transfers between devices  13.5 us (51%)
  Pallas kernels  8.29 us (31%)
  waiting for transfers between devices  2.56 us (10%)
  between operations  1.38 us (5%)
  other arithmetic  0.51 us (2%)
    ppermute x9, starting transfers between devices, flipped(): return lax.ppermute(block, axes, [(i, i ^ bit) for i in range(size)])  9.37 us
    pallas_call x4, Pallas kernels, phase(): pl.pallas_call(functools.partial(phase_kernel, sizes, arrays, masks, firs...  5.46 us
    ppermute x3, starting transfers between devices, shared_out(): lax.ppermute(block, PROMPT_AXES, [(i, i ^ (odd if i & core else even)) fo...  4.17 us
    ppermute x3, waiting for transfers between devices, shared_out(): lax.ppermute(block, PROMPT_AXES, [(i, i ^ (odd if i & core else even)) fo...  1.48 us
    pallas_call x1, Pallas kernels, staged(): pl.pallas_call(stage_kernel, out_shape=(like(prompt_q), like(cand_q), lik...  1.24 us
    ppermute x9, waiting for transfers between devices, flipped(): return lax.ppermute(block, axes, [(i, i ^ bit) for i in range(size)])  1.08 us
    pallas_call x1, Pallas kernels, early_steps(): pl.pallas_call(functools.partial(early_step_kernel, sizes, arrays, [mask...  0.95 us
    pallas_call x1, Pallas kernels, step_shares(): pl.pallas_call(functools.partial(step_kernel, sizes, arrays), out_shape=j...  0.6 us
  transfers between devices with their start and end apart: 12, of which 3 were waited for; matrix products, arithmetic and copies ran while one was open for 0% of the time, Pallas kernels for 29%

profile of v10, /device:TPU:0, one launch (start us, length us, event | category | flops | bytes accessed | tf_op | source)
XLA Modules:
  0.0 26.3 jit_solution(13797972672385100536)
XLA Ops:
  0.6 4.1 %collective-permute-start = (bf16[1,2,64,256]{3,2,1,0:T(8,128)(2,1)}, bf16[1,2,64,256]{3,2,1,0:T(8,128)(2,1)S(1)}, u32[]{:S(2)}, u32[]{:S(2)}) collective-permute-start(bf16[1,2,64,256]{3,2,1,0:T(8,128)(2,1)} %bitcast.11), channel_id=1, source_target_pairs={{0,4},{2,6},{4,0},{6,2},{8,12},{10,14},{12,8},{14,10},{16,20},{18,... | collective-permute-start | bytes 196616 | tf_op jit(solution)/shard_map/ppermute | solution.py:36
  4.7 1.2 %stage_operands.1 = (bf16[64,2048]{1,0:T(8,128)(2,1)S(1)}, bf16[64,2048]{1,0:T(8,128)(2,1)S(1)}, bf16[2,64,256]{2,1,0:T(8,128)(2,1)S(1)}, bf16[3,64,256]{2,1,0:T...) custom-call(bf16[64,2048]{1,0:T(8,128)(2,1)} %prompt_q.1, bf16[64,2048]{1,0:T(8,128)(2,1)} %bitcast.9, ...), custom_call_target="tpu_custom_call" | custom-call | tf_op jit(solution)/shard_map/stage_operands/pallas_call | solution.py:124
  6.0 1.6 %collective-permute-start.4 = (bf16[3,64,256]{2,1,0:T(8,128)(2,1)S(1)}, bf16[3,64,256]{2,1,0:T(8,128)(2,1)S(1)}, u32[]{:S(2)}, u32[]{:S(2)}) collective-permute-start(bf16[3,64,256]{2,1,0:T(8,128)(2,1)S(1)} %get-tuple-element.30.refs_4_.refs_0_), channel_id=1, source_target_pairs={{0,16},{8,24},{16,0},{24,8},{1,17},{9,25},{17,1},{25,9},{2,18},{10... | collective-permute-start | bytes 294920 | tf_op jit(solution)/shard_map/ppermute | solution.py:36
  7.6 1.0 %collective-permute-done.refs_1_ = bf16[1,2,64,256]{3,2,1,0:T(8,128)(2,1)S(1)} collective-permute-done((bf16[1,2,64,256]{3,2,1,0:T(8,128)(2,1)}, bf16[1,2,64,256]{3,2,1,0:T(8,128)(2,1)S(1)}, u32[]{:S(2)}, u32[]{:S(2)}) %collective-permute-start) | collective-permute-done | bytes 65568 | tf_op jit(solution)/shard_map/ppermute | solution.py:36
  8.6 0.1 collective-permute-start.2
  8.7 0.7 %collective-permute-start.1 = (bf16[2,2,64,256]{3,2,1,0:T(8,128)(2,1)S(1)}, bf16[2,2,64,256]{3,2,1,0:T(8,128)(2,1)S(1)}, u32[]{:S(2)}, u32[]{:S(2)}) collective-permute-start(bf16[2,2,64,256]{3,2,1,0:T(8,128)(2,1)S(1)} %pack_blocks.3.refs_2_.refs_4_), channel_id=1, source_target_pairs={{0,2},{2,0},{4,6},{6,4},{8,24},{10,26},{12,28},{14,30},{16,18},{18... | collective-permute-start | bytes 393224 | tf_op jit(solution)/shard_map/ppermute | solution.py:434
  9.4 1.2 %collective-permute-start.3 = (bf16[3,64,256]{2,1,0:T(8,128)(2,1)S(1)}, bf16[3,64,256]{2,1,0:T(8,128)(2,1)S(1)}, u32[]{:S(2)}, u32[]{:S(2)}) collective-permute-start(bf16[3,64,256]{2,1,0:T(8,128)(2,1)S(1)} %get-tuple-element.30.refs_4_.refs_0_), channel_id=1, source_target_pairs={{0,8},{8,0},{16,24},{24,16},{1,9},{9,1},{17,25},{25,17},{2,10},{10... | collective-permute-start | bytes 294920 | tf_op jit(solution)/shard_map/ppermute | solution.py:36
  10.6 0.0 collective-permute-done.4.refs_3_.refs_6_.refs_2_
  10.7 0.0 collective-permute-start.5
  10.7 1.5 %collective-permute-start.7 = (bf16[2,2,64,256]{3,2,1,0:T(8,128)(2,1)S(1)}, bf16[2,2,64,256]{3,2,1,0:T(8,128)(2,1)S(1)}, u32[]{:S(2)}, u32[]{:S(2)}) collective-permute-start(bf16[2,2,64,256]{3,2,1,0:T(8,128)(2,1)S(1)} %pack_blocks.3.refs_2_.refs_4_), channel_id=1, source_target_pairs={{0,16},{2,18},{4,20},{6,22},{8,10},{10,8},{12,14},{14,12},{16,0},{... | collective-permute-start | bytes 393224 | tf_op jit(solution)/shard_map/ppermute | solution.py:434
  12.2 0.0 collective-permute-done.2.refs_3_.refs_7_
  12.2 0.9 %attend_0_4.1 = (f32[1024,128]{1,0:T(8,128)S(1)}, f32[1024,256]{1,0:T(8,128)S(1)}, f32[1024,128]{1,0:T(8,128)S(1)}, f32[1024,256]{1,0:T(8,128)S(1)}) custom-call(bf16[64,2048]{1,0:T(8,128)(2,1)S(1)} %get-tuple-element.26.refs_0_, bf16[64,2048]{1,0:T(8,128)(2,1)S(1)} %get-tuple-element.27.refs_1_, bf16[2,2,64,256]{3,2,1,0:T(8,128)(2,1)S(1)} %pack_blocks.3.refs_2_.refs_4_, ...), custom_call_target="tpu_custom_call" | custom-call | flops 402653184 | bytes 524288 | tf_op jit(solution)/shard_map/attend_0_4/pallas_call | solution.py:273
  13.1 0.0 collective-permute-done.3.refs_2_.refs_5_.refs_1_
  13.1 0.6 %collective-permute-done.1.refs_0_.refs_2_.refs_5_ = bf16[2,2,64,256]{3,2,1,0:T(8,128)(2,1)S(1)} collective-permute-done((bf16[2,2,64,256]{3,2,1,0:T(8,128)(2,1)S(1)}, bf16[2,2,64,256]{3,2,1,0:T(8,128)(2,1)S(1)}, u32[]{:S(2)}, u32[]{:S(2)}) %collective-permute-start.1) | collective-permute-done | bytes 131104 | tf_op jit(solution)/shard_map/ppermute | solution.py:434
  13.7 0.0 collective-permute-done.5.refs_4_.refs_7_.refs_3_
  13.7 1.9 %collective-permute-start.6 = (bf16[2,2,64,256]{3,2,1,0:T(8,128)(2,1)S(1)}, bf16[2,2,64,256]{3,2,1,0:T(8,128)(2,1)S(1)}, u32[]{:S(2)}, u32[]{:S(2)}) collective-permute-start(bf16[2,2,64,256]{3,2,1,0:T(8,128)(2,1)S(1)} %pack_blocks.4), channel_id=1, source_target_pairs={{0,16},{2,18},{4,20},{6,22},{8,10},{10,8},{12,14},{14,12},{16,0},{... | collective-permute-start | bytes 393224 | tf_op jit(solution)/shard_map/ppermute | solution.py:434
  15.7 0.0 collective-permute-start.9
  15.7 0.0 collective-permute-done.7.refs_3_.refs_6_
  15.7 0.5 %collective-permute-start.10 = (bf16[2,2,64,256]{3,2,1,0:T(8,128)(2,1)S(1)}, bf16[2,2,64,256]{3,2,1,0:T(8,128)(2,1)S(1)}, u32[]{:S(2)}, u32[]{:S(2)}) collective-permute-start(bf16[2,2,64,256]{3,2,1,0:T(8,128)(2,1)S(1)} %collective-permute-done.7.refs_3_.refs_6_), channel_id=1, source_target_pairs={{0,8},{2,10},{4,12},{6,14},{8,0},{10,2},{12,4},{14,6},{16,24},{18,... | collective-permute-start | bytes 393224 | tf_op jit(solution)/shard_map/ppermute | solution.py:36
  16.2 1.7 %attend_1_2.1 = (f32[1024,128]{1,0:T(8,128)S(1)}, f32[1024,256]{1,0:T(8,128)S(1)}, f32[1024,128]{1,0:T(8,128)S(1)}, f32[1024,256]{1,0:T(8,128)S(1)}) custom-call(bf16[64,2048]{1,0:T(8,128)(2,1)S(1)} %get-tuple-element.26.refs_0_, bf16[64,2048]{1,0:T(8,128)(2,1)S(1)} %get-tuple-element.27.refs_1_, ...), custom_call_target="tpu_custom_call" | custom-call | flops 402653184 | bytes 524288 | tf_op jit(solution)/shard_map/attend_1_2/pallas_call | solution.py:273
  17.9 0.9 %collective-permute-done.6.refs_0_.refs_2_ = bf16[2,2,64,256]{3,2,1,0:T(8,128)(2,1)S(1)} collective-permute-done((bf16[2,2,64,256]{3,2,1,0:T(8,128)(2,1)S(1)}, bf16[2,2,64,256]{3,2,1,0:T(8,128)(2,1)S(1)}, u32[]{:S(2)}, u32[]{:S(2)}) %collective-permute-start.6) | collective-permute-done | bytes 131104 | tf_op jit(solution)/shard_map/ppermute | solution.py:434
  18.8 0.1 collective-permute-start.8
  19.5 0.0 collective-permute-done.9.refs_2_.refs_8_
  19.5 0.0 collective-permute-done.10.refs_3_.refs_9_
  19.5 0.9 %early_steps.1 = (f32[2,64,128]{2,1,0:T(8,128)S(1)}, f32[5,2,64,128]{3,2,1,0:T(8,128)S(1)}, f32[5,2,64,256]{3,2,1,0:T(8,128)S(1)}) custom-call(s32[1,8]{1,0:T(1,128)S(1)} %get-tuple-element.44.ends_ref, bf16[3,64,256]{2,1,0:T(8,128)(2,1)S(1)} %get-tuple-element.30.refs_4_.refs_0_, bf16[3,64,256]{2,1,0:T(8,128)(2,1)S(1)} %collective-permute-done.3.refs_2_.refs_5_.refs_1_, ...), custom_call_target="tpu_custom_call" | custom-call | tf_op jit(solution)/shard_map/early_steps/pallas_call | solution.py:361
  20.5 1.0 %attend_5_6.1 = (f32[1024,128]{1,0:T(8,128)S(1)}, f32[1024,256]{1,0:T(8,128)S(1)}, f32[1024,128]{1,0:T(8,128)S(1)}, f32[1024,256]{1,0:T(8,128)S(1)}) custom-call(bf16[64,2048]{1,0:T(8,128)(2,1)S(1)} %get-tuple-element.26.refs_0_, bf16[64,2048]{1,0:T(8,128)(2,1)S(1)} %get-tuple-element.27.refs_1_, ...), custom_call_target="tpu_custom_call" | custom-call | flops 402653184 | bytes 524288 | tf_op jit(solution)/shard_map/attend_5_6/pallas_call | solution.py:273
  21.5 0.0 collective-permute-done.8.refs_3_.refs_1_
  21.5 0.6 %step_logits.1 = f32[1,8]{1,0:T(1,128)S(1)} custom-call(s32[1,8]{1,0:T(1,128)S(1)} %get-tuple-element.44.ends_ref, f32[1,2048]{1,0:T(1,128)S(1)} %get-tuple-element.45.head_ref, s32[1,128]{1,0:T(1,128)S(1)} %broadcast_in_dim.24.refs_4_.lengths_ref, f32[2,64,128]{2,1,0:T(8,128)S(1)} %get-tuple-element.46.query_ref, ...), custom_call_target="tpu_custom_call" | custom-call | tf_op jit(solution)/shard_map/step_logits/pallas_call | solution.py:408
  22.1 1.8 %collective-permute-start.11 = (f32[1,8]{1,0:T(1,128)S(1)}, f32[1,8]{1,0:T(1,128)S(1)}, u32[]{:S(2)}, u32[]{:S(2)}) collective-permute-start(f32[1,8]{1,0:T(1,128)S(1)} %step_logits.1), channel_id=1, source_target_pairs={{0,1},{1,0},{2,3},{3,2},{4,5},{5,4},{6,7},{7,6},{8,9},{9,8},{10,11... | collective-permute-start | bytes 104 | tf_op jit(solution)/shard_map/ppermute | solution.py:36
  23.9 1.8 %attend_3_7.1 = (bf16[64,2048]{1,0:T(8,128)(2,1)}, bf16[64,2048]{1,0:T(8,128)(2,1)}) custom-call(bf16[64,2048]{1,0:T(8,128)(2,1)S(1)} %get-tuple-element.26.refs_0_, bf16[64,2048]{1,0:T(8,128)(2,1)S(1)} %get-tuple-element.27.refs_1_, bf16[2,2,64,256]{3,2,1,0:T(8,128)(2,1)S(1)} %collective-permute-done.6.refs_0_.refs_2_, ...), custom_call_target="tpu_custom_call" | custom-call | flops 402653184 | bytes 524288 | tf_op jit(solution)/shard_map/attend_3_7/pallas_call | solution.py:273
  25.8 0.0 collective-permute-done.11
  25.8 0.5 %add.3 = f32[1,8]{1,0:T(1,128)} add(f32[1,8]{1,0:T(1,128)S(1)} %step_logits.1, f32[1,8]{1,0:T(1,128)S(1)} %collective-permute-done.11) | non-fusion elementwise | flops 8 | bytes 96 | tf_op jit(solution)/shard_map/add | solution.py:458
  (4 shorter events, 0.0 us)
Async XLA Ops:
  0.6 8.0 %collective-permute-start = (bf16[1,2,64,256]{3,2,1,0:T(8,128)(2,1)}, bf16[1,2,64,256]{3,2,1,0:T(8,128)(2,1)S(1)}, u32[]{:S(2)}, u32[]{:S(2)}) collective-permute-start(bf16[1,2,64,256]{3,2,1,0:T(8,128)(2,1)} %bitcast.11), channel_id=1, source_target_pairs={{0,4},{2,6},{4,0},{6,2},{8,12},{10,14},{12,8},{14,10},{16,20},{18,... | collective-permute-start | bytes 196616 | tf_op jit(solution)/shard_map/ppermute | solution.py:36
  6.0 4.7 %collective-permute-start.4 = (bf16[3,64,256]{2,1,0:T(8,128)(2,1)S(1)}, bf16[3,64,256]{2,1,0:T(8,128)(2,1)S(1)}, u32[]{:S(2)}, u32[]{:S(2)}) collective-permute-start(bf16[3,64,256]{2,1,0:T(8,128)(2,1)S(1)} %get-tuple-element.30.refs_4_.refs_0_), channel_id=1, source_target_pairs={{0,16},{8,24},{16,0},{24,8},{1,17},{9,25},{17,1},{25,9},{2,18},{10... | collective-permute-start | bytes 294920 | tf_op jit(solution)/shard_map/ppermute | solution.py:36
  8.6 3.6 %collective-permute-start.2 = (bf16[2,2,64,256]{3,2,1,0:T(8,128)(2,1)S(1)}, bf16[2,2,64,256]{3,2,1,0:T(8,128)(2,1)S(1)}, u32[]{:S(2)}, u32[]{:S(2)}) collective-permute-start(bf16[2,2,64,256]{3,2,1,0:T(8,128)(2,1)S(1)} %pack_blocks.3.refs_2_.refs_4_), channel_id=1, source_target_pairs={{0,8},{2,10},{4,12},{6,14},{8,0},{10,2},{12,4},{14,6},{16,24},{18,... | collective-permute-start | bytes 393224 | tf_op jit(solution)/shard_map/ppermute | solution.py:36
  8.7 5.0 %collective-permute-start.1 = (bf16[2,2,64,256]{3,2,1,0:T(8,128)(2,1)S(1)}, bf16[2,2,64,256]{3,2,1,0:T(8,128)(2,1)S(1)}, u32[]{:S(2)}, u32[]{:S(2)}) collective-permute-start(bf16[2,2,64,256]{3,2,1,0:T(8,128)(2,1)S(1)} %pack_blocks.3.refs_2_.refs_4_), channel_id=1, source_target_pairs={{0,2},{2,0},{4,6},{6,4},{8,24},{10,26},{12,28},{14,30},{16,18},{18... | collective-permute-start | bytes 393224 | tf_op jit(solution)/shard_map/ppermute | solution.py:434
  9.4 3.7 %collective-permute-start.3 = (bf16[3,64,256]{2,1,0:T(8,128)(2,1)S(1)}, bf16[3,64,256]{2,1,0:T(8,128)(2,1)S(1)}, u32[]{:S(2)}, u32[]{:S(2)}) collective-permute-start(bf16[3,64,256]{2,1,0:T(8,128)(2,1)S(1)} %get-tuple-element.30.refs_4_.refs_0_), channel_id=1, source_target_pairs={{0,8},{8,0},{16,24},{24,16},{1,9},{9,1},{17,25},{25,17},{2,10},{10... | collective-permute-start | bytes 294920 | tf_op jit(solution)/shard_map/ppermute | solution.py:36
  10.7 3.1 %collective-permute-start.5 = (bf16[3,64,256]{2,1,0:T(8,128)(2,1)S(1)}, bf16[3,64,256]{2,1,0:T(8,128)(2,1)S(1)}, u32[]{:S(2)}, u32[]{:S(2)}) collective-permute-start(bf16[3,64,256]{2,1,0:T(8,128)(2,1)S(1)} %collective-permute-done.4.refs_3_.refs_6_.refs_2_), channel_id=1, source_target_pairs={{0,8},{8,0},{16,24},{24,16},{1,9},{9,1},{17,25},{25,17},{2,10},{10... | collective-permute-start | bytes 294920 | tf_op jit(solution)/shard_map/ppermute | solution.py:36
  10.7 5.0 %collective-permute-start.7 = (bf16[2,2,64,256]{3,2,1,0:T(8,128)(2,1)S(1)}, bf16[2,2,64,256]{3,2,1,0:T(8,128)(2,1)S(1)}, u32[]{:S(2)}, u32[]{:S(2)}) collective-permute-start(bf16[2,2,64,256]{3,2,1,0:T(8,128)(2,1)S(1)} %pack_blocks.3.refs_2_.refs_4_), channel_id=1, source_target_pairs={{0,16},{2,18},{4,20},{6,22},{8,10},{10,8},{12,14},{14,12},{16,0},{... | collective-permute-start | bytes 393224 | tf_op jit(solution)/shard_map/ppermute | solution.py:434
  13.7 5.0 %collective-permute-start.6 = (bf16[2,2,64,256]{3,2,1,0:T(8,128)(2,1)S(1)}, bf16[2,2,64,256]{3,2,1,0:T(8,128)(2,1)S(1)}, u32[]{:S(2)}, u32[]{:S(2)}) collective-permute-start(bf16[2,2,64,256]{3,2,1,0:T(8,128)(2,1)S(1)} %pack_blocks.4), channel_id=1, source_target_pairs={{0,16},{2,18},{4,20},{6,22},{8,10},{10,8},{12,14},{14,12},{16,0},{... | collective-permute-start | bytes 393224 | tf_op jit(solution)/shard_map/ppermute | solution.py:434
  15.7 3.9 %collective-permute-start.9 = (bf16[2,2,64,256]{3,2,1,0:T(8,128)(2,1)S(1)}, bf16[2,2,64,256]{3,2,1,0:T(8,128)(2,1)S(1)}, u32[]{:S(2)}, u32[]{:S(2)}) collective-permute-start(bf16[2,2,64,256]{3,2,1,0:T(8,128)(2,1)S(1)} %collective-permute-done.1.refs_0_.refs_2_.refs_5_), channel_id=1, source_target_pairs={{0,8},{2,10},{4,12},{6,14},{8,0},{10,2},{12,4},{14,6},{16,24},{18,... | collective-permute-start | bytes 393224 | tf_op jit(solution)/shard_map/ppermute | solution.py:36
  15.7 3.9 %collective-permute-start.10 = (bf16[2,2,64,256]{3,2,1,0:T(8,128)(2,1)S(1)}, bf16[2,2,64,256]{3,2,1,0:T(8,128)(2,1)S(1)}, u32[]{:S(2)}, u32[]{:S(2)}) collective-permute-start(bf16[2,2,64,256]{3,2,1,0:T(8,128)(2,1)S(1)} %collective-permute-done.7.refs_3_.refs_6_), channel_id=1, source_target_pairs={{0,8},{2,10},{4,12},{6,14},{8,0},{10,2},{12,4},{14,6},{16,24},{18,... | collective-permute-start | bytes 393224 | tf_op jit(solution)/shard_map/ppermute | solution.py:36
  18.8 2.7 %collective-permute-start.8 = (bf16[2,2,64,256]{3,2,1,0:T(8,128)(2,1)S(1)}, bf16[2,2,64,256]{3,2,1,0:T(8,128)(2,1)S(1)}, u32[]{:S(2)}, u32[]{:S(2)}) collective-permute-start(bf16[2,2,64,256]{3,2,1,0:T(8,128)(2,1)S(1)} %pack_blocks.5), channel_id=1, source_target_pairs={{0,8},{2,10},{4,12},{6,14},{8,0},{10,2},{12,4},{14,6},{16,24},{18,... | collective-permute-start | bytes 393224 | tf_op jit(solution)/shard_map/ppermute | solution.py:36
  22.1 3.7 %collective-permute-start.11 = (f32[1,8]{1,0:T(1,128)S(1)}, f32[1,8]{1,0:T(1,128)S(1)}, u32[]{:S(2)}, u32[]{:S(2)}) collective-permute-start(f32[1,8]{1,0:T(1,128)S(1)} %step_logits.1), channel_id=1, source_target_pairs={{0,1},{1,0},{2,3},{3,2},{4,5},{5,4},{6,7},{7,6},{8,9},{9,8},{10,11... | collective-permute-start | bytes 104 | tf_op jit(solution)/shard_map/ppermute | solution.py:36

commit v11 on v10

--- a/solution.py
+++ b/solution.py
@@ -12,7 +12,9 @@
 GROUP = 8
 SUBLANES = 8
 NEG_FILL = -1e30
-GROUPS = 4
+GROUPS = 8
+EARLY_GROUPS = 0, 1, 2, 4
+LATE_GROUPS = 3, 5, 6, 7
 SCALE = HEADDIM ** -0.5 * math.log2(math.e)
 ROW_TILE = 256
 VMEM_LIMIT = 28 * 1024 * 1024
@@ -83,16 +85,17 @@
     return blocks
 
 
-def stage_kernel(prompt_q, cand_q, prompt_kv, cand_kv, ends, head, *refs):
-    q_out, cand_out, own_out, pay_out, ends_out, head_out, sems = refs
+def stage_kernel(length_ref, prompt_q, cand_q, prompt_kv, cand_kv, ends, head, *refs):
+    q_out, cand_out, kv_out, pay_out, ends_out, head_out, length_out, length_here, sems = refs
     steps = ends.shape[1]
     pairs = [
         (cand_q, cand_out),
         (ends, ends_out),
-        (prompt_kv, own_out),
         (cand_kv, pay_out.at[0:2]),
+        (prompt_kv, kv_out),
         (prompt_q, q_out),
         (head, head_out),
+        (length_ref, length_here),
     ]
     copies = [pltpu.make_async_copy(a, b, sems.at[i]) for i, (a, b) in enumerate(pairs)]
     for copy in copies:
@@ -109,6 +112,7 @@
     pay_out[2] = jnp.concatenate(pieces, axis=0).astype(jnp.bfloat16)
     for copy in copies[2:]:
         copy.wait()
+    length_out[...] = jnp.full(length_out.shape, length_here[0], jnp.int32)
 
 
 def column_of(row):
@@ -118,18 +122,20 @@
     return jnp.sum(jnp.where(down == right, row, 0), axis=1, keepdims=True)
 
 
-def staged(prompt_q, cand_q, prompt_kv, cand_kv, ends, head):
+def staged(length, prompt_q, cand_q, prompt_kv, cand_kv, ends, head):
     arrays = (prompt_q, cand_q, prompt_kv, cand_kv, ends, head)
-    pay = jax.ShapeDtypeStruct((3,) + cand_kv.shape[1:], cand_kv.dtype)
+    payload = jax.ShapeDtypeStruct((3,) + cand_kv.shape[1:], cand_kv.dtype)
+    lengths = jax.ShapeDtypeStruct((1, HEADDIM), jnp.int32)
     return pl.pallas_call(
         stage_kernel,
-        out_shape=(like(prompt_q), like(cand_q), like(prompt_kv), pay, like(ends), like(head)),
-        in_specs=[pl.BlockSpec(memory_space=pltpu.HBM)] * len(arrays),
-        out_specs=tuple(vmem(6)),
-        scratch_shapes=[pltpu.SemaphoreType.DMA((len(arrays),))],
+        out_shape=(like(prompt_q), like(cand_q), like(prompt_kv), payload, like(ends), like(head), lengths),
+        in_specs=[pl.BlockSpec(memory_space=pl.ANY)]
+        + [pl.BlockSpec(memory_space=pltpu.HBM)] * len(arrays),
+        out_specs=tuple(vmem(7)),
+        scratch_shapes=[pltpu.SMEM((1,), jnp.int32), pltpu.SemaphoreType.DMA((len(arrays) + 1,))],
         compiler_params=PARAMS,
         name="stage_operands",
-    )(*(pltpu.with_memory_space_constraint(a, pltpu.HBM) for a in arrays))
+    )(length, *(pltpu.with_memory_space_constraint(a, pltpu.HBM) for a in arrays))
 
 
 def tiles(q_ref, head):
@@ -285,28 +291,27 @@
 
 def rank_of(owner, sizes):
     _, along, across, core = prompt_bits(*sizes)
-    low = lax.rem(owner, 2 * along)
-    side = lax.rem(owner // across, 2)
-    rank = lax.rem(owner, core) // 2 + (lax.rem(owner, across) // core) * (core // 2)
-    rank += (owner // (2 * across)) * core
-    return 2 * side + low, rank
-
-
-def placed_blocks(sizes, arrays, refs, kv_ref, grouped):
+    group = lax.rem(owner, 2 * along) + 2 * lax.rem(owner // across, 2) + 4 * lax.rem(owner // core, 2)
+    return group, lax.rem(owner, core) // 2 + (owner // (2 * across)) * (core // 2)
+
+
+def placed_blocks(sizes, arrays, refs, kv_ref):
     owners = prompt_owners(*sizes)
     count = sizes[0] * sizes[1] // GROUPS
     for ref, array in zip(refs, arrays):
         rows = ref.shape[2]
         for index, owner in enumerate(owners[array]):
             group, rank = rank_of(owner, sizes)
-            place = (group * count + rank) if grouped else rank
-            at = pl.ds(pl.multiple_of(place * rows, rows), rows)
+            at = pl.ds(pl.multiple_of((group * count + rank) * rows, rows), rows)
             kv_ref[0, at, :] = ref[index, 0]
             kv_ref[1, at, :] = ref[index, 1]
 
 
-def late_group(sizes):
-    return rank_of(prompt_place(sizes[1]), sizes)[0] ^ (GROUPS - 1)
+def group_keys(sizes, others, rows):
+    count = rows * sizes[0] * sizes[1] // GROUPS
+    own = rank_of(prompt_place(sizes[1]), sizes)[0]
+    groups = [own ^ other for other in others]
+    return [(group, pl.ds(pl.multiple_of(group * count, count), count), None) for group in groups]
 
 
 def step_parts(query_ref, kv_ref, at, allowed):
@@ -322,7 +327,7 @@
 def early_step_kernel(sizes, arrays, masks, ends_ref, *refs):
     pays, blocks = refs[: len(masks)], refs[len(masks) : -4]
     query_ref, peak_ref, sum_ref, kv_ref = refs[-4:]
-    placed_blocks(sizes, arrays, blocks, kv_ref, True)
+    placed_blocks(sizes, arrays, blocks, kv_ref)
     rows, width = pays[0].shape[1:]
     own_count = rows * len(masks)
     free = kv_ref.shape[1] - own_count
@@ -340,13 +345,8 @@
         )
     row_pos = jnp.concatenate([column_of(ends_ref[...])] * GROUP, axis=0)
     own_pos = lax.broadcasted_iota(jnp.int32, (1, own_count), 1)
-    late = late_group(sizes)
-    group_count = free // GROUPS
     sources = [(GROUPS, slice(free, None), own_pos <= row_pos)]
-    for other in range(1, GROUPS):
-        group = late ^ other
-        at = pl.ds(pl.multiple_of(group * group_count, group_count), group_count)
-        sources.append((group, at, None))
+    sources += group_keys(sizes, EARLY_GROUPS, rows)
     for group, at, allowed in sources:
         for head, (peak, blended) in enumerate(step_parts(query_ref, kv_ref, at, allowed)):
             peak_ref[group, head] = peak
@@ -373,23 +373,24 @@
     )(ends, *(b for b, _ in pays), *(blocks[index] for index in arrays))
 
 
-def step_kernel(sizes, arrays, ends_ref, head_ref, lengths_ref, query_ref, peak_ref, sum_ref, *refs):
-    blocks = refs[: len(arrays)]
-    logit_ref, kv_ref = refs[-2:]
-    placed_blocks(sizes, arrays, blocks, kv_ref, False)
-    late = late_group(sizes)
+def step_kernel(sizes, arrays, ends_ref, head_ref, lengths_ref, query_ref, *refs):
+    blocks = refs[2 : 2 + len(arrays)]
+    logit_ref, peak_ref, sum_ref, kv_ref = refs[-4:]
+    placed_blocks(sizes, arrays, blocks, kv_ref)
     steps = ends_ref.shape[1]
     ends = column_of(ends_ref[...])
     alive = ends < lengths_ref[:, :1]
+    for group, at, _ in group_keys(sizes, LATE_GROUPS, blocks[0].shape[2]):
+        for head, (peak, blended) in enumerate(step_parts(query_ref, kv_ref, at, None)):
+            peak_ref[group, head] = peak
+            sum_ref[group, head] = blended
     total = jnp.zeros((steps, HEADDIM), jnp.float32)
-    for head, newest in enumerate(step_parts(query_ref, kv_ref, slice(None), None)):
-        parts = [
-            tuple(jnp.where(late == group, new, ref[group, head]) for new, ref in zip(newest, (peak_ref, sum_ref)))
-            for group in range(GROUPS)
-        ]
-        parts.append((peak_ref[GROUPS, head], sum_ref[GROUPS, head]))
-        peak = functools.reduce(jnp.maximum, [part[0] for part in parts])
-        blended = sum(part[1] * spread(jnp.exp2((part[0] - peak) * SCALE), 2 * HEADDIM) for part in parts)
+    for head in range(query_ref.shape[0]):
+        peaks = [peak_ref[group, head] for group in range(GROUPS + 1)]
+        peak = functools.reduce(jnp.maximum, peaks)
+        blended = jnp.zeros(sum_ref.shape[2:], jnp.float32)
+        for group in range(GROUPS + 1):
+            blended += sum_ref[group, head] * spread(jnp.exp2((peaks[group] - peak) * SCALE), 2 * HEADDIM)
         result = blended[:, :HEADDIM] / blended[:, HEADDIM:]
         for index in range(GROUP):
             kept = jnp.where(alive, result[index * steps : (index + 1) * steps], 0.0)
@@ -404,25 +405,25 @@
 
 def step_shares(sizes, arrays, ends, head, lengths, early, blocks, after):
     rows, width = blocks[0].shape[2:]
-    count = rows * sizes[0] * sizes[1] // GROUPS
+    count = rows * sizes[0] * sizes[1]
     return pl.pallas_call(
         functools.partial(step_kernel, sizes, arrays),
-        out_shape=jax.ShapeDtypeStruct(ends.shape, jnp.float32),
+        out_shape=(jax.ShapeDtypeStruct(ends.shape, jnp.float32),) + tuple(like(a) for a in early[1:]),
         in_specs=vmem(6 + len(arrays)) + [pl.BlockSpec(memory_space=pl.ANY)],
-        out_specs=vmem(1)[0],
+        out_specs=tuple(vmem(3)),
         scratch_shapes=[pltpu.VMEM((2, count, width), blocks[0].dtype)],
+        input_output_aliases={4: 1, 5: 2},
         compiler_params=PARAMS,
         name="step_logits",
-    )(ends, head, lengths, *early, *(blocks[index] for index in arrays), after)
+    )(ends, head, lengths, *early, *(blocks[index] for index in arrays), after)[0]
 
 
 def per_device(ctx_size, cand_size, prompt_q, prompt_kv, cand_q, cand_kv, cand_lengths, step_ends, reward_head):
     sizes = ctx_size, cand_size
     size = ctx_size * cand_size
-    prompt_rows, cand_rows, own, payload, ends, head = staged(
-        prompt_q, cand_q[0], prompt_kv, cand_kv[:, 0], step_ends, reward_head[None]
+    prompt_rows, cand_rows, own, payload, ends, head, lengths = staged(
+        cand_lengths, prompt_q, cand_q[0], prompt_kv, cand_kv[:, 0], step_ends, reward_head[None]
     )
-    lengths = jnp.broadcast_to(cand_lengths[None], (1, HEADDIM))
     q_rows = prompt_rows, cand_rows
     pays = gather_cand(payload, ctx_size)
     early, along, across, core = prompt_bits(ctx_size, cand_size)
@@ -448,10 +449,10 @@
     blocks[3] = fourth
     blocks[5:7] = across_cores(second), across_cores(third)
     state = phase(sizes, [1, 2], q_rows, blocks, pays=pays, state=state)
-    early_parts = early_steps(sizes, [0, 1, 2, 4, 5, 6], ends, head.shape[1] // HEADDIM, pays, blocks)
-    blocks[7] = across_cores(packed(fourth, after=state[:1]))
+    early_parts = early_steps(sizes, [0, 1, 2, 4], ends, head.shape[1] // HEADDIM, pays, blocks)
+    blocks[7] = across_cores(packed(fourth, after=[state[0], early_parts[0]]))
     state = phase(sizes, [5, 6], q_rows, blocks, state=state)
-    step_logits = step_shares(sizes, [3, 7], ends, head, lengths, early_parts, blocks, state[0])
+    step_logits = step_shares(sizes, [3, 5, 6, 7], ends, head, lengths, early_parts, blocks, state[0])
     cand_out, prompt_out = phase(sizes, [3, 7], q_rows, blocks, state=state, lengths=lengths)
     tp_size = lax.axis_size("tp")
     for bit in high_bits(tp_size, 1):

time: 26.4 us -> 28.6 us (1.083)
  Pallas kernels: 8.29 us -> 11.4 us
  starting transfers between devices: 13.5 us -> 13 us
  waiting for transfers between devices: 2.56 us -> 2.06 us
    pallas_call x1, Pallas kernels: 0.6 us -> 2.38 us  [step_shares(): pl.pallas_call(functools.partial(step_kernel, sizes, arrays), out_shape=(...]
    pallas_call x1, Pallas kernels: 0.95 us -> 2.27 us  [early_steps(): pl.pallas_call(functools.partial(early_step_kernel, sizes, arrays, [mask...]
    ppermute x9, starting transfers between devices: 9.37 us -> 8.48 us  [flipped(): return lax.ppermute(block, axes, [(i, i ^ bit) for i in range(size)])]
    ppermute x3, waiting for transfers between devices: 1.48 us -> 0.79 us  [shared_out(): lax.ppermute(block, PROMPT_AXES, [(i, i ^ (odd if i & core else even)) fo...]
    ppermute x3, starting transfers between devices: 4.17 us -> 4.52 us  [shared_out(): lax.ppermute(block, PROMPT_AXES, [(i, i ^ (odd if i & core else even)) fo...]
  transfers between devices with their start and end apart: 12 -> 12, of which waited for: 3 -> 4; matrix products, arithmetic and copies ran while one was open for 0% -> 0% of each run, Pallas kernels for 29% -> 32%
where the time goes in v11:
time: 28.6 us; the launch traced here: 28.4 us
  starting transfers between devices  13 us (45%)
  Pallas kernels  11.4 us (40%)
  waiting for transfers between devices  2.06 us (7%)
  between operations  1.39 us (5%)
  other arithmetic  0.51 us (2%)
    ppermute x9, starting transfers between devices, flipped(): return lax.ppermute(block, axes, [(i, i ^ bit) for i in range(size)])  8.48 us
    pallas_call x4, Pallas kernels, phase(): pl.pallas_call(functools.partial(phase_kernel, sizes, arrays, masks, firs...  5.49 us
    ppermute x3, starting transfers between devices, shared_out(): lax.ppermute(block, PROMPT_AXES, [(i, i ^ (odd if i & core else even)) fo...  4.52 us
    pallas_call x1, Pallas kernels, step_shares(): pl.pallas_call(functools.partial(step_kernel, sizes, arrays), out_shape=(...  2.38 us
    pallas_call x1, Pallas kernels, early_steps(): pl.pallas_call(functools.partial(early_step_kernel, sizes, arrays, [mask...  2.27 us
    ppermute x9, waiting for transfers between devices, flipped(): return lax.ppermute(block, axes, [(i, i ^ bit) for i in range(size)])  1.28 us
    pallas_call x1, Pallas kernels, staged(): pl.pallas_call(stage_kernel, out_shape=(like(prompt_q), like(cand_q), lik...  1.27 us
    ppermute x3, waiting for transfers between devices, shared_out(): lax.ppermute(block, PROMPT_AXES, [(i, i ^ (odd if i & core else even)) fo...  0.79 us
  transfers between devices with their start and end apart: 12, of which 4 were waited for; matrix products, arithmetic and copies ran while one was open for 0% of the time, Pallas kernels for 32%

profile of v11, /device:TPU:0, one launch (start us, length us, event | category | flops | bytes accessed | tf_op | source)
XLA Modules:
  0.0 28.4 jit_solution(17299542690133362620)
XLA Ops:
  0.6 4.1 %collective-permute-start = (bf16[1,2,64,256]{3,2,1,0:T(8,128)(2,1)}, bf16[1,2,64,256]{3,2,1,0:T(8,128)(2,1)S(1)}, u32[]{:S(2)}, u32[]{:S(2)}) collective-permute-start(bf16[1,2,64,256]{3,2,1,0:T(8,128)(2,1)} %bitcast.9), channel_id=1, source_target_pairs={{0,4},{2,6},{4,0},{6,2},{8,12},{10,14},{12,8},{14,10},{16,20},{18,... | collective-permute-start | bytes 196616 | tf_op jit(solution)/shard_map/ppermute | solution.py:38
  5.4 1.3 %stage_operands.1 = (bf16[64,2048]{1,0:T(8,128)(2,1)S(1)}, bf16[64,2048]{1,0:T(8,128)(2,1)S(1)}, bf16[2,64,256]{2,1,0:T(8,128)(2,1)S(1)}, bf16[3,64,256]{2,1,0:T...) custom-call(s32[1]{0:T(128)S(6)} %copy.14.length_ref, ...), custom_call_target="tpu_custom_call" | custom-call | tf_op jit(solution)/shard_map/stage_operands/pallas_call | solution.py:129
  6.7 1.6 %collective-permute-start.4 = (bf16[3,64,256]{2,1,0:T(8,128)(2,1)S(1)}, bf16[3,64,256]{2,1,0:T(8,128)(2,1)S(1)}, u32[]{:S(2)}, u32[]{:S(2)}) collective-permute-start(bf16[3,64,256]{2,1,0:T(8,128)(2,1)S(1)} %get-tuple-element.32.refs_4_.refs_0_), channel_id=1, source_target_pairs={{0,16},{8,24},{16,0},{24,8},{1,17},{9,25},{17,1},{25,9},{2,18},{10... | collective-permute-start | bytes 294920 | tf_op jit(solution)/shard_map/ppermute | solution.py:38
  8.2 0.3 %collective-permute-done.refs_1_ = bf16[1,2,64,256]{3,2,1,0:T(8,128)(2,1)S(1)} collective-permute-done((bf16[1,2,64,256]{3,2,1,0:T(8,128)(2,1)}, bf16[1,2,64,256]{3,2,1,0:T(8,128)(2,1)S(1)}, u32[]{:S(2)}, u32[]{:S(2)}) %collective-permute-start) | collective-permute-done | bytes 65568 | tf_op jit(solution)/shard_map/ppermute | solution.py:38
  8.6 0.1 collective-permute-start.2
  8.7 1.3 %collective-permute-start.1 = (bf16[2,2,64,256]{3,2,1,0:T(8,128)(2,1)S(1)}, bf16[2,2,64,256]{3,2,1,0:T(8,128)(2,1)S(1)}, u32[]{:S(2)}, u32[]{:S(2)}) collective-permute-start(bf16[2,2,64,256]{3,2,1,0:T(8,128)(2,1)S(1)} %pack_blocks.3.refs_2_.refs_4_), channel_id=1, source_target_pairs={{0,2},{2,0},{4,6},{6,4},{8,24},{10,26},{12,28},{14,30},{16,18},{18... | collective-permute-start | bytes 393224 | tf_op jit(solution)/shard_map/ppermute | solution.py:435
  10.0 0.6 %collective-permute-start.3 = (bf16[3,64,256]{2,1,0:T(8,128)(2,1)S(1)}, bf16[3,64,256]{2,1,0:T(8,128)(2,1)S(1)}, u32[]{:S(2)}, u32[]{:S(2)}) collective-permute-start(bf16[3,64,256]{2,1,0:T(8,128)(2,1)S(1)} %get-tuple-element.32.refs_4_.refs_0_), channel_id=1, source_target_pairs={{0,8},{8,0},{16,24},{24,16},{1,9},{9,1},{17,25},{25,17},{2,10},{10... | collective-permute-start | bytes 294920 | tf_op jit(solution)/shard_map/ppermute | solution.py:38
  10.6 0.7 %collective-permute-done.4.refs_3_.refs_6_.refs_2_ = bf16[3,64,256]{2,1,0:T(8,128)(2,1)S(1)} collective-permute-done((bf16[3,64,256]{2,1,0:T(8,128)(2,1)S(1)}, bf16[3,64,256]{2,1,0:T(8,128)(2,1)S(1)}, u32[]{:S(2)}, u32[]{:S(2)}) %collective-permute-start.4) | collective-permute-done | bytes 98336 | tf_op jit(solution)/shard_map/ppermute | solution.py:38
  11.3 0.0 collective-permute-start.5
  11.3 1.5 %collective-permute-start.7 = (bf16[2,2,64,256]{3,2,1,0:T(8,128)(2,1)S(1)}, bf16[2,2,64,256]{3,2,1,0:T(8,128)(2,1)S(1)}, u32[]{:S(2)}, u32[]{:S(2)}) collective-permute-start(bf16[2,2,64,256]{3,2,1,0:T(8,128)(2,1)S(1)} %pack_blocks.3.refs_2_.refs_4_), channel_id=1, source_target_pairs={{0,16},{2,18},{4,20},{6,22},{8,10},{10,8},{12,14},{14,12},{16,0},{... | collective-permute-start | bytes 393224 | tf_op jit(solution)/shard_map/ppermute | solution.py:435
  12.9 0.0 collective-permute-done.2.refs_3_.refs_7_
  12.9 0.9 %attend_0_4.1 = (f32[1024,128]{1,0:T(8,128)S(1)}, f32[1024,256]{1,0:T(8,128)S(1)}, f32[1024,128]{1,0:T(8,128)S(1)}, f32[1024,256]{1,0:T(8,128)S(1)}) custom-call(bf16[64,2048]{1,0:T(8,128)(2,1)S(1)} %get-tuple-element.28.refs_0_, bf16[64,2048]{1,0:T(8,128)(2,1)S(1)} %get-tuple-element.29.refs_1_, bf16[2,2,64,256]{3,2,1,0:T(8,128)(2,1)S(1)} %pack_blocks.3.refs_2_.refs_4_, ...), custom_call_target="tpu_custom_call" | custom-call | flops 402653184 | bytes 524288 | tf_op jit(solution)/shard_map/attend_0_4/pallas_call | solution.py:279
  13.8 0.0 collective-permute-done.3.refs_2_.refs_5_.refs_1_
  13.8 0.0 collective-permute-done.1.refs_0_.refs_2_.refs_5_
  13.8 0.0 collective-permute-done.5.refs_4_.refs_7_.refs_3_
  13.8 1.7 %collective-permute-start.6 = (bf16[2,2,64,256]{3,2,1,0:T(8,128)(2,1)S(1)}, bf16[2,2,64,256]{3,2,1,0:T(8,128)(2,1)S(1)}, u32[]{:S(2)}, u32[]{:S(2)}) collective-permute-start(bf16[2,2,64,256]{3,2,1,0:T(8,128)(2,1)S(1)} %pack_blocks.4), channel_id=1, source_target_pairs={{0,16},{2,18},{4,20},{6,22},{8,10},{10,8},{12,14},{14,12},{16,0},{... | collective-permute-start | bytes 393224 | tf_op jit(solution)/shard_map/ppermute | solution.py:435
  15.5 0.0 collective-permute-start.9
  15.5 0.8 %collective-permute-done.7.refs_3_.refs_6_ = bf16[2,2,64,256]{3,2,1,0:T(8,128)(2,1)S(1)} collective-permute-done((bf16[2,2,64,256]{3,2,1,0:T(8,128)(2,1)S(1)}, bf16[2,2,64,256]{3,2,1,0:T(8,128)(2,1)S(1)}, u32[]{:S(2)}, u32[]{:S(2)}) %collective-permute-start.7) | collective-permute-done | bytes 131104 | tf_op jit(solution)/shard_map/ppermute | solution.py:435
  16.3 0.0 collective-permute-start.10
  16.3 2.3 %early_steps.1 = (f32[2,64,128]{2,1,0:T(8,128)S(1)}, f32[9,2,64,128]{3,2,1,0:T(8,128)S(1)}, f32[9,2,64,256]{3,2,1,0:T(8,128)S(1)}) custom-call(s32[1,8]{1,0:T(1,128)S(1)} %get-tuple-element.37.ends_ref, bf16[3,64,256]{2,1,0:T(8,128)(2,1)S(1)} %get-tuple-element.32.refs_4_.refs_0_, bf16[3,64,256]{2,1,0:T(8,128)(2,1)S(1)} %collective-permute-done.3.refs_2_.refs_5_.refs_1_, ...), custom_call_target="tpu_custom_call" | custom-call | tf_op jit(solution)/shard_map/early_steps/pallas_call | solution.py:361
  18.6 1.7 %attend_1_2.1 = (f32[1024,128]{1,0:T(8,128)S(1)}, f32[1024,256]{1,0:T(8,128)S(1)}, f32[1024,128]{1,0:T(8,128)S(1)}, f32[1024,256]{1,0:T(8,128)S(1)}) custom-call(bf16[64,2048]{1,0:T(8,128)(2,1)S(1)} %get-tuple-element.28.refs_0_, bf16[64,2048]{1,0:T(8,128)(2,1)S(1)} %get-tuple-element.29.refs_1_, ...), custom_call_target="tpu_custom_call" | custom-call | flops 402653184 | bytes 524288 | tf_op jit(solution)/shard_map/attend_1_2/pallas_call | solution.py:279
  20.3 0.0 collective-permute-done.6.refs_0_.refs_2_
  20.4 0.6 %collective-permute-start.8 = (bf16[2,2,64,256]{3,2,1,0:T(8,128)(2,1)S(1)}, bf16[2,2,64,256]{3,2,1,0:T(8,128)(2,1)S(1)}, u32[]{:S(2)}, u32[]{:S(2)}) collective-permute-start(bf16[2,2,64,256]{3,2,1,0:T(8,128)(2,1)S(1)} %pack_blocks.5), channel_id=1, source_target_pairs={{0,8},{2,10},{4,12},{6,14},{8,0},{10,2},{12,4},{14,6},{16,24},{18,... | collective-permute-start | bytes 393224 | tf_op jit(solution)/shard_map/ppermute | solution.py:38
  20.9 0.0 collective-permute-done.9.refs_2_.refs_3_
  20.9 0.0 collective-permute-done.10.refs_3_.refs_4_
  20.9 1.0 %attend_5_6.1 = (f32[1024,128]{1,0:T(8,128)S(1)}, f32[1024,256]{1,0:T(8,128)S(1)}, f32[1024,128]{1,0:T(8,128)S(1)}, f32[1024,256]{1,0:T(8,128)S(1)}) custom-call(bf16[64,2048]{1,0:T(8,128)(2,1)S(1)} %get-tuple-element.28.refs_0_, bf16[64,2048]{1,0:T(8,128)(2,1)S(1)} %get-tuple-element.29.refs_1_, ...), custom_call_target="tpu_custom_call" | custom-call | flops 402653184 | bytes 524288 | tf_op jit(solution)/shard_map/attend_5_6/pallas_call | solution.py:279
  22.0 0.0 collective-permute-done.8.refs_3_.refs_5_
  22.0 2.4 %step_logits.1 = (f32[1,8]{1,0:T(1,128)S(1)}, f32[9,2,64,128]{3,2,1,0:T(8,128)S(1)}, f32[9,2,64,256]{3,2,1,0:T(8,128)S(1)}) custom-call(s32[1,8]{1,0:T(1,128)S(1)} %get-tuple-element.37.ends_ref, f32[1,2048]{1,0:T(1,128)S(1)} %get-tuple-element.49.head_ref, ...), custom_call_target="tpu_custom_call", output_to_operand_aliasing={{1}: (4, {}), {2}: (5, {})} | custom-call | tf_op jit(solution)/shard_map/step_logits/pallas_call | solution.py:409
  24.4 1.5 %collective-permute-start.11 = (f32[1,8]{1,0:T(1,128)S(1)}, f32[1,8]{1,0:T(1,128)S(1)}, u32[]{:S(2)}, u32[]{:S(2)}) collective-permute-start(f32[1,8]{1,0:T(1,128)S(1)} %get-tuple-element.52), channel_id=1, source_target_pairs={{0,1},{1,0},{2,3},{3,2},{4,5},{5,4},{6,7},{7,6},{8,9},{9,8},{10,11... | collective-permute-start | bytes 104 | tf_op jit(solution)/shard_map/ppermute | solution.py:38
  25.9 1.8 %attend_3_7.1 = (bf16[64,2048]{1,0:T(8,128)(2,1)}, bf16[64,2048]{1,0:T(8,128)(2,1)}) custom-call(bf16[64,2048]{1,0:T(8,128)(2,1)S(1)} %get-tuple-element.28.refs_0_, bf16[64,2048]{1,0:T(8,128)(2,1)S(1)} %get-tuple-element.29.refs_1_, bf16[2,2,64,256]{3,2,1,0:T(8,128)(2,1)S(1)} %collective-permute-done.6.refs_0_.refs_2_, ...), custom_call_target="tpu_custom_call" | custom-call | flops 402653184 | bytes 524288 | tf_op jit(solution)/shard_map/attend_3_7/pallas_call | solution.py:279
  27.7 0.2 collective-permute-done.11
  27.9 0.5 %add.3 = f32[1,8]{1,0:T(1,128)} add(f32[1,8]{1,0:T(1,128)S(1)} %get-tuple-element.52, f32[1,8]{1,0:T(1,128)S(1)} %collective-permute-done.11) | non-fusion elementwise | flops 8 | bytes 96 | tf_op jit(solution)/shard_map/add | solution.py:459
  (3 shorter events, 0.0 us)
Async XLA Ops:
  0.6 8.0 %collective-permute-start = (bf16[1,2,64,256]{3,2,1,0:T(8,128)(2,1)}, bf16[1,2,64,256]{3,2,1,0:T(8,128)(2,1)S(1)}, u32[]{:S(2)}, u32[]{:S(2)}) collective-permute-start(bf16[1,2,64,256]{3,2,1,0:T(8,128)(2,1)} %bitcast.9), channel_id=1, source_target_pairs={{0,4},{2,6},{4,0},{6,2},{8,12},{10,14},{12,8},{14,10},{16,20},{18,... | collective-permute-start | bytes 196616 | tf_op jit(solution)/shard_map/ppermute | solution.py:38
  6.7 4.7 %collective-permute-start.4 = (bf16[3,64,256]{2,1,0:T(8,128)(2,1)S(1)}, bf16[3,64,256]{2,1,0:T(8,128)(2,1)S(1)}, u32[]{:S(2)}, u32[]{:S(2)}) collective-permute-start(bf16[3,64,256]{2,1,0:T(8,128)(2,1)S(1)} %get-tuple-element.32.refs_4_.refs_0_), channel_id=1, source_target_pairs={{0,16},{8,24},{16,0},{24,8},{1,17},{9,25},{17,1},{25,9},{2,18},{10... | collective-permute-start | bytes 294920 | tf_op jit(solution)/shard_map/ppermute | solution.py:38
  8.6 4.3 %collective-permute-start.2 = (bf16[2,2,64,256]{3,2,1,0:T(8,128)(2,1)S(1)}, bf16[2,2,64,256]{3,2,1,0:T(8,128)(2,1)S(1)}, u32[]{:S(2)}, u32[]{:S(2)}) collective-permute-start(bf16[2,2,64,256]{3,2,1,0:T(8,128)(2,1)S(1)} %pack_blocks.3.refs_2_.refs_4_), channel_id=1, source_target_pairs={{0,8},{2,10},{4,12},{6,14},{8,0},{10,2},{12,4},{14,6},{16,24},{18,... | collective-permute-start | bytes 393224 | tf_op jit(solution)/shard_map/ppermute | solution.py:38
  8.7 5.1 %collective-permute-start.1 = (bf16[2,2,64,256]{3,2,1,0:T(8,128)(2,1)S(1)}, bf16[2,2,64,256]{3,2,1,0:T(8,128)(2,1)S(1)}, u32[]{:S(2)}, u32[]{:S(2)}) collective-permute-start(bf16[2,2,64,256]{3,2,1,0:T(8,128)(2,1)S(1)} %pack_blocks.3.refs_2_.refs_4_), channel_id=1, source_target_pairs={{0,2},{2,0},{4,6},{6,4},{8,24},{10,26},{12,28},{14,30},{16,18},{18... | collective-permute-start | bytes 393224 | tf_op jit(solution)/shard_map/ppermute | solution.py:435
  10.0 3.8 %collective-permute-start.3 = (bf16[3,64,256]{2,1,0:T(8,128)(2,1)S(1)}, bf16[3,64,256]{2,1,0:T(8,128)(2,1)S(1)}, u32[]{:S(2)}, u32[]{:S(2)}) collective-permute-start(bf16[3,64,256]{2,1,0:T(8,128)(2,1)S(1)} %get-tuple-element.32.refs_4_.refs_0_), channel_id=1, source_target_pairs={{0,8},{8,0},{16,24},{24,16},{1,9},{9,1},{17,25},{25,17},{2,10},{10... | collective-permute-start | bytes 294920 | tf_op jit(solution)/shard_map/ppermute | solution.py:38
  11.3 2.5 %collective-permute-start.5 = (bf16[3,64,256]{2,1,0:T(8,128)(2,1)S(1)}, bf16[3,64,256]{2,1,0:T(8,128)(2,1)S(1)}, u32[]{:S(2)}, u32[]{:S(2)}) collective-permute-start(bf16[3,64,256]{2,1,0:T(8,128)(2,1)S(1)} %collective-permute-done.4.refs_3_.refs_6_.refs_2_), channel_id=1, source_target_pairs={{0,8},{8,0},{16,24},{24,16},{1,9},{9,1},{17,25},{25,17},{2,10},{10... | collective-permute-start | bytes 294920 | tf_op jit(solution)/shard_map/ppermute | solution.py:38
  11.3 5.0 %collective-permute-start.7 = (bf16[2,2,64,256]{3,2,1,0:T(8,128)(2,1)S(1)}, bf16[2,2,64,256]{3,2,1,0:T(8,128)(2,1)S(1)}, u32[]{:S(2)}, u32[]{:S(2)}) collective-permute-start(bf16[2,2,64,256]{3,2,1,0:T(8,128)(2,1)S(1)} %pack_blocks.3.refs_2_.refs_4_), channel_id=1, source_target_pairs={{0,16},{2,18},{4,20},{6,22},{8,10},{10,8},{12,14},{14,12},{16,0},{... | collective-permute-start | bytes 393224 | tf_op jit(solution)/shard_map/ppermute | solution.py:435
  13.8 6.5 %collective-permute-start.6 = (bf16[2,2,64,256]{3,2,1,0:T(8,128)(2,1)S(1)}, bf16[2,2,64,256]{3,2,1,0:T(8,128)(2,1)S(1)}, u32[]{:S(2)}, u32[]{:S(2)}) collective-permute-start(bf16[2,2,64,256]{3,2,1,0:T(8,128)(2,1)S(1)} %pack_blocks.4), channel_id=1, source_target_pairs={{0,16},{2,18},{4,20},{6,22},{8,10},{10,8},{12,14},{14,12},{16,0},{... | collective-permute-start | bytes 393224 | tf_op jit(solution)/shard_map/ppermute | solution.py:435
  15.5 5.4 %collective-permute-start.9 = (bf16[2,2,64,256]{3,2,1,0:T(8,128)(2,1)S(1)}, bf16[2,2,64,256]{3,2,1,0:T(8,128)(2,1)S(1)}, u32[]{:S(2)}, u32[]{:S(2)}) collective-permute-start(bf16[2,2,64,256]{3,2,1,0:T(8,128)(2,1)S(1)} %collective-permute-done.1.refs_0_.refs_2_.refs_5_), channel_id=1, source_target_pairs={{0,8},{2,10},{4,12},{6,14},{8,0},{10,2},{12,4},{14,6},{16,24},{18,... | collective-permute-start | bytes 393224 | tf_op jit(solution)/shard_map/ppermute | solution.py:38
  16.3 4.6 %collective-permute-start.10 = (bf16[2,2,64,256]{3,2,1,0:T(8,128)(2,1)S(1)}, bf16[2,2,64,256]{3,2,1,0:T(8,128)(2,1)S(1)}, u32[]{:S(2)}, u32[]{:S(2)}) collective-permute-start(bf16[2,2,64,256]{3,2,1,0:T(8,128)(2,1)S(1)} %collective-permute-done.7.refs_3_.refs_6_), channel_id=1, source_target_pairs={{0,8},{2,10},{4,12},{6,14},{8,0},{10,2},{12,4},{14,6},{16,24},{18,... | collective-permute-start | bytes 393224 | tf_op jit(solution)/shard_map/ppermute | solution.py:38
  20.4 1.6 %collective-permute-start.8 = (bf16[2,2,64,256]{3,2,1,0:T(8,128)(2,1)S(1)}, bf16[2,2,64,256]{3,2,1,0:T(8,128)(2,1)S(1)}, u32[]{:S(2)}, u32[]{:S(2)}) collective-permute-start(bf16[2,2,64,256]{3,2,1,0:T(8,128)(2,1)S(1)} %pack_blocks.5), channel_id=1, source_target_pairs={{0,8},{2,10},{4,12},{6,14},{8,0},{10,2},{12,4},{14,6},{16,24},{18,... | collective-permute-start | bytes 393224 | tf_op jit(solution)/shard_map/ppermute | solution.py:38
  24.4 3.5 %collective-permute-start.11 = (f32[1,8]{1,0:T(1,128)S(1)}, f32[1,8]{1,0:T(1,128)S(1)}, u32[]{:S(2)}, u32[]{:S(2)}) collective-permute-start(f32[1,8]{1,0:T(1,128)S(1)} %get-tuple-element.52), channel_id=1, source_target_pairs={{0,1},{1,0},{2,3},{3,2},{4,5},{5,4},{6,7},{7,6},{8,9},{9,8},{10,11... | collective-permute-start | bytes 104 | tf_op jit(solution)/shard_map/ppermute | solution.py:38

commit v12 on v5

--- a/solution.py
+++ b/solution.py
@@ -310,24 +310,38 @@
     step_rows = [picked[at : at + steps] for at in range(0, steps * head_ref.shape[1] // width, steps)]
 
     ends = column_of(ends_ref[...])
-    own_pos = lax.broadcasted_iota(jnp.int32, (1, own_rows * len(masks)), 1)
-    row_pos = jnp.concatenate([ends] * GROUP, axis=0)
+    kinds = width // HEADDIM
+    stacked = GROUP * steps
+    parts = []
+    for head in range(kinds):
+        places = [divmod(h * HEADDIM, width) for h in range(head * GROUP, (head + 1) * GROUP)]
+        part = jnp.concatenate([step_rows[a][:, b : b + HEADDIM] for a, b in places], axis=0)
+        sides = [part if other == head else jnp.zeros_like(part) for other in range(kinds)]
+        parts.append(jnp.concatenate(sides, axis=1))
+    queries = jnp.concatenate(parts, axis=0).astype(jnp.bfloat16)
+    count = kinds * stacked
+    step_of = lax.rem(lax.broadcasted_iota(jnp.int32, (steps, count), 1), jnp.int32(steps))
+    mine = step_of == lax.broadcasted_iota(jnp.int32, (steps, count), 0)
+    row_pos = jnp.sum(jnp.where(mine, ends, 0), axis=0, keepdims=True)
+    own_pos = lax.broadcasted_iota(jnp.int32, (own_rows * len(masks), 1), 0)
+    scores = product(kv_ref[0], queries)
+    bound = jnp.where(own_pos <= row_pos, scores[free:], NEG_FILL)
+    scores = jnp.concatenate([scores[:free], bound], axis=0)
+    peak = jnp.max(scores, axis=0, keepdims=True)
+    weights = jnp.exp2((scores - peak) * SCALE).astype(jnp.bfloat16)
+    value_rows = kv_ref[1]
+    widened = jnp.concatenate([value_rows, jnp.ones_like(value_rows[:, :HEADDIM])], axis=1)
+    blended = lax.dot_general(
+        weights, widened, (((0,), (0,)), ((), ())), preferred_element_type=jnp.float32
+    )
     total = jnp.zeros((steps, HEADDIM), jnp.float32)
-    for head in range(width // HEADDIM):
-        columns = slice(head * HEADDIM, (head + 1) * HEADDIM)
-        heads = range(head * GROUP, (head + 1) * GROUP)
-        places = [divmod(h * HEADDIM, width) for h in heads]
-        queries = jnp.concatenate([step_rows[a][:, b : b + HEADDIM] for a, b in places], axis=0)
-        scores = product(queries.astype(jnp.bfloat16), kv_ref[0, :, columns])
-        bound = jnp.where(own_pos <= row_pos, scores[:, free:], NEG_FILL)
-        scores = jnp.concatenate([scores[:, :free], bound], axis=1)
-        peak = jnp.max(scores, axis=1, keepdims=True)
-        weights = jnp.exp2((scores - peak) * SCALE).astype(jnp.bfloat16)
-        blended = jnp.dot(weights, with_ones(kv_ref[1, :, columns]), preferred_element_type=jnp.float32)
-        result = blended[:, :HEADDIM] / blended[:, HEADDIM:]
-        for index, h in enumerate(heads):
+    for head in range(kinds):
+        mixed = blended[head * stacked : (head + 1) * stacked]
+        result = mixed[:, head * HEADDIM : (head + 1) * HEADDIM] / mixed[:, width:]
+        for index in range(GROUP):
             kept = jnp.where(ends < lengths_ref[:, :1], result[index * steps : (index + 1) * steps], 0.0)
             kept = kept.astype(jnp.bfloat16).astype(jnp.float32)
+            h = head * GROUP + index
             total += kept * head_ref[:, h * HEADDIM : (h + 1) * HEADDIM]
     logits = jnp.sum(total, axis=1, keepdims=True)
     down = lax.broadcasted_iota(jnp.int32, (steps, steps), 0)

time: 25.5 us -> 25.7 us (level)
  transfers between devices with their start and end apart: 12 -> 12, of which waited for: 6 -> 6; matrix products, arithmetic and copies ran while one was open for 0% -> 0% of each run, Pallas kernels for 27% -> 26%
where the time goes in v12:
time: 25.7 us; the launch traced here: 25.5 us
  starting transfers between devices  12.6 us (49%)
  Pallas kernels  7.93 us (31%)
  waiting for transfers between devices  3.08 us (12%)
  between operations  1.39 us (5%)
  other arithmetic  0.51 us (2%)
    ppermute x9, starting transfers between devices, flipped(): return lax.ppermute(block, axes, [(i, i ^ bit) for i in range(size)])  8.11 us
    pallas_call x4, Pallas kernels, phase(): pl.pallas_call(functools.partial(phase_kernel, sizes, arrays, masks, firs...  5.44 us
    ppermute x3, starting transfers between devices, shared_out(): lax.ppermute(block, PROMPT_AXES, [(i, i ^ (odd if i & core else even)) fo...  4.53 us
    ppermute x3, waiting for transfers between devices, shared_out(): lax.ppermute(block, PROMPT_AXES, [(i, i ^ (odd if i & core else even)) fo...  1.57 us
    ppermute x9, waiting for transfers between devices, flipped(): return lax.ppermute(block, axes, [(i, i ^ bit) for i in range(size)])  1.5 us
    pallas_call x1, Pallas kernels, staged(): pl.pallas_call(stage_kernel, out_shape=(like(prompt_q), like(cand_q), lik...  1.27 us
    pallas_call x1, Pallas kernels, step_shares(): pl.pallas_call(functools.partial(step_kernel, sizes, [mask for _, mask in...  1.2 us
  transfers between devices with their start and end apart: 12, of which 6 were waited for; matrix products, arithmetic and copies ran while one was open for 0% of the time, Pallas kernels for 26%

profile of v12, /device:TPU:0, one launch (start us, length us, event | category | flops | bytes accessed | tf_op | source)
XLA Modules:
  0.0 25.5 jit_solution(12861614425093376799)
XLA Ops:
  0.6 4.1 %collective-permute-start = (bf16[1,2,64,256]{3,2,1,0:T(8,128)(2,1)}, bf16[1,2,64,256]{3,2,1,0:T(8,128)(2,1)S(1)}, u32[]{:S(2)}, u32[]{:S(2)}) collective-permute-start(bf16[1,2,64,256]{3,2,1,0:T(8,128)(2,1)} %bitcast.9), channel_id=1, source_target_pairs={{0,4},{2,6},{4,0},{6,2},{8,12},{10,14},{12,8},{14,10},{16,20},{18,... | collective-permute-start | bytes 196616 | tf_op jit(solution)/shard_map/ppermute | solution.py:35
  5.4 1.3 %stage_operands.1 = (bf16[64,2048]{1,0:T(8,128)(2,1)S(1)}, bf16[64,2048]{1,0:T(8,128)(2,1)S(1)}, bf16[2,64,256]{2,1,0:T(8,128)(2,1)S(1)}, bf16[3,64,256]{2,1,0:T...) custom-call(s32[1]{0:T(128)S(6)} %copy.10.length_ref, ...), custom_call_target="tpu_custom_call" | custom-call | tf_op jit(solution)/shard_map/stage_operands/pallas_call | solution.py:126
  6.7 1.6 %collective-permute-start.4 = (bf16[3,64,256]{2,1,0:T(8,128)(2,1)S(1)}, bf16[3,64,256]{2,1,0:T(8,128)(2,1)S(1)}, u32[]{:S(2)}, u32[]{:S(2)}) collective-permute-start(bf16[3,64,256]{2,1,0:T(8,128)(2,1)S(1)} %get-tuple-element.28.refs_4_.refs_0_), channel_id=1, source_target_pairs={{0,16},{8,24},{16,0},{24,8},{1,17},{9,25},{17,1},{25,9},{2,18},{10... | collective-permute-start | bytes 294920 | tf_op jit(solution)/shard_map/ppermute | solution.py:35
  8.2 0.3 %collective-permute-done.refs_1_ = bf16[1,2,64,256]{3,2,1,0:T(8,128)(2,1)S(1)} collective-permute-done((bf16[1,2,64,256]{3,2,1,0:T(8,128)(2,1)}, bf16[1,2,64,256]{3,2,1,0:T(8,128)(2,1)S(1)}, u32[]{:S(2)}, u32[]{:S(2)}) %collective-permute-start) | collective-permute-done | bytes 65568 | tf_op jit(solution)/shard_map/ppermute | solution.py:35
  8.6 0.1 collective-permute-start.2
  8.7 1.3 %collective-permute-start.1 = (bf16[2,2,64,256]{3,2,1,0:T(8,128)(2,1)S(1)}, bf16[2,2,64,256]{3,2,1,0:T(8,128)(2,1)S(1)}, u32[]{:S(2)}, u32[]{:S(2)}) collective-permute-start(bf16[2,2,64,256]{3,2,1,0:T(8,128)(2,1)S(1)} %pack_blocks.3.refs_2_.refs_4_), channel_id=1, source_target_pairs={{0,2},{2,0},{4,6},{6,4},{8,24},{10,26},{12,28},{14,30},{16,18},{18... | collective-permute-start | bytes 393224 | tf_op jit(solution)/shard_map/ppermute | solution.py:385
  10.0 0.6 %collective-permute-start.3 = (bf16[3,64,256]{2,1,0:T(8,128)(2,1)S(1)}, bf16[3,64,256]{2,1,0:T(8,128)(2,1)S(1)}, u32[]{:S(2)}, u32[]{:S(2)}) collective-permute-start(bf16[3,64,256]{2,1,0:T(8,128)(2,1)S(1)} %get-tuple-element.28.refs_4_.refs_0_), channel_id=1, source_target_pairs={{0,8},{8,0},{16,24},{24,16},{1,9},{9,1},{17,25},{25,17},{2,10},{10... | collective-permute-start | bytes 294920 | tf_op jit(solution)/shard_map/ppermute | solution.py:35
  10.6 0.7 %collective-permute-done.4.refs_3_.refs_6_.refs_2_ = bf16[3,64,256]{2,1,0:T(8,128)(2,1)S(1)} collective-permute-done((bf16[3,64,256]{2,1,0:T(8,128)(2,1)S(1)}, bf16[3,64,256]{2,1,0:T(8,128)(2,1)S(1)}, u32[]{:S(2)}, u32[]{:S(2)}) %collective-permute-start.4) | collective-permute-done | bytes 98336 | tf_op jit(solution)/shard_map/ppermute | solution.py:35
  11.3 0.0 collective-permute-start.5
  11.3 1.5 %collective-permute-start.7 = (bf16[2,2,64,256]{3,2,1,0:T(8,128)(2,1)S(1)}, bf16[2,2,64,256]{3,2,1,0:T(8,128)(2,1)S(1)}, u32[]{:S(2)}, u32[]{:S(2)}) collective-permute-start(bf16[2,2,64,256]{3,2,1,0:T(8,128)(2,1)S(1)} %pack_blocks.3.refs_2_.refs_4_), channel_id=1, source_target_pairs={{0,16},{2,18},{4,20},{6,22},{8,10},{10,8},{12,14},{14,12},{16,0},{... | collective-permute-start | bytes 393224 | tf_op jit(solution)/shard_map/ppermute | solution.py:385
  12.9 0.0 collective-permute-done.2.refs_3_.refs_8_
  12.9 0.9 %attend_0_4.1 = (f32[1024,128]{1,0:T(8,128)S(1)}, f32[1024,256]{1,0:T(8,128)S(1)}, f32[1024,128]{1,0:T(8,128)S(1)}, f32[1024,256]{1,0:T(8,128)S(1)}) custom-call(bf16[64,2048]{1,0:T(8,128)(2,1)S(1)} %get-tuple-element.24.refs_0_, bf16[64,2048]{1,0:T(8,128)(2,1)S(1)} %get-tuple-element.25.refs_1_, bf16[2,2,64,256]{3,2,1,0:T(8,128)(2,1)S(1)} %pack_blocks.3.refs_2_.refs_4_, ...), custom_call_target="tpu_custom_call" | custom-call | flops 402653184 | bytes 524288 | tf_op jit(solution)/shard_map/attend_0_4/pallas_call | solution.py:276
  13.8 0.0 collective-permute-done.3.refs_2_.refs_5_.refs_1_
  13.8 0.0 collective-permute-done.1.refs_0_.refs_2_.refs_5_
  13.8 0.0 collective-permute-done.5.refs_4_.refs_7_.refs_3_
  13.8 1.7 %collective-permute-start.6 = (bf16[2,2,64,256]{3,2,1,0:T(8,128)(2,1)S(1)}, bf16[2,2,64,256]{3,2,1,0:T(8,128)(2,1)S(1)}, u32[]{:S(2)}, u32[]{:S(2)}) collective-permute-start(bf16[2,2,64,256]{3,2,1,0:T(8,128)(2,1)S(1)} %pack_blocks.4), channel_id=1, source_target_pairs={{0,16},{2,18},{4,20},{6,22},{8,10},{10,8},{12,14},{14,12},{16,0},{... | collective-permute-start | bytes 393224 | tf_op jit(solution)/shard_map/ppermute | solution.py:385
  15.5 0.0 collective-permute-start.9
  15.5 0.8 %collective-permute-done.7.refs_3_.refs_6_ = bf16[2,2,64,256]{3,2,1,0:T(8,128)(2,1)S(1)} collective-permute-done((bf16[2,2,64,256]{3,2,1,0:T(8,128)(2,1)S(1)}, bf16[2,2,64,256]{3,2,1,0:T(8,128)(2,1)S(1)}, u32[]{:S(2)}, u32[]{:S(2)}) %collective-permute-start.7) | collective-permute-done | bytes 131104 | tf_op jit(solution)/shard_map/ppermute | solution.py:385
  16.3 0.0 collective-permute-start.10
  16.3 1.7 %attend_1_2.1 = (f32[1024,128]{1,0:T(8,128)S(1)}, f32[1024,256]{1,0:T(8,128)S(1)}, f32[1024,128]{1,0:T(8,128)S(1)}, f32[1024,256]{1,0:T(8,128)S(1)}) custom-call(bf16[64,2048]{1,0:T(8,128)(2,1)S(1)} %get-tuple-element.24.refs_0_, bf16[64,2048]{1,0:T(8,128)(2,1)S(1)} %get-tuple-element.25.refs_1_, ...), custom_call_target="tpu_custom_call" | custom-call | flops 402653184 | bytes 524288 | tf_op jit(solution)/shard_map/attend_1_2/pallas_call | solution.py:276
  18.1 0.8 %collective-permute-done.6.refs_0_.refs_2_.refs_7_ = bf16[2,2,64,256]{3,2,1,0:T(8,128)(2,1)S(1)} collective-permute-done((bf16[2,2,64,256]{3,2,1,0:T(8,128)(2,1)S(1)}, bf16[2,2,64,256]{3,2,1,0:T(8,128)(2,1)S(1)}, u32[]{:S(2)}, u32[]{:S(2)}) %collective-permute-start.6) | collective-permute-done | bytes 131104 | tf_op jit(solution)/shard_map/ppermute | solution.py:385
  18.9 0.1 collective-permute-start.8
  18.9 0.0 collective-permute-done.9.refs_2_.refs_9_
  19.0 0.0 collective-permute-done.10.refs_3_.refs_10_
  19.0 1.0 %attend_5_6.1 = (f32[1024,128]{1,0:T(8,128)S(1)}, f32[1024,256]{1,0:T(8,128)S(1)}, f32[1024,128]{1,0:T(8,128)S(1)}, f32[1024,256]{1,0:T(8,128)S(1)}) custom-call(bf16[64,2048]{1,0:T(8,128)(2,1)S(1)} %get-tuple-element.24.refs_0_, bf16[64,2048]{1,0:T(8,128)(2,1)S(1)} %get-tuple-element.25.refs_1_, ...), custom_call_target="tpu_custom_call" | custom-call | flops 402653184 | bytes 524288 | tf_op jit(solution)/shard_map/attend_5_6/pallas_call | solution.py:276
  20.0 0.3 %collective-permute-done.8.refs_3_.refs_11_ = bf16[2,2,64,256]{3,2,1,0:T(8,128)(2,1)S(1)} collective-permute-done((bf16[2,2,64,256]{3,2,1,0:T(8,128)(2,1)S(1)}, bf16[2,2,64,256]{3,2,1,0:T(8,128)(2,1)S(1)}, u32[]{:S(2)}, u32[]{:S(2)}) %collective-permute-start.8) | collective-permute-done | bytes 131104 | tf_op jit(solution)/shard_map/ppermute | solution.py:35
  20.3 1.2 %step_logits.1 = f32[1,8]{1,0:T(1,128)S(1)} custom-call(s32[1,8]{1,0:T(1,128)S(1)} %get-tuple-element.43.ends_ref, f32[1,2048]{1,0:T(1,128)S(1)} %get-tuple-element.44.head_ref, s32[1,128]{1,0:T(1,128)S(1)} %get-tuple-element.33.refs_4_.lengths_ref, bf16[3,64,256]{2,1,0:T(8,128)(2,1)S(1)} %get-tuple-element.28.refs_4_.refs_0_, ...), custom_call_target="tpu_custom_call" | custom-call | flops 125829120 | bytes 163840 | tf_op jit(solution)/shard_map/step_logits/pallas_call | solution.py:357
  21.5 1.6 %collective-permute-start.11 = (f32[1,8]{1,0:T(1,128)S(1)}, f32[1,8]{1,0:T(1,128)S(1)}, u32[]{:S(2)}, u32[]{:S(2)}) collective-permute-start(f32[1,8]{1,0:T(1,128)S(1)} %step_logits.1), channel_id=1, source_target_pairs={{0,1},{1,0},{2,3},{3,2},{4,5},{5,4},{6,7},{7,6},{8,9},{9,8},{10,11... | collective-permute-start | bytes 104 | tf_op jit(solution)/shard_map/ppermute | solution.py:35
  23.1 1.8 %attend_3_7.1 = (bf16[64,2048]{1,0:T(8,128)(2,1)}, bf16[64,2048]{1,0:T(8,128)(2,1)}) custom-call(bf16[64,2048]{1,0:T(8,128)(2,1)S(1)} %get-tuple-element.24.refs_0_, bf16[64,2048]{1,0:T(8,128)(2,1)S(1)} %get-tuple-element.25.refs_1_, bf16[2,2,64,256]{3,2,1,0:T(8,128)(2,1)S(1)} %collective-permute-done.6.refs_0_.refs_2_.refs_7_, ...), custom_call_target="tpu_custom_call" | custom-call | flops 402653184 | bytes 524288 | tf_op jit(solution)/shard_map/attend_3_7/pallas_call | solution.py:276
  24.9 0.1 collective-permute-done.11
  25.0 0.5 %add.3 = f32[1,8]{1,0:T(1,128)} add(f32[1,8]{1,0:T(1,128)S(1)} %step_logits.1, f32[1,8]{1,0:T(1,128)S(1)} %collective-permute-done.11) | non-fusion elementwise | flops 8 | bytes 96 | tf_op jit(solution)/shard_map/add | solution.py:408
  (3 shorter events, 0.0 us)
Async XLA Ops:
  0.6 8.0 %collective-permute-start = (bf16[1,2,64,256]{3,2,1,0:T(8,128)(2,1)}, bf16[1,2,64,256]{3,2,1,0:T(8,128)(2,1)S(1)}, u32[]{:S(2)}, u32[]{:S(2)}) collective-permute-start(bf16[1,2,64,256]{3,2,1,0:T(8,128)(2,1)} %bitcast.9), channel_id=1, source_target_pairs={{0,4},{2,6},{4,0},{6,2},{8,12},{10,14},{12,8},{14,10},{16,20},{18,... | collective-permute-start | bytes 196616 | tf_op jit(solution)/shard_map/ppermute | solution.py:35
  6.7 4.7 %collective-permute-start.4 = (bf16[3,64,256]{2,1,0:T(8,128)(2,1)S(1)}, bf16[3,64,256]{2,1,0:T(8,128)(2,1)S(1)}, u32[]{:S(2)}, u32[]{:S(2)}) collective-permute-start(bf16[3,64,256]{2,1,0:T(8,128)(2,1)S(1)} %get-tuple-element.28.refs_4_.refs_0_), channel_id=1, source_target_pairs={{0,16},{8,24},{16,0},{24,8},{1,17},{9,25},{17,1},{25,9},{2,18},{10... | collective-permute-start | bytes 294920 | tf_op jit(solution)/shard_map/ppermute | solution.py:35
  8.6 4.3 %collective-permute-start.2 = (bf16[2,2,64,256]{3,2,1,0:T(8,128)(2,1)S(1)}, bf16[2,2,64,256]{3,2,1,0:T(8,128)(2,1)S(1)}, u32[]{:S(2)}, u32[]{:S(2)}) collective-permute-start(bf16[2,2,64,256]{3,2,1,0:T(8,128)(2,1)S(1)} %pack_blocks.3.refs_2_.refs_4_), channel_id=1, source_target_pairs={{0,8},{2,10},{4,12},{6,14},{8,0},{10,2},{12,4},{14,6},{16,24},{18,... | collective-permute-start | bytes 393224 | tf_op jit(solution)/shard_map/ppermute | solution.py:35
  8.7 5.1 %collective-permute-start.1 = (bf16[2,2,64,256]{3,2,1,0:T(8,128)(2,1)S(1)}, bf16[2,2,64,256]{3,2,1,0:T(8,128)(2,1)S(1)}, u32[]{:S(2)}, u32[]{:S(2)}) collective-permute-start(bf16[2,2,64,256]{3,2,1,0:T(8,128)(2,1)S(1)} %pack_blocks.3.refs_2_.refs_4_), channel_id=1, source_target_pairs={{0,2},{2,0},{4,6},{6,4},{8,24},{10,26},{12,28},{14,30},{16,18},{18... | collective-permute-start | bytes 393224 | tf_op jit(solution)/shard_map/ppermute | solution.py:385
  10.0 3.8 %collective-permute-start.3 = (bf16[3,64,256]{2,1,0:T(8,128)(2,1)S(1)}, bf16[3,64,256]{2,1,0:T(8,128)(2,1)S(1)}, u32[]{:S(2)}, u32[]{:S(2)}) collective-permute-start(bf16[3,64,256]{2,1,0:T(8,128)(2,1)S(1)} %get-tuple-element.28.refs_4_.refs_0_), channel_id=1, source_target_pairs={{0,8},{8,0},{16,24},{24,16},{1,9},{9,1},{17,25},{25,17},{2,10},{10... | collective-permute-start | bytes 294920 | tf_op jit(solution)/shard_map/ppermute | solution.py:35
  11.3 2.5 %collective-permute-start.5 = (bf16[3,64,256]{2,1,0:T(8,128)(2,1)S(1)}, bf16[3,64,256]{2,1,0:T(8,128)(2,1)S(1)}, u32[]{:S(2)}, u32[]{:S(2)}) collective-permute-start(bf16[3,64,256]{2,1,0:T(8,128)(2,1)S(1)} %collective-permute-done.4.refs_3_.refs_6_.refs_2_), channel_id=1, source_target_pairs={{0,8},{8,0},{16,24},{24,16},{1,9},{9,1},{17,25},{25,17},{2,10},{10... | collective-permute-start | bytes 294920 | tf_op jit(solution)/shard_map/ppermute | solution.py:35
  11.3 5.0 %collective-permute-start.7 = (bf16[2,2,64,256]{3,2,1,0:T(8,128)(2,1)S(1)}, bf16[2,2,64,256]{3,2,1,0:T(8,128)(2,1)S(1)}, u32[]{:S(2)}, u32[]{:S(2)}) collective-permute-start(bf16[2,2,64,256]{3,2,1,0:T(8,128)(2,1)S(1)} %pack_blocks.3.refs_2_.refs_4_), channel_id=1, source_target_pairs={{0,16},{2,18},{4,20},{6,22},{8,10},{10,8},{12,14},{14,12},{16,0},{... | collective-permute-start | bytes 393224 | tf_op jit(solution)/shard_map/ppermute | solution.py:385
  13.8 5.0 %collective-permute-start.6 = (bf16[2,2,64,256]{3,2,1,0:T(8,128)(2,1)S(1)}, bf16[2,2,64,256]{3,2,1,0:T(8,128)(2,1)S(1)}, u32[]{:S(2)}, u32[]{:S(2)}) collective-permute-start(bf16[2,2,64,256]{3,2,1,0:T(8,128)(2,1)S(1)} %pack_blocks.4), channel_id=1, source_target_pairs={{0,16},{2,18},{4,20},{6,22},{8,10},{10,8},{12,14},{14,12},{16,0},{... | collective-permute-start | bytes 393224 | tf_op jit(solution)/shard_map/ppermute | solution.py:385
  15.5 3.4 %collective-permute-start.9 = (bf16[2,2,64,256]{3,2,1,0:T(8,128)(2,1)S(1)}, bf16[2,2,64,256]{3,2,1,0:T(8,128)(2,1)S(1)}, u32[]{:S(2)}, u32[]{:S(2)}) collective-permute-start(bf16[2,2,64,256]{3,2,1,0:T(8,128)(2,1)S(1)} %collective-permute-done.1.refs_0_.refs_2_.refs_5_), channel_id=1, source_target_pairs={{0,8},{2,10},{4,12},{6,14},{8,0},{10,2},{12,4},{14,6},{16,24},{18,... | collective-permute-start | bytes 393224 | tf_op jit(solution)/shard_map/ppermute | solution.py:35
  16.3 2.6 %collective-permute-start.10 = (bf16[2,2,64,256]{3,2,1,0:T(8,128)(2,1)S(1)}, bf16[2,2,64,256]{3,2,1,0:T(8,128)(2,1)S(1)}, u32[]{:S(2)}, u32[]{:S(2)}) collective-permute-start(bf16[2,2,64,256]{3,2,1,0:T(8,128)(2,1)S(1)} %collective-permute-done.7.refs_3_.refs_6_), channel_id=1, source_target_pairs={{0,8},{2,10},{4,12},{6,14},{8,0},{10,2},{12,4},{14,6},{16,24},{18,... | collective-permute-start | bytes 393224 | tf_op jit(solution)/shard_map/ppermute | solution.py:35
  18.9 1.4 %collective-permute-start.8 = (bf16[2,2,64,256]{3,2,1,0:T(8,128)(2,1)S(1)}, bf16[2,2,64,256]{3,2,1,0:T(8,128)(2,1)S(1)}, u32[]{:S(2)}, u32[]{:S(2)}) collective-permute-start(bf16[2,2,64,256]{3,2,1,0:T(8,128)(2,1)S(1)} %pack_blocks.5), channel_id=1, source_target_pairs={{0,8},{2,10},{4,12},{6,14},{8,0},{10,2},{12,4},{14,6},{16,24},{18,... | collective-permute-start | bytes 393224 | tf_op jit(solution)/shard_map/ppermute | solution.py:35
  21.5 3.5 %collective-permute-start.11 = (f32[1,8]{1,0:T(1,128)S(1)}, f32[1,8]{1,0:T(1,128)S(1)}, u32[]{:S(2)}, u32[]{:S(2)}) collective-permute-start(f32[1,8]{1,0:T(1,128)S(1)} %step_logits.1), channel_id=1, source_target_pairs={{0,1},{1,0},{2,3},{3,2},{4,5},{5,4},{6,7},{7,6},{8,9},{9,8},{10,11... | collective-permute-start | bytes 104 | tf_op jit(solution)/shard_map/ppermute | solution.py:35

commit v13 on v5

--- a/solution.py
+++ b/solution.py
@@ -82,17 +82,16 @@
     return blocks
 
 
-def stage_kernel(length_ref, prompt_q, cand_q, prompt_kv, cand_kv, ends, head, *refs):
-    q_out, cand_out, kv_out, pay_out, ends_out, head_out, length_out, length_here, sems = refs
+def stage_kernel(prompt_q, cand_q, prompt_kv, cand_kv, ends, head, *refs):
+    q_out, cand_out, own_out, pay_out, ends_out, head_out, sems = refs
     steps = ends.shape[1]
     pairs = [
         (cand_q, cand_out),
         (ends, ends_out),
+        (prompt_kv, own_out),
         (cand_kv, pay_out.at[0:2]),
-        (prompt_kv, kv_out),
         (prompt_q, q_out),
         (head, head_out),
-        (length_ref, length_here),
     ]
     copies = [pltpu.make_async_copy(a, b, sems.at[i]) for i, (a, b) in enumerate(pairs)]
     for copy in copies:
@@ -109,7 +108,6 @@
     pay_out[2] = jnp.concatenate(pieces, axis=0).astype(jnp.bfloat16)
     for copy in copies[2:]:
         copy.wait()
-    length_out[...] = jnp.full(length_out.shape, length_here[0], jnp.int32)
 
 
 def column_of(row):
@@ -119,20 +117,22 @@
     return jnp.sum(jnp.where(down == right, row, 0), axis=1, keepdims=True)
 
 
-def staged(length, prompt_q, cand_q, prompt_kv, cand_kv, ends, head):
+def length_of(ends):
+    return ends[:, ends.shape[1] - 1 :] + 1
+
+
+def staged(prompt_q, cand_q, prompt_kv, cand_kv, ends, head):
     arrays = (prompt_q, cand_q, prompt_kv, cand_kv, ends, head)
-    payload = jax.ShapeDtypeStruct((3,) + cand_kv.shape[1:], cand_kv.dtype)
-    lengths = jax.ShapeDtypeStruct((1, HEADDIM), jnp.int32)
+    pay = jax.ShapeDtypeStruct((3,) + cand_kv.shape[1:], cand_kv.dtype)
     return pl.pallas_call(
         stage_kernel,
-        out_shape=(like(prompt_q), like(cand_q), like(prompt_kv), payload, like(ends), like(head), lengths),
-        in_specs=[pl.BlockSpec(memory_space=pl.ANY)]
-        + [pl.BlockSpec(memory_space=pltpu.HBM)] * len(arrays),
-        out_specs=tuple(vmem(7)),
-        scratch_shapes=[pltpu.SMEM((1,), jnp.int32), pltpu.SemaphoreType.DMA((len(arrays) + 1,))],
+        out_shape=(like(prompt_q), like(cand_q), like(prompt_kv), pay, like(ends), like(head)),
+        in_specs=[pl.BlockSpec(memory_space=pltpu.HBM)] * len(arrays),
+        out_specs=tuple(vmem(6)),
+        scratch_shapes=[pltpu.SemaphoreType.DMA((len(arrays),))],
         compiler_params=PARAMS,
         name="stage_operands",
-    )(length, *(pltpu.with_memory_space_constraint(a, pltpu.HBM) for a in arrays))
+    )(*(pltpu.with_memory_space_constraint(a, pltpu.HBM) for a in arrays))
 
 
 def tiles(q_ref, head):
@@ -205,7 +205,7 @@
     prompt_q, cand_q = next(take), next(take)
     block_refs = [next(take) for _ in arrays]
     pays = [next(take) for _ in masks]
-    lengths = next(take) if last else None
+    ends = next(take) if last else None
     old = None if first else [(next(take), next(take)) for _ in range(2)]
     outs = refs[-2:] if last else refs[-4:]
     rows = prompt_q.shape[0]
@@ -216,7 +216,7 @@
     own = [(ref, ()) for ref in pays]
     ctx = lax.axis_index("ctx")
     own_pos = key_positions([ctx ^ mask for mask in masks], cand_rows) if masks else None
-    alive = stacked_rows(ctx * cand_rows, cand_rows, cand_rows) < lengths[:, :1] if last else None
+    alive = stacked_rows(ctx * cand_rows, cand_rows, cand_rows) < length_of(ends[...]) if last else None
 
     for head in range(block_refs[0].shape[3] // HEADDIM):
         key_rows = head_rows(blocks, 0, head)
@@ -252,13 +252,13 @@
                     outs[kind][:, h * HEADDIM : (h + 1) * HEADDIM] = kept.astype(jnp.bfloat16)
 
 
-def phase(sizes, arrays, q_rows, blocks, pays=(), state=None, lengths=None, after=()):
+def phase(sizes, arrays, q_rows, blocks, pays=(), state=None, ends=None, after=()):
     prompt_q, cand_q = q_rows
-    first, last = state is None, lengths is not None
+    first, last = state is None, ends is not None
     operands = [prompt_q, cand_q] + [blocks[index] for index in arrays]
     operands += [b for b, _ in pays]
     if last:
-        operands.append(lengths)
+        operands.append(ends)
     if not first:
         operands += state
     heads = prompt_q.shape[1] // HEADDIM
@@ -286,7 +286,7 @@
     )(*operands, *after)
 
 
-def step_kernel(sizes, masks, ends_ref, head_ref, lengths_ref, *refs):
+def step_kernel(sizes, masks, ends_ref, head_ref, *refs):
     ctx_size, cand_size = sizes
     pays, blocks = refs[: len(masks)], refs[len(masks) : -2]
     logit_ref, kv_ref = refs[-2:]
@@ -310,6 +310,7 @@
     step_rows = [picked[at : at + steps] for at in range(0, steps * head_ref.shape[1] // width, steps)]
 
     ends = column_of(ends_ref[...])
+    alive = ends < length_of(ends_ref[...])
     own_pos = lax.broadcasted_iota(jnp.int32, (1, own_rows * len(masks)), 1)
     row_pos = jnp.concatenate([ends] * GROUP, axis=0)
     total = jnp.zeros((steps, HEADDIM), jnp.float32)
@@ -326,7 +327,7 @@
         blended = jnp.dot(weights, with_ones(kv_ref[1, :, columns]), preferred_element_type=jnp.float32)
         result = blended[:, :HEADDIM] / blended[:, HEADDIM:]
         for index, h in enumerate(heads):
-            kept = jnp.where(ends < lengths_ref[:, :1], result[index * steps : (index + 1) * steps], 0.0)
+            kept = jnp.where(alive, result[index * steps : (index + 1) * steps], 0.0)
             kept = kept.astype(jnp.bfloat16).astype(jnp.float32)
             total += kept * head_ref[:, h * HEADDIM : (h + 1) * HEADDIM]
     logits = jnp.sum(total, axis=1, keepdims=True)
@@ -335,7 +336,7 @@
     logit_ref[...] = jnp.sum(jnp.where(down == right, logits, 0.0), axis=0, keepdims=True)
 
 
-def step_shares(sizes, ends, head, lengths, pays, blocks):
+def step_shares(sizes, ends, head, pays, blocks):
     ctx_size, cand_size = sizes
     rows, width = blocks[0].shape[2:]
     count = rows * ctx_size * cand_size + pays[0][0].shape[1] * ctx_size
@@ -343,7 +344,7 @@
     return pl.pallas_call(
         functools.partial(step_kernel, sizes, [mask for _, mask in pays]),
         out_shape=jax.ShapeDtypeStruct(ends.shape, jnp.float32),
-        in_specs=vmem(3 + len(pays) + len(blocks)),
+        in_specs=vmem(2 + len(pays) + len(blocks)),
         out_specs=vmem(1)[0],
         scratch_shapes=[pltpu.VMEM((2, count, width), blocks[0].dtype)],
         compiler_params=PARAMS,
@@ -351,14 +352,14 @@
             flops=6 * scores * HEADDIM, bytes_accessed=scores, transcendentals=scores
         ),
         name="step_logits",
-    )(ends, head, lengths, *(b for b, _ in pays), *blocks)
+    )(ends, head, *(b for b, _ in pays), *blocks)
 
 
 def per_device(ctx_size, cand_size, prompt_q, prompt_kv, cand_q, cand_kv, cand_lengths, step_ends, reward_head):
     sizes = ctx_size, cand_size
     size = ctx_size * cand_size
-    prompt_rows, cand_rows, own, payload, ends, head, lengths = staged(
-        cand_lengths, prompt_q, cand_q[0], prompt_kv, cand_kv[:, 0], step_ends, reward_head[None]
+    prompt_rows, cand_rows, own, payload, ends, head = staged(
+        prompt_q, cand_q[0], prompt_kv, cand_kv[:, 0], step_ends, reward_head[None]
     )
     q_rows = prompt_rows, cand_rows
     pays = gather_cand(payload, ctx_size)
@@ -387,8 +388,8 @@
     state = phase(sizes, [1, 2], q_rows, blocks, pays=pays, state=state)
     blocks[7] = across_cores(packed(fourth, after=state[:1]))
     state = phase(sizes, [5, 6], q_rows, blocks, state=state)
-    step_logits = step_shares(sizes, ends, head, lengths, pays, blocks)
-    cand_out, prompt_out = phase(sizes, [3, 7], q_rows, blocks, state=state, lengths=lengths)
+    step_logits = step_shares(sizes, ends, head, pays, blocks)
+    cand_out, prompt_out = phase(sizes, [3, 7], q_rows, blocks, state=state, ends=ends)
     tp_size = lax.axis_size("tp")
     for bit in high_bits(tp_size, 1):
         step_logits = step_logits + flipped(step_logits, "tp", tp_size, bit)

time: 25.5 us -> 25.5 us (level)
  starting transfers between devices: 12.6 us -> 13.5 us
  between operations: 1.39 us -> 0.72 us
    ppermute x9, starting transfers between devices: 8.1 us -> 9.37 us  [flipped(): return lax.ppermute(block, axes, [(i, i ^ bit) for i in range(size)])]
    ppermute x3, starting transfers between devices: 4.53 us -> 4.17 us  [shared_out(): lax.ppermute(block, PROMPT_AXES, [(i, i ^ (odd if i & core else even)) fo...]
  transfers between devices with their start and end apart: 12 -> 12, of which waited for: 6 -> 4; matrix products, arithmetic and copies ran while one was open for 0% -> 0% of each run, Pallas kernels for 27% -> 26%
where the time goes in v13:
time: 25.5 us; the launch traced here: 25.4 us
  starting transfers between devices  13.5 us (53%)
  Pallas kernels  7.73 us (30%)
  waiting for transfers between devices  2.87 us (11%)
  between operations  0.72 us (3%)
  other arithmetic  0.51 us (2%)
    ppermute x9, starting transfers between devices, flipped(): return lax.ppermute(block, axes, [(i, i ^ bit) for i in range(size)])  9.37 us
    pallas_call x4, Pallas kernels, phase(): pl.pallas_call(functools.partial(phase_kernel, sizes, arrays, masks, firs...  5.4 us
    ppermute x3, starting transfers between devices, shared_out(): lax.ppermute(block, PROMPT_AXES, [(i, i ^ (odd if i & core else even)) fo...  4.17 us
    ppermute x3, waiting for transfers between devices, shared_out(): lax.ppermute(block, PROMPT_AXES, [(i, i ^ (odd if i & core else even)) fo...  1.48 us
    ppermute x9, waiting for transfers between devices, flipped(): return lax.ppermute(block, axes, [(i, i ^ bit) for i in range(size)])  1.39 us
    pallas_call x1, Pallas kernels, staged(): pl.pallas_call(stage_kernel, out_shape=(like(prompt_q), like(cand_q), lik...  1.24 us
    pallas_call x1, Pallas kernels, step_shares(): pl.pallas_call(functools.partial(step_kernel, sizes, [mask for _, mask in...  1.05 us
    add x1, other arithmetic, per_device(): step_logits = step_logits + flipped(step_logits, 'tp', tp_size, bit)  0.51 us
  transfers between devices with their start and end apart: 12, of which 4 were waited for; matrix products, arithmetic and copies ran while one was open for 0% of the time, Pallas kernels for 26%

profile of v13, /device:TPU:0, one launch (start us, length us, event | category | flops | bytes accessed | tf_op | source)
XLA Modules:
  0.0 25.4 jit_solution(1057509941843307455)
XLA Ops:
  0.6 4.1 %collective-permute-start = (bf16[1,2,64,256]{3,2,1,0:T(8,128)(2,1)}, bf16[1,2,64,256]{3,2,1,0:T(8,128)(2,1)S(1)}, u32[]{:S(2)}, u32[]{:S(2)}) collective-permute-start(bf16[1,2,64,256]{3,2,1,0:T(8,128)(2,1)} %bitcast.9), channel_id=1, source_target_pairs={{0,4},{2,6},{4,0},{6,2},{8,12},{10,14},{12,8},{14,10},{16,20},{18,... | collective-permute-start | bytes 196616 | tf_op jit(solution)/shard_map/ppermute | solution.py:35
  4.7 1.2 %stage_operands.1 = (bf16[64,2048]{1,0:T(8,128)(2,1)S(1)}, bf16[64,2048]{1,0:T(8,128)(2,1)S(1)}, bf16[2,64,256]{2,1,0:T(8,128)(2,1)S(1)}, bf16[3,64,256]{2,1,0:T...) custom-call(bf16[64,2048]{1,0:T(8,128)(2,1)} %prompt_q.1, bf16[64,2048]{1,0:T(8,128)(2,1)} %bitcast.7, ...), custom_call_target="tpu_custom_call" | custom-call | tf_op jit(solution)/shard_map/stage_operands/pallas_call | solution.py:127
  6.0 1.6 %collective-permute-start.4 = (bf16[3,64,256]{2,1,0:T(8,128)(2,1)S(1)}, bf16[3,64,256]{2,1,0:T(8,128)(2,1)S(1)}, u32[]{:S(2)}, u32[]{:S(2)}) collective-permute-start(bf16[3,64,256]{2,1,0:T(8,128)(2,1)S(1)} %get-tuple-element.27.refs_4_.refs_0_), channel_id=1, source_target_pairs={{0,16},{8,24},{16,0},{24,8},{1,17},{9,25},{17,1},{25,9},{2,18},{10... | collective-permute-start | bytes 294920 | tf_op jit(solution)/shard_map/ppermute | solution.py:35
  7.6 1.0 %collective-permute-done.refs_1_ = bf16[1,2,64,256]{3,2,1,0:T(8,128)(2,1)S(1)} collective-permute-done((bf16[1,2,64,256]{3,2,1,0:T(8,128)(2,1)}, bf16[1,2,64,256]{3,2,1,0:T(8,128)(2,1)S(1)}, u32[]{:S(2)}, u32[]{:S(2)}) %collective-permute-start) | collective-permute-done | bytes 65568 | tf_op jit(solution)/shard_map/ppermute | solution.py:35
  8.6 0.1 collective-permute-start.2
  8.7 0.7 %collective-permute-start.1 = (bf16[2,2,64,256]{3,2,1,0:T(8,128)(2,1)S(1)}, bf16[2,2,64,256]{3,2,1,0:T(8,128)(2,1)S(1)}, u32[]{:S(2)}, u32[]{:S(2)}) collective-permute-start(bf16[2,2,64,256]{3,2,1,0:T(8,128)(2,1)S(1)} %pack_blocks.3.refs_2_.refs_4_), channel_id=1, source_target_pairs={{0,2},{2,0},{4,6},{6,4},{8,24},{10,26},{12,28},{14,30},{16,18},{18... | collective-permute-start | bytes 393224 | tf_op jit(solution)/shard_map/ppermute | solution.py:372
  9.4 1.2 %collective-permute-start.3 = (bf16[3,64,256]{2,1,0:T(8,128)(2,1)S(1)}, bf16[3,64,256]{2,1,0:T(8,128)(2,1)S(1)}, u32[]{:S(2)}, u32[]{:S(2)}) collective-permute-start(bf16[3,64,256]{2,1,0:T(8,128)(2,1)S(1)} %get-tuple-element.27.refs_4_.refs_0_), channel_id=1, source_target_pairs={{0,8},{8,0},{16,24},{24,16},{1,9},{9,1},{17,25},{25,17},{2,10},{10... | collective-permute-start | bytes 294920 | tf_op jit(solution)/shard_map/ppermute | solution.py:35
  10.6 0.0 collective-permute-done.4.refs_3_.refs_6_.refs_2_
  10.7 0.0 collective-permute-start.5
  10.7 1.5 %collective-permute-start.7 = (bf16[2,2,64,256]{3,2,1,0:T(8,128)(2,1)S(1)}, bf16[2,2,64,256]{3,2,1,0:T(8,128)(2,1)S(1)}, u32[]{:S(2)}, u32[]{:S(2)}) collective-permute-start(bf16[2,2,64,256]{3,2,1,0:T(8,128)(2,1)S(1)} %pack_blocks.3.refs_2_.refs_4_), channel_id=1, source_target_pairs={{0,16},{2,18},{4,20},{6,22},{8,10},{10,8},{12,14},{14,12},{16,0},{... | collective-permute-start | bytes 393224 | tf_op jit(solution)/shard_map/ppermute | solution.py:372
  12.2 0.0 collective-permute-done.2.refs_3_.refs_8_
  12.2 0.9 %attend_0_4.1 = (f32[1024,128]{1,0:T(8,128)S(1)}, f32[1024,256]{1,0:T(8,128)S(1)}, f32[1024,128]{1,0:T(8,128)S(1)}, f32[1024,256]{1,0:T(8,128)S(1)}) custom-call(bf16[64,2048]{1,0:T(8,128)(2,1)S(1)} %get-tuple-element.23.refs_0_, bf16[64,2048]{1,0:T(8,128)(2,1)S(1)} %get-tuple-element.24.refs_1_, bf16[2,2,64,256]{3,2,1,0:T(8,128)(2,1)S(1)} %pack_blocks.3.refs_2_.refs_4_, ...), custom_call_target="tpu_custom_call" | custom-call | flops 402653184 | bytes 524288 | tf_op jit(solution)/shard_map/attend_0_4/pallas_call | solution.py:276
  13.1 0.0 collective-permute-done.3.refs_2_.refs_5_.refs_1_
  13.1 0.6 %collective-permute-done.1.refs_0_.refs_2_.refs_5_ = bf16[2,2,64,256]{3,2,1,0:T(8,128)(2,1)S(1)} collective-permute-done((bf16[2,2,64,256]{3,2,1,0:T(8,128)(2,1)S(1)}, bf16[2,2,64,256]{3,2,1,0:T(8,128)(2,1)S(1)}, u32[]{:S(2)}, u32[]{:S(2)}) %collective-permute-start.1) | collective-permute-done | bytes 131104 | tf_op jit(solution)/shard_map/ppermute | solution.py:372
  13.7 0.0 collective-permute-done.5.refs_4_.refs_7_.refs_3_
  13.7 1.9 %collective-permute-start.6 = (bf16[2,2,64,256]{3,2,1,0:T(8,128)(2,1)S(1)}, bf16[2,2,64,256]{3,2,1,0:T(8,128)(2,1)S(1)}, u32[]{:S(2)}, u32[]{:S(2)}) collective-permute-start(bf16[2,2,64,256]{3,2,1,0:T(8,128)(2,1)S(1)} %pack_blocks.4), channel_id=1, source_target_pairs={{0,16},{2,18},{4,20},{6,22},{8,10},{10,8},{12,14},{14,12},{16,0},{... | collective-permute-start | bytes 393224 | tf_op jit(solution)/shard_map/ppermute | solution.py:372
  15.7 0.0 collective-permute-start.9
  15.7 0.0 collective-permute-done.7.refs_3_.refs_6_
  15.7 0.5 %collective-permute-start.10 = (bf16[2,2,64,256]{3,2,1,0:T(8,128)(2,1)S(1)}, bf16[2,2,64,256]{3,2,1,0:T(8,128)(2,1)S(1)}, u32[]{:S(2)}, u32[]{:S(2)}) collective-permute-start(bf16[2,2,64,256]{3,2,1,0:T(8,128)(2,1)S(1)} %collective-permute-done.7.refs_3_.refs_6_), channel_id=1, source_target_pairs={{0,8},{2,10},{4,12},{6,14},{8,0},{10,2},{12,4},{14,6},{16,24},{18,... | collective-permute-start | bytes 393224 | tf_op jit(solution)/shard_map/ppermute | solution.py:35
  16.2 1.7 %attend_1_2.1 = (f32[1024,128]{1,0:T(8,128)S(1)}, f32[1024,256]{1,0:T(8,128)S(1)}, f32[1024,128]{1,0:T(8,128)S(1)}, f32[1024,256]{1,0:T(8,128)S(1)}) custom-call(bf16[64,2048]{1,0:T(8,128)(2,1)S(1)} %get-tuple-element.23.refs_0_, bf16[64,2048]{1,0:T(8,128)(2,1)S(1)} %get-tuple-element.24.refs_1_, ...), custom_call_target="tpu_custom_call" | custom-call | flops 402653184 | bytes 524288 | tf_op jit(solution)/shard_map/attend_1_2/pallas_call | solution.py:276
  17.9 0.9 %collective-permute-done.6.refs_0_.refs_2_.refs_7_ = bf16[2,2,64,256]{3,2,1,0:T(8,128)(2,1)S(1)} collective-permute-done((bf16[2,2,64,256]{3,2,1,0:T(8,128)(2,1)S(1)}, bf16[2,2,64,256]{3,2,1,0:T(8,128)(2,1)S(1)}, u32[]{:S(2)}, u32[]{:S(2)}) %collective-permute-start.6) | collective-permute-done | bytes 131104 | tf_op jit(solution)/shard_map/ppermute | solution.py:372
  18.8 0.1 collective-permute-start.8
  18.9 0.0 collective-permute-done.9.refs_2_.refs_9_
  18.9 0.0 collective-permute-done.10.refs_3_.refs_10_
  18.9 1.0 %attend_5_6.1 = (f32[1024,128]{1,0:T(8,128)S(1)}, f32[1024,256]{1,0:T(8,128)S(1)}, f32[1024,128]{1,0:T(8,128)S(1)}, f32[1024,256]{1,0:T(8,128)S(1)}) custom-call(bf16[64,2048]{1,0:T(8,128)(2,1)S(1)} %get-tuple-element.23.refs_0_, bf16[64,2048]{1,0:T(8,128)(2,1)S(1)} %get-tuple-element.24.refs_1_, ...), custom_call_target="tpu_custom_call" | custom-call | flops 402653184 | bytes 524288 | tf_op jit(solution)/shard_map/attend_5_6/pallas_call | solution.py:276
  19.9 0.3 %collective-permute-done.8.refs_3_.refs_11_ = bf16[2,2,64,256]{3,2,1,0:T(8,128)(2,1)S(1)} collective-permute-done((bf16[2,2,64,256]{3,2,1,0:T(8,128)(2,1)S(1)}, bf16[2,2,64,256]{3,2,1,0:T(8,128)(2,1)S(1)}, u32[]{:S(2)}, u32[]{:S(2)}) %collective-permute-start.8) | collective-permute-done | bytes 131104 | tf_op jit(solution)/shard_map/ppermute | solution.py:35
  20.2 1.1 %step_logits.1 = f32[1,8]{1,0:T(1,128)S(1)} custom-call(s32[1,8]{1,0:T(1,128)S(1)} %get-tuple-element.32.refs_4_.ends_ref, f32[1,2048]{1,0:T(1,128)S(1)} %get-tuple-element.42.head_ref, bf16[3,64,256]{2,1,0:T(8,128)(2,1)S(1)} %get-tuple-element.27.refs_4_.refs_0_, bf16[3,64,256]{2,1,0:T(8,128)(2,1)S(1)} %collective-permute-done.3.refs_2_.refs_5_.refs_1_, ...), custom_call_target="tpu_custom_call" | custom-call | flops 125829120 | bytes 163840 | tf_op jit(solution)/shard_map/step_logits/pallas_call | solution.py:344
  21.3 1.8 %collective-permute-start.11 = (f32[1,8]{1,0:T(1,128)S(1)}, f32[1,8]{1,0:T(1,128)S(1)}, u32[]{:S(2)}, u32[]{:S(2)}) collective-permute-start(f32[1,8]{1,0:T(1,128)S(1)} %step_logits.1), channel_id=1, source_target_pairs={{0,1},{1,0},{2,3},{3,2},{4,5},{5,4},{6,7},{7,6},{8,9},{9,8},{10,11... | collective-permute-start | bytes 104 | tf_op jit(solution)/shard_map/ppermute | solution.py:35
  23.1 1.8 %attend_3_7.1 = (bf16[64,2048]{1,0:T(8,128)(2,1)}, bf16[64,2048]{1,0:T(8,128)(2,1)}) custom-call(bf16[64,2048]{1,0:T(8,128)(2,1)S(1)} %get-tuple-element.23.refs_0_, bf16[64,2048]{1,0:T(8,128)(2,1)S(1)} %get-tuple-element.24.refs_1_, bf16[2,2,64,256]{3,2,1,0:T(8,128)(2,1)S(1)} %collective-permute-done.6.refs_0_.refs_2_.refs_7_, ...), custom_call_target="tpu_custom_call" | custom-call | flops 402653184 | bytes 524288 | tf_op jit(solution)/shard_map/attend_3_7/pallas_call | solution.py:276
  24.9 0.0 collective-permute-done.11
  24.9 0.5 %add.3 = f32[1,8]{1,0:T(1,128)} add(f32[1,8]{1,0:T(1,128)S(1)} %step_logits.1, f32[1,8]{1,0:T(1,128)S(1)} %collective-permute-done.11) | non-fusion elementwise | flops 8 | bytes 96 | tf_op jit(solution)/shard_map/add | solution.py:395
  (3 shorter events, 0.0 us)
Async XLA Ops:
  0.6 8.0 %collective-permute-start = (bf16[1,2,64,256]{3,2,1,0:T(8,128)(2,1)}, bf16[1,2,64,256]{3,2,1,0:T(8,128)(2,1)S(1)}, u32[]{:S(2)}, u32[]{:S(2)}) collective-permute-start(bf16[1,2,64,256]{3,2,1,0:T(8,128)(2,1)} %bitcast.9), channel_id=1, source_target_pairs={{0,4},{2,6},{4,0},{6,2},{8,12},{10,14},{12,8},{14,10},{16,20},{18,... | collective-permute-start | bytes 196616 | tf_op jit(solution)/shard_map/ppermute | solution.py:35
  6.0 4.7 %collective-permute-start.4 = (bf16[3,64,256]{2,1,0:T(8,128)(2,1)S(1)}, bf16[3,64,256]{2,1,0:T(8,128)(2,1)S(1)}, u32[]{:S(2)}, u32[]{:S(2)}) collective-permute-start(bf16[3,64,256]{2,1,0:T(8,128)(2,1)S(1)} %get-tuple-element.27.refs_4_.refs_0_), channel_id=1, source_target_pairs={{0,16},{8,24},{16,0},{24,8},{1,17},{9,25},{17,1},{25,9},{2,18},{10... | collective-permute-start | bytes 294920 | tf_op jit(solution)/shard_map/ppermute | solution.py:35
  8.6 3.6 %collective-permute-start.2 = (bf16[2,2,64,256]{3,2,1,0:T(8,128)(2,1)S(1)}, bf16[2,2,64,256]{3,2,1,0:T(8,128)(2,1)S(1)}, u32[]{:S(2)}, u32[]{:S(2)}) collective-permute-start(bf16[2,2,64,256]{3,2,1,0:T(8,128)(2,1)S(1)} %pack_blocks.3.refs_2_.refs_4_), channel_id=1, source_target_pairs={{0,8},{2,10},{4,12},{6,14},{8,0},{10,2},{12,4},{14,6},{16,24},{18,... | collective-permute-start | bytes 393224 | tf_op jit(solution)/shard_map/ppermute | solution.py:35
  8.7 5.0 %collective-permute-start.1 = (bf16[2,2,64,256]{3,2,1,0:T(8,128)(2,1)S(1)}, bf16[2,2,64,256]{3,2,1,0:T(8,128)(2,1)S(1)}, u32[]{:S(2)}, u32[]{:S(2)}) collective-permute-start(bf16[2,2,64,256]{3,2,1,0:T(8,128)(2,1)S(1)} %pack_blocks.3.refs_2_.refs_4_), channel_id=1, source_target_pairs={{0,2},{2,0},{4,6},{6,4},{8,24},{10,26},{12,28},{14,30},{16,18},{18... | collective-permute-start | bytes 393224 | tf_op jit(solution)/shard_map/ppermute | solution.py:372
  9.4 3.7 %collective-permute-start.3 = (bf16[3,64,256]{2,1,0:T(8,128)(2,1)S(1)}, bf16[3,64,256]{2,1,0:T(8,128)(2,1)S(1)}, u32[]{:S(2)}, u32[]{:S(2)}) collective-permute-start(bf16[3,64,256]{2,1,0:T(8,128)(2,1)S(1)} %get-tuple-element.27.refs_4_.refs_0_), channel_id=1, source_target_pairs={{0,8},{8,0},{16,24},{24,16},{1,9},{9,1},{17,25},{25,17},{2,10},{10... | collective-permute-start | bytes 294920 | tf_op jit(solution)/shard_map/ppermute | solution.py:35
  10.7 3.1 %collective-permute-start.5 = (bf16[3,64,256]{2,1,0:T(8,128)(2,1)S(1)}, bf16[3,64,256]{2,1,0:T(8,128)(2,1)S(1)}, u32[]{:S(2)}, u32[]{:S(2)}) collective-permute-start(bf16[3,64,256]{2,1,0:T(8,128)(2,1)S(1)} %collective-permute-done.4.refs_3_.refs_6_.refs_2_), channel_id=1, source_target_pairs={{0,8},{8,0},{16,24},{24,16},{1,9},{9,1},{17,25},{25,17},{2,10},{10... | collective-permute-start | bytes 294920 | tf_op jit(solution)/shard_map/ppermute | solution.py:35
  10.7 5.0 %collective-permute-start.7 = (bf16[2,2,64,256]{3,2,1,0:T(8,128)(2,1)S(1)}, bf16[2,2,64,256]{3,2,1,0:T(8,128)(2,1)S(1)}, u32[]{:S(2)}, u32[]{:S(2)}) collective-permute-start(bf16[2,2,64,256]{3,2,1,0:T(8,128)(2,1)S(1)} %pack_blocks.3.refs_2_.refs_4_), channel_id=1, source_target_pairs={{0,16},{2,18},{4,20},{6,22},{8,10},{10,8},{12,14},{14,12},{16,0},{... | collective-permute-start | bytes 393224 | tf_op jit(solution)/shard_map/ppermute | solution.py:372
  13.7 5.0 %collective-permute-start.6 = (bf16[2,2,64,256]{3,2,1,0:T(8,128)(2,1)S(1)}, bf16[2,2,64,256]{3,2,1,0:T(8,128)(2,1)S(1)}, u32[]{:S(2)}, u32[]{:S(2)}) collective-permute-start(bf16[2,2,64,256]{3,2,1,0:T(8,128)(2,1)S(1)} %pack_blocks.4), channel_id=1, source_target_pairs={{0,16},{2,18},{4,20},{6,22},{8,10},{10,8},{12,14},{14,12},{16,0},{... | collective-permute-start | bytes 393224 | tf_op jit(solution)/shard_map/ppermute | solution.py:372
  15.7 3.2 %collective-permute-start.9 = (bf16[2,2,64,256]{3,2,1,0:T(8,128)(2,1)S(1)}, bf16[2,2,64,256]{3,2,1,0:T(8,128)(2,1)S(1)}, u32[]{:S(2)}, u32[]{:S(2)}) collective-permute-start(bf16[2,2,64,256]{3,2,1,0:T(8,128)(2,1)S(1)} %collective-permute-done.1.refs_0_.refs_2_.refs_5_), channel_id=1, source_target_pairs={{0,8},{2,10},{4,12},{6,14},{8,0},{10,2},{12,4},{14,6},{16,24},{18,... | collective-permute-start | bytes 393224 | tf_op jit(solution)/shard_map/ppermute | solution.py:35
  15.7 3.2 %collective-permute-start.10 = (bf16[2,2,64,256]{3,2,1,0:T(8,128)(2,1)S(1)}, bf16[2,2,64,256]{3,2,1,0:T(8,128)(2,1)S(1)}, u32[]{:S(2)}, u32[]{:S(2)}) collective-permute-start(bf16[2,2,64,256]{3,2,1,0:T(8,128)(2,1)S(1)} %collective-permute-done.7.refs_3_.refs_6_), channel_id=1, source_target_pairs={{0,8},{2,10},{4,12},{6,14},{8,0},{10,2},{12,4},{14,6},{16,24},{18,... | collective-permute-start | bytes 393224 | tf_op jit(solution)/shard_map/ppermute | solution.py:35
  18.8 1.4 %collective-permute-start.8 = (bf16[2,2,64,256]{3,2,1,0:T(8,128)(2,1)S(1)}, bf16[2,2,64,256]{3,2,1,0:T(8,128)(2,1)S(1)}, u32[]{:S(2)}, u32[]{:S(2)}) collective-permute-start(bf16[2,2,64,256]{3,2,1,0:T(8,128)(2,1)S(1)} %pack_blocks.5), channel_id=1, source_target_pairs={{0,8},{2,10},{4,12},{6,14},{8,0},{10,2},{12,4},{14,6},{16,24},{18,... | collective-permute-start | bytes 393224 | tf_op jit(solution)/shard_map/ppermute | solution.py:35
  21.3 3.6 %collective-permute-start.11 = (f32[1,8]{1,0:T(1,128)S(1)}, f32[1,8]{1,0:T(1,128)S(1)}, u32[]{:S(2)}, u32[]{:S(2)}) collective-permute-start(f32[1,8]{1,0:T(1,128)S(1)} %step_logits.1), channel_id=1, source_target_pairs={{0,1},{1,0},{2,3},{3,2},{4,5},{5,4},{6,7},{7,6},{8,9},{9,8},{10,11... | collective-permute-start | bytes 104 | tf_op jit(solution)/shard_map/ppermute | solution.py:35

commit v14 on v13

--- a/solution.py
+++ b/solution.py
@@ -311,24 +311,33 @@
 
     ends = column_of(ends_ref[...])
     alive = ends < length_of(ends_ref[...])
+    kinds = width // HEADDIM
+    stacked = GROUP * steps
+    parts = []
+    for head in range(kinds):
+        places = [divmod(h * HEADDIM, width) for h in range(head * GROUP, (head + 1) * GROUP)]
+        part = jnp.concatenate([step_rows[a][:, b : b + HEADDIM] for a, b in places], axis=0)
+        sides = [part if other == head else jnp.zeros_like(part) for other in range(kinds)]
+        parts.append(jnp.concatenate(sides, axis=1))
+    queries = jnp.concatenate(parts, axis=0).astype(jnp.bfloat16)
     own_pos = lax.broadcasted_iota(jnp.int32, (1, own_rows * len(masks)), 1)
-    row_pos = jnp.concatenate([ends] * GROUP, axis=0)
+    row_pos = jnp.concatenate([ends] * (GROUP * kinds), axis=0)
+    scores = product(queries, kv_ref[0])
+    bound = jnp.where(own_pos <= row_pos, scores[:, free:], NEG_FILL)
+    scores = jnp.concatenate([scores[:, :free], bound], axis=1)
+    peak = jnp.max(scores, axis=1, keepdims=True)
+    weights = jnp.exp2((scores - peak) * SCALE).astype(jnp.bfloat16)
+    value_rows = kv_ref[1]
+    widened = jnp.concatenate([value_rows, jnp.ones_like(value_rows[:, :HEADDIM])], axis=1)
+    blended = jnp.dot(weights, widened, preferred_element_type=jnp.float32)
     total = jnp.zeros((steps, HEADDIM), jnp.float32)
-    for head in range(width // HEADDIM):
-        columns = slice(head * HEADDIM, (head + 1) * HEADDIM)
-        heads = range(head * GROUP, (head + 1) * GROUP)
-        places = [divmod(h * HEADDIM, width) for h in heads]
-        queries = jnp.concatenate([step_rows[a][:, b : b + HEADDIM] for a, b in places], axis=0)
-        scores = product(queries.astype(jnp.bfloat16), kv_ref[0, :, columns])
-        bound = jnp.where(own_pos <= row_pos, scores[:, free:], NEG_FILL)
-        scores = jnp.concatenate([scores[:, :free], bound], axis=1)
-        peak = jnp.max(scores, axis=1, keepdims=True)
-        weights = jnp.exp2((scores - peak) * SCALE).astype(jnp.bfloat16)
-        blended = jnp.dot(weights, with_ones(kv_ref[1, :, columns]), preferred_element_type=jnp.float32)
-        result = blended[:, :HEADDIM] / blended[:, HEADDIM:]
-        for index, h in enumerate(heads):
+    for head in range(kinds):
+        mixed = blended[head * stacked : (head + 1) * stacked]
+        result = mixed[:, head * HEADDIM : (head + 1) * HEADDIM] / mixed[:, width:]
+        for index in range(GROUP):
             kept = jnp.where(alive, result[index * steps : (index + 1) * steps], 0.0)
             kept = kept.astype(jnp.bfloat16).astype(jnp.float32)
+            h = head * GROUP + index
             total += kept * head_ref[:, h * HEADDIM : (h + 1) * HEADDIM]
     logits = jnp.sum(total, axis=1, keepdims=True)
     down = lax.broadcasted_iota(jnp.int32, (steps, steps), 0)

time: 25.5 us -> 25.5 us (level)
  no operation moved by 1% of the time
where the time goes in v14:
time: 25.5 us; the launch traced here: 25.3 us
  starting transfers between devices  13.5 us (53%)
  Pallas kernels  7.66 us (30%)
  waiting for transfers between devices  2.87 us (11%)
  between operations  0.72 us (3%)
  other arithmetic  0.51 us (2%)
    ppermute x9, starting transfers between devices, flipped(): return lax.ppermute(block, axes, [(i, i ^ bit) for i in range(size)])  9.37 us
    pallas_call x4, Pallas kernels, phase(): pl.pallas_call(functools.partial(phase_kernel, sizes, arrays, masks, firs...  5.4 us
    ppermute x3, starting transfers between devices, shared_out(): lax.ppermute(block, PROMPT_AXES, [(i, i ^ (odd if i & core else even)) fo...  4.17 us
    ppermute x3, waiting for transfers between devices, shared_out(): lax.ppermute(block, PROMPT_AXES, [(i, i ^ (odd if i & core else even)) fo...  1.48 us
    ppermute x9, waiting for transfers between devices, flipped(): return lax.ppermute(block, axes, [(i, i ^ bit) for i in range(size)])  1.39 us
    pallas_call x1, Pallas kernels, staged(): pl.pallas_call(stage_kernel, out_shape=(like(prompt_q), like(cand_q), lik...  1.24 us
    pallas_call x1, Pallas kernels, step_shares(): pl.pallas_call(functools.partial(step_kernel, sizes, [mask for _, mask in...  0.99 us
    add x1, other arithmetic, per_device(): step_logits = step_logits + flipped(step_logits, 'tp', tp_size, bit)  0.51 us
  transfers between devices with their start and end apart: 12, of which 4 were waited for; matrix products, arithmetic and copies ran while one was open for 0% of the time, Pallas kernels for 26%

profile of v14, /device:TPU:0, one launch (start us, length us, event | category | flops | bytes accessed | tf_op | source)
XLA Modules:
  0.0 25.3 jit_solution(10860228114942439443)
XLA Ops:
  0.6 4.1 %collective-permute-start = (bf16[1,2,64,256]{3,2,1,0:T(8,128)(2,1)}, bf16[1,2,64,256]{3,2,1,0:T(8,128)(2,1)S(1)}, u32[]{:S(2)}, u32[]{:S(2)}) collective-permute-start(bf16[1,2,64,256]{3,2,1,0:T(8,128)(2,1)} %bitcast.9), channel_id=1, source_target_pairs={{0,4},{2,6},{4,0},{6,2},{8,12},{10,14},{12,8},{14,10},{16,20},{18,... | collective-permute-start | bytes 196616 | tf_op jit(solution)/shard_map/ppermute | solution.py:35
  4.7 1.2 %stage_operands.1 = (bf16[64,2048]{1,0:T(8,128)(2,1)S(1)}, bf16[64,2048]{1,0:T(8,128)(2,1)S(1)}, bf16[2,64,256]{2,1,0:T(8,128)(2,1)S(1)}, bf16[3,64,256]{2,1,0:T...) custom-call(bf16[64,2048]{1,0:T(8,128)(2,1)} %prompt_q.1, bf16[64,2048]{1,0:T(8,128)(2,1)} %bitcast.7, ...), custom_call_target="tpu_custom_call" | custom-call | tf_op jit(solution)/shard_map/stage_operands/pallas_call | solution.py:127
  6.0 1.6 %collective-permute-start.4 = (bf16[3,64,256]{2,1,0:T(8,128)(2,1)S(1)}, bf16[3,64,256]{2,1,0:T(8,128)(2,1)S(1)}, u32[]{:S(2)}, u32[]{:S(2)}) collective-permute-start(bf16[3,64,256]{2,1,0:T(8,128)(2,1)S(1)} %get-tuple-element.27.refs_4_.refs_0_), channel_id=1, source_target_pairs={{0,16},{8,24},{16,0},{24,8},{1,17},{9,25},{17,1},{25,9},{2,18},{10... | collective-permute-start | bytes 294920 | tf_op jit(solution)/shard_map/ppermute | solution.py:35
  7.6 1.0 %collective-permute-done.refs_1_ = bf16[1,2,64,256]{3,2,1,0:T(8,128)(2,1)S(1)} collective-permute-done((bf16[1,2,64,256]{3,2,1,0:T(8,128)(2,1)}, bf16[1,2,64,256]{3,2,1,0:T(8,128)(2,1)S(1)}, u32[]{:S(2)}, u32[]{:S(2)}) %collective-permute-start) | collective-permute-done | bytes 65568 | tf_op jit(solution)/shard_map/ppermute | solution.py:35
  8.6 0.1 collective-permute-start.2
  8.7 0.7 %collective-permute-start.1 = (bf16[2,2,64,256]{3,2,1,0:T(8,128)(2,1)S(1)}, bf16[2,2,64,256]{3,2,1,0:T(8,128)(2,1)S(1)}, u32[]{:S(2)}, u32[]{:S(2)}) collective-permute-start(bf16[2,2,64,256]{3,2,1,0:T(8,128)(2,1)S(1)} %pack_blocks.3.refs_2_.refs_4_), channel_id=1, source_target_pairs={{0,2},{2,0},{4,6},{6,4},{8,24},{10,26},{12,28},{14,30},{16,18},{18... | collective-permute-start | bytes 393224 | tf_op jit(solution)/shard_map/ppermute | solution.py:381
  9.4 1.2 %collective-permute-start.3 = (bf16[3,64,256]{2,1,0:T(8,128)(2,1)S(1)}, bf16[3,64,256]{2,1,0:T(8,128)(2,1)S(1)}, u32[]{:S(2)}, u32[]{:S(2)}) collective-permute-start(bf16[3,64,256]{2,1,0:T(8,128)(2,1)S(1)} %get-tuple-element.27.refs_4_.refs_0_), channel_id=1, source_target_pairs={{0,8},{8,0},{16,24},{24,16},{1,9},{9,1},{17,25},{25,17},{2,10},{10... | collective-permute-start | bytes 294920 | tf_op jit(solution)/shard_map/ppermute | solution.py:35
  10.6 0.0 collective-permute-done.4.refs_3_.refs_6_.refs_2_
  10.7 0.0 collective-permute-start.5
  10.7 1.5 %collective-permute-start.7 = (bf16[2,2,64,256]{3,2,1,0:T(8,128)(2,1)S(1)}, bf16[2,2,64,256]{3,2,1,0:T(8,128)(2,1)S(1)}, u32[]{:S(2)}, u32[]{:S(2)}) collective-permute-start(bf16[2,2,64,256]{3,2,1,0:T(8,128)(2,1)S(1)} %pack_blocks.3.refs_2_.refs_4_), channel_id=1, source_target_pairs={{0,16},{2,18},{4,20},{6,22},{8,10},{10,8},{12,14},{14,12},{16,0},{... | collective-permute-start | bytes 393224 | tf_op jit(solution)/shard_map/ppermute | solution.py:381
  12.2 0.0 collective-permute-done.2.refs_3_.refs_8_
  12.2 0.9 %attend_0_4.1 = (f32[1024,128]{1,0:T(8,128)S(1)}, f32[1024,256]{1,0:T(8,128)S(1)}, f32[1024,128]{1,0:T(8,128)S(1)}, f32[1024,256]{1,0:T(8,128)S(1)}) custom-call(bf16[64,2048]{1,0:T(8,128)(2,1)S(1)} %get-tuple-element.23.refs_0_, bf16[64,2048]{1,0:T(8,128)(2,1)S(1)} %get-tuple-element.24.refs_1_, bf16[2,2,64,256]{3,2,1,0:T(8,128)(2,1)S(1)} %pack_blocks.3.refs_2_.refs_4_, ...), custom_call_target="tpu_custom_call" | custom-call | flops 402653184 | bytes 524288 | tf_op jit(solution)/shard_map/attend_0_4/pallas_call | solution.py:276
  13.1 0.0 collective-permute-done.3.refs_2_.refs_5_.refs_1_
  13.1 0.6 %collective-permute-done.1.refs_0_.refs_2_.refs_5_ = bf16[2,2,64,256]{3,2,1,0:T(8,128)(2,1)S(1)} collective-permute-done((bf16[2,2,64,256]{3,2,1,0:T(8,128)(2,1)S(1)}, bf16[2,2,64,256]{3,2,1,0:T(8,128)(2,1)S(1)}, u32[]{:S(2)}, u32[]{:S(2)}) %collective-permute-start.1) | collective-permute-done | bytes 131104 | tf_op jit(solution)/shard_map/ppermute | solution.py:381
  13.7 0.0 collective-permute-done.5.refs_4_.refs_7_.refs_3_
  13.7 1.9 %collective-permute-start.6 = (bf16[2,2,64,256]{3,2,1,0:T(8,128)(2,1)S(1)}, bf16[2,2,64,256]{3,2,1,0:T(8,128)(2,1)S(1)}, u32[]{:S(2)}, u32[]{:S(2)}) collective-permute-start(bf16[2,2,64,256]{3,2,1,0:T(8,128)(2,1)S(1)} %pack_blocks.4), channel_id=1, source_target_pairs={{0,16},{2,18},{4,20},{6,22},{8,10},{10,8},{12,14},{14,12},{16,0},{... | collective-permute-start | bytes 393224 | tf_op jit(solution)/shard_map/ppermute | solution.py:381
  15.7 0.0 collective-permute-start.9
  15.7 0.0 collective-permute-done.7.refs_3_.refs_6_
  15.7 0.5 %collective-permute-start.10 = (bf16[2,2,64,256]{3,2,1,0:T(8,128)(2,1)S(1)}, bf16[2,2,64,256]{3,2,1,0:T(8,128)(2,1)S(1)}, u32[]{:S(2)}, u32[]{:S(2)}) collective-permute-start(bf16[2,2,64,256]{3,2,1,0:T(8,128)(2,1)S(1)} %collective-permute-done.7.refs_3_.refs_6_), channel_id=1, source_target_pairs={{0,8},{2,10},{4,12},{6,14},{8,0},{10,2},{12,4},{14,6},{16,24},{18,... | collective-permute-start | bytes 393224 | tf_op jit(solution)/shard_map/ppermute | solution.py:35
  16.2 1.7 %attend_1_2.1 = (f32[1024,128]{1,0:T(8,128)S(1)}, f32[1024,256]{1,0:T(8,128)S(1)}, f32[1024,128]{1,0:T(8,128)S(1)}, f32[1024,256]{1,0:T(8,128)S(1)}) custom-call(bf16[64,2048]{1,0:T(8,128)(2,1)S(1)} %get-tuple-element.23.refs_0_, bf16[64,2048]{1,0:T(8,128)(2,1)S(1)} %get-tuple-element.24.refs_1_, ...), custom_call_target="tpu_custom_call" | custom-call | flops 402653184 | bytes 524288 | tf_op jit(solution)/shard_map/attend_1_2/pallas_call | solution.py:276
  17.9 0.9 %collective-permute-done.6.refs_0_.refs_2_.refs_7_ = bf16[2,2,64,256]{3,2,1,0:T(8,128)(2,1)S(1)} collective-permute-done((bf16[2,2,64,256]{3,2,1,0:T(8,128)(2,1)S(1)}, bf16[2,2,64,256]{3,2,1,0:T(8,128)(2,1)S(1)}, u32[]{:S(2)}, u32[]{:S(2)}) %collective-permute-start.6) | collective-permute-done | bytes 131104 | tf_op jit(solution)/shard_map/ppermute | solution.py:381
  18.8 0.1 collective-permute-start.8
  18.9 0.0 collective-permute-done.9.refs_2_.refs_9_
  18.9 0.0 collective-permute-done.10.refs_3_.refs_10_
  18.9 1.0 %attend_5_6.1 = (f32[1024,128]{1,0:T(8,128)S(1)}, f32[1024,256]{1,0:T(8,128)S(1)}, f32[1024,128]{1,0:T(8,128)S(1)}, f32[1024,256]{1,0:T(8,128)S(1)}) custom-call(bf16[64,2048]{1,0:T(8,128)(2,1)S(1)} %get-tuple-element.23.refs_0_, bf16[64,2048]{1,0:T(8,128)(2,1)S(1)} %get-tuple-element.24.refs_1_, ...), custom_call_target="tpu_custom_call" | custom-call | flops 402653184 | bytes 524288 | tf_op jit(solution)/shard_map/attend_5_6/pallas_call | solution.py:276
  19.9 0.3 %collective-permute-done.8.refs_3_.refs_11_ = bf16[2,2,64,256]{3,2,1,0:T(8,128)(2,1)S(1)} collective-permute-done((bf16[2,2,64,256]{3,2,1,0:T(8,128)(2,1)S(1)}, bf16[2,2,64,256]{3,2,1,0:T(8,128)(2,1)S(1)}, u32[]{:S(2)}, u32[]{:S(2)}) %collective-permute-start.8) | collective-permute-done | bytes 131104 | tf_op jit(solution)/shard_map/ppermute | solution.py:35
  20.2 1.0 %step_logits.1 = f32[1,8]{1,0:T(1,128)S(1)} custom-call(s32[1,8]{1,0:T(1,128)S(1)} %get-tuple-element.32.refs_4_.ends_ref, f32[1,2048]{1,0:T(1,128)S(1)} %get-tuple-element.42.head_ref, bf16[3,64,256]{2,1,0:T(8,128)(2,1)S(1)} %get-tuple-element.27.refs_4_.refs_0_, bf16[3,64,256]{2,1,0:T(8,128)(2,1)S(1)} %collective-permute-done.3.refs_2_.refs_5_.refs_1_, ...), custom_call_target="tpu_custom_call" | custom-call | flops 125829120 | bytes 163840 | tf_op jit(solution)/shard_map/step_logits/pallas_call | solution.py:353
  21.2 1.8 %collective-permute-start.11 = (f32[1,8]{1,0:T(1,128)S(1)}, f32[1,8]{1,0:T(1,128)S(1)}, u32[]{:S(2)}, u32[]{:S(2)}) collective-permute-start(f32[1,8]{1,0:T(1,128)S(1)} %step_logits.1), channel_id=1, source_target_pairs={{0,1},{1,0},{2,3},{3,2},{4,5},{5,4},{6,7},{7,6},{8,9},{9,8},{10,11... | collective-permute-start | bytes 104 | tf_op jit(solution)/shard_map/ppermute | solution.py:35
  23.0 1.8 %attend_3_7.1 = (bf16[64,2048]{1,0:T(8,128)(2,1)}, bf16[64,2048]{1,0:T(8,128)(2,1)}) custom-call(bf16[64,2048]{1,0:T(8,128)(2,1)S(1)} %get-tuple-element.23.refs_0_, bf16[64,2048]{1,0:T(8,128)(2,1)S(1)} %get-tuple-element.24.refs_1_, bf16[2,2,64,256]{3,2,1,0:T(8,128)(2,1)S(1)} %collective-permute-done.6.refs_0_.refs_2_.refs_7_, ...), custom_call_target="tpu_custom_call" | custom-call | flops 402653184 | bytes 524288 | tf_op jit(solution)/shard_map/attend_3_7/pallas_call | solution.py:276
  24.8 0.0 collective-permute-done.11
  24.8 0.5 %add.3 = f32[1,8]{1,0:T(1,128)} add(f32[1,8]{1,0:T(1,128)S(1)} %step_logits.1, f32[1,8]{1,0:T(1,128)S(1)} %collective-permute-done.11) | non-fusion elementwise | flops 8 | bytes 96 | tf_op jit(solution)/shard_map/add | solution.py:404
  (3 shorter events, 0.0 us)
Async XLA Ops:
  0.6 8.0 %collective-permute-start = (bf16[1,2,64,256]{3,2,1,0:T(8,128)(2,1)}, bf16[1,2,64,256]{3,2,1,0:T(8,128)(2,1)S(1)}, u32[]{:S(2)}, u32[]{:S(2)}) collective-permute-start(bf16[1,2,64,256]{3,2,1,0:T(8,128)(2,1)} %bitcast.9), channel_id=1, source_target_pairs={{0,4},{2,6},{4,0},{6,2},{8,12},{10,14},{12,8},{14,10},{16,20},{18,... | collective-permute-start | bytes 196616 | tf_op jit(solution)/shard_map/ppermute | solution.py:35
  6.0 4.7 %collective-permute-start.4 = (bf16[3,64,256]{2,1,0:T(8,128)(2,1)S(1)}, bf16[3,64,256]{2,1,0:T(8,128)(2,1)S(1)}, u32[]{:S(2)}, u32[]{:S(2)}) collective-permute-start(bf16[3,64,256]{2,1,0:T(8,128)(2,1)S(1)} %get-tuple-element.27.refs_4_.refs_0_), channel_id=1, source_target_pairs={{0,16},{8,24},{16,0},{24,8},{1,17},{9,25},{17,1},{25,9},{2,18},{10... | collective-permute-start | bytes 294920 | tf_op jit(solution)/shard_map/ppermute | solution.py:35
  8.6 3.6 %collective-permute-start.2 = (bf16[2,2,64,256]{3,2,1,0:T(8,128)(2,1)S(1)}, bf16[2,2,64,256]{3,2,1,0:T(8,128)(2,1)S(1)}, u32[]{:S(2)}, u32[]{:S(2)}) collective-permute-start(bf16[2,2,64,256]{3,2,1,0:T(8,128)(2,1)S(1)} %pack_blocks.3.refs_2_.refs_4_), channel_id=1, source_target_pairs={{0,8},{2,10},{4,12},{6,14},{8,0},{10,2},{12,4},{14,6},{16,24},{18,... | collective-permute-start | bytes 393224 | tf_op jit(solution)/shard_map/ppermute | solution.py:35
  8.7 5.0 %collective-permute-start.1 = (bf16[2,2,64,256]{3,2,1,0:T(8,128)(2,1)S(1)}, bf16[2,2,64,256]{3,2,1,0:T(8,128)(2,1)S(1)}, u32[]{:S(2)}, u32[]{:S(2)}) collective-permute-start(bf16[2,2,64,256]{3,2,1,0:T(8,128)(2,1)S(1)} %pack_blocks.3.refs_2_.refs_4_), channel_id=1, source_target_pairs={{0,2},{2,0},{4,6},{6,4},{8,24},{10,26},{12,28},{14,30},{16,18},{18... | collective-permute-start | bytes 393224 | tf_op jit(solution)/shard_map/ppermute | solution.py:381
  9.4 3.7 %collective-permute-start.3 = (bf16[3,64,256]{2,1,0:T(8,128)(2,1)S(1)}, bf16[3,64,256]{2,1,0:T(8,128)(2,1)S(1)}, u32[]{:S(2)}, u32[]{:S(2)}) collective-permute-start(bf16[3,64,256]{2,1,0:T(8,128)(2,1)S(1)} %get-tuple-element.27.refs_4_.refs_0_), channel_id=1, source_target_pairs={{0,8},{8,0},{16,24},{24,16},{1,9},{9,1},{17,25},{25,17},{2,10},{10... | collective-permute-start | bytes 294920 | tf_op jit(solution)/shard_map/ppermute | solution.py:35
  10.7 3.1 %collective-permute-start.5 = (bf16[3,64,256]{2,1,0:T(8,128)(2,1)S(1)}, bf16[3,64,256]{2,1,0:T(8,128)(2,1)S(1)}, u32[]{:S(2)}, u32[]{:S(2)}) collective-permute-start(bf16[3,64,256]{2,1,0:T(8,128)(2,1)S(1)} %collective-permute-done.4.refs_3_.refs_6_.refs_2_), channel_id=1, source_target_pairs={{0,8},{8,0},{16,24},{24,16},{1,9},{9,1},{17,25},{25,17},{2,10},{10... | collective-permute-start | bytes 294920 | tf_op jit(solution)/shard_map/ppermute | solution.py:35
  10.7 5.0 %collective-permute-start.7 = (bf16[2,2,64,256]{3,2,1,0:T(8,128)(2,1)S(1)}, bf16[2,2,64,256]{3,2,1,0:T(8,128)(2,1)S(1)}, u32[]{:S(2)}, u32[]{:S(2)}) collective-permute-start(bf16[2,2,64,256]{3,2,1,0:T(8,128)(2,1)S(1)} %pack_blocks.3.refs_2_.refs_4_), channel_id=1, source_target_pairs={{0,16},{2,18},{4,20},{6,22},{8,10},{10,8},{12,14},{14,12},{16,0},{... | collective-permute-start | bytes 393224 | tf_op jit(solution)/shard_map/ppermute | solution.py:381
  13.7 5.0 %collective-permute-start.6 = (bf16[2,2,64,256]{3,2,1,0:T(8,128)(2,1)S(1)}, bf16[2,2,64,256]{3,2,1,0:T(8,128)(2,1)S(1)}, u32[]{:S(2)}, u32[]{:S(2)}) collective-permute-start(bf16[2,2,64,256]{3,2,1,0:T(8,128)(2,1)S(1)} %pack_blocks.4), channel_id=1, source_target_pairs={{0,16},{2,18},{4,20},{6,22},{8,10},{10,8},{12,14},{14,12},{16,0},{... | collective-permute-start | bytes 393224 | tf_op jit(solution)/shard_map/ppermute | solution.py:381
  15.7 3.2 %collective-permute-start.9 = (bf16[2,2,64,256]{3,2,1,0:T(8,128)(2,1)S(1)}, bf16[2,2,64,256]{3,2,1,0:T(8,128)(2,1)S(1)}, u32[]{:S(2)}, u32[]{:S(2)}) collective-permute-start(bf16[2,2,64,256]{3,2,1,0:T(8,128)(2,1)S(1)} %collective-permute-done.1.refs_0_.refs_2_.refs_5_), channel_id=1, source_target_pairs={{0,8},{2,10},{4,12},{6,14},{8,0},{10,2},{12,4},{14,6},{16,24},{18,... | collective-permute-start | bytes 393224 | tf_op jit(solution)/shard_map/ppermute | solution.py:35
  15.7 3.2 %collective-permute-start.10 = (bf16[2,2,64,256]{3,2,1,0:T(8,128)(2,1)S(1)}, bf16[2,2,64,256]{3,2,1,0:T(8,128)(2,1)S(1)}, u32[]{:S(2)}, u32[]{:S(2)}) collective-permute-start(bf16[2,2,64,256]{3,2,1,0:T(8,128)(2,1)S(1)} %collective-permute-done.7.refs_3_.refs_6_), channel_id=1, source_target_pairs={{0,8},{2,10},{4,12},{6,14},{8,0},{10,2},{12,4},{14,6},{16,24},{18,... | collective-permute-start | bytes 393224 | tf_op jit(solution)/shard_map/ppermute | solution.py:35
  18.8 1.4 %collective-permute-start.8 = (bf16[2,2,64,256]{3,2,1,0:T(8,128)(2,1)S(1)}, bf16[2,2,64,256]{3,2,1,0:T(8,128)(2,1)S(1)}, u32[]{:S(2)}, u32[]{:S(2)}) collective-permute-start(bf16[2,2,64,256]{3,2,1,0:T(8,128)(2,1)S(1)} %pack_blocks.5), channel_id=1, source_target_pairs={{0,8},{2,10},{4,12},{6,14},{8,0},{10,2},{12,4},{14,6},{16,24},{18,... | collective-permute-start | bytes 393224 | tf_op jit(solution)/shard_map/ppermute | solution.py:35
  21.2 3.6 %collective-permute-start.11 = (f32[1,8]{1,0:T(1,128)S(1)}, f32[1,8]{1,0:T(1,128)S(1)}, u32[]{:S(2)}, u32[]{:S(2)}) collective-permute-start(f32[1,8]{1,0:T(1,128)S(1)} %step_logits.1), channel_id=1, source_target_pairs={{0,1},{1,0},{2,3},{3,2},{4,5},{5,4},{6,7},{7,6},{8,9},{9,8},{10,11... | collective-permute-start | bytes 104 | tf_op jit(solution)/shard_map/ppermute | solution.py:35

commit v15 on v14

--- a/solution.py
+++ b/solution.py
@@ -207,7 +207,9 @@
     pays = [next(take) for _ in masks]
     ends = next(take) if last else None
     old = None if first else [(next(take), next(take)) for _ in range(2)]
-    outs = refs[-2:] if last else refs[-4:]
+    outs = refs[-6:-4] if last else refs[-4:]
+    halls, sems = refs[-4:-2], refs[-2:]
+    leaving = []
     rows = prompt_q.shape[0]
     cand_rows = cand_q.shape[0]
     owners = prompt_owners(ctx_size, cand_size)
@@ -243,13 +245,26 @@
                     outs[2 * kind][at] = state[0]
                     outs[2 * kind + 1][at] = state[1]
                     continue
-                result = state[1][:, :HEADDIM] / state[1][:, HEADDIM:]
+                sums = state[1][:, HEADDIM:]
+                inverse = pl.reciprocal(sums, approx=True)
+                result = state[1][:, :HEADDIM] * (inverse * (2.0 - sums * inverse))
                 each = q_ref.shape[0]
                 for index, h in enumerate(heads):
                     kept = result[index * each : (index + 1) * each]
                     if kind == 0:
                         kept = jnp.where(alive, kept, 0.0)
-                    outs[kind][:, h * HEADDIM : (h + 1) * HEADDIM] = kept.astype(jnp.bfloat16)
+                    halls[kind][:, h * HEADDIM : (h + 1) * HEADDIM] = kept.astype(jnp.bfloat16)
+                part = slice(heads[0] * HEADDIM, (heads[-1] + 1) * HEADDIM)
+                leaving.append(
+                    pltpu.make_async_copy(
+                        halls[kind].at[:, part],
+                        outs[kind].at[:, part],
+                        sems[kind].at[heads[0] // len(heads)],
+                    )
+                )
+                leaving[-1].start()
+    for copy in leaving:
+        copy.wait()
 
 
 def phase(sizes, arrays, q_rows, blocks, pays=(), state=None, ends=None, after=()):
@@ -262,8 +277,11 @@
     if not first:
         operands += state
     heads = prompt_q.shape[1] // HEADDIM
+    scratch = []
     if last:
         shapes = [like(cand_q), like(prompt_q)]
+        scratch = [pltpu.VMEM(q.shape, q.dtype) for q in (cand_q, prompt_q)]
+        scratch += [pltpu.SemaphoreType.DMA((heads,))] * 2
     else:
         shapes = []
         for q in (cand_q, prompt_q):
@@ -277,7 +295,8 @@
         functools.partial(phase_kernel, sizes, arrays, masks, first, last),
         out_shape=tuple(shapes),
         in_specs=vmem(len(operands)) + [pl.BlockSpec(memory_space=pl.ANY)] * len(after),
-        out_specs=tuple(vmem(len(shapes))),
+        out_specs=(pl.BlockSpec(memory_space=pl.ANY),) * 2 if last else tuple(vmem(len(shapes))),
+        scratch_shapes=scratch,
         compiler_params=PARAMS,
         cost_estimate=pl.CostEstimate(
             flops=6 * scores * HEADDIM, bytes_accessed=scores, transcendentals=scores

time: 25.5 us -> 25.8 us (1.012)
  Pallas kernels: 7.66 us -> 7.95 us
    pallas_call x4, Pallas kernels: 5.4 us -> 5.69 us  [phase(): pl.pallas_call(functools.partial(phase_kernel, sizes, arrays, masks, firs...]
  transfers between devices with their start and end apart: 12 -> 12, of which waited for: 4 -> 4; matrix products, arithmetic and copies ran while one was open for 0% -> 0% of each run, Pallas kernels for 26% -> 27%
where the time goes in v15:
time: 25.8 us; the launch traced here: 25.6 us
  starting transfers between devices  13.5 us (52%)
  Pallas kernels  7.95 us (31%)
  waiting for transfers between devices  2.87 us (11%)
  between operations  0.73 us (3%)
  other arithmetic  0.51 us (2%)
    ppermute x9, starting transfers between devices, flipped(): return lax.ppermute(block, axes, [(i, i ^ bit) for i in range(size)])  9.37 us
    pallas_call x4, Pallas kernels, phase(): pl.pallas_call(functools.partial(phase_kernel, sizes, arrays, masks, firs...  5.69 us
    ppermute x3, starting transfers between devices, shared_out(): lax.ppermute(block, PROMPT_AXES, [(i, i ^ (odd if i & core else even)) fo...  4.17 us
    ppermute x3, waiting for transfers between devices, shared_out(): lax.ppermute(block, PROMPT_AXES, [(i, i ^ (odd if i & core else even)) fo...  1.48 us
    ppermute x9, waiting for transfers between devices, flipped(): return lax.ppermute(block, axes, [(i, i ^ bit) for i in range(size)])  1.39 us
    pallas_call x1, Pallas kernels, staged(): pl.pallas_call(stage_kernel, out_shape=(like(prompt_q), like(cand_q), lik...  1.24 us
    pallas_call x1, Pallas kernels, step_shares(): pl.pallas_call(functools.partial(step_kernel, sizes, [mask for _, mask in...  0.99 us
  transfers between devices with their start and end apart: 12, of which 4 were waited for; matrix products, arithmetic and copies ran while one was open for 0% of the time, Pallas kernels for 27%

profile of v15, /device:TPU:0, one launch (start us, length us, event | category | flops | bytes accessed | tf_op | source)
XLA Modules:
  0.0 25.6 jit_solution(8779579264925954926)
XLA Ops:
  0.6 4.1 %collective-permute-start = (bf16[1,2,64,256]{3,2,1,0:T(8,128)(2,1)}, bf16[1,2,64,256]{3,2,1,0:T(8,128)(2,1)S(1)}, u32[]{:S(2)}, u32[]{:S(2)}) collective-permute-start(bf16[1,2,64,256]{3,2,1,0:T(8,128)(2,1)} %bitcast.9), channel_id=1, source_target_pairs={{0,4},{2,6},{4,0},{6,2},{8,12},{10,14},{12,8},{14,10},{16,20},{18,... | collective-permute-start | bytes 196616 | tf_op jit(solution)/shard_map/ppermute | solution.py:35
  4.7 1.2 %stage_operands.1 = (bf16[64,2048]{1,0:T(8,128)(2,1)S(1)}, bf16[64,2048]{1,0:T(8,128)(2,1)S(1)}, bf16[2,64,256]{2,1,0:T(8,128)(2,1)S(1)}, bf16[3,64,256]{2,1,0:T...) custom-call(bf16[64,2048]{1,0:T(8,128)(2,1)} %prompt_q.1, bf16[64,2048]{1,0:T(8,128)(2,1)} %bitcast.7, ...), custom_call_target="tpu_custom_call" | custom-call | tf_op jit(solution)/shard_map/stage_operands/pallas_call | solution.py:127
  6.0 1.6 %collective-permute-start.4 = (bf16[3,64,256]{2,1,0:T(8,128)(2,1)S(1)}, bf16[3,64,256]{2,1,0:T(8,128)(2,1)S(1)}, u32[]{:S(2)}, u32[]{:S(2)}) collective-permute-start(bf16[3,64,256]{2,1,0:T(8,128)(2,1)S(1)} %get-tuple-element.27.refs_4_.refs_0_), channel_id=1, source_target_pairs={{0,16},{8,24},{16,0},{24,8},{1,17},{9,25},{17,1},{25,9},{2,18},{10... | collective-permute-start | bytes 294920 | tf_op jit(solution)/shard_map/ppermute | solution.py:35
  7.6 1.0 %collective-permute-done.refs_1_ = bf16[1,2,64,256]{3,2,1,0:T(8,128)(2,1)S(1)} collective-permute-done((bf16[1,2,64,256]{3,2,1,0:T(8,128)(2,1)}, bf16[1,2,64,256]{3,2,1,0:T(8,128)(2,1)S(1)}, u32[]{:S(2)}, u32[]{:S(2)}) %collective-permute-start) | collective-permute-done | bytes 65568 | tf_op jit(solution)/shard_map/ppermute | solution.py:35
  8.6 0.1 collective-permute-start.2
  8.7 0.7 %collective-permute-start.1 = (bf16[2,2,64,256]{3,2,1,0:T(8,128)(2,1)S(1)}, bf16[2,2,64,256]{3,2,1,0:T(8,128)(2,1)S(1)}, u32[]{:S(2)}, u32[]{:S(2)}) collective-permute-start(bf16[2,2,64,256]{3,2,1,0:T(8,128)(2,1)S(1)} %pack_blocks.3.refs_2_.refs_4_), channel_id=1, source_target_pairs={{0,2},{2,0},{4,6},{6,4},{8,24},{10,26},{12,28},{14,30},{16,18},{18... | collective-permute-start | bytes 393224 | tf_op jit(solution)/shard_map/ppermute | solution.py:400
  9.4 1.2 %collective-permute-start.3 = (bf16[3,64,256]{2,1,0:T(8,128)(2,1)S(1)}, bf16[3,64,256]{2,1,0:T(8,128)(2,1)S(1)}, u32[]{:S(2)}, u32[]{:S(2)}) collective-permute-start(bf16[3,64,256]{2,1,0:T(8,128)(2,1)S(1)} %get-tuple-element.27.refs_4_.refs_0_), channel_id=1, source_target_pairs={{0,8},{8,0},{16,24},{24,16},{1,9},{9,1},{17,25},{25,17},{2,10},{10... | collective-permute-start | bytes 294920 | tf_op jit(solution)/shard_map/ppermute | solution.py:35
  10.6 0.0 collective-permute-done.4.refs_3_.refs_6_.refs_2_
  10.7 0.0 collective-permute-start.5
  10.7 1.5 %collective-permute-start.7 = (bf16[2,2,64,256]{3,2,1,0:T(8,128)(2,1)S(1)}, bf16[2,2,64,256]{3,2,1,0:T(8,128)(2,1)S(1)}, u32[]{:S(2)}, u32[]{:S(2)}) collective-permute-start(bf16[2,2,64,256]{3,2,1,0:T(8,128)(2,1)S(1)} %pack_blocks.3.refs_2_.refs_4_), channel_id=1, source_target_pairs={{0,16},{2,18},{4,20},{6,22},{8,10},{10,8},{12,14},{14,12},{16,0},{... | collective-permute-start | bytes 393224 | tf_op jit(solution)/shard_map/ppermute | solution.py:400
  12.2 0.0 collective-permute-done.2.refs_3_.refs_8_
  12.2 0.9 %attend_0_4.1 = (f32[1024,128]{1,0:T(8,128)S(1)}, f32[1024,256]{1,0:T(8,128)S(1)}, f32[1024,128]{1,0:T(8,128)S(1)}, f32[1024,256]{1,0:T(8,128)S(1)}) custom-call(bf16[64,2048]{1,0:T(8,128)(2,1)S(1)} %get-tuple-element.23.refs_0_, bf16[64,2048]{1,0:T(8,128)(2,1)S(1)} %get-tuple-element.24.refs_1_, bf16[2,2,64,256]{3,2,1,0:T(8,128)(2,1)S(1)} %pack_blocks.3.refs_2_.refs_4_, ...), custom_call_target="tpu_custom_call" | custom-call | flops 402653184 | bytes 524288 | tf_op jit(solution)/shard_map/attend_0_4/pallas_call | solution.py:294
  13.1 0.0 collective-permute-done.3.refs_2_.refs_5_.refs_1_
  13.1 0.6 %collective-permute-done.1.refs_0_.refs_2_.refs_5_ = bf16[2,2,64,256]{3,2,1,0:T(8,128)(2,1)S(1)} collective-permute-done((bf16[2,2,64,256]{3,2,1,0:T(8,128)(2,1)S(1)}, bf16[2,2,64,256]{3,2,1,0:T(8,128)(2,1)S(1)}, u32[]{:S(2)}, u32[]{:S(2)}) %collective-permute-start.1) | collective-permute-done | bytes 131104 | tf_op jit(solution)/shard_map/ppermute | solution.py:400
  13.7 0.0 collective-permute-done.5.refs_4_.refs_7_.refs_3_
  13.7 1.9 %collective-permute-start.6 = (bf16[2,2,64,256]{3,2,1,0:T(8,128)(2,1)S(1)}, bf16[2,2,64,256]{3,2,1,0:T(8,128)(2,1)S(1)}, u32[]{:S(2)}, u32[]{:S(2)}) collective-permute-start(bf16[2,2,64,256]{3,2,1,0:T(8,128)(2,1)S(1)} %pack_blocks.4), channel_id=1, source_target_pairs={{0,16},{2,18},{4,20},{6,22},{8,10},{10,8},{12,14},{14,12},{16,0},{... | collective-permute-start | bytes 393224 | tf_op jit(solution)/shard_map/ppermute | solution.py:400
  15.7 0.0 collective-permute-start.9
  15.7 0.0 collective-permute-done.7.refs_3_.refs_6_
  15.7 0.5 %collective-permute-start.10 = (bf16[2,2,64,256]{3,2,1,0:T(8,128)(2,1)S(1)}, bf16[2,2,64,256]{3,2,1,0:T(8,128)(2,1)S(1)}, u32[]{:S(2)}, u32[]{:S(2)}) collective-permute-start(bf16[2,2,64,256]{3,2,1,0:T(8,128)(2,1)S(1)} %collective-permute-done.7.refs_3_.refs_6_), channel_id=1, source_target_pairs={{0,8},{2,10},{4,12},{6,14},{8,0},{10,2},{12,4},{14,6},{16,24},{18,... | collective-permute-start | bytes 393224 | tf_op jit(solution)/shard_map/ppermute | solution.py:35
  16.2 1.7 %attend_1_2.1 = (f32[1024,128]{1,0:T(8,128)S(1)}, f32[1024,256]{1,0:T(8,128)S(1)}, f32[1024,128]{1,0:T(8,128)S(1)}, f32[1024,256]{1,0:T(8,128)S(1)}) custom-call(bf16[64,2048]{1,0:T(8,128)(2,1)S(1)} %get-tuple-element.23.refs_0_, bf16[64,2048]{1,0:T(8,128)(2,1)S(1)} %get-tuple-element.24.refs_1_, ...), custom_call_target="tpu_custom_call" | custom-call | flops 402653184 | bytes 524288 | tf_op jit(solution)/shard_map/attend_1_2/pallas_call | solution.py:294
  17.9 0.9 %collective-permute-done.6.refs_0_.refs_2_.refs_7_ = bf16[2,2,64,256]{3,2,1,0:T(8,128)(2,1)S(1)} collective-permute-done((bf16[2,2,64,256]{3,2,1,0:T(8,128)(2,1)S(1)}, bf16[2,2,64,256]{3,2,1,0:T(8,128)(2,1)S(1)}, u32[]{:S(2)}, u32[]{:S(2)}) %collective-permute-start.6) | collective-permute-done | bytes 131104 | tf_op jit(solution)/shard_map/ppermute | solution.py:400
  18.8 0.1 collective-permute-start.8
  18.9 0.0 collective-permute-done.9.refs_2_.refs_9_
  18.9 0.0 collective-permute-done.10.refs_3_.refs_10_
  18.9 1.0 %attend_5_6.1 = (f32[1024,128]{1,0:T(8,128)S(1)}, f32[1024,256]{1,0:T(8,128)S(1)}, f32[1024,128]{1,0:T(8,128)S(1)}, f32[1024,256]{1,0:T(8,128)S(1)}) custom-call(bf16[64,2048]{1,0:T(8,128)(2,1)S(1)} %get-tuple-element.23.refs_0_, bf16[64,2048]{1,0:T(8,128)(2,1)S(1)} %get-tuple-element.24.refs_1_, ...), custom_call_target="tpu_custom_call" | custom-call | flops 402653184 | bytes 524288 | tf_op jit(solution)/shard_map/attend_5_6/pallas_call | solution.py:294
  19.9 0.3 %collective-permute-done.8.refs_3_.refs_11_ = bf16[2,2,64,256]{3,2,1,0:T(8,128)(2,1)S(1)} collective-permute-done((bf16[2,2,64,256]{3,2,1,0:T(8,128)(2,1)S(1)}, bf16[2,2,64,256]{3,2,1,0:T(8,128)(2,1)S(1)}, u32[]{:S(2)}, u32[]{:S(2)}) %collective-permute-start.8) | collective-permute-done | bytes 131104 | tf_op jit(solution)/shard_map/ppermute | solution.py:35
  20.2 1.0 %step_logits.1 = f32[1,8]{1,0:T(1,128)S(1)} custom-call(s32[1,8]{1,0:T(1,128)S(1)} %get-tuple-element.32.refs_4_.ends_ref, f32[1,2048]{1,0:T(1,128)S(1)} %get-tuple-element.42.head_ref, bf16[3,64,256]{2,1,0:T(8,128)(2,1)S(1)} %get-tuple-element.27.refs_4_.refs_0_, bf16[3,64,256]{2,1,0:T(8,128)(2,1)S(1)} %collective-permute-done.3.refs_2_.refs_5_.refs_1_, ...), custom_call_target="tpu_custom_call" | custom-call | flops 125829120 | bytes 163840 | tf_op jit(solution)/shard_map/step_logits/pallas_call | solution.py:372
  21.2 1.8 %collective-permute-start.11 = (f32[1,8]{1,0:T(1,128)S(1)}, f32[1,8]{1,0:T(1,128)S(1)}, u32[]{:S(2)}, u32[]{:S(2)}) collective-permute-start(f32[1,8]{1,0:T(1,128)S(1)} %step_logits.1), channel_id=1, source_target_pairs={{0,1},{1,0},{2,3},{3,2},{4,5},{5,4},{6,7},{7,6},{8,9},{9,8},{10,11... | collective-permute-start | bytes 104 | tf_op jit(solution)/shard_map/ppermute | solution.py:35
  23.0 2.1 %attend_3_7.1 = (bf16[64,2048]{1,0:T(8,128)(2,1)}, bf16[64,2048]{1,0:T(8,128)(2,1)}) custom-call(bf16[64,2048]{1,0:T(8,128)(2,1)S(1)} %get-tuple-element.23.refs_0_, bf16[64,2048]{1,0:T(8,128)(2,1)S(1)} %get-tuple-element.24.refs_1_, bf16[2,2,64,256]{3,2,1,0:T(8,128)(2,1)S(1)} %collective-permute-done.6.refs_0_.refs_2_.refs_7_, ...), custom_call_target="tpu_custom_call" | custom-call | flops 402653184 | bytes 524288 | tf_op jit(solution)/shard_map/attend_3_7/pallas_call | solution.py:294
  25.1 0.0 collective-permute-done.11
  25.1 0.5 %add.3 = f32[1,8]{1,0:T(1,128)} add(f32[1,8]{1,0:T(1,128)S(1)} %step_logits.1, f32[1,8]{1,0:T(1,128)S(1)} %collective-permute-done.11) | non-fusion elementwise | flops 8 | bytes 96 | tf_op jit(solution)/shard_map/add | solution.py:423
  (3 shorter events, 0.0 us)
Async XLA Ops:
  0.6 8.0 %collective-permute-start = (bf16[1,2,64,256]{3,2,1,0:T(8,128)(2,1)}, bf16[1,2,64,256]{3,2,1,0:T(8,128)(2,1)S(1)}, u32[]{:S(2)}, u32[]{:S(2)}) collective-permute-start(bf16[1,2,64,256]{3,2,1,0:T(8,128)(2,1)} %bitcast.9), channel_id=1, source_target_pairs={{0,4},{2,6},{4,0},{6,2},{8,12},{10,14},{12,8},{14,10},{16,20},{18,... | collective-permute-start | bytes 196616 | tf_op jit(solution)/shard_map/ppermute | solution.py:35
  6.0 4.7 %collective-permute-start.4 = (bf16[3,64,256]{2,1,0:T(8,128)(2,1)S(1)}, bf16[3,64,256]{2,1,0:T(8,128)(2,1)S(1)}, u32[]{:S(2)}, u32[]{:S(2)}) collective-permute-start(bf16[3,64,256]{2,1,0:T(8,128)(2,1)S(1)} %get-tuple-element.27.refs_4_.refs_0_), channel_id=1, source_target_pairs={{0,16},{8,24},{16,0},{24,8},{1,17},{9,25},{17,1},{25,9},{2,18},{10... | collective-permute-start | bytes 294920 | tf_op jit(solution)/shard_map/ppermute | solution.py:35
  8.6 3.6 %collective-permute-start.2 = (bf16[2,2,64,256]{3,2,1,0:T(8,128)(2,1)S(1)}, bf16[2,2,64,256]{3,2,1,0:T(8,128)(2,1)S(1)}, u32[]{:S(2)}, u32[]{:S(2)}) collective-permute-start(bf16[2,2,64,256]{3,2,1,0:T(8,128)(2,1)S(1)} %pack_blocks.3.refs_2_.refs_4_), channel_id=1, source_target_pairs={{0,8},{2,10},{4,12},{6,14},{8,0},{10,2},{12,4},{14,6},{16,24},{18,... | collective-permute-start | bytes 393224 | tf_op jit(solution)/shard_map/ppermute | solution.py:35
  8.7 5.0 %collective-permute-start.1 = (bf16[2,2,64,256]{3,2,1,0:T(8,128)(2,1)S(1)}, bf16[2,2,64,256]{3,2,1,0:T(8,128)(2,1)S(1)}, u32[]{:S(2)}, u32[]{:S(2)}) collective-permute-start(bf16[2,2,64,256]{3,2,1,0:T(8,128)(2,1)S(1)} %pack_blocks.3.refs_2_.refs_4_), channel_id=1, source_target_pairs={{0,2},{2,0},{4,6},{6,4},{8,24},{10,26},{12,28},{14,30},{16,18},{18... | collective-permute-start | bytes 393224 | tf_op jit(solution)/shard_map/ppermute | solution.py:400
  9.4 3.7 %collective-permute-start.3 = (bf16[3,64,256]{2,1,0:T(8,128)(2,1)S(1)}, bf16[3,64,256]{2,1,0:T(8,128)(2,1)S(1)}, u32[]{:S(2)}, u32[]{:S(2)}) collective-permute-start(bf16[3,64,256]{2,1,0:T(8,128)(2,1)S(1)} %get-tuple-element.27.refs_4_.refs_0_), channel_id=1, source_target_pairs={{0,8},{8,0},{16,24},{24,16},{1,9},{9,1},{17,25},{25,17},{2,10},{10... | collective-permute-start | bytes 294920 | tf_op jit(solution)/shard_map/ppermute | solution.py:35
  10.7 3.1 %collective-permute-start.5 = (bf16[3,64,256]{2,1,0:T(8,128)(2,1)S(1)}, bf16[3,64,256]{2,1,0:T(8,128)(2,1)S(1)}, u32[]{:S(2)}, u32[]{:S(2)}) collective-permute-start(bf16[3,64,256]{2,1,0:T(8,128)(2,1)S(1)} %collective-permute-done.4.refs_3_.refs_6_.refs_2_), channel_id=1, source_target_pairs={{0,8},{8,0},{16,24},{24,16},{1,9},{9,1},{17,25},{25,17},{2,10},{10... | collective-permute-start | bytes 294920 | tf_op jit(solution)/shard_map/ppermute | solution.py:35
  10.7 5.0 %collective-permute-start.7 = (bf16[2,2,64,256]{3,2,1,0:T(8,128)(2,1)S(1)}, bf16[2,2,64,256]{3,2,1,0:T(8,128)(2,1)S(1)}, u32[]{:S(2)}, u32[]{:S(2)}) collective-permute-start(bf16[2,2,64,256]{3,2,1,0:T(8,128)(2,1)S(1)} %pack_blocks.3.refs_2_.refs_4_), channel_id=1, source_target_pairs={{0,16},{2,18},{4,20},{6,22},{8,10},{10,8},{12,14},{14,12},{16,0},{... | collective-permute-start | bytes 393224 | tf_op jit(solution)/shard_map/ppermute | solution.py:400
  13.7 5.0 %collective-permute-start.6 = (bf16[2,2,64,256]{3,2,1,0:T(8,128)(2,1)S(1)}, bf16[2,2,64,256]{3,2,1,0:T(8,128)(2,1)S(1)}, u32[]{:S(2)}, u32[]{:S(2)}) collective-permute-start(bf16[2,2,64,256]{3,2,1,0:T(8,128)(2,1)S(1)} %pack_blocks.4), channel_id=1, source_target_pairs={{0,16},{2,18},{4,20},{6,22},{8,10},{10,8},{12,14},{14,12},{16,0},{... | collective-permute-start | bytes 393224 | tf_op jit(solution)/shard_map/ppermute | solution.py:400
  15.7 3.2 %collective-permute-start.9 = (bf16[2,2,64,256]{3,2,1,0:T(8,128)(2,1)S(1)}, bf16[2,2,64,256]{3,2,1,0:T(8,128)(2,1)S(1)}, u32[]{:S(2)}, u32[]{:S(2)}) collective-permute-start(bf16[2,2,64,256]{3,2,1,0:T(8,128)(2,1)S(1)} %collective-permute-done.1.refs_0_.refs_2_.refs_5_), channel_id=1, source_target_pairs={{0,8},{2,10},{4,12},{6,14},{8,0},{10,2},{12,4},{14,6},{16,24},{18,... | collective-permute-start | bytes 393224 | tf_op jit(solution)/shard_map/ppermute | solution.py:35
  15.7 3.2 %collective-permute-start.10 = (bf16[2,2,64,256]{3,2,1,0:T(8,128)(2,1)S(1)}, bf16[2,2,64,256]{3,2,1,0:T(8,128)(2,1)S(1)}, u32[]{:S(2)}, u32[]{:S(2)}) collective-permute-start(bf16[2,2,64,256]{3,2,1,0:T(8,128)(2,1)S(1)} %collective-permute-done.7.refs_3_.refs_6_), channel_id=1, source_target_pairs={{0,8},{2,10},{4,12},{6,14},{8,0},{10,2},{12,4},{14,6},{16,24},{18,... | collective-permute-start | bytes 393224 | tf_op jit(solution)/shard_map/ppermute | solution.py:35
  18.8 1.4 %collective-permute-start.8 = (bf16[2,2,64,256]{3,2,1,0:T(8,128)(2,1)S(1)}, bf16[2,2,64,256]{3,2,1,0:T(8,128)(2,1)S(1)}, u32[]{:S(2)}, u32[]{:S(2)}) collective-permute-start(bf16[2,2,64,256]{3,2,1,0:T(8,128)(2,1)S(1)} %pack_blocks.5), channel_id=1, source_target_pairs={{0,8},{2,10},{4,12},{6,14},{8,0},{10,2},{12,4},{14,6},{16,24},{18,... | collective-permute-start | bytes 393224 | tf_op jit(solution)/shard_map/ppermute | solution.py:35
  21.2 3.9 %collective-permute-start.11 = (f32[1,8]{1,0:T(1,128)S(1)}, f32[1,8]{1,0:T(1,128)S(1)}, u32[]{:S(2)}, u32[]{:S(2)}) collective-permute-start(f32[1,8]{1,0:T(1,128)S(1)} %step_logits.1), channel_id=1, source_target_pairs={{0,1},{1,0},{2,3},{3,2},{4,5},{5,4},{6,7},{7,6},{8,9},{9,8},{10,11... | collective-permute-start | bytes 104 | tf_op jit(solution)/shard_map/ppermute | solution.py:35

commit v16 on v14

--- a/solution.py
+++ b/solution.py
@@ -243,7 +243,9 @@
                     outs[2 * kind][at] = state[0]
                     outs[2 * kind + 1][at] = state[1]
                     continue
-                result = state[1][:, :HEADDIM] / state[1][:, HEADDIM:]
+                sums = state[1][:, HEADDIM:]
+                inverse = pl.reciprocal(sums, approx=True)
+                result = state[1][:, :HEADDIM] * (inverse * (2.0 - sums * inverse))
                 each = q_ref.shape[0]
                 for index, h in enumerate(heads):
                     kept = result[index * each : (index + 1) * each]

time: 25.5 us -> 25.5 us (level)
  transfers between devices with their start and end apart: 12 -> 12, of which waited for: 4 -> 4; matrix products, arithmetic and copies ran while one was open for 0% -> 0% of each run, Pallas kernels for 26% -> 27%
where the time goes in v16:
time: 25.5 us; the launch traced here: 25.4 us
  starting transfers between devices  13.5 us (53%)
  Pallas kernels  7.74 us (30%)
  waiting for transfers between devices  2.87 us (11%)
  between operations  0.72 us (3%)
  other arithmetic  0.51 us (2%)
    ppermute x9, starting transfers between devices, flipped(): return lax.ppermute(block, axes, [(i, i ^ bit) for i in range(size)])  9.37 us
    pallas_call x4, Pallas kernels, phase(): pl.pallas_call(functools.partial(phase_kernel, sizes, arrays, masks, firs...  5.48 us
    ppermute x3, starting transfers between devices, shared_out(): lax.ppermute(block, PROMPT_AXES, [(i, i ^ (odd if i & core else even)) fo...  4.17 us
    ppermute x3, waiting for transfers between devices, shared_out(): lax.ppermute(block, PROMPT_AXES, [(i, i ^ (odd if i & core else even)) fo...  1.48 us
    ppermute x9, waiting for transfers between devices, flipped(): return lax.ppermute(block, axes, [(i, i ^ bit) for i in range(size)])  1.39 us
    pallas_call x1, Pallas kernels, staged(): pl.pallas_call(stage_kernel, out_shape=(like(prompt_q), like(cand_q), lik...  1.24 us
    pallas_call x1, Pallas kernels, step_shares(): pl.pallas_call(functools.partial(step_kernel, sizes, [mask for _, mask in...  0.99 us
    add x1, other arithmetic, per_device(): step_logits = step_logits + flipped(step_logits, 'tp', tp_size, bit)  0.51 us
  transfers between devices with their start and end apart: 12, of which 4 were waited for; matrix products, arithmetic and copies ran while one was open for 0% of the time, Pallas kernels for 27%

profile of v16, /device:TPU:0, one launch (start us, length us, event | category | flops | bytes accessed | tf_op | source)
XLA Modules:
  0.0 25.4 jit_solution(1390215583034311680)
XLA Ops:
  0.6 4.1 %collective-permute-start = (bf16[1,2,64,256]{3,2,1,0:T(8,128)(2,1)}, bf16[1,2,64,256]{3,2,1,0:T(8,128)(2,1)S(1)}, u32[]{:S(2)}, u32[]{:S(2)}) collective-permute-start(bf16[1,2,64,256]{3,2,1,0:T(8,128)(2,1)} %bitcast.9), channel_id=1, source_target_pairs={{0,4},{2,6},{4,0},{6,2},{8,12},{10,14},{12,8},{14,10},{16,20},{18,... | collective-permute-start | bytes 196616 | tf_op jit(solution)/shard_map/ppermute | solution.py:35
  4.7 1.2 %stage_operands.1 = (bf16[64,2048]{1,0:T(8,128)(2,1)S(1)}, bf16[64,2048]{1,0:T(8,128)(2,1)S(1)}, bf16[2,64,256]{2,1,0:T(8,128)(2,1)S(1)}, bf16[3,64,256]{2,1,0:T...) custom-call(bf16[64,2048]{1,0:T(8,128)(2,1)} %prompt_q.1, bf16[64,2048]{1,0:T(8,128)(2,1)} %bitcast.7, ...), custom_call_target="tpu_custom_call" | custom-call | tf_op jit(solution)/shard_map/stage_operands/pallas_call | solution.py:127
  6.0 1.6 %collective-permute-start.4 = (bf16[3,64,256]{2,1,0:T(8,128)(2,1)S(1)}, bf16[3,64,256]{2,1,0:T(8,128)(2,1)S(1)}, u32[]{:S(2)}, u32[]{:S(2)}) collective-permute-start(bf16[3,64,256]{2,1,0:T(8,128)(2,1)S(1)} %get-tuple-element.27.refs_4_.refs_0_), channel_id=1, source_target_pairs={{0,16},{8,24},{16,0},{24,8},{1,17},{9,25},{17,1},{25,9},{2,18},{10... | collective-permute-start | bytes 294920 | tf_op jit(solution)/shard_map/ppermute | solution.py:35
  7.6 1.0 %collective-permute-done.refs_1_ = bf16[1,2,64,256]{3,2,1,0:T(8,128)(2,1)S(1)} collective-permute-done((bf16[1,2,64,256]{3,2,1,0:T(8,128)(2,1)}, bf16[1,2,64,256]{3,2,1,0:T(8,128)(2,1)S(1)}, u32[]{:S(2)}, u32[]{:S(2)}) %collective-permute-start) | collective-permute-done | bytes 65568 | tf_op jit(solution)/shard_map/ppermute | solution.py:35
  8.6 0.1 collective-permute-start.2
  8.7 0.7 %collective-permute-start.1 = (bf16[2,2,64,256]{3,2,1,0:T(8,128)(2,1)S(1)}, bf16[2,2,64,256]{3,2,1,0:T(8,128)(2,1)S(1)}, u32[]{:S(2)}, u32[]{:S(2)}) collective-permute-start(bf16[2,2,64,256]{3,2,1,0:T(8,128)(2,1)S(1)} %pack_blocks.3.refs_2_.refs_4_), channel_id=1, source_target_pairs={{0,2},{2,0},{4,6},{6,4},{8,24},{10,26},{12,28},{14,30},{16,18},{18... | collective-permute-start | bytes 393224 | tf_op jit(solution)/shard_map/ppermute | solution.py:383
  9.4 1.2 %collective-permute-start.3 = (bf16[3,64,256]{2,1,0:T(8,128)(2,1)S(1)}, bf16[3,64,256]{2,1,0:T(8,128)(2,1)S(1)}, u32[]{:S(2)}, u32[]{:S(2)}) collective-permute-start(bf16[3,64,256]{2,1,0:T(8,128)(2,1)S(1)} %get-tuple-element.27.refs_4_.refs_0_), channel_id=1, source_target_pairs={{0,8},{8,0},{16,24},{24,16},{1,9},{9,1},{17,25},{25,17},{2,10},{10... | collective-permute-start | bytes 294920 | tf_op jit(solution)/shard_map/ppermute | solution.py:35
  10.6 0.0 collective-permute-done.4.refs_3_.refs_6_.refs_2_
  10.7 0.0 collective-permute-start.5
  10.7 1.5 %collective-permute-start.7 = (bf16[2,2,64,256]{3,2,1,0:T(8,128)(2,1)S(1)}, bf16[2,2,64,256]{3,2,1,0:T(8,128)(2,1)S(1)}, u32[]{:S(2)}, u32[]{:S(2)}) collective-permute-start(bf16[2,2,64,256]{3,2,1,0:T(8,128)(2,1)S(1)} %pack_blocks.3.refs_2_.refs_4_), channel_id=1, source_target_pairs={{0,16},{2,18},{4,20},{6,22},{8,10},{10,8},{12,14},{14,12},{16,0},{... | collective-permute-start | bytes 393224 | tf_op jit(solution)/shard_map/ppermute | solution.py:383
  12.2 0.0 collective-permute-done.2.refs_3_.refs_8_
  12.2 0.9 %attend_0_4.1 = (f32[1024,128]{1,0:T(8,128)S(1)}, f32[1024,256]{1,0:T(8,128)S(1)}, f32[1024,128]{1,0:T(8,128)S(1)}, f32[1024,256]{1,0:T(8,128)S(1)}) custom-call(bf16[64,2048]{1,0:T(8,128)(2,1)S(1)} %get-tuple-element.23.refs_0_, bf16[64,2048]{1,0:T(8,128)(2,1)S(1)} %get-tuple-element.24.refs_1_, bf16[2,2,64,256]{3,2,1,0:T(8,128)(2,1)S(1)} %pack_blocks.3.refs_2_.refs_4_, ...), custom_call_target="tpu_custom_call" | custom-call | flops 402653184 | bytes 524288 | tf_op jit(solution)/shard_map/attend_0_4/pallas_call | solution.py:278
  13.1 0.0 collective-permute-done.3.refs_2_.refs_5_.refs_1_
  13.1 0.6 %collective-permute-done.1.refs_0_.refs_2_.refs_5_ = bf16[2,2,64,256]{3,2,1,0:T(8,128)(2,1)S(1)} collective-permute-done((bf16[2,2,64,256]{3,2,1,0:T(8,128)(2,1)S(1)}, bf16[2,2,64,256]{3,2,1,0:T(8,128)(2,1)S(1)}, u32[]{:S(2)}, u32[]{:S(2)}) %collective-permute-start.1) | collective-permute-done | bytes 131104 | tf_op jit(solution)/shard_map/ppermute | solution.py:383
  13.7 0.0 collective-permute-done.5.refs_4_.refs_7_.refs_3_
  13.7 1.9 %collective-permute-start.6 = (bf16[2,2,64,256]{3,2,1,0:T(8,128)(2,1)S(1)}, bf16[2,2,64,256]{3,2,1,0:T(8,128)(2,1)S(1)}, u32[]{:S(2)}, u32[]{:S(2)}) collective-permute-start(bf16[2,2,64,256]{3,2,1,0:T(8,128)(2,1)S(1)} %pack_blocks.4), channel_id=1, source_target_pairs={{0,16},{2,18},{4,20},{6,22},{8,10},{10,8},{12,14},{14,12},{16,0},{... | collective-permute-start | bytes 393224 | tf_op jit(solution)/shard_map/ppermute | solution.py:383
  15.7 0.0 collective-permute-start.9
  15.7 0.0 collective-permute-done.7.refs_3_.refs_6_
  15.7 0.5 %collective-permute-start.10 = (bf16[2,2,64,256]{3,2,1,0:T(8,128)(2,1)S(1)}, bf16[2,2,64,256]{3,2,1,0:T(8,128)(2,1)S(1)}, u32[]{:S(2)}, u32[]{:S(2)}) collective-permute-start(bf16[2,2,64,256]{3,2,1,0:T(8,128)(2,1)S(1)} %collective-permute-done.7.refs_3_.refs_6_), channel_id=1, source_target_pairs={{0,8},{2,10},{4,12},{6,14},{8,0},{10,2},{12,4},{14,6},{16,24},{18,... | collective-permute-start | bytes 393224 | tf_op jit(solution)/shard_map/ppermute | solution.py:35
  16.2 1.7 %attend_1_2.1 = (f32[1024,128]{1,0:T(8,128)S(1)}, f32[1024,256]{1,0:T(8,128)S(1)}, f32[1024,128]{1,0:T(8,128)S(1)}, f32[1024,256]{1,0:T(8,128)S(1)}) custom-call(bf16[64,2048]{1,0:T(8,128)(2,1)S(1)} %get-tuple-element.23.refs_0_, bf16[64,2048]{1,0:T(8,128)(2,1)S(1)} %get-tuple-element.24.refs_1_, ...), custom_call_target="tpu_custom_call" | custom-call | flops 402653184 | bytes 524288 | tf_op jit(solution)/shard_map/attend_1_2/pallas_call | solution.py:278
  17.9 0.9 %collective-permute-done.6.refs_0_.refs_2_.refs_7_ = bf16[2,2,64,256]{3,2,1,0:T(8,128)(2,1)S(1)} collective-permute-done((bf16[2,2,64,256]{3,2,1,0:T(8,128)(2,1)S(1)}, bf16[2,2,64,256]{3,2,1,0:T(8,128)(2,1)S(1)}, u32[]{:S(2)}, u32[]{:S(2)}) %collective-permute-start.6) | collective-permute-done | bytes 131104 | tf_op jit(solution)/shard_map/ppermute | solution.py:383
  18.8 0.1 collective-permute-start.8
  18.9 0.0 collective-permute-done.9.refs_2_.refs_9_
  18.9 0.0 collective-permute-done.10.refs_3_.refs_10_
  18.9 1.0 %attend_5_6.1 = (f32[1024,128]{1,0:T(8,128)S(1)}, f32[1024,256]{1,0:T(8,128)S(1)}, f32[1024,128]{1,0:T(8,128)S(1)}, f32[1024,256]{1,0:T(8,128)S(1)}) custom-call(bf16[64,2048]{1,0:T(8,128)(2,1)S(1)} %get-tuple-element.23.refs_0_, bf16[64,2048]{1,0:T(8,128)(2,1)S(1)} %get-tuple-element.24.refs_1_, ...), custom_call_target="tpu_custom_call" | custom-call | flops 402653184 | bytes 524288 | tf_op jit(solution)/shard_map/attend_5_6/pallas_call | solution.py:278
  19.9 0.3 %collective-permute-done.8.refs_3_.refs_11_ = bf16[2,2,64,256]{3,2,1,0:T(8,128)(2,1)S(1)} collective-permute-done((bf16[2,2,64,256]{3,2,1,0:T(8,128)(2,1)S(1)}, bf16[2,2,64,256]{3,2,1,0:T(8,128)(2,1)S(1)}, u32[]{:S(2)}, u32[]{:S(2)}) %collective-permute-start.8) | collective-permute-done | bytes 131104 | tf_op jit(solution)/shard_map/ppermute | solution.py:35
  20.2 1.0 %step_logits.1 = f32[1,8]{1,0:T(1,128)S(1)} custom-call(s32[1,8]{1,0:T(1,128)S(1)} %get-tuple-element.32.refs_4_.ends_ref, f32[1,2048]{1,0:T(1,128)S(1)} %get-tuple-element.42.head_ref, bf16[3,64,256]{2,1,0:T(8,128)(2,1)S(1)} %get-tuple-element.27.refs_4_.refs_0_, bf16[3,64,256]{2,1,0:T(8,128)(2,1)S(1)} %collective-permute-done.3.refs_2_.refs_5_.refs_1_, ...), custom_call_target="tpu_custom_call" | custom-call | flops 125829120 | bytes 163840 | tf_op jit(solution)/shard_map/step_logits/pallas_call | solution.py:355
  21.2 1.8 %collective-permute-start.11 = (f32[1,8]{1,0:T(1,128)S(1)}, f32[1,8]{1,0:T(1,128)S(1)}, u32[]{:S(2)}, u32[]{:S(2)}) collective-permute-start(f32[1,8]{1,0:T(1,128)S(1)} %step_logits.1), channel_id=1, source_target_pairs={{0,1},{1,0},{2,3},{3,2},{4,5},{5,4},{6,7},{7,6},{8,9},{9,8},{10,11... | collective-permute-start | bytes 104 | tf_op jit(solution)/shard_map/ppermute | solution.py:35
  23.0 1.9 %attend_3_7.1 = (bf16[64,2048]{1,0:T(8,128)(2,1)}, bf16[64,2048]{1,0:T(8,128)(2,1)}) custom-call(bf16[64,2048]{1,0:T(8,128)(2,1)S(1)} %get-tuple-element.23.refs_0_, bf16[64,2048]{1,0:T(8,128)(2,1)S(1)} %get-tuple-element.24.refs_1_, bf16[2,2,64,256]{3,2,1,0:T(8,128)(2,1)S(1)} %collective-permute-done.6.refs_0_.refs_2_.refs_7_, ...), custom_call_target="tpu_custom_call" | custom-call | flops 402653184 | bytes 524288 | tf_op jit(solution)/shard_map/attend_3_7/pallas_call | solution.py:278
  24.9 0.0 collective-permute-done.11
  24.9 0.5 %add.3 = f32[1,8]{1,0:T(1,128)} add(f32[1,8]{1,0:T(1,128)S(1)} %step_logits.1, f32[1,8]{1,0:T(1,128)S(1)} %collective-permute-done.11) | non-fusion elementwise | flops 8 | bytes 96 | tf_op jit(solution)/shard_map/add | solution.py:406
  (3 shorter events, 0.0 us)
Async XLA Ops:
  0.6 8.0 %collective-permute-start = (bf16[1,2,64,256]{3,2,1,0:T(8,128)(2,1)}, bf16[1,2,64,256]{3,2,1,0:T(8,128)(2,1)S(1)}, u32[]{:S(2)}, u32[]{:S(2)}) collective-permute-start(bf16[1,2,64,256]{3,2,1,0:T(8,128)(2,1)} %bitcast.9), channel_id=1, source_target_pairs={{0,4},{2,6},{4,0},{6,2},{8,12},{10,14},{12,8},{14,10},{16,20},{18,... | collective-permute-start | bytes 196616 | tf_op jit(solution)/shard_map/ppermute | solution.py:35
  6.0 4.7 %collective-permute-start.4 = (bf16[3,64,256]{2,1,0:T(8,128)(2,1)S(1)}, bf16[3,64,256]{2,1,0:T(8,128)(2,1)S(1)}, u32[]{:S(2)}, u32[]{:S(2)}) collective-permute-start(bf16[3,64,256]{2,1,0:T(8,128)(2,1)S(1)} %get-tuple-element.27.refs_4_.refs_0_), channel_id=1, source_target_pairs={{0,16},{8,24},{16,0},{24,8},{1,17},{9,25},{17,1},{25,9},{2,18},{10... | collective-permute-start | bytes 294920 | tf_op jit(solution)/shard_map/ppermute | solution.py:35
  8.6 3.6 %collective-permute-start.2 = (bf16[2,2,64,256]{3,2,1,0:T(8,128)(2,1)S(1)}, bf16[2,2,64,256]{3,2,1,0:T(8,128)(2,1)S(1)}, u32[]{:S(2)}, u32[]{:S(2)}) collective-permute-start(bf16[2,2,64,256]{3,2,1,0:T(8,128)(2,1)S(1)} %pack_blocks.3.refs_2_.refs_4_), channel_id=1, source_target_pairs={{0,8},{2,10},{4,12},{6,14},{8,0},{10,2},{12,4},{14,6},{16,24},{18,... | collective-permute-start | bytes 393224 | tf_op jit(solution)/shard_map/ppermute | solution.py:35
  8.7 5.0 %collective-permute-start.1 = (bf16[2,2,64,256]{3,2,1,0:T(8,128)(2,1)S(1)}, bf16[2,2,64,256]{3,2,1,0:T(8,128)(2,1)S(1)}, u32[]{:S(2)}, u32[]{:S(2)}) collective-permute-start(bf16[2,2,64,256]{3,2,1,0:T(8,128)(2,1)S(1)} %pack_blocks.3.refs_2_.refs_4_), channel_id=1, source_target_pairs={{0,2},{2,0},{4,6},{6,4},{8,24},{10,26},{12,28},{14,30},{16,18},{18... | collective-permute-start | bytes 393224 | tf_op jit(solution)/shard_map/ppermute | solution.py:383
  9.4 3.7 %collective-permute-start.3 = (bf16[3,64,256]{2,1,0:T(8,128)(2,1)S(1)}, bf16[3,64,256]{2,1,0:T(8,128)(2,1)S(1)}, u32[]{:S(2)}, u32[]{:S(2)}) collective-permute-start(bf16[3,64,256]{2,1,0:T(8,128)(2,1)S(1)} %get-tuple-element.27.refs_4_.refs_0_), channel_id=1, source_target_pairs={{0,8},{8,0},{16,24},{24,16},{1,9},{9,1},{17,25},{25,17},{2,10},{10... | collective-permute-start | bytes 294920 | tf_op jit(solution)/shard_map/ppermute | solution.py:35
  10.7 3.1 %collective-permute-start.5 = (bf16[3,64,256]{2,1,0:T(8,128)(2,1)S(1)}, bf16[3,64,256]{2,1,0:T(8,128)(2,1)S(1)}, u32[]{:S(2)}, u32[]{:S(2)}) collective-permute-start(bf16[3,64,256]{2,1,0:T(8,128)(2,1)S(1)} %collective-permute-done.4.refs_3_.refs_6_.refs_2_), channel_id=1, source_target_pairs={{0,8},{8,0},{16,24},{24,16},{1,9},{9,1},{17,25},{25,17},{2,10},{10... | collective-permute-start | bytes 294920 | tf_op jit(solution)/shard_map/ppermute | solution.py:35
  10.7 5.0 %collective-permute-start.7 = (bf16[2,2,64,256]{3,2,1,0:T(8,128)(2,1)S(1)}, bf16[2,2,64,256]{3,2,1,0:T(8,128)(2,1)S(1)}, u32[]{:S(2)}, u32[]{:S(2)}) collective-permute-start(bf16[2,2,64,256]{3,2,1,0:T(8,128)(2,1)S(1)} %pack_blocks.3.refs_2_.refs_4_), channel_id=1, source_target_pairs={{0,16},{2,18},{4,20},{6,22},{8,10},{10,8},{12,14},{14,12},{16,0},{... | collective-permute-start | bytes 393224 | tf_op jit(solution)/shard_map/ppermute | solution.py:383
  13.7 5.0 %collective-permute-start.6 = (bf16[2,2,64,256]{3,2,1,0:T(8,128)(2,1)S(1)}, bf16[2,2,64,256]{3,2,1,0:T(8,128)(2,1)S(1)}, u32[]{:S(2)}, u32[]{:S(2)}) collective-permute-start(bf16[2,2,64,256]{3,2,1,0:T(8,128)(2,1)S(1)} %pack_blocks.4), channel_id=1, source_target_pairs={{0,16},{2,18},{4,20},{6,22},{8,10},{10,8},{12,14},{14,12},{16,0},{... | collective-permute-start | bytes 393224 | tf_op jit(solution)/shard_map/ppermute | solution.py:383
  15.7 3.2 %collective-permute-start.9 = (bf16[2,2,64,256]{3,2,1,0:T(8,128)(2,1)S(1)}, bf16[2,2,64,256]{3,2,1,0:T(8,128)(2,1)S(1)}, u32[]{:S(2)}, u32[]{:S(2)}) collective-permute-start(bf16[2,2,64,256]{3,2,1,0:T(8,128)(2,1)S(1)} %collective-permute-done.1.refs_0_.refs_2_.refs_5_), channel_id=1, source_target_pairs={{0,8},{2,10},{4,12},{6,14},{8,0},{10,2},{12,4},{14,6},{16,24},{18,... | collective-permute-start | bytes 393224 | tf_op jit(solution)/shard_map/ppermute | solution.py:35
  15.7 3.2 %collective-permute-start.10 = (bf16[2,2,64,256]{3,2,1,0:T(8,128)(2,1)S(1)}, bf16[2,2,64,256]{3,2,1,0:T(8,128)(2,1)S(1)}, u32[]{:S(2)}, u32[]{:S(2)}) collective-permute-start(bf16[2,2,64,256]{3,2,1,0:T(8,128)(2,1)S(1)} %collective-permute-done.7.refs_3_.refs_6_), channel_id=1, source_target_pairs={{0,8},{2,10},{4,12},{6,14},{8,0},{10,2},{12,4},{14,6},{16,24},{18,... | collective-permute-start | bytes 393224 | tf_op jit(solution)/shard_map/ppermute | solution.py:35
  18.8 1.4 %collective-permute-start.8 = (bf16[2,2,64,256]{3,2,1,0:T(8,128)(2,1)S(1)}, bf16[2,2,64,256]{3,2,1,0:T(8,128)(2,1)S(1)}, u32[]{:S(2)}, u32[]{:S(2)}) collective-permute-start(bf16[2,2,64,256]{3,2,1,0:T(8,128)(2,1)S(1)} %pack_blocks.5), channel_id=1, source_target_pairs={{0,8},{2,10},{4,12},{6,14},{8,0},{10,2},{12,4},{14,6},{16,24},{18,... | collective-permute-start | bytes 393224 | tf_op jit(solution)/shard_map/ppermute | solution.py:35
  21.2 3.7 %collective-permute-start.11 = (f32[1,8]{1,0:T(1,128)S(1)}, f32[1,8]{1,0:T(1,128)S(1)}, u32[]{:S(2)}, u32[]{:S(2)}) collective-permute-start(f32[1,8]{1,0:T(1,128)S(1)} %step_logits.1), channel_id=1, source_target_pairs={{0,1},{1,0},{2,3},{3,2},{4,5},{5,4},{6,7},{7,6},{8,9},{9,8},{10,11... | collective-permute-start | bytes 104 | tf_op jit(solution)/shard_map/ppermute | solution.py:35

commit v17 on v14

--- a/solution.py
+++ b/solution.py
@@ -13,7 +13,7 @@
 SUBLANES = 8
 NEG_FILL = -1e30
 SCALE = HEADDIM ** -0.5 * math.log2(math.e)
-ROW_TILE = 256
+ROW_TILE = 512
 VMEM_LIMIT = 28 * 1024 * 1024
 PARAMS = pltpu.CompilerParams(vmem_limit_bytes=VMEM_LIMIT)
 PROMPT_AXES = ("ctx", "cand")

time: 25.5 us -> 25.5 us (level)
  waiting for transfers between devices: 2.87 us -> 3.35 us
  Pallas kernels: 7.66 us -> 7.2 us
    ppermute x3, waiting for transfers between devices: 1.48 us -> 1.97 us  [shared_out(): lax.ppermute(block, PROMPT_AXES, [(i, i ^ (odd if i & core else even)) fo...]
    pallas_call x4, Pallas kernels: 5.4 us -> 4.94 us  [phase(): pl.pallas_call(functools.partial(phase_kernel, sizes, arrays, masks, firs...]
  transfers between devices with their start and end apart: 12 -> 12, of which waited for: 4 -> 4; matrix products, arithmetic and copies ran while one was open for 0% -> 0% of each run, Pallas kernels for 26% -> 25%
where the time goes in v17:
time: 25.5 us; the launch traced here: 25.3 us
  starting transfers between devices  13.5 us (53%)
  Pallas kernels  7.2 us (28%)
  waiting for transfers between devices  3.35 us (13%)
  between operations  0.72 us (3%)
  other arithmetic  0.51 us (2%)
    ppermute x9, starting transfers between devices, flipped(): return lax.ppermute(block, axes, [(i, i ^ bit) for i in range(size)])  9.37 us
    pallas_call x4, Pallas kernels, phase(): pl.pallas_call(functools.partial(phase_kernel, sizes, arrays, masks, firs...  4.94 us
    ppermute x3, starting transfers between devices, shared_out(): lax.ppermute(block, PROMPT_AXES, [(i, i ^ (odd if i & core else even)) fo...  4.17 us
    ppermute x3, waiting for transfers between devices, shared_out(): lax.ppermute(block, PROMPT_AXES, [(i, i ^ (odd if i & core else even)) fo...  1.97 us
    ppermute x9, waiting for transfers between devices, flipped(): return lax.ppermute(block, axes, [(i, i ^ bit) for i in range(size)])  1.38 us
    pallas_call x1, Pallas kernels, staged(): pl.pallas_call(stage_kernel, out_shape=(like(prompt_q), like(cand_q), lik...  1.24 us
    pallas_call x1, Pallas kernels, step_shares(): pl.pallas_call(functools.partial(step_kernel, sizes, [mask for _, mask in...  0.99 us
    add x1, other arithmetic, per_device(): step_logits = step_logits + flipped(step_logits, 'tp', tp_size, bit)  0.51 us
  transfers between devices with their start and end apart: 12, of which 4 were waited for; matrix products, arithmetic and copies ran while one was open for 0% of the time, Pallas kernels for 25%

profile of v17, /device:TPU:0, one launch (start us, length us, event | category | flops | bytes accessed | tf_op | source)
XLA Modules:
  0.0 25.3 jit_solution(5149560699132932434)
XLA Ops:
  0.6 4.1 %collective-permute-start = (bf16[1,2,64,256]{3,2,1,0:T(8,128)(2,1)}, bf16[1,2,64,256]{3,2,1,0:T(8,128)(2,1)S(1)}, u32[]{:S(2)}, u32[]{:S(2)}) collective-permute-start(bf16[1,2,64,256]{3,2,1,0:T(8,128)(2,1)} %bitcast.9), channel_id=1, source_target_pairs={{0,4},{2,6},{4,0},{6,2},{8,12},{10,14},{12,8},{14,10},{16,20},{18,... | collective-permute-start | bytes 196616 | tf_op jit(solution)/shard_map/ppermute | solution.py:35
  4.7 1.2 %stage_operands.1 = (bf16[64,2048]{1,0:T(8,128)(2,1)S(1)}, bf16[64,2048]{1,0:T(8,128)(2,1)S(1)}, bf16[2,64,256]{2,1,0:T(8,128)(2,1)S(1)}, bf16[3,64,256]{2,1,0:T...) custom-call(bf16[64,2048]{1,0:T(8,128)(2,1)} %prompt_q.1, bf16[64,2048]{1,0:T(8,128)(2,1)} %bitcast.7, ...), custom_call_target="tpu_custom_call" | custom-call | tf_op jit(solution)/shard_map/stage_operands/pallas_call | solution.py:127
  6.0 1.6 %collective-permute-start.4 = (bf16[3,64,256]{2,1,0:T(8,128)(2,1)S(1)}, bf16[3,64,256]{2,1,0:T(8,128)(2,1)S(1)}, u32[]{:S(2)}, u32[]{:S(2)}) collective-permute-start(bf16[3,64,256]{2,1,0:T(8,128)(2,1)S(1)} %get-tuple-element.27.refs_4_.refs_0_), channel_id=1, source_target_pairs={{0,16},{8,24},{16,0},{24,8},{1,17},{9,25},{17,1},{25,9},{2,18},{10... | collective-permute-start | bytes 294920 | tf_op jit(solution)/shard_map/ppermute | solution.py:35
  7.6 1.0 %collective-permute-done.refs_1_ = bf16[1,2,64,256]{3,2,1,0:T(8,128)(2,1)S(1)} collective-permute-done((bf16[1,2,64,256]{3,2,1,0:T(8,128)(2,1)}, bf16[1,2,64,256]{3,2,1,0:T(8,128)(2,1)S(1)}, u32[]{:S(2)}, u32[]{:S(2)}) %collective-permute-start) | collective-permute-done | bytes 65568 | tf_op jit(solution)/shard_map/ppermute | solution.py:35
  8.6 0.1 collective-permute-start.2
  8.7 0.7 %collective-permute-start.1 = (bf16[2,2,64,256]{3,2,1,0:T(8,128)(2,1)S(1)}, bf16[2,2,64,256]{3,2,1,0:T(8,128)(2,1)S(1)}, u32[]{:S(2)}, u32[]{:S(2)}) collective-permute-start(bf16[2,2,64,256]{3,2,1,0:T(8,128)(2,1)S(1)} %pack_blocks.3.refs_2_.refs_4_), channel_id=1, source_target_pairs={{0,2},{2,0},{4,6},{6,4},{8,24},{10,26},{12,28},{14,30},{16,18},{18... | collective-permute-start | bytes 393224 | tf_op jit(solution)/shard_map/ppermute | solution.py:381
  9.4 1.2 %collective-permute-start.3 = (bf16[3,64,256]{2,1,0:T(8,128)(2,1)S(1)}, bf16[3,64,256]{2,1,0:T(8,128)(2,1)S(1)}, u32[]{:S(2)}, u32[]{:S(2)}) collective-permute-start(bf16[3,64,256]{2,1,0:T(8,128)(2,1)S(1)} %get-tuple-element.27.refs_4_.refs_0_), channel_id=1, source_target_pairs={{0,8},{8,0},{16,24},{24,16},{1,9},{9,1},{17,25},{25,17},{2,10},{10... | collective-permute-start | bytes 294920 | tf_op jit(solution)/shard_map/ppermute | solution.py:35
  10.6 0.0 collective-permute-done.4.refs_3_.refs_6_.refs_2_
  10.7 0.0 collective-permute-start.5
  10.7 1.5 %collective-permute-start.7 = (bf16[2,2,64,256]{3,2,1,0:T(8,128)(2,1)S(1)}, bf16[2,2,64,256]{3,2,1,0:T(8,128)(2,1)S(1)}, u32[]{:S(2)}, u32[]{:S(2)}) collective-permute-start(bf16[2,2,64,256]{3,2,1,0:T(8,128)(2,1)S(1)} %pack_blocks.3.refs_2_.refs_4_), channel_id=1, source_target_pairs={{0,16},{2,18},{4,20},{6,22},{8,10},{10,8},{12,14},{14,12},{16,0},{... | collective-permute-start | bytes 393224 | tf_op jit(solution)/shard_map/ppermute | solution.py:381
  12.2 0.0 collective-permute-done.2.refs_3_.refs_8_
  12.2 0.9 %attend_0_4.1 = (f32[1024,128]{1,0:T(8,128)S(1)}, f32[1024,256]{1,0:T(8,128)S(1)}, f32[1024,128]{1,0:T(8,128)S(1)}, f32[1024,256]{1,0:T(8,128)S(1)}) custom-call(bf16[64,2048]{1,0:T(8,128)(2,1)S(1)} %get-tuple-element.23.refs_0_, bf16[64,2048]{1,0:T(8,128)(2,1)S(1)} %get-tuple-element.24.refs_1_, bf16[2,2,64,256]{3,2,1,0:T(8,128)(2,1)S(1)} %pack_blocks.3.refs_2_.refs_4_, ...), custom_call_target="tpu_custom_call" | custom-call | flops 402653184 | bytes 524288 | tf_op jit(solution)/shard_map/attend_0_4/pallas_call | solution.py:276
  13.1 0.0 collective-permute-done.3.refs_2_.refs_5_.refs_1_
  13.1 0.6 %collective-permute-done.1.refs_0_.refs_2_.refs_5_ = bf16[2,2,64,256]{3,2,1,0:T(8,128)(2,1)S(1)} collective-permute-done((bf16[2,2,64,256]{3,2,1,0:T(8,128)(2,1)S(1)}, bf16[2,2,64,256]{3,2,1,0:T(8,128)(2,1)S(1)}, u32[]{:S(2)}, u32[]{:S(2)}) %collective-permute-start.1) | collective-permute-done | bytes 131104 | tf_op jit(solution)/shard_map/ppermute | solution.py:381
  13.7 0.0 collective-permute-done.5.refs_4_.refs_7_.refs_3_
  13.7 1.9 %collective-permute-start.6 = (bf16[2,2,64,256]{3,2,1,0:T(8,128)(2,1)S(1)}, bf16[2,2,64,256]{3,2,1,0:T(8,128)(2,1)S(1)}, u32[]{:S(2)}, u32[]{:S(2)}) collective-permute-start(bf16[2,2,64,256]{3,2,1,0:T(8,128)(2,1)S(1)} %pack_blocks.4), channel_id=1, source_target_pairs={{0,16},{2,18},{4,20},{6,22},{8,10},{10,8},{12,14},{14,12},{16,0},{... | collective-permute-start | bytes 393224 | tf_op jit(solution)/shard_map/ppermute | solution.py:381
  15.7 0.0 collective-permute-start.9
  15.7 0.0 collective-permute-done.7.refs_3_.refs_6_
  15.7 0.5 %collective-permute-start.10 = (bf16[2,2,64,256]{3,2,1,0:T(8,128)(2,1)S(1)}, bf16[2,2,64,256]{3,2,1,0:T(8,128)(2,1)S(1)}, u32[]{:S(2)}, u32[]{:S(2)}) collective-permute-start(bf16[2,2,64,256]{3,2,1,0:T(8,128)(2,1)S(1)} %collective-permute-done.7.refs_3_.refs_6_), channel_id=1, source_target_pairs={{0,8},{2,10},{4,12},{6,14},{8,0},{10,2},{12,4},{14,6},{16,24},{18,... | collective-permute-start | bytes 393224 | tf_op jit(solution)/shard_map/ppermute | solution.py:35
  16.2 1.2 %attend_1_2.1 = (f32[1024,128]{1,0:T(8,128)S(1)}, f32[1024,256]{1,0:T(8,128)S(1)}, f32[1024,128]{1,0:T(8,128)S(1)}, f32[1024,256]{1,0:T(8,128)S(1)}) custom-call(bf16[64,2048]{1,0:T(8,128)(2,1)S(1)} %get-tuple-element.23.refs_0_, bf16[64,2048]{1,0:T(8,128)(2,1)S(1)} %get-tuple-element.24.refs_1_, ...), custom_call_target="tpu_custom_call" | custom-call | flops 402653184 | bytes 524288 | tf_op jit(solution)/shard_map/attend_1_2/pallas_call | solution.py:276
  17.4 1.4 %collective-permute-done.6.refs_0_.refs_2_.refs_7_ = bf16[2,2,64,256]{3,2,1,0:T(8,128)(2,1)S(1)} collective-permute-done((bf16[2,2,64,256]{3,2,1,0:T(8,128)(2,1)S(1)}, bf16[2,2,64,256]{3,2,1,0:T(8,128)(2,1)S(1)}, u32[]{:S(2)}, u32[]{:S(2)}) %collective-permute-start.6) | collective-permute-done | bytes 131104 | tf_op jit(solution)/shard_map/ppermute | solution.py:381
  18.8 0.1 collective-permute-start.8
  18.9 0.0 collective-permute-done.9.refs_2_.refs_9_
  18.9 0.0 collective-permute-done.10.refs_3_.refs_10_
  18.9 1.0 %attend_5_6.1 = (f32[1024,128]{1,0:T(8,128)S(1)}, f32[1024,256]{1,0:T(8,128)S(1)}, f32[1024,128]{1,0:T(8,128)S(1)}, f32[1024,256]{1,0:T(8,128)S(1)}) custom-call(bf16[64,2048]{1,0:T(8,128)(2,1)S(1)} %get-tuple-element.23.refs_0_, bf16[64,2048]{1,0:T(8,128)(2,1)S(1)} %get-tuple-element.24.refs_1_, ...), custom_call_target="tpu_custom_call" | custom-call | flops 402653184 | bytes 524288 | tf_op jit(solution)/shard_map/attend_5_6/pallas_call | solution.py:276
  19.9 0.3 %collective-permute-done.8.refs_3_.refs_11_ = bf16[2,2,64,256]{3,2,1,0:T(8,128)(2,1)S(1)} collective-permute-done((bf16[2,2,64,256]{3,2,1,0:T(8,128)(2,1)S(1)}, bf16[2,2,64,256]{3,2,1,0:T(8,128)(2,1)S(1)}, u32[]{:S(2)}, u32[]{:S(2)}) %collective-permute-start.8) | collective-permute-done | bytes 131104 | tf_op jit(solution)/shard_map/ppermute | solution.py:35
  20.2 1.0 %step_logits.1 = f32[1,8]{1,0:T(1,128)S(1)} custom-call(s32[1,8]{1,0:T(1,128)S(1)} %get-tuple-element.32.refs_4_.ends_ref, f32[1,2048]{1,0:T(1,128)S(1)} %get-tuple-element.42.head_ref, bf16[3,64,256]{2,1,0:T(8,128)(2,1)S(1)} %get-tuple-element.27.refs_4_.refs_0_, bf16[3,64,256]{2,1,0:T(8,128)(2,1)S(1)} %collective-permute-done.3.refs_2_.refs_5_.refs_1_, ...), custom_call_target="tpu_custom_call" | custom-call | flops 125829120 | bytes 163840 | tf_op jit(solution)/shard_map/step_logits/pallas_call | solution.py:353
  21.2 1.8 %collective-permute-start.11 = (f32[1,8]{1,0:T(1,128)S(1)}, f32[1,8]{1,0:T(1,128)S(1)}, u32[]{:S(2)}, u32[]{:S(2)}) collective-permute-start(f32[1,8]{1,0:T(1,128)S(1)} %step_logits.1), channel_id=1, source_target_pairs={{0,1},{1,0},{2,3},{3,2},{4,5},{5,4},{6,7},{7,6},{8,9},{9,8},{10,11... | collective-permute-start | bytes 104 | tf_op jit(solution)/shard_map/ppermute | solution.py:35
  23.0 1.8 %attend_3_7.1 = (bf16[64,2048]{1,0:T(8,128)(2,1)}, bf16[64,2048]{1,0:T(8,128)(2,1)}) custom-call(bf16[64,2048]{1,0:T(8,128)(2,1)S(1)} %get-tuple-element.23.refs_0_, bf16[64,2048]{1,0:T(8,128)(2,1)S(1)} %get-tuple-element.24.refs_1_, bf16[2,2,64,256]{3,2,1,0:T(8,128)(2,1)S(1)} %collective-permute-done.6.refs_0_.refs_2_.refs_7_, ...), custom_call_target="tpu_custom_call" | custom-call | flops 402653184 | bytes 524288 | tf_op jit(solution)/shard_map/attend_3_7/pallas_call | solution.py:276
  24.8 0.0 collective-permute-done.11
  24.8 0.5 %add.3 = f32[1,8]{1,0:T(1,128)} add(f32[1,8]{1,0:T(1,128)S(1)} %step_logits.1, f32[1,8]{1,0:T(1,128)S(1)} %collective-permute-done.11) | non-fusion elementwise | flops 8 | bytes 96 | tf_op jit(solution)/shard_map/add | solution.py:404
  (3 shorter events, 0.0 us)
Async XLA Ops:
  0.6 8.0 %collective-permute-start = (bf16[1,2,64,256]{3,2,1,0:T(8,128)(2,1)}, bf16[1,2,64,256]{3,2,1,0:T(8,128)(2,1)S(1)}, u32[]{:S(2)}, u32[]{:S(2)}) collective-permute-start(bf16[1,2,64,256]{3,2,1,0:T(8,128)(2,1)} %bitcast.9), channel_id=1, source_target_pairs={{0,4},{2,6},{4,0},{6,2},{8,12},{10,14},{12,8},{14,10},{16,20},{18,... | collective-permute-start | bytes 196616 | tf_op jit(solution)/shard_map/ppermute | solution.py:35
  6.0 4.7 %collective-permute-start.4 = (bf16[3,64,256]{2,1,0:T(8,128)(2,1)S(1)}, bf16[3,64,256]{2,1,0:T(8,128)(2,1)S(1)}, u32[]{:S(2)}, u32[]{:S(2)}) collective-permute-start(bf16[3,64,256]{2,1,0:T(8,128)(2,1)S(1)} %get-tuple-element.27.refs_4_.refs_0_), channel_id=1, source_target_pairs={{0,16},{8,24},{16,0},{24,8},{1,17},{9,25},{17,1},{25,9},{2,18},{10... | collective-permute-start | bytes 294920 | tf_op jit(solution)/shard_map/ppermute | solution.py:35
  8.6 3.6 %collective-permute-start.2 = (bf16[2,2,64,256]{3,2,1,0:T(8,128)(2,1)S(1)}, bf16[2,2,64,256]{3,2,1,0:T(8,128)(2,1)S(1)}, u32[]{:S(2)}, u32[]{:S(2)}) collective-permute-start(bf16[2,2,64,256]{3,2,1,0:T(8,128)(2,1)S(1)} %pack_blocks.3.refs_2_.refs_4_), channel_id=1, source_target_pairs={{0,8},{2,10},{4,12},{6,14},{8,0},{10,2},{12,4},{14,6},{16,24},{18,... | collective-permute-start | bytes 393224 | tf_op jit(solution)/shard_map/ppermute | solution.py:35
  8.7 5.0 %collective-permute-start.1 = (bf16[2,2,64,256]{3,2,1,0:T(8,128)(2,1)S(1)}, bf16[2,2,64,256]{3,2,1,0:T(8,128)(2,1)S(1)}, u32[]{:S(2)}, u32[]{:S(2)}) collective-permute-start(bf16[2,2,64,256]{3,2,1,0:T(8,128)(2,1)S(1)} %pack_blocks.3.refs_2_.refs_4_), channel_id=1, source_target_pairs={{0,2},{2,0},{4,6},{6,4},{8,24},{10,26},{12,28},{14,30},{16,18},{18... | collective-permute-start | bytes 393224 | tf_op jit(solution)/shard_map/ppermute | solution.py:381
  9.4 3.7 %collective-permute-start.3 = (bf16[3,64,256]{2,1,0:T(8,128)(2,1)S(1)}, bf16[3,64,256]{2,1,0:T(8,128)(2,1)S(1)}, u32[]{:S(2)}, u32[]{:S(2)}) collective-permute-start(bf16[3,64,256]{2,1,0:T(8,128)(2,1)S(1)} %get-tuple-element.27.refs_4_.refs_0_), channel_id=1, source_target_pairs={{0,8},{8,0},{16,24},{24,16},{1,9},{9,1},{17,25},{25,17},{2,10},{10... | collective-permute-start | bytes 294920 | tf_op jit(solution)/shard_map/ppermute | solution.py:35
  10.7 3.1 %collective-permute-start.5 = (bf16[3,64,256]{2,1,0:T(8,128)(2,1)S(1)}, bf16[3,64,256]{2,1,0:T(8,128)(2,1)S(1)}, u32[]{:S(2)}, u32[]{:S(2)}) collective-permute-start(bf16[3,64,256]{2,1,0:T(8,128)(2,1)S(1)} %collective-permute-done.4.refs_3_.refs_6_.refs_2_), channel_id=1, source_target_pairs={{0,8},{8,0},{16,24},{24,16},{1,9},{9,1},{17,25},{25,17},{2,10},{10... | collective-permute-start | bytes 294920 | tf_op jit(solution)/shard_map/ppermute | solution.py:35
  10.7 5.0 %collective-permute-start.7 = (bf16[2,2,64,256]{3,2,1,0:T(8,128)(2,1)S(1)}, bf16[2,2,64,256]{3,2,1,0:T(8,128)(2,1)S(1)}, u32[]{:S(2)}, u32[]{:S(2)}) collective-permute-start(bf16[2,2,64,256]{3,2,1,0:T(8,128)(2,1)S(1)} %pack_blocks.3.refs_2_.refs_4_), channel_id=1, source_target_pairs={{0,16},{2,18},{4,20},{6,22},{8,10},{10,8},{12,14},{14,12},{16,0},{... | collective-permute-start | bytes 393224 | tf_op jit(solution)/shard_map/ppermute | solution.py:381
  13.7 5.0 %collective-permute-start.6 = (bf16[2,2,64,256]{3,2,1,0:T(8,128)(2,1)S(1)}, bf16[2,2,64,256]{3,2,1,0:T(8,128)(2,1)S(1)}, u32[]{:S(2)}, u32[]{:S(2)}) collective-permute-start(bf16[2,2,64,256]{3,2,1,0:T(8,128)(2,1)S(1)} %pack_blocks.4), channel_id=1, source_target_pairs={{0,16},{2,18},{4,20},{6,22},{8,10},{10,8},{12,14},{14,12},{16,0},{... | collective-permute-start | bytes 393224 | tf_op jit(solution)/shard_map/ppermute | solution.py:381
  15.7 3.2 %collective-permute-start.9 = (bf16[2,2,64,256]{3,2,1,0:T(8,128)(2,1)S(1)}, bf16[2,2,64,256]{3,2,1,0:T(8,128)(2,1)S(1)}, u32[]{:S(2)}, u32[]{:S(2)}) collective-permute-start(bf16[2,2,64,256]{3,2,1,0:T(8,128)(2,1)S(1)} %collective-permute-done.1.refs_0_.refs_2_.refs_5_), channel_id=1, source_target_pairs={{0,8},{2,10},{4,12},{6,14},{8,0},{10,2},{12,4},{14,6},{16,24},{18,... | collective-permute-start | bytes 393224 | tf_op jit(solution)/shard_map/ppermute | solution.py:35
  15.7 3.2 %collective-permute-start.10 = (bf16[2,2,64,256]{3,2,1,0:T(8,128)(2,1)S(1)}, bf16[2,2,64,256]{3,2,1,0:T(8,128)(2,1)S(1)}, u32[]{:S(2)}, u32[]{:S(2)}) collective-permute-start(bf16[2,2,64,256]{3,2,1,0:T(8,128)(2,1)S(1)} %collective-permute-done.7.refs_3_.refs_6_), channel_id=1, source_target_pairs={{0,8},{2,10},{4,12},{6,14},{8,0},{10,2},{12,4},{14,6},{16,24},{18,... | collective-permute-start | bytes 393224 | tf_op jit(solution)/shard_map/ppermute | solution.py:35
  18.8 1.4 %collective-permute-start.8 = (bf16[2,2,64,256]{3,2,1,0:T(8,128)(2,1)S(1)}, bf16[2,2,64,256]{3,2,1,0:T(8,128)(2,1)S(1)}, u32[]{:S(2)}, u32[]{:S(2)}) collective-permute-start(bf16[2,2,64,256]{3,2,1,0:T(8,128)(2,1)S(1)} %pack_blocks.5), channel_id=1, source_target_pairs={{0,8},{2,10},{4,12},{6,14},{8,0},{10,2},{12,4},{14,6},{16,24},{18,... | collective-permute-start | bytes 393224 | tf_op jit(solution)/shard_map/ppermute | solution.py:35
  21.2 3.6 %collective-permute-start.11 = (f32[1,8]{1,0:T(1,128)S(1)}, f32[1,8]{1,0:T(1,128)S(1)}, u32[]{:S(2)}, u32[]{:S(2)}) collective-permute-start(f32[1,8]{1,0:T(1,128)S(1)} %step_logits.1), channel_id=1, source_target_pairs={{0,1},{1,0},{2,3},{3,2},{4,5},{5,4},{6,7},{7,6},{8,9},{9,8},{10,11... | collective-permute-start | bytes 104 | tf_op jit(solution)/shard_map/ppermute | solution.py:35
